TPU v7x, 128 devices: a whole 4x4x4 slice. The times are simulated.
128 devices in a mesh: seq: 128 (over z, x, y, core).
Axes of the slice: x: 4, y: 4, z: 4, core: 2. Of those that a mesh axis runs over, the one named last changes fastest.
Arguments:
- block_input: float32 [16384, 2560], P('seq'), may hold values from -6 to 6
- cotangent: float32 [16384, 2560], P('seq'), may hold values from -6 to 6
- segments: int32 [16384], P('seq'), may hold values from 0 to 7, as said below
- adapter_index: int32 [8], replicated, may hold values from 0 to 7, each once
- norm_first: float32 [2560], replicated, may hold values from 0.5 to 1.5
- norm_second: float32 [2560], replicated, may hold values from 0.5 to 1.5
- conv_taps: float32 [4, 2560], replicated, may hold values from -3 to 3
- decay_rate: float32 [2560], replicated, may hold values from 7.6293945e-06 to 0.03
- gelu_proj: bfloat16 [2560, 2560], P('seq'), may hold values from -0.125 to 0.125
- input_proj: bfloat16 [2560, 2560], P('seq'), may hold values from -0.125 to 0.125
- inner_gate: bfloat16 [2560, 256], P('seq'), may hold values from -0.375 to 0.375
- decay_gate: bfloat16 [2560, 256], P('seq'), may hold values from -0.375 to 0.375
- output_proj: bfloat16 [2560, 2560], P('seq'), may hold values from -0.125 to 0.125
- widen_proj: bfloat16 [2560, 15360], P('seq'), may hold values from -0.125 to 0.125
- narrow_proj: bfloat16 [7680, 2560], P('seq'), may hold values from -0.0625 to 0.0625
- enter_square: bfloat16 [5, 2560, 128], replicated, may hold values from -0.125 to 0.125
- leave_square: bfloat16 [5, 128, 2560], replicated, may hold values from -1.5 to 1.5
- enter_widen: bfloat16 [2560, 128], replicated, may hold values from -0.125 to 0.125
- leave_widen: bfloat16 [128, 15360], replicated, may hold values from -1.5 to 1.5
- enter_narrow: bfloat16 [7680, 128], replicated, may hold values from -0.0625 to 0.0625
- leave_narrow: bfloat16 [128, 2560], replicated, may hold values from -1.5 to 1.5
Outputs:
- block_output: float32 [16384, 2560], P('seq')
- input_grad: float32 [16384, 2560], P('seq')
- grad_enter_square: float32 [5, 2560, 128], replicated
- grad_leave_square: float32 [5, 128, 2560], replicated
- grad_enter_widen: float32 [2560, 128], replicated
- grad_leave_widen: float32 [128, 15360], replicated
- grad_enter_narrow: float32 [7680, 128], replicated
- grad_leave_narrow: float32 [128, 2560], replicated
Inputs may be any that keep to these rules, and one draw needn't show every extreme that they name: `segments`: document numbers never fall along the tokens and every number is used; documents 0 to 2 lie within the first 128 tokens, documents 4 to 7 within the last 128 tokens, and document 3 covers all tokens between. `adapter_index`: each document uses an adapter of its own.
All inputs are finite; a program needn't handle non-finite values.
Results may differ from a plain program's by a relative error of at most 0.017.
Values may be sent and summed in bfloat16 or wider, within the bound.
No kernel may reach another device: no remote copies, remote signals or barrier semaphores. Data moves between devices by JAX's collectives and lax.ppermute only.
A program may use at most 512 MiB of HBM per device.

v0:
```python
import jax
import jax.numpy as jnp
from jax import lax
from jax.sharding import PartitionSpec as P

HEADS = 10
ADAPTERS = 8


eps_norm = 1e-06
floor_scale = 0.001


def from_behind(value, axis, by):
    devices = lax.axis_size(axis)
    pairs = [(i, i + by) for i in range(devices) if 0 <= i + by < devices]
    return lax.ppermute(value, axis, pairs)


def carried_in(value, axis, combine, identity, reverse):
    devices, here = (lax.axis_size(axis), lax.axis_index(axis))
    everything = jax.tree.map(lambda part: lax.all_gather(part, axis), value)
    start = jax.tree.map(
        lambda part, zero: jnp.broadcast_to(jnp.asarray(zero, part.dtype), part.shape),
        value,
        identity,
    )

    def hop(k, before):
        at = devices - 1 - k if reverse else k
        reached = at > here if reverse else at < here
        new = combine(before, jax.tree.map(lambda part: part[at], everything))
        return jax.tree.map(lambda a, b: jnp.where(reached, a, b), new, before)

    return lax.fori_loop(0, devices, hop, start)


def stacked_forward(values, stacked):
    pieces = values.reshape(values.shape[0], stacked.shape[0], stacked.shape[1])
    return jnp.einsum("tnr,nrj->tj", pieces, stacked, preferred_element_type=jnp.float32)


def stacked_back(grad_rows, stacked):
    result = jnp.einsum("tj,nrj->tnr", grad_rows, stacked, preferred_element_type=jnp.float32)
    return result.reshape(grad_rows.shape[0], -1)


def forward_dot(left_side, right_side):
    return jnp.dot(left_side, right_side, preferred_element_type=jnp.float32)


def back_dot(left_side, right_side):
    return lax.dot_general(
        left_side, right_side, (((1,), (1,)), ((), ())), preferred_element_type=jnp.float32
    )


def grad_dot(left_side, right_side):
    return lax.dot_general(
        left_side, right_side, (((0,), (0,)), ((), ())), preferred_element_type=jnp.float32
    )


def rms_scale(values, gain):
    return values * lax.rsqrt(jnp.mean(values * values, axis=-1, keepdims=True) + eps_norm) * gain


def flat_gate(stacked):
    return stacked.reshape(stacked.shape[0] * stacked.shape[1], stacked.shape[2])


def block_apply(values, weight):
    head_rows = values.reshape(values.shape[0], HEADS, -1)
    shaped = weight.reshape(HEADS, -1, weight.shape[1])
    return jnp.einsum(
        "thi,hij->thj", head_rows, shaped, preferred_element_type=jnp.float32
    ).reshape(values.shape[0], -1)


def block_back(grad_rows, weight):
    head_rows = grad_rows.reshape(grad_rows.shape[0], HEADS, -1)
    shaped = weight.reshape(HEADS, -1, weight.shape[1])
    return jnp.einsum(
        "thj,hij->thi", head_rows, shaped, preferred_element_type=jnp.float32
    ).reshape(grad_rows.shape[0], -1)


def adapt_forward(inputs, base_term, down_map, up_map, select):
    latent = forward_dot(inputs, down_map)
    picked = (latent * select).astype(jnp.bfloat16)
    return (base_term + forward_dot(picked, up_map), picked)


def adapt_backward(grad_rows, inputs, picked, weight_term, down_map, up_map, select):
    grad_latent = (back_dot(grad_rows, up_map) * select).astype(jnp.bfloat16)
    grad_up = grad_dot(picked, grad_rows)
    grad_down = grad_dot(inputs, grad_latent)
    return (weight_term + back_dot(grad_latent, down_map), grad_down, grad_up)


def linked(former, latter):
    return (former[0] * latter[0], latter[0] * former[1] + latter[1])


def recur_inputs(inner_pre, decay_pre, convolved, retain, decay_rate):
    gate_in = jax.nn.sigmoid(inner_pre)
    log_decay = -8.0 * decay_rate * jax.nn.sigmoid(decay_pre)
    decays = jnp.exp(log_decay) * retain
    scale = jnp.where(
        retain > 0.5, jnp.sqrt(jnp.maximum(-jnp.expm1(2.0 * log_decay), floor_scale)), 1.0
    )
    return (decays, convolved * gate_in * scale)


def gelu_tanh(values):
    return jax.nn.gelu(values, approximate=True)


def per_device(
    block_input,
    cotangent,
    segments,
    adapter_index,
    norm_first,
    norm_second,
    conv_taps,
    decay_rate,
    gelu_proj,
    input_proj,
    inner_gate,
    decay_gate,
    output_proj,
    widen_proj,
    narrow_proj,
    enter_square,
    leave_square,
    enter_widen,
    leave_widen,
    enter_narrow,
    leave_narrow,
):
    gathered = (
        lax.all_gather(gelu_proj[None], "seq", axis=0, tiled=True),
        lax.all_gather(input_proj[None], "seq", axis=0, tiled=True),
        lax.all_gather(inner_gate[None], "seq", axis=0, tiled=True),
        lax.all_gather(decay_gate[None], "seq", axis=0, tiled=True),
        lax.all_gather(output_proj[None], "seq", axis=0, tiled=True),
        lax.all_gather(widen_proj[None], "seq", axis=0, tiled=True),
        lax.all_gather(narrow_proj[None], "seq", axis=0, tiled=True),
    )
    inner_full = flat_gate(gathered[2])
    decay_full = flat_gate(gathered[3])
    rows_here = block_input.shape[0]
    model_width = block_input.shape[1]
    columns = enter_square.shape[-1]
    rank_size = columns // ADAPTERS
    doc_count = adapter_index.shape[0]
    owners = jnp.sum(
        (segments[:, None] == jnp.arange(doc_count)[None, :]).astype(jnp.int32)
        * adapter_index[None, :],
        axis=1,
    )
    select = (owners[:, None] == (jnp.arange(columns) // rank_size)[None, :]).astype(jnp.float32)
    unit_row = jnp.ones((model_width,), jnp.float32)
    zero_row = jnp.zeros((model_width,), jnp.float32)
    normed = rms_scale(block_input, norm_first).astype(jnp.bfloat16)
    gelu_pre, gelu_pick = adapt_forward(
        normed, stacked_forward(normed, gathered[0]), enter_square[0], leave_square[0], select
    )
    branch, gelu_pull = jax.vjp(gelu_tanh, gelu_pre)
    filler, filler_pick = adapt_forward(
        normed, stacked_forward(normed, gathered[1]), enter_square[1], leave_square[1], select
    )
    lead_rows = conv_taps.shape[0] - 1
    doc_marks = (segments + 1).astype(jnp.float32)
    prev_rows, prev_marks = from_behind(
        (filler[rows_here - lead_rows :], doc_marks[rows_here - lead_rows :]), "seq", 1
    )
    lagged = jnp.concatenate([prev_rows, filler], axis=0)
    marks_all = jnp.concatenate([prev_marks, doc_marks], axis=0)
    combined = conv_taps[0] * filler
    same_docs = []
    for offset in range(1, lead_rows + 1):
        same_doc = (
            marks_all[lead_rows - offset : lead_rows - offset + rows_here] == doc_marks
        ).astype(jnp.float32)[:, None]
        same_docs.append(same_doc)
        combined = (
            combined
            + conv_taps[offset]
            * lagged[lead_rows - offset : lead_rows - offset + rows_here]
            * same_doc
        )
    convolved = combined.astype(jnp.bfloat16)
    conv_wide = convolved.astype(jnp.float32)
    retain = same_docs[0]
    inner_pre, inner_pick = adapt_forward(
        convolved, block_apply(convolved, inner_full), enter_square[2], leave_square[2], select
    )
    decay_pre, decay_pick = adapt_forward(
        convolved, block_apply(convolved, decay_full), enter_square[3], leave_square[3], select
    )

    def recur_local(pre_in, pre_decay, conv_values):
        return recur_inputs(pre_in, pre_decay, conv_values, retain, decay_rate)

    (decays, pushed), recur_pull = jax.vjp(recur_local, inner_pre, decay_pre, conv_wide)
    products, local_state = lax.associative_scan(linked, (decays, pushed))
    entering = carried_in(
        (products[-1], local_state[-1]), "seq", linked, (unit_row, zero_row), False
    )[1]
    states = local_state + products * entering[None, :]
    mixed_rows = (branch * states).astype(jnp.bfloat16)
    out_pre, out_pick = adapt_forward(
        mixed_rows,
        stacked_forward(mixed_rows, gathered[4]),
        enter_square[4],
        leave_square[4],
        select,
    )
    residual = block_input + out_pre
    normed_two = rms_scale(residual, norm_second).astype(jnp.bfloat16)
    gate_up, widen_pick = adapt_forward(
        normed_two, stacked_forward(normed_two, gathered[5]), enter_widen, leave_widen, select
    )
    hidden_ff = gate_up.shape[1] // 2

    def geglu_local(values):
        return gelu_tanh(values[:, :hidden_ff]) * values[:, hidden_ff:]

    hidden_wide, geglu_pull = jax.vjp(geglu_local, gate_up)
    hidden = hidden_wide.astype(jnp.bfloat16)
    down_pre, narrow_pick = adapt_forward(
        hidden, stacked_forward(hidden, gathered[6]), enter_narrow, leave_narrow, select
    )
    result = residual + down_pre
    gathered = (
        lax.all_gather(gelu_proj[None], "seq", axis=0, tiled=True),
        lax.all_gather(input_proj[None], "seq", axis=0, tiled=True),
        lax.all_gather(inner_gate[None], "seq", axis=0, tiled=True),
        lax.all_gather(decay_gate[None], "seq", axis=0, tiled=True),
        lax.all_gather(output_proj[None], "seq", axis=0, tiled=True),
        lax.all_gather(widen_proj[None], "seq", axis=0, tiled=True),
        lax.all_gather(narrow_proj[None], "seq", axis=0, tiled=True),
    )
    inner_full = flat_gate(gathered[2])
    decay_full = flat_gate(gathered[3])
    grad_down = cotangent.astype(jnp.bfloat16)
    grad_hidden, grad_enter_narrow, grad_leave_narrow = adapt_backward(
        grad_down,
        hidden,
        narrow_pick,
        stacked_back(grad_down, gathered[6]),
        enter_narrow,
        leave_narrow,
        select,
    )
    grad_gate_up = geglu_pull(grad_hidden)[0].astype(jnp.bfloat16)
    grad_normed_two, grad_enter_widen, grad_leave_widen = adapt_backward(
        grad_gate_up,
        normed_two,
        widen_pick,
        stacked_back(grad_gate_up, gathered[5]),
        enter_widen,
        leave_widen,
        select,
    )
    norm_pull = jax.vjp(lambda values: rms_scale(values, norm_second), residual)[1]
    grad_residual = cotangent + norm_pull(grad_normed_two)[0]
    grad_out = grad_residual.astype(jnp.bfloat16)
    grad_mixed, grad_enter_out, grad_leave_out = adapt_backward(
        grad_out,
        mixed_rows,
        out_pick,
        stacked_back(grad_out, gathered[4]),
        enter_square[4],
        leave_square[4],
        select,
    )
    grad_branch = grad_mixed * states
    grad_states = grad_mixed * branch
    decay_next = jnp.concatenate([decays[1:], unit_row[None, :]], axis=0)
    trailing, back_local = lax.associative_scan(linked, (decay_next, grad_states), reverse=True)
    carry_decay = decays[0] * trailing[0]
    carry_state = decays[0] * back_local[0]
    coming = carried_in((carry_decay, carry_state), "seq", linked, (unit_row, zero_row), True)[1]
    carried = back_local + trailing * coming[None, :]
    states_before = jnp.concatenate([entering[None, :], states[:-1]], axis=0)
    grad_inner_pre, grad_decay_pre, grad_conv_local = recur_pull((carried * states_before, carried))
    grad_inner_low = grad_inner_pre.astype(jnp.bfloat16)
    grad_decay_low = grad_decay_pre.astype(jnp.bfloat16)
    grad_conv_inner, grad_enter_inner, grad_leave_inner = adapt_backward(
        grad_inner_low,
        convolved,
        inner_pick,
        block_back(grad_inner_low, inner_full),
        enter_square[2],
        leave_square[2],
        select,
    )
    grad_conv_decay, grad_enter_decay, grad_leave_decay = adapt_backward(
        grad_decay_low,
        convolved,
        decay_pick,
        block_back(grad_decay_low, decay_full),
        enter_square[3],
        leave_square[3],
        select,
    )
    grad_conv = grad_conv_local + grad_conv_inner + grad_conv_decay
    spread = jnp.pad(conv_taps[0] * grad_conv, ((lead_rows, 0), (0, 0)))
    for offset in range(1, lead_rows + 1):
        spread = spread + jnp.pad(
            conv_taps[offset] * grad_conv * same_docs[offset - 1],
            ((lead_rows - offset, offset), (0, 0)),
        )
    returned = from_behind(spread[:lead_rows], "seq", -1)
    grad_filler = spread[lead_rows:] + jnp.pad(returned, ((rows_here - lead_rows, 0), (0, 0)))
    grad_filler_low = grad_filler.astype(jnp.bfloat16)
    grad_gelu_low = gelu_pull(grad_branch)[0].astype(jnp.bfloat16)
    grad_normed_gelu, grad_enter_gelu, grad_leave_gelu = adapt_backward(
        grad_gelu_low,
        normed,
        gelu_pick,
        stacked_back(grad_gelu_low, gathered[0]),
        enter_square[0],
        leave_square[0],
        select,
    )
    grad_normed_fill, grad_enter_fill, grad_leave_fill = adapt_backward(
        grad_filler_low,
        normed,
        filler_pick,
        stacked_back(grad_filler_low, gathered[1]),
        enter_square[1],
        leave_square[1],
        select,
    )
    first_pull = jax.vjp(lambda values: rms_scale(values, norm_first), block_input)[1]
    input_grad = grad_residual + first_pull(grad_normed_gelu + grad_normed_fill)[0]
    enter_stack = jnp.stack(
        [grad_enter_gelu, grad_enter_fill, grad_enter_inner, grad_enter_decay, grad_enter_out]
    )
    leave_stack = jnp.stack(
        [grad_leave_gelu, grad_leave_fill, grad_leave_inner, grad_leave_decay, grad_leave_out]
    )
    summed = lax.psum(
        (
            enter_stack,
            leave_stack,
            grad_enter_widen,
            grad_leave_widen,
            grad_enter_narrow,
            grad_leave_narrow,
        ),
        "seq",
    )
    return (result, input_grad, summed[0], summed[1], summed[2], summed[3], summed[4], summed[5])


def solution(mesh):
    return jax.shard_map(
        per_device,
        mesh=mesh,
        in_specs=(
            P("seq", None),
            P("seq", None),
            P("seq"),
            P(),
            P(),
            P(),
            P(),
            P(),
            P("seq", None),
            P("seq", None),
            P("seq", None),
            P("seq", None),
            P("seq", None),
            P("seq", None),
            P("seq", None),
            P(),
            P(),
            P(),
            P(),
            P(),
            P(),
        ),
        out_specs=(P("seq", None), P("seq", None), P(), P(), P(), P(), P(), P()),
        check_vma=False,
    )
```

profile of v0, /device:TPU:1, one launch (start us, length us, event | category | flops | bytes accessed | tf_op | source)
XLA Modules:
  0.0 1937.1 jit_solution(4303227433970983161)
XLA Ops:
  27.7 65.6 %all-gather.32.cloned.1.call-done = bf16[128,20,2560]{2,1,0:T(8,128)(2,1)} async-done(((bf16[1,20,2560]{2,1,0:T(8,128)(2,1)}), bf16[128,20,2560]{2,1,0:T(8,128)(2,1)}) %all-gather.32.cloned.1.call-update) | async-done | bytes 13107216 | tf_op jit(solution)/shard_map/all_gather | solution.py:144
  93.2 10.3 fusion.40
  109.6 50.1 %all-gather.34.cloned.1.call-done = bf16[128,20,256]{2,1,0:T(8,128)(2,1)} async-done(((bf16[1,20,256]{2,1,0:T(8,128)(2,1)}), bf16[128,20,256]{2,1,0:T(8,128)(2,1)}) %all-gather.34.cloned.1.call-update) | async-done | bytes 1310736 | tf_op jit(solution)/shard_map/all_gather | solution.py:145
  163.0 61.2 %all-gather.36.cloned.1.call-done = bf16[128,20,256]{2,1,0:T(8,128)(2,1)} async-done(((bf16[1,20,256]{2,1,0:T(8,128)(2,1)}), bf16[128,20,256]{2,1,0:T(8,128)(2,1)}) %all-gather.36.cloned.1.call-update) | async-done | bytes 1310736 | tf_op jit(solution)/shard_map/all_gather | solution.py:146
  423.8 14.7 fusion.37
  449.8 9.9 slice.634
  459.7 10.0 slice.625
  469.6 9.8 slice.627
  481.9 45.8 %all-gather.40.cloned.1.call-done = f32[128,1,2560]{2,1,0:T(1,128)} async-done(((f32[1,1,2560]{2,1,0:T(1,128)}), f32[128,1,2560]{2,1,0:T(1,128)}) %all-gather.40.cloned.1.call-update) | async-done | bytes 1310736 | tf_op jit(solution)/shard_map/all_gather | solution.py:22
  530.2 133.2 %while.30 = (s32[]{:T(128)}, f32[2560]{0:T(1024)S(1)}, s32[]{:T(128)}, f32[128,2560]{1,0:T(8,128)}, f32[128,2560]{1,0:T(8,128)}, /*index=5*/s32[]{:T(128)}, s32[]{:T(128)}) while((s32[]{:T(128)}, f32[2560]{0:T(1024)S(1)}, s32[]{:T(128)}, f32[128,2560]{1,0:T(8,128)}, f32[128,2560]{1,0:T(8,128)}, /*index=5*/s32[]{:T(128)}, ...), condition=%wide.region_3.4_spmd.clone, body=%wide.region_2.3_spmd.clone.sunk | while | flops 10244 | bytes 82029 | solution.py:35
  675.5 9.8 fusion.43
  693.9 35.8 %all-gather.46.cloned.1.call-done = bf16[128,60,2560]{2,1,0:T(8,128)(2,1)} async-done(((bf16[1,60,2560]{2,1,0:T(8,128)(2,1)}), bf16[128,60,2560]{2,1,0:T(8,128)(2,1)}) %all-gather.46.cloned.1.call-update) | async-done | bytes 39321616 | tf_op jit(solution)/shard_map/all_gather | solution.py:149
  729.7 61.7 %fusion.4 = f32[128,128,60]{0,1,2:T(8,128)} fusion(bf16[128,60,2560]{2,1,0:T(8,128)(2,1)} %all-gather.46.cloned.1.call-done, f32[128,2560]{1,0:T(8,128)S(1)} %copy-done.17), kind=kOutput, calls=%fused_computation.10 | convolution fusion | flops 5033492480 | bytes 44564480 | tf_op jit(solution)/shard_map/tj,nrj->tnr/dot_general | solution.py:44
  791.4 9.4 copy.180
  800.7 9.2 reshape.189
  809.9 134.8 %all-gather.44.cloned.1.call-done = bf16[128,20,15360]{2,1,0:T(8,128)(2,1)} async-done(((bf16[1,20,15360]{2,1,0:T(8,128)(2,1)}), bf16[128,20,15360]{2,1,0:T(8,128)(2,1)}) %all-gather.44.cloned.1.call-update) | async-done | bytes 78643216 | tf_op jit(solution)/shard_map/all_gather | solution.py:148
  944.8 119.2 %fusion.8 = f32[128,15360]{1,0:T(8,128)} fusion(bf16[128,20,15360]{2,1,0:T(8,128)(2,1)} %all-gather.44.cloned.1.call-done, bf16[128,128,20]{0,2,1:T(8,128)(2,1)S(1)} %copy-done.52), kind=kOutput, calls=%fused_computation.14 | convolution fusion | flops 10066329600 | bytes 87162880 | tf_op jit(solution)/shard_map/tnr,nrj->tj/dot_general | solution.py:40
  1079.5 69.4 %fusion = f32[128,128,20]{0,1,2:T(8,128)} fusion(bf16[128,20,15360]{2,1,0:T(8,128)(2,1)} %all-gather.44.cloned.1.call-done, f32[128,7680]{1,0:T(8,128)} %copy-done.14, f32[128,7680]{1,0:T(8,128)} %copy-done.12), kind=kOutput, calls=%fused_computation.6 | convolution fusion | flops 10070261760 | bytes 87818240 | tf_op jit(solution)/shard_map/tj,nrj->tnr/dot_general | solution.py:44
  1159.8 11.5 fusion.11
  1194.3 9.8 slice.629
  1204.1 9.8 slice.631
  1262.0 9.9 slice.679
  1356.4 10.7 rev.8
  1367.1 10.7 rev.9
  1396.3 18.0 all-gather.50.cloned.1.call-done
  1416.8 61.8 %all-gather.48.cloned.1.call-done = f32[128,1,2560]{2,1,0:T(1,128)} async-done(((f32[1,1,2560]{2,1,0:T(1,128)}), f32[128,1,2560]{2,1,0:T(1,128)}) %all-gather.48.cloned.1.call-update) | async-done | bytes 1310736 | tf_op jit(solution)/shard_map/all_gather | solution.py:22
  1481.0 133.0 %while.31 = (s32[]{:T(128)}, f32[2560]{0:T(1024)S(1)}, s32[]{:T(128)}, f32[128,2560]{1,0:T(8,128)}, f32[128,2560]{1,0:T(8,128)}, /*index=5*/s32[]{:T(128)}, s32[]{:T(128)}, s32[]{:T(128)}, s32[]{:T(128)}) while((s32[]{:T(128)}, f32[2560]{0:T(1024)S(1)}, s32[]{:T(128)}, f32[128,2560]{1,0:T(8,128)}, f32[128,2560]{1,0:T(8,128)}, ...), condition=%wide.region_7.8_spmd.clone, body=%wide.region_6.7_spmd.clone.sunk | while | flops 10248 | bytes 82091 | solution.py:35
  1668.6 15.0 reshape.188
  1683.6 11.6 fusion.19
  1711.4 58.4 %fusion.64 = f32[128,2560]{1,0:T(8,128)S(1)} fusion(bf16[128,128,60]{1,0,2:T(8,128)(2,1)S(1)} %copy-done.60, bf16[128,60,2560]{2,1,0:T(8,128)(2,1)} %all-gather.46.cloned.1.call-done), kind=kOutput, calls=%fused_computation.90 | convolution fusion | flops 5033164800 | bytes 42598400 | tf_op jit(solution)/shard_map/tnr,nrj->tj/dot_general | solution.py:40
  1771.2 11.2 fusion.15
  1791.3 117.6 %all-reduce.68.cloned.1.call-done = (f32[5,2560,128]{2,1,0:T(8,128)}, f32[5,128,2560]{2,1,0:T(8,128)}, f32[2560,128]{1,0:T(8,128)}, f32[128,15360]{1,0:T(8,128)}...) async-done(((f32[5,2560,128]{2,1,0:T(8,128)}, f32[5,128,2560]{2,1,0:T(8,128)}, f32[2560,128]{1,0:T(8,128)}, f32[128,15360]{1,0:T(8,128)}, f32[7680,128]{1,0:T(8,128)}, ...) | async-done | bytes 27525136 | tf_op jit(solution)/shard_map/psum | solution.py:347
  (1176 shorter events, 829.1 us)
Async XLA Ops:
  7.2 1062.7 %copy-start = (bf16[7680,128]{1,0:T(8,128)(2,1)S(1)}, bf16[7680,128]{1,0:T(8,128)(2,1)}, u32[]{:S(2)}) copy-start(bf16[7680,128]{1,0:T(8,128)(2,1)} %param.44) | copy-start | bytes 5898244
  7.2 86.0 %all-gather.32.cloned.1.call-start = ((), (), s32[]{:S(2)}) async-start(), calls=%async_computation.1 | async-start | bytes 15851520 | tf_op jit(solution)/shard_map/all_gather | solution.py:144
  7.9 151.8 %all-gather.34.cloned.1.call-start = ((), (), s32[]{:S(2)}) async-start(), calls=%async_computation.2 | async-start | bytes 1585152 | tf_op jit(solution)/shard_map/all_gather | solution.py:145
  8.7 215.5 %all-gather.36.cloned.1.call-start = ((), (), s32[]{:S(2)}) async-start(), calls=%async_computation.3 | async-start | bytes 1585152 | tf_op jit(solution)/shard_map/all_gather | solution.py:146
  9.4 414.3 %all-gather.30.cloned.1.call-start = ((), (), s32[]{:S(2)}) async-start(), calls=%async_computation | async-start | bytes 15851520 | tf_op jit(solution)/shard_map/all_gather | solution.py:143
  10.0 469.5 %all-gather.38.cloned.1.call-start = ((), (), s32[]{:S(2)}) async-start(), calls=%async_computation.4 | async-start | bytes 1320960 | tf_op jit(solution)/shard_map/all_gather | solution.py:22
  10.8 16.8 collective-permute-start.1
  25.7 227.5 %copy-start.122 = (s32[128]{0:T(128)}, s32[128]{0:T(128)S(1)}, u32[]{:S(2)}) copy-start(s32[128]{0:T(128)S(1)} %and_select_fusion) | copy-start | bytes 1540
  25.8 227.4 %copy-start.124 = (s32[128]{0:T(128)}, s32[128]{0:T(128)S(1)}, u32[]{:S(2)}) copy-start(s32[128]{0:T(128)S(1)} %select_reduce_fusion) | copy-start | bytes 1540
  25.9 201.6 %copy-start.88 = (f32[2560]{0:T(1024)}, f32[2560]{0:T(1024)S(1)}, u32[]{:S(2)}) copy-start(f32[2560]{0:T(1024)S(1)} %get-tuple-element.272) | copy-start | bytes 30724
  25.9 201.6 %copy-start.90 = (f32[2560]{0:T(1024)}, f32[2560]{0:T(1024)S(1)}, u32[]{:S(2)}) copy-start(f32[2560]{0:T(1024)S(1)} %get-tuple-element.273) | copy-start | bytes 30724
  25.9 201.5 %copy-start.92 = (f32[2560]{0:T(1024)}, f32[2560]{0:T(1024)S(1)}, u32[]{:S(2)}) copy-start(f32[2560]{0:T(1024)S(1)} %get-tuple-element.274) | copy-start | bytes 30724
  25.9 201.5 %copy-start.94 = (f32[2560]{0:T(1024)}, f32[2560]{0:T(1024)S(1)}, u32[]{:S(2)}) copy-start(f32[2560]{0:T(1024)S(1)} %get-tuple-element.275) | copy-start | bytes 30724
  25.9 230.5 %copy-start.96 = (f32[2560]{0:T(1024)}, f32[2560]{0:T(1024)S(1)}, u32[]{:S(2)}) copy-start(f32[2560]{0:T(1024)S(1)} %broadcast_multiply_fusion.1) | copy-start | bytes 30724
  106.0 121.4 %collective-permute-start = (f32[3,2560]{1,0:T(4,128)S(1)}, f32[3,2560]{1,0:T(4,128)S(1)}, u32[]{:S(2)}, u32[]{:S(2)}) collective-permute-start(f32[3,2560]{1,0:T(4,128)S(1)} %slice.697), channel_id=1, source_target_pairs={{0,1},{1,2},{2,3},{3,4},{4,5},{5,6},{6,7},{7,8},{8,9},{9,10},{10,1... | collective-permute-start | bytes 92168 | tf_op jit(solution)/shard_map/ppermute | solution.py:17
  109.6 146.9 %copy-start.128 = (f32[128]{0:T(128)}, f32[128]{0:T(128)S(1)}, u32[]{:S(2)}) copy-start(f32[128]{0:T(128)S(1)} %get-tuple-element.307) | copy-start | bytes 1540
  109.6 146.9 %copy-start.138 = (pred[128]{0:T(512)(128)(4,1)}, pred[128]{0:T(512)(128)(4,1)S(1)}, u32[]{:S(2)}) copy-start(pred[128]{0:T(512)(128)(4,1)S(1)} %get-tuple-element.306) | copy-start | bytes 388
  401.4 126.4 %all-gather.40.cloned.1.call-start = ((), (), s32[]{:S(2)}) async-start(), calls=%async_computation.5 | async-start | bytes 1320960 | tf_op jit(solution)/shard_map/all_gather | solution.py:22
  417.7 257.8 %all-gather.42.cloned.1.call-start = ((), (), s32[]{:S(2)}) async-start(), calls=%async_computation.6 | async-start | bytes 15851520 | tf_op jit(solution)/shard_map/all_gather | solution.py:147
  418.5 311.2 %all-gather.46.cloned.1.call-start = ((), (), s32[]{:S(2)}) async-start(), calls=%async_computation.8 | async-start | bytes 42270720 | tf_op jit(solution)/shard_map/all_gather | solution.py:149
  419.2 525.6 %all-gather.44.cloned.1.call-start = ((), (), s32[]{:S(2)}) async-start(), calls=%async_computation.7 | async-start | bytes 95109120 | tf_op jit(solution)/shard_map/all_gather | solution.py:148
  420.0 994.3 %all-gather.50.cloned.1.call-start = ((), (), s32[]{:S(2)}) async-start(), calls=%async_computation.10 | async-start | bytes 1320960 | tf_op jit(solution)/shard_map/all_gather | solution.py:22
  422.3 241.2 %copy-start.82 = (bf16[128,128]{1,0:T(8,128)(2,1)}, bf16[128,128]{1,0:T(8,128)(2,1)S(1)}, u32[]{:S(2)}) copy-start(bf16[128,128]{1,0:T(8,128)(2,1)S(1)} %fusion.99) | copy-start | bytes 98308
  423.7 646.1 %copy-start.80 = (bf16[128,128]{1,0:T(8,128)(2,1)}, bf16[128,128]{1,0:T(8,128)(2,1)S(1)}, u32[]{:S(2)}) copy-start(bf16[128,128]{1,0:T(8,128)(2,1)S(1)} %fusion.105) | copy-start | bytes 98308
  693.9 370.2 %copy-start.74 = (bf16[128,128]{1,0:T(8,128)(2,1)}, bf16[128,128]{1,0:T(8,128)(2,1)S(1)}, u32[]{:S(2)}) copy-start(bf16[128,128]{1,0:T(8,128)(2,1)S(1)} %fusion.104) | copy-start | bytes 98308
  800.7 144.1 %copy-start.52 = (bf16[128,128,20]{0,2,1:T(8,128)(2,1)S(1)}, bf16[128,128,20]{0,2,1:T(8,128)(2,1)}, u32[]{:S(2)}) copy-start(bf16[128,128,20]{0,2,1:T(8,128)(2,1)} %reshape.129) | copy-start | bytes 1966084
  1351.3 127.3 %all-gather.48.cloned.1.call-start = ((), (), s32[]{:S(2)}) async-start(), calls=%async_computation.9 | async-start | bytes 1320960 | tf_op jit(solution)/shard_map/all_gather | solution.py:22
  1352.0 556.9 %all-reduce.68.cloned.1.call-start = ((), (), s32[]{:S(2)}) async-start(), calls=%async_computation.11 | async-start | bytes 55050240 | tf_op jit(solution)/shard_map/psum | solution.py:347
  1416.8 197.3 %copy-start.97 = (f32[2560]{0:T(1024)S(1)}, f32[2560]{0:T(1024)}, u32[]{:S(2)}) copy-start(f32[2560]{0:T(1024)} %copy-done.96) | copy-start | bytes 30724
  1416.8 197.3 %copy-start.129 = (f32[128]{0:T(128)S(1)}, f32[128]{0:T(128)}, u32[]{:S(2)}) copy-start(f32[128]{0:T(128)} %copy-done.128) | copy-start | bytes 1540
  1416.8 197.3 %copy-start.139 = (pred[128]{0:T(512)(128)(4,1)S(1)}, pred[128]{0:T(512)(128)(4,1)}, u32[]{:S(2)}) copy-start(pred[128]{0:T(512)(128)(4,1)} %copy-done.138) | copy-start | bytes 388
  1650.0 5.6 collective-permute-start.2
  (133 other events, 892.7 us)
Sparse Core Ops, SparseCore 0:
  11.2 82.0 all-gather.31
  96.0 63.6 all-gather.33
  162.5 61.5 all-gather.35
  227.1 75.8 all-gather.29
  401.5 62.0 all-gather.37
  466.3 61.4 all-gather.39
  530.9 75.9 all-gather.41
  610.0 119.6 all-gather.45
  732.8 211.9 all-gather.43
  1351.4 62.8 all-gather.49
  1417.1 61.4 all-gather.47
  1668.7 240.1 all-reduce.67
where the time goes:
time: 1970 us; the launch traced here: 1940 us
  local copies, waits for them, and re-layouts  716 us (36%)
  waiting for transfers between devices  599 us (30%)
  matrix products  476 us (24%)
  other arithmetic  109 us (6%)
    dynamic_slice x256, local copies, waits for them, and re-layouts, hop(): new = combine(before, jax.tree.map(lambda part: part[at], everything))  254 us
    dot_general x5, matrix products, stacked_forward(): jnp.einsum('tnr,nrj->tj', pieces, stacked, preferred_element_type=jnp.flo...  212 us
    dot_general x5, matrix products, stacked_back(): jnp.einsum('tj,nrj->tnr', grad_rows, stacked, preferred_element_type=jnp....  165 us
    all_gather x1, waiting for transfers between devices, per_device(): lax.all_gather(widen_proj[None], 'seq', axis=0, tiled=True)  135 us
    all_gather x4, waiting for transfers between devices, carried_in(): everything = jax.tree.map(lambda part: lax.all_gather(part, axis), value)  126 us
    psum x1, waiting for transfers between devices, per_device(): lax.psum((enter_stack, leave_stack, grad_enter_widen, grad_leave_widen, g...  118 us
    slice x49, local copies, waits for them, and re-layouts, per_device(): lax.associative_scan(linked, (decay_next, grad_states), reverse=True)  116 us
    all_gather x1, waiting for transfers between devices, per_device(): lax.all_gather(input_proj[None], 'seq', axis=0, tiled=True)  65.6 us
  transfers between devices with their start and end apart: 15, of which 10 were waited for; matrix products, arithmetic and copies ran while one was open for 35% of the time, Pallas kernels for 0%

commit v1 on v0

v1 whole, which is shorter than its diff:
```python
import functools
import jax
import jax.numpy as jnp
from jax import lax
from jax.experimental import pallas as pl
from jax.experimental.pallas import tpu as pltpu
from jax.sharding import Mesh, PartitionSpec as P

HEADS = 10
ADAPTERS = 8
HALO = 16
MIDDLE = 3
AXES = ("z", "x", "v", "u", "c")
SIZES = (4, 4, 2, 2, 2)
YAX = ("v", "u")
RING = ("v", "u", "c")
PLANE = ("z", "x")

eps_norm = 1e-06
floor_scale = 0.001
bf16 = jnp.bfloat16
f32 = jnp.float32


def dot(a, b):
    return jnp.dot(a, b, preferred_element_type=f32)


def dot_nt(a, b):
    return lax.dot_general(a, b, (((1,), (1,)), ((), ())), preferred_element_type=f32)


def dot_tn(a, b):
    return lax.dot_general(a, b, (((0,), (0,)), ((), ())), preferred_element_type=f32)


def low(v):
    return lax.reduce_precision(v, 8, 7)


def norm_scale(values):
    return lax.rsqrt(jnp.mean(values * values, axis=-1, keepdims=True) + eps_norm)


def norm_apply(values, gain):
    return (values * norm_scale(values) * gain).astype(bf16)


def norm_back(values, gain, grad):
    s = norm_scale(values)
    gq = gain * grad
    return s * gq - values * (s * s * s) * jnp.mean(values * gq, axis=-1, keepdims=True)


def gelu_parts(a):
    k = 0.7978845608028654
    a2 = a * a
    th = jnp.tanh(k * (a + 0.044715 * a2 * a))
    value = 0.5 * a * (1.0 + th)
    slope = 0.5 * (1.0 + th) + 0.5 * a * (1.0 - th * th) * (k * (1.0 + 3.0 * 0.044715 * a2))
    return value, slope


def swap(v):
    return lax.ppermute(v, "c", [(0, 1), (1, 0)])


def shift4(v, axis, by):
    return lax.ppermute(v, axis, [(i, (i + by) % 4) for i in range(4)])


def chip_shift(v, by):
    chips = 64
    pairs = [
        (2 * p + c, 2 * (p + by) + c) for p in range(chips) for c in range(2) if 0 <= p + by < chips
    ]
    return lax.ppermute(v, AXES, pairs)


def both(own, other, c):
    rows = own.shape[0]
    three = jnp.concatenate([own, other, own], axis=0)
    return lax.dynamic_slice_in_dim(three, c * rows, 2 * rows, axis=0)


def half(v, c, axis):
    size = v.shape[axis] // 2
    return lax.dynamic_slice_in_dim(v, c * size, size, axis=axis)


def scan_kernel(d_ref, p_ref, s_ref, q_ref):
    rows, width = d_ref.shape
    row = lax.broadcasted_iota(jnp.int32, (8, width), 0)

    def tile(i, carry):
        state, product = carry
        at = pl.ds(pl.multiple_of(i * 8, 8), 8)
        a = d_ref[at, :]
        b = p_ref[at, :]
        for s in (1, 2, 4):
            b = a * jnp.where(row >= s, pltpu.roll(b, s, 0), 0.0) + b
            a = a * jnp.where(row >= s, pltpu.roll(a, s, 0), 1.0)
        value = b + a * state
        through = a * product
        s_ref[at, :] = value
        q_ref[at, :] = through
        return value[7:8, :], through[7:8, :]

    lax.fori_loop(
        0, rows // 8, tile, (jnp.zeros((1, width), f32), jnp.ones((1, width), f32))
    )


def scan_back_kernel(main, d_ref, g_ref, s_ref, q_ref):
    rows, width = d_ref.shape
    row = lax.broadcasted_iota(jnp.int32, (8, width), 0)

    def tile(i, carry):
        state, product, after = carry
        at = pl.ds(pl.multiple_of(i * 8, 8), 8)
        d = d_ref[at, :]
        b = g_ref[at, :]
        a = jnp.where(row < 7, pltpu.roll(d, 7, 0), after)
        for s in (1, 2, 4):
            b = a * jnp.where(row < 8 - s, pltpu.roll(b, 8 - s, 0), 0.0) + b
            a = a * jnp.where(row < 8 - s, pltpu.roll(a, 8 - s, 0), 1.0)
        value = b + a * state
        through = a * product
        s_ref[at, :] = value
        q_ref[at, :] = through
        return value[0:1, :], through[0:1, :], d[0:1, :]

    zero = jnp.zeros((1, width), f32)
    one = jnp.ones((1, width), f32)
    last = rows // 8 - 1
    lax.fori_loop(0, (rows - main) // 8, lambda k, t: tile(last - k, t), (zero, zero, one))
    lax.fori_loop(0, main // 8, lambda k, t: tile(main // 8 - 1 - k, t), (zero, one, one))


def scan_call(kernel, a, b):
    rows, cols = a.shape
    wide = 256 if cols % 256 == 0 else 128
    block = pl.BlockSpec((rows, wide), lambda i: (0, i))
    return pl.pallas_call(
        kernel,
        grid=(cols // wide,),
        in_specs=[block, block],
        out_specs=[block, block],
        out_shape=[jax.ShapeDtypeStruct((rows, cols), f32)] * 2,
        compiler_params=pltpu.CompilerParams(vmem_limit_bytes=32 * 2**20),
        cost_estimate=pl.CostEstimate(
            flops=20 * rows * cols, bytes_accessed=16 * rows * cols, transcendentals=0
        ),
    )(a, b)


def linked(former, latter):
    return (former[0] * latter[0], latter[0] * former[1] + latter[1])


def line_carry(value, axis, reverse):
    sign = -1 if reverse else 1
    here = lax.axis_index(axis)
    here = 3 - here if reverse else here
    came = {by: shift4(value, axis, sign * by) for by in (1, 2, 3)}
    unit = (jnp.ones_like(value[0]), jnp.zeros_like(value[0]))

    def take(so_far, by, valid):
        new = linked(so_far, (came[by][0], came[by][1]))
        return tuple(jnp.where(valid, a, b) for a, b in zip(new, so_far))

    enter = unit
    for by in (3, 2, 1):
        enter = take(enter, by, here >= by)
    total = linked(enter, (value[0], value[1]))
    for by in (3, 2, 1):
        total = take(total, by, here < by)
    return enter, jnp.stack(total)


def chips_carry(value, reverse):
    by_y, line = line_carry(value, YAX, reverse)
    by_x, plane = line_carry(line, "x", reverse)
    by_z, _ = line_carry(plane, "z", reverse)
    return linked(linked(by_z, by_x), by_y)[1]


def index_of(place):
    at = 0
    for i, n in zip(place, (4, 4, 4, 2)):
        at = at * n + i
    return at


def spread_rounds(order):
    reached = {0: {(0, 0, 0)}, 1: {(3, 3, 3)}}
    rounds = []
    for axis in order:
        for hop in (2, 1):
            pairs = []
            for c in (0, 1):
                new = set()
                for place in sorted(reached[c]):
                    to = list(place)
                    to[axis] = place[axis] ^ hop
                    new.add(tuple(to))
                    pairs.append((index_of((*place, c)), index_of((*to, c))))
                reached[c] |= new
            rounds.append(pairs)
    return rounds


def spread(payload):
    rows = payload.shape[0]
    cut = rows // 3 // 16 * 16
    bounds = [0, rows - 2 * cut, rows - cut, rows]
    parts = []
    for k, order in enumerate(((0, 1, 2), (1, 2, 0), (2, 0, 1))):
        part = payload[bounds[k] : bounds[k + 1]]
        for pairs in spread_rounds(order):
            part = part + lax.ppermute(part, AXES, pairs)
        parts.append(part)
    return jnp.concatenate(parts, axis=0)


def line_sum(v, axis):
    one, two, three = (shift4(v, axis, by).astype(f32) for by in (1, 2, 3))
    return (v.astype(f32) + two) + (one + three)


def to_low(v):
    return low(v).astype(bf16)


def ring_rows(own):
    parts = [own] + [shift4(own, YAX, by) for by in (1, 2, 3)]
    rows = []
    for part in parts:
        rows += [part, swap(part)]
    return rows


def ring_scatter(part, rows):
    mine = [part[(2 * k) * rows : (2 * k + 1) * rows] for k in range(4)]
    theirs = jnp.concatenate([part[(2 * k + 1) * rows : (2 * k + 2) * rows] for k in range(4)], axis=0)
    got = swap(theirs.astype(bf16)).astype(f32)
    mine = [m + got[k * rows : (k + 1) * rows] for k, m in enumerate(mine)]
    total = mine[0]
    for by in (1, 2, 3):
        total = total + shift4(mine[by].astype(bf16), YAX, -by).astype(f32)
    return total


def per_device(
    block_input,
    cotangent,
    segments,
    adapter_index,
    norm_first,
    norm_second,
    conv_taps,
    decay_rate,
    gelu_proj,
    input_proj,
    inner_gate,
    decay_gate,
    output_proj,
    widen_proj,
    narrow_proj,
    enter_square,
    leave_square,
    enter_widen,
    leave_widen,
    enter_narrow,
    leave_narrow,
):
    c = lax.axis_index("c")
    y = lax.axis_index(YAX)
    member = lax.axis_index(RING)
    plane = lax.axis_index(PLANE)
    chip = lax.axis_index(("z", "x", "v", "u"))
    place = lax.axis_index(AXES)
    toks, width = block_input.shape
    halfw = width // 2
    heads = HEADS // 2
    head = width // HEADS
    columns = enter_square.shape[-1]
    rank = columns // ADAPTERS
    main = 2 * toks
    extra = 2 * toks
    rows = main + extra
    per = gelu_proj.shape[0]
    gate_rows = per * head // width
    ff = widen_proj.shape[1] // 2
    slot = ff // 8
    slotp = slot * 16 // 15
    per_n = narrow_proj.shape[0]
    chunk = slotp // 16

    shard = jnp.concatenate(
        [
            gelu_proj,
            input_proj,
            output_proj,
            inner_gate.reshape(gate_rows, width),
            decay_gate.reshape(gate_rows, width),
        ],
        axis=0,
    )
    near = lax.all_gather(shard[None], AXES, axis=0, tiled=True)

    pieces = widen_proj.reshape(per, 2, 8, slot).transpose(2, 0, 1, 3)
    pieces = jnp.pad(pieces, ((0, 0), (0, 0), (0, 0), (0, slotp - slot)))
    pieces = lax.all_to_all(pieces.reshape(8 * per, 2 * slotp), RING, 0, 0, tiled=True)
    to_first = [(16 * m + p, 8 * p + m) for p in range(16) for m in range(8)]
    to_second = [(16 * m + p + 1, 8 * p + m) for p in range(16) for m in range(8) if 16 * m + p + 1 < 128]
    two = jnp.concatenate(
        [lax.ppermute(narrow_proj, AXES, to_first), lax.ppermute(narrow_proj, AXES, to_second)], axis=0
    )
    two = jnp.pad(two, ((0, 2 * chunk - 2 * per_n), (0, 0)))
    rows_n = lax.dynamic_slice_in_dim(two, jnp.minimum(plane, 14) * (chunk - per_n), chunk, axis=0)
    rows_n = jnp.where(plane < 15, rows_n, jnp.zeros_like(rows_n))
    far = lax.all_gather(
        jnp.concatenate([pieces, rows_n.reshape(-1, 2 * slotp)], axis=0)[None], PLANE, axis=0, tiled=True
    )

    middle_at = adapter_index[MIDDLE] * rank
    column_owner = jnp.arange(columns) // rank
    owner_of = jnp.arange(adapter_index.shape[0])

    def select_of(segs):
        owners = jnp.sum((segs[:, None] == owner_of[None, :]).astype(jnp.int32) * adapter_index[None, :], axis=1)
        return (owners[:, None] == column_owner[None, :]).astype(f32)

    def middle(v):
        return lax.dynamic_slice_in_dim(v, middle_at, rank, axis=1)

    grad_down_own = cotangent.astype(bf16)
    seg_row = jnp.pad(segments.astype(bf16)[None, :], ((0, 15), (0, width - toks)))
    payload = jnp.concatenate([block_input.astype(bf16), grad_down_own, seg_row], axis=0)
    source = (place == 0) | (place == 127)
    payload = spread(jnp.where(source, payload, jnp.zeros_like(payload)))
    paired = both(payload, swap(payload), c)
    count = payload.shape[0]
    x_extra = jnp.concatenate([paired[:toks], paired[count : count + toks]], axis=0).astype(f32)
    down_extra = jnp.concatenate([paired[toks : 2 * toks], paired[count + toks : count + 2 * toks]], axis=0)
    seg_first = paired[2 * toks, :toks].astype(jnp.int32)
    seg_last = paired[count + 2 * toks, :toks].astype(jnp.int32)
    seg_extra = jnp.concatenate([seg_first, seg_last])
    select_extra = select_of(seg_extra) * (seg_extra != MIDDLE).astype(f32)[:, None]

    normed_own = norm_apply(block_input, norm_first)
    normed_main = both(normed_own, swap(normed_own), c)
    normed_halo = chip_shift(normed_main[main - HALO :], 1)
    seg_main = both(segments, swap(segments), c)
    halo_seg = jnp.where(chip > 0, MIDDLE, -1)
    seg_all = jnp.concatenate(
        [jnp.broadcast_to(halo_seg, (HALO,)), seg_main, seg_first + 100, seg_last + 200]
    )
    select_main = select_of(seg_main)
    select = jnp.concatenate([select_main, select_extra], axis=0)
    select_halo = jnp.broadcast_to((column_owner == adapter_index[MIDDLE]).astype(f32)[None, :], (HALO, columns))
    select_long = jnp.concatenate([select_halo, select], axis=0)
    normed_extra = norm_apply(x_extra, norm_first)
    normed_long = jnp.concatenate([normed_halo, normed_main, normed_extra], axis=0)
    normed = normed_long[HALO:]

    ring_down = jnp.concatenate(ring_rows(grad_down_own) + [down_extra], axis=0)
    ring_seg = jnp.concatenate(ring_rows(segments))
    ring_select = jnp.concatenate([select_of(ring_seg), select_extra], axis=0)
    latent_grad_n = (dot_nt(ring_down, leave_narrow) * ring_select).astype(bf16)

    taps = half(conv_taps, c, 1)
    rate = half(decay_rate, c, 0)[None, :]
    enter_half = half(enter_square, c, 1)
    leave_half = half(leave_square, c, 2)

    w_gelu = lax.dynamic_slice(near, (0, 0, c * halfw), (128, per, halfw)).reshape(width, halfw)
    w_in = lax.dynamic_slice(near, (0, per, c * halfw), (128, per, halfw)).reshape(width, halfw)
    w_out = lax.dynamic_slice(near, (c * 64, 2 * per, 0), (64, per, width)).reshape(halfw, width)
    w_gates = lax.dynamic_slice(near, (c * 64, 3 * per, 0), (64, 2 * gate_rows, width))
    w_inner = w_gates[:, :gate_rows].reshape(heads, head, head)
    w_decay = w_gates[:, gate_rows:].reshape(heads, head, head)

    def block_apply(values, weight):
        return jnp.einsum(
            "thi,hij->thj", values.reshape(-1, heads, head), weight, preferred_element_type=f32
        ).reshape(-1, halfw)

    def block_back(grads, weight):
        return jnp.einsum(
            "thj,hij->thi", grads.reshape(-1, heads, head), weight, preferred_element_type=f32
        ).reshape(-1, halfw)

    picked_fill = (dot(normed_long, enter_square[1]) * select_long).astype(bf16)
    filler = dot(normed_long, w_in) + dot(picked_fill, leave_half[1])
    picked_fill = picked_fill[HALO:]
    same_docs = []
    combined = taps[0] * filler[HALO:]
    for k in range(1, conv_taps.shape[0]):
        same = (seg_all[HALO - k : -k] == seg_all[HALO:]).astype(f32)[:, None]
        same_docs.append(same)
        combined = combined + taps[k] * filler[HALO - k : -k] * same
    convolved = combined.astype(bf16)
    conv_wide = convolved.astype(f32)
    retain = same_docs[0]
    latent = jnp.concatenate([dot(convolved, enter_half[2]), dot(convolved, enter_half[3])], axis=1)
    latent = latent + swap(latent)
    picked_inner = (latent[:, :columns] * select).astype(bf16)
    picked_decay = (latent[:, columns:] * select).astype(bf16)
    inner_pre = block_apply(convolved, w_inner) + dot(picked_inner, leave_half[2])
    decay_pre = block_apply(convolved, w_decay) + dot(picked_decay, leave_half[3])
    sig_in = jax.nn.sigmoid(inner_pre)
    sig_decay = jax.nn.sigmoid(decay_pre)
    log_decay = -8.0 * rate * sig_decay
    raw_decay = jnp.exp(log_decay)
    decays = raw_decay * retain
    grown = -jnp.expm1(2.0 * log_decay)
    scale = jnp.where(retain > 0.5, jnp.sqrt(jnp.maximum(grown, floor_scale)), 1.0)
    pushed = conv_wide * sig_in * scale
    local_state, products = scan_call(scan_kernel, decays, pushed)
    entering = chips_carry(jnp.stack([products[main - 1], local_state[main - 1]]), False)
    picked_gelu = (dot(normed, enter_square[0]) * select).astype(bf16)
    gelu_pre = dot(normed, w_gelu) + dot(picked_gelu, leave_half[0])
    branch, gelu_slope = gelu_parts(gelu_pre)
    states = local_state + products * entering[None, :]
    mixed = (branch * states).astype(bf16)
    latent_out = dot(mixed, enter_half[4])
    out_part = dot(mixed, w_out) + dot((latent_out * select).astype(bf16), leave_square[4])
    picked_out = ((latent_out + swap(latent_out)) * select).astype(bf16)
    mine = lax.dynamic_slice_in_dim(out_part, c * toks, toks, axis=0)
    theirs = lax.dynamic_slice_in_dim(out_part, (1 - c) * toks, toks, axis=0)
    out_extra = to_low(out_part[main:])
    got = swap(jnp.concatenate([theirs.astype(bf16), out_extra], axis=0)).astype(f32)
    residual = block_input + mine + got[:toks]
    residual_extra = x_extra + (out_extra.astype(f32) + got[toks:])
    normed_two_own = norm_apply(residual, norm_second)
    normed_two_extra = norm_apply(residual_extra, norm_second)

    n2 = jnp.concatenate(ring_rows(normed_two_own) + [normed_two_extra], axis=0)
    ring_main = 8 * toks
    w_wide = far[:, : 8 * per].reshape(width, 2 * slotp)
    w_narrow = far[:, 8 * per :].reshape(slotp, width)
    pad_cols = ((0, 0), (0, slotp - slot))
    leave_a = jnp.pad(lax.dynamic_slice_in_dim(leave_widen, member * slot, slot, axis=1), pad_cols)
    leave_b = jnp.pad(lax.dynamic_slice_in_dim(leave_widen, ff + member * slot, slot, axis=1), pad_cols)
    leave_wide = jnp.concatenate([leave_a, leave_b], axis=1)
    enter_down = jnp.pad(
        lax.dynamic_slice_in_dim(enter_narrow, member * slot, slot, axis=0), ((0, slotp - slot), (0, 0))
    )
    picked_wide = (dot(n2, enter_widen) * ring_select).astype(bf16)
    gate_up = dot(n2, w_wide) + dot(picked_wide, leave_wide)
    grad_hidden = dot_nt(ring_down, w_narrow) + dot_nt(latent_grad_n, enter_down)
    act, act_slope = gelu_parts(gate_up[:, :slotp])
    up = gate_up[:, slotp:]
    hidden = (act * up).astype(bf16)
    grad_gate_up = jnp.concatenate([act_slope * up * grad_hidden, act * grad_hidden], axis=1).astype(bf16)
    latent_grad_w = (dot_nt(grad_gate_up, leave_wide) * ring_select).astype(bf16)
    n2_part = dot_nt(grad_gate_up, w_wide) + dot_nt(latent_grad_w, enter_widen)
    latent_n = dot(hidden, enter_down)
    picked_n = (latent_n * ring_select).astype(bf16)
    down_part = dot(hidden[:ring_main], w_narrow) + dot(picked_n[:ring_main], leave_narrow)

    wide_mid = dot_tn(middle(picked_wide[:ring_main]), grad_gate_up[:ring_main])
    down_mid = dot_tn(middle(latent_grad_n[:ring_main]), hidden[:ring_main])
    leave_n_mid = dot_tn(middle(picked_n[:ring_main]), ring_down[:ring_main])
    enter_w_mid = dot_tn(middle(latent_grad_w[:ring_main]), n2[:ring_main])
    ffn_mid = jnp.concatenate([wide_mid, down_mid, leave_n_mid, enter_w_mid], axis=1)
    ffn_mid = to_low(line_sum(to_low(line_sum(to_low(ffn_mid), "x")), "z"))
    wide_extra = dot_tn(picked_wide[ring_main:], grad_gate_up[ring_main:])
    down_extra_grad = dot_tn(latent_grad_n[ring_main:], hidden[ring_main:])
    leave_n_extra = dot_tn(picked_n[ring_main:], ring_down[ring_main:])
    enter_w_extra = dot_tn(latent_grad_w[ring_main:], n2[ring_main:])
    ffn_extra = jnp.concatenate([wide_extra, down_extra_grad, leave_n_extra, enter_w_extra], axis=1).astype(bf16)
    ffn_all = lax.all_gather(jnp.concatenate([ffn_mid, ffn_extra], axis=0), RING, axis=0)
    ffn_all = ffn_all.astype(f32)

    ffn_full = ffn_all[:, rank:] + jnp.tile(ffn_all[:, :rank], (1, ADAPTERS, 1)) * (
        column_owner == adapter_index[MIDDLE]
    ).astype(f32)[None, :, None]
    grad_leave_widen = jnp.concatenate(
        [ffn_full[m, :, s * slotp : s * slotp + slot] for s in (0, 1) for m in range(8)], axis=1
    )
    grad_enter_narrow = jnp.concatenate(
        [ffn_full[m, :, 2 * slotp : 2 * slotp + slot].T for m in range(8)], axis=0
    )
    ffn_sum = jnp.sum(ffn_full[:, :, 3 * slotp :], axis=0)
    grad_leave_narrow = ffn_sum[:, :width]
    grad_enter_widen = ffn_sum[:, width:].T

    quarter = extra // 8
    main_part = n2_part[:ring_main]
    mine_rows = [main_part[(2 * k) * toks : (2 * k + 1) * toks] for k in range(4)]
    their_rows = [main_part[(2 * k + 1) * toks : (2 * k + 2) * toks] for k in range(4)]
    extra_part = n2_part[ring_main:]
    mine_extra = half(extra_part, c, 0)
    their_extra = half(extra_part, 1 - c, 0)
    got = swap(jnp.concatenate(their_rows + [their_extra], axis=0).astype(bf16)).astype(f32)
    mine_extra = mine_extra + got[4 * toks :]
    mine_rows = [m + got[k * toks : (k + 1) * toks] for k, m in enumerate(mine_rows)]
    grad_normed_two = mine_rows[0]
    extra_sum = lax.dynamic_slice_in_dim(mine_extra, y * quarter, quarter, axis=0)
    for by in (1, 2, 3):
        at = jnp.remainder(y - by, 4)
        send = jnp.concatenate(
            [mine_rows[by], lax.dynamic_slice_in_dim(mine_extra, at * quarter, quarter, axis=0)], axis=0
        ).astype(bf16)
        came = shift4(send, YAX, -by).astype(f32)
        grad_normed_two = grad_normed_two + came[:toks]
        extra_sum = extra_sum + came[toks:]
    extra_sum = extra_sum.astype(bf16)
    quarters = [extra_sum] + [shift4(extra_sum, YAX, by) for by in (1, 2, 3)]
    ordered = jnp.concatenate(quarters[::-1] + quarters[::-1], axis=0)
    half_extra = lax.dynamic_slice_in_dim(ordered, (3 - y) * quarter, 4 * quarter, axis=0)
    grad_normed_two_extra = both(half_extra, swap(half_extra), c).astype(f32)
    down_own = ring_scatter(down_part, toks)
    block_output = residual + down_own

    grad_residual = cotangent + norm_back(residual, norm_second, grad_normed_two)
    grad_residual_extra = down_extra.astype(f32) + norm_back(residual_extra, norm_second, grad_normed_two_extra)
    grad_out_own = grad_residual.astype(bf16)
    grad_out = jnp.concatenate(
        [both(grad_out_own, swap(grad_out_own), c), grad_residual_extra.astype(bf16)], axis=0
    )
    lg_out = (dot_nt(grad_out, leave_square[4]) * select).astype(bf16)
    grad_mixed = dot_nt(grad_out, w_out) + dot_nt(lg_out, enter_half[4])
    grad_gelu = (gelu_slope * (grad_mixed * states)).astype(bf16)
    grad_states = grad_mixed * branch
    back_local, trailing = scan_call(functools.partial(scan_back_kernel, main), decays, grad_states)
    coming = chips_carry(jnp.stack([decays[0] * trailing[0], decays[0] * back_local[0]]), True)
    carried = back_local + trailing * coming[None, :]
    states_before = jnp.concatenate([entering[None, :], states[:-1]], axis=0)
    through_in = carried * conv_wide * scale
    grad_inner = (through_in * sig_in * (1.0 - sig_in)).astype(bf16)
    grad_grown = jnp.where(
        (grown > floor_scale) & (retain > 0.5), carried * conv_wide * sig_in * 0.5 / scale, 0.0
    )
    grad_log = carried * states_before * decays - 2.0 * raw_decay * raw_decay * grad_grown
    grad_decay = (grad_log * (-8.0 * rate) * sig_decay * (1.0 - sig_decay)).astype(bf16)
    latent = jnp.concatenate([dot_nt(grad_inner, leave_half[2]), dot_nt(grad_decay, leave_half[3])], axis=1)
    latent = latent + swap(latent)
    lg_inner = (latent[:, :columns] * select).astype(bf16)
    lg_decay = (latent[:, columns:] * select).astype(bf16)
    grad_conv = (
        carried * sig_in * scale
        + block_back(grad_inner, w_inner)
        + block_back(grad_decay, w_decay)
        + dot_nt(lg_inner, enter_half[2])
        + dot_nt(lg_decay, enter_half[3])
    )
    conv_halo = chip_shift(grad_conv[:HALO], -1)
    halo_on = jnp.ones((HALO, 1), f32)
    long_conv = jnp.concatenate([grad_conv[:main], conv_halo, grad_conv[main:], jnp.zeros((HALO, halfw), f32)], axis=0)
    grad_filler = taps[0] * long_conv[: rows + HALO]
    for k in range(1, conv_taps.shape[0]):
        same = same_docs[k - 1]
        long_same = jnp.concatenate([same[:main], halo_on, same[main:], jnp.zeros((HALO, 1), f32)], axis=0)
        grad_filler = grad_filler + taps[k] * (long_conv * long_same)[k : k + rows + HALO]
    grad_filler = jnp.concatenate([grad_filler[:main], grad_filler[main + HALO :]], axis=0).astype(bf16)
    latent = jnp.concatenate([dot_nt(grad_gelu, leave_half[0]), dot_nt(grad_filler, leave_half[1])], axis=1)
    two_select = jnp.concatenate([select, select], axis=1)
    own_lg = (latent[:main] * two_select[:main]).astype(bf16)
    grad_normed = (
        dot_nt(grad_gelu[:main], w_gelu)
        + dot_nt(grad_filler[:main], w_in)
        + dot_nt(own_lg[:, :columns], enter_square[0])
        + dot_nt(own_lg[:, columns:], enter_square[1])
    )
    mine = lax.dynamic_slice_in_dim(grad_normed, c * toks, toks, axis=0)
    theirs = lax.dynamic_slice_in_dim(grad_normed, (1 - c) * toks, toks, axis=0)
    grad_normed = mine + swap(theirs.astype(bf16)).astype(f32)
    input_grad = grad_residual + norm_back(block_input, norm_first, grad_normed)
    latent = latent + swap(latent)
    lg_two = (latent * two_select).astype(bf16)
    lg_gelu, lg_fill = lg_two[:, :columns], lg_two[:, columns:]

    normed_half = half(normed, c, 1)
    grad_out_half = half(grad_out, c, 1)
    enters = [
        (normed_half, lg_gelu),
        (normed_half, lg_fill),
        (convolved, lg_inner),
        (convolved, lg_decay),
        (mixed, lg_out),
    ]
    leaves = [
        (picked_gelu, grad_gelu),
        (picked_fill, grad_filler),
        (picked_inner, grad_inner),
        (picked_decay, grad_decay),
        (picked_out, grad_out_half),
    ]
    mid = [dot_tn(middle(lg[:main]), v[:main]) for v, lg in enters]
    mid += [dot_tn(middle(pick[:main]), g[:main]) for pick, g in leaves]
    mid = to_low(jnp.concatenate(mid, axis=0))
    for axis in (YAX, "x", "z"):
        mid = to_low(line_sum(mid, axis))
    enter_extra = jnp.stack([dot_tn(v[main:], lg[main:]) for v, lg in enters]).astype(bf16)
    leave_extra = jnp.stack([dot_tn(pick[main:], g[main:]) for pick, g in leaves]).astype(bf16)

    def halves(v, axis):
        other = swap(v)
        first = jnp.where(c == 0, v, other)
        second = jnp.where(c == 0, other, v)
        return jnp.concatenate([first, second], axis=axis).astype(f32)

    mid = halves(mid, 1).reshape(10, rank, width)
    mask = (column_owner == adapter_index[MIDDLE]).astype(f32)
    grad_leave_square = halves(leave_extra, 2) + jnp.tile(mid[5:], (1, ADAPTERS, 1)) * mask[None, :, None]
    grad_enter_square = (
        halves(enter_extra, 1) + jnp.tile(mid[:5].transpose(0, 2, 1), (1, 1, ADAPTERS)) * mask[None, None, :]
    )
    return (
        block_output,
        input_grad,
        grad_enter_square,
        grad_leave_square,
        grad_enter_widen,
        grad_leave_widen,
        grad_enter_narrow,
        grad_leave_narrow,
    )


def solution(mesh):
    split = Mesh(mesh.devices.reshape(SIZES), AXES)
    by_row = P(AXES, None)
    return jax.shard_map(
        per_device,
        mesh=split,
        in_specs=(by_row, by_row, P(AXES), P(), P(), P(), P(), P())
        + (by_row,) * 7
        + (P(),) * 6,
        out_specs=(by_row, by_row, P(), P(), P(), P(), P(), P()),
        check_vma=False,
    )
```

time: 1970 us -> 1050 us (0.53); the launches traced: 1940 us -> 1040 us
  local copies, waits for them, and re-layouts: 716 us -> 228 us
  waiting for transfers between devices: 599 us -> 206 us
  matrix products: 476 us -> 211 us
  starting transfers between devices: 11.7 us -> 223 us
  other arithmetic: 109 us -> 141 us
    all_gather x11 -> x3, waiting for transfers between devices: 473 us -> 0.01 us  [the longest x1 0.01 us: per_device(): near = lax.all_gather(shard[None], AXES, axis=0, tiled=True)]
    dot_general x56 -> x70, matrix products: 476 us -> 211 us  [the longest x19 90.9 us: dot(): return jnp.dot(a, b, preferred_element_type=f32)]
    dynamic_slice x256 -> x6, local copies, waits for them, and re-layouts: 254 us -> 24.9 us  [the longest x1 15 us: per_device(): lax.dynamic_slice(near, (0, per, c * halfw), (128, per, halfw))]
    ppermute x3 -> x100, starting transfers between devices: 10.8 us -> 216 us  [the longest x27 97 us: swap(): return lax.ppermute(v, 'c', [(0, 1), (1, 0)])]
    ppermute x3 -> x100, waiting for transfers between devices: 2.32 us -> 206 us  [the longest x51 174 us: shift4(): return lax.ppermute(v, axis, [(i, (i + by) % 4) for i in range(4)])]
    slice x97 -> x41, local copies, waits for them, and re-layouts: 176 us -> 36.3 us  [the longest x1 10.1 us: per_device(): w_wide = far[:, :8 * per].reshape(width, 2 * slotp)]
    psum x1 -> x0, waiting for transfers between devices: 118 us -> none  [per_device(): lax.psum((enter_stack, leave_stack, grad_enter_widen, grad_leave_widen, g...]
    pad x48 -> x1, local copies, waits for them, and re-layouts: 96.4 us -> 1.76 us  [per_device(): pieces = jnp.pad(pieces, ((0, 0), (0, 0), (0, 0), (0, slotp - slot)))]
  transfers between devices with their start and end apart: 15 -> 104, of which waited for: 10 -> 28; matrix products, arithmetic and copies ran while one was open for 35% -> 38% of each run, Pallas kernels for 0% -> 1%
where the time goes in v1:
time: 1050 us; the launch traced here: 1040 us
  local copies, waits for them, and re-layouts  228 us (22%)
  starting transfers between devices  223 us (21%)
  matrix products  211 us (20%)
  waiting for transfers between devices  206 us (20%)
  other arithmetic  141 us (13%)
  between operations  18.2 us (2%)
  Pallas kernels  11.5 us (1%)
    ppermute x51, waiting for transfers between devices, shift4(): return lax.ppermute(v, axis, [(i, (i + by) % 4) for i in range(4)])  174 us
    ppermute x27, starting transfers between devices, swap(): return lax.ppermute(v, 'c', [(0, 1), (1, 0)])  97 us
    dot_general x19, matrix products, dot(): return jnp.dot(a, b, preferred_element_type=f32)  90.9 us
    dot_general x19, matrix products, dot_nt(): lax.dot_general(a, b, (((1,), (1,)), ((), ())), preferred_element_type=f32)  88.5 us
    ppermute x51, starting transfers between devices, shift4(): return lax.ppermute(v, axis, [(i, (i + by) % 4) for i in range(4)])  72.8 us
    unnamed x435, local copies, waits for them, and re-layouts  43.6 us
    ppermute x18, waiting for transfers between devices, spread(): part = part + lax.ppermute(part, AXES, pairs)  24.5 us
    dot_general x28, matrix products, dot_tn(): lax.dot_general(a, b, (((0,), (0,)), ((), ())), preferred_element_type=f32)  22.8 us
  transfers between devices with their start and end apart: 104, of which 28 were waited for; matrix products, arithmetic and copies ran while one was open for 38% of the time, Pallas kernels for 1%

profile of v1, /device:TPU:1, one launch (start us, length us, event | category | flops | bytes accessed | tf_op | source)
XLA Modules:
  0.0 1039.3 jit_solution(1647565561616649765)
XLA Ops:
  15.1 11.9 %collective-permute-start.41 = (bf16[60,2560]{1,0:T(8,128)(2,1)}, bf16[60,2560]{1,0:T(8,128)(2,1)}, u32[]{:S(2)}, u32[]{:S(2)}) collective-permute-start(bf16[60,2560]{1,0:T(8,128)(2,1)} %param.35), channel_id=1, source_target_pairs={{1,0},{17,1},{33,2},{49,3},{65,4},{81,5},{97,6},{113,7},{2,8},{18,... | collective-permute-start | bytes 921608 | tf_op jit(solution)/shard_map/ppermute | solution.py:318
  27.0 11.0 %collective-permute-start.40 = (bf16[60,2560]{1,0:T(8,128)(2,1)}, bf16[60,2560]{1,0:T(8,128)(2,1)}, u32[]{:S(2)}, u32[]{:S(2)}) collective-permute-start(bf16[60,2560]{1,0:T(8,128)(2,1)} %param.35), channel_id=1, source_target_pairs={{0,0},{16,1},{32,2},{48,3},{64,4},{80,5},{96,6},{112,7},{1,8},{17,... | collective-permute-start | bytes 921608 | tf_op jit(solution)/shard_map/ppermute | solution.py:318
  93.7 25.4 %collective-permute-start.20 = (s32[128]{0:T(128)S(1)}, s32[128]{0:T(128)S(1)}, u32[]{:S(2)}, u32[]{:S(2)}) collective-permute-start(s32[128]{0:T(128)S(1)} %copy-done.177), channel_id=1, source_target_pairs={{0,1},{1,0},{2,3},{3,2},{4,5},{5,4},{6,7},{7,6},{8,9},{9,8},{10,11... | collective-permute-start | bytes 1544 | tf_op jit(solution)/shard_map/ppermute | solution.py:65
  137.3 24.1 %collective-permute-done.53 = bf16[128,2560]{1,0:T(8,128)(2,1)S(1)} collective-permute-done((bf16[128,2560]{1,0:T(8,128)(2,1)S(1)}, bf16[128,2560]{1,0:T(8,128)(2,1)S(1)}, u32[]{:S(2)}, u32[]{:S(2)}) %collective-permute-start.53) | collective-permute-done | bytes 655392 | tf_op jit(solution)/shard_map/ppermute | solution.py:69
  161.4 14.1 %collective-permute-start.54 = (bf16[128,2560]{1,0:T(8,128)(2,1)S(1)}, bf16[128,2560]{1,0:T(8,128)(2,1)S(1)}, u32[]{:S(2)}, u32[]{:S(2)}) collective-permute-start(bf16[128,2560]{1,0:T(8,128)(2,1)S(1)} %collective-permute-done.53), channel_id=1, source_target_pairs={{0,1},{1,0},{2,3},{3,2},{4,5},{5,4},{6,7},{7,6},{8,9},{9,8},{10,11... | collective-permute-start | bytes 1966088 | tf_op jit(solution)/shard_map/ppermute | solution.py:65
  192.3 9.9 collective-permute-start.45
  213.8 16.4 %collective-permute-done.18 = bf16[80,2560]{1,0:T(8,128)(2,1)S(1)} collective-permute-done((bf16[80,2560]{1,0:T(8,128)(2,1)S(1)}, bf16[80,2560]{1,0:T(8,128)(2,1)S(1)}, u32[]{:S(2)}, u32[]{:S(2)}) %collective-permute-start.18) | collective-permute-done | bytes 409632 | tf_op jit(solution)/shard_map/ppermute | solution.py:221
  261.4 15.0 %constant_dynamic-slice_fusion.22 = (bf16[128,20,1280]{2,1,0:T(8,128)(2,1)}, bf16[128,20,1280]{2,1,0:T(8,128)(2,1)}) fusion(bf16[128,64,2560]{2,1,0:T(8,128)(2,1)} %bitcast.273, s32[]{:T(128)S(6)} %select_n.581), kind=kLoop, calls=%fused_computation.507 | loop fusion | bytes 26214404 | tf_op jit(solution)/shard_map/dynamic_slice | solution.py:379
  276.4 10.8 %reshape.246 = bf16[2560,1280]{1,0:T(8,128)(2,1)} reshape(bf16[128,20,1280]{2,1,0:T(8,128)(2,1)} %get-tuple-element.103) | data formatting | bytes 13107200 | tf_op jit(solution)/shard_map/reshape | solution.py:379
  339.4 10.6 %reshape.244 = bf16[2560,1280]{1,0:T(8,128)(2,1)} reshape(bf16[128,20,1280]{2,1,0:T(8,128)(2,1)} %get-tuple-element.104) | data formatting | bytes 13107200 | tf_op jit(solution)/shard_map/reshape | solution.py:378
  356.1 8.8 fusion.77
  376.5 9.9 reshape.251
  423.7 10.1 slice.1008
  433.8 9.3 reshape.255
  454.0 10.7 %collective-permute-done.38 = bf16[128,2560]{1,0:T(8,128)(2,1)S(1)} collective-permute-done((bf16[128,2560]{1,0:T(8,128)(2,1)S(1)}, bf16[128,2560]{1,0:T(8,128)(2,1)S(1)}, u32[]{:S(2)}, u32[]{:S(2)}) %collective-permute-start.38) | collective-permute-done | bytes 655392 | tf_op jit(solution)/shard_map/ppermute | solution.py:69
  468.0 12.7 %collective-permute-done.34 = bf16[128,2560]{1,0:T(8,128)(2,1)S(1)} collective-permute-done((bf16[128,2560]{1,0:T(8,128)(2,1)S(1)}, bf16[128,2560]{1,0:T(8,128)(2,1)S(1)}, u32[]{:S(2)}, u32[]{:S(2)}) %collective-permute-start.34) | collective-permute-done | bytes 655392 | tf_op jit(solution)/shard_map/ppermute | solution.py:69
  493.0 21.1 %convolution_add_fusion.1 = f32[1280,2048]{1,0:T(8,128)} fusion(f32[1280,2048]{1,0:T(8,128)} %fusion.172, bf16[1280,2560]{1,0:T(8,128)(2,1)S(1)} %constant_dynamic-update-slice_fusion.7, bf16[2560,2048]{1,0:T(8,128)(2,1)} %bitcast.277), kind=kOutput, calls=%fused_computation.4 | convolution fusion | flops 13424394240 | bytes 38010880 | tf_op jit(solution)/shard_map/dot_general | solution.py:26
  514.1 18.6 %multiply_convert_fusion.1 = (bf16[1280,1024]{1,0:T(8,128)(2,1)S(1)}, bf16[1280,1024]{1,0:T(8,128)(2,1)}, bf16[1280,1024]{1,0:T(8,128)(2,1)S(1)}) fusion(f32[1280,2048]{1,0:T(8,128)} %convolution_add_fusion.1, f32[1280,1024]{1,0:T(8,128)} %fusion.168, bf16[1280,2560]{1,0:T(8,128)(2,1)} %get-tuple-element.73, bf16[1024,2560]{1,0:T(8,128)(2,1)} %reshape.255), kind=kOutput, calls=%fused_computation.18 | convolution fusion | flops 6743654400 | bytes 35389440 | tf_op jit(solution)/shard_map/dot_general | solution.py:30
  537.9 21.3 %fusion.7 = f32[1280,2560]{1,0:T(8,128)} fusion(bf16[2560,2048]{1,0:T(8,128)(2,1)} %bitcast.278, bf16[1280,1024]{1,0:T(8,128)(2,1)} %get-tuple-element.133, bf16[1280,1024]{1,0:T(8,128)(2,1)} %copy-done.65), kind=kOutput, calls=%fused_computation.42 | convolution fusion | flops 13432258560 | bytes 28835840 | tf_op jit(solution)/shard_map/dot_general | solution.py:30
  585.8 9.7 fusion.272
  653.3 31.9 %collective-permute-done.62 = bf16[160,2560]{1,0:T(8,128)(2,1)} collective-permute-done((bf16[160,2560]{1,0:T(8,128)(2,1)}, bf16[160,2560]{1,0:T(8,128)(2,1)}, u32[]{:S(2)}, u32[]{:S(2)}) %collective-permute-start.62) | collective-permute-done | bytes 819232 | tf_op jit(solution)/shard_map/ppermute | solution.py:69
  689.0 8.5 collective-permute-start.65
  699.9 12.0 %collective-permute-done.49 = bf16[128,2560]{1,0:T(8,128)(2,1)S(1)} collective-permute-done((bf16[128,2560]{1,0:T(8,128)(2,1)S(1)}, bf16[128,2560]{1,0:T(8,128)(2,1)S(1)}, u32[]{:S(2)}, u32[]{:S(2)}) %collective-permute-start.49) | collective-permute-done | bytes 655392 | tf_op jit(solution)/shard_map/ppermute | solution.py:69
  716.1 21.1 %collective-permute-done.50 = bf16[128,2560]{1,0:T(8,128)(2,1)S(1)} collective-permute-done((bf16[128,2560]{1,0:T(8,128)(2,1)S(1)}, bf16[128,2560]{1,0:T(8,128)(2,1)S(1)}, u32[]{:S(2)}, u32[]{:S(2)}) %collective-permute-start.50) | collective-permute-done | bytes 655392 | tf_op jit(solution)/shard_map/ppermute | solution.py:69
  741.3 9.0 collective-permute-start.63
  884.5 8.6 collective-permute-done.83
  898.8 14.4 %collective-permute-done.88 = bf16[160,1280]{1,0:T(8,128)(2,1)S(1)} collective-permute-done((bf16[160,1280]{1,0:T(8,128)(2,1)S(1)}, bf16[160,1280]{1,0:T(8,128)(2,1)S(1)}, u32[]{:S(2)}, u32[]{:S(2)}) %collective-permute-start.88) | collective-permute-done | bytes 409632 | tf_op jit(solution)/shard_map/ppermute | solution.py:69
  924.6 9.5 collective-permute-done.89
  968.1 10.5 %convert.135 = f32[8,144,8192]{2,1,0:T(8,128)S(1)} convert(bf16[8,144,8192]{2,1,0:T(8,128)(2,1)} %bitcast.264) | non-fusion elementwise | flops 9437184 | bytes 56623104 | tf_op jit(solution)/shard_map/convert_element_type | solution.py:476
  978.5 12.9 %slice_add_fusion = f32[8,128,8192]{2,1,0:T(8,128)} fusion(f32[8,144,8192]{2,1,0:T(8,128)S(1)} %convert.135, f32[128]{0:T(128)S(1)} %copy-done.156, f32[8,16,8192]{2,1,0:T(8,128)} %slice.1133), kind=kLoop, calls=%fused_computation | loop fusion | flops 16777216 | bytes 71303680 | tf_op jit(solution)/shard_map/add | solution.py:478
  991.5 8.4 slice_reduce_fusion
  1023.3 9.0 concatenate.233
  (912 shorter events, 583.6 us)
Async XLA Ops:
  7.2 247.6 %all-gather.7.cloned.1.call-start = ((), (), s32[]{:S(2)}) async-start(), calls=%async_computation.1 | async-start | bytes 42270720 | tf_op jit(solution)/shard_map/all_gather | solution.py:310
  15.1 50.1 %collective-permute-start.41 = (bf16[60,2560]{1,0:T(8,128)(2,1)}, bf16[60,2560]{1,0:T(8,128)(2,1)}, u32[]{:S(2)}, u32[]{:S(2)}) collective-permute-start(bf16[60,2560]{1,0:T(8,128)(2,1)} %param.35), channel_id=1, source_target_pairs={{1,0},{17,1},{33,2},{49,3},{65,4},{81,5},{97,6},{113,7},{2,8},{18,... | collective-permute-start | bytes 921608 | tf_op jit(solution)/shard_map/ppermute | solution.py:318
  27.0 39.5 %collective-permute-start.40 = (bf16[60,2560]{1,0:T(8,128)(2,1)}, bf16[60,2560]{1,0:T(8,128)(2,1)}, u32[]{:S(2)}, u32[]{:S(2)}) collective-permute-start(bf16[60,2560]{1,0:T(8,128)(2,1)} %param.35), channel_id=1, source_target_pairs={{0,0},{16,1},{32,2},{48,3},{64,4},{80,5},{96,6},{112,7},{1,8},{17,... | collective-permute-start | bytes 921608 | tf_op jit(solution)/shard_map/ppermute | solution.py:318
  38.0 55.7 %collective-permute-start.42 = (s32[128]{0:T(128)}, s32[128]{0:T(128)S(1)}, u32[]{:S(2)}, u32[]{:S(2)}) collective-permute-start(s32[128]{0:T(128)} %param.23), channel_id=1, source_target_pairs={{0,2},{2,4},{4,6},{6,0},{1,3},{3,5},{5,7},{7,1},{8,10},{10,12},{12... | collective-permute-start | bytes 1544 | tf_op jit(solution)/shard_map/ppermute | solution.py:69
  55.8 362.3 %all-gather.9.cloned.1.call-start = ((), (), s32[]{:S(2)}) async-start(), calls=%async_computation.2 | async-start | bytes 16711680 | tf_op jit(solution)/shard_map/all_gather | solution.py:323
  57.8 76.2 %collective-permute-start = (bf16[128,2560]{1,0:T(8,128)(2,1)}, bf16[128,2560]{1,0:T(8,128)(2,1)}, u32[]{:S(2)}, u32[]{:S(2)}) collective-permute-start(bf16[128,2560]{1,0:T(8,128)(2,1)} %get-tuple-element.176), channel_id=1, source_target_pairs={{0,1},{1,0},{2,3},{3,2},{4,5},{5,4},{6,7},{7,6},{8,9},{9,8},{10,11... | collective-permute-start | bytes 1966088 | tf_op jit(solution)/shard_map/ppermute | solution.py:65
  76.4 887.6 %all-gather.11.cloned.1.call-start = ((), (), s32[]{:S(2)}) async-start(), calls=%async_computation.3 | async-start | bytes 21233664 | tf_op jit(solution)/shard_map/all_gather | solution.py:475
  88.1 41.6 %collective-permute-start.15 = (bf16[80,2560]{1,0:T(8,128)(2,1)S(1)}, bf16[80,2560]{1,0:T(8,128)(2,1)}, u32[]{:S(2)}, u32[]{:S(2)}) collective-permute-start(bf16[80,2560]{1,0:T(8,128)(2,1)S(1)} %add.714), channel_id=1, source_target_pairs={{0,64},{2,66},{4,68},{6,70},{121,57},{123,59},{125,61},{127,63}} | collective-permute-start | bytes 1228808 | tf_op jit(solution)/shard_map/ppermute | solution.py:221
  89.7 43.4 %collective-permute-start.4 = (bf16[112,2560]{1,0:T(8,128)(2,1)S(1)}, bf16[112,2560]{1,0:T(8,128)(2,1)S(1)}, u32[]{:S(2)}, u32[]{:S(2)}) collective-permute-start(bf16[112,2560]{1,0:T(8,128)(2,1)S(1)} %add.703), channel_id=1, source_target_pairs={{0,8},{16,24},{32,40},{48,56},{64,72},{80,88},{96,104},{112,120},{... | collective-permute-start | bytes 1720328 | tf_op jit(solution)/shard_map/ppermute | solution.py:221
  132.3 44.2 %collective-permute-start.16 = (bf16[80,2560]{1,0:T(8,128)(2,1)S(1)}, bf16[80,2560]{1,0:T(8,128)(2,1)S(1)}, u32[]{:S(2)}, u32[]{:S(2)}) collective-permute-start(bf16[80,2560]{1,0:T(8,128)(2,1)S(1)} %add.715), channel_id=1, source_target_pairs={{0,32},{2,34},{4,36},{6,38},{64,96},{66,98},{68,100},{70,102},{57,... | collective-permute-start | bytes 1228808 | tf_op jit(solution)/shard_map/ppermute | solution.py:221
  133.1 44.2 %collective-permute-start.10 = (bf16[80,2560]{1,0:T(8,128)(2,1)S(1)}, bf16[80,2560]{1,0:T(8,128)(2,1)S(1)}, u32[]{:S(2)}, u32[]{:S(2)}) collective-permute-start(bf16[80,2560]{1,0:T(8,128)(2,1)S(1)} %add.709), channel_id=1, source_target_pairs={{0,2},{4,6},{8,10},{12,14},{16,18},{20,22},{24,26},{28,30},{99,97}... | collective-permute-start | bytes 1228808 | tf_op jit(solution)/shard_map/ppermute | solution.py:221
  133.9 44.2 %collective-permute-start.5 = (bf16[112,2560]{1,0:T(8,128)(2,1)S(1)}, bf16[112,2560]{1,0:T(8,128)(2,1)S(1)}, u32[]{:S(2)}, u32[]{:S(2)}) collective-permute-start(bf16[112,2560]{1,0:T(8,128)(2,1)S(1)} %add.704), channel_id=1, source_target_pairs={{0,4},{8,12},{16,20},{24,28},{32,36},{40,44},{48,52},{56,60},{64,6... | collective-permute-start | bytes 1720328 | tf_op jit(solution)/shard_map/ppermute | solution.py:221
  161.4 40.9 %collective-permute-start.55 = (bf16[128,2560]{1,0:T(8,128)(2,1)S(1)}, bf16[128,2560]{1,0:T(8,128)(2,1)S(1)}, u32[]{:S(2)}, u32[]{:S(2)}) collective-permute-start(bf16[128,2560]{1,0:T(8,128)(2,1)S(1)} %copy-done.38), channel_id=1, source_target_pairs={{0,4},{2,6},{4,0},{6,2},{1,5},{3,7},{5,1},{7,3},{8,12},{10,14},{12... | collective-permute-start | bytes 1966088 | tf_op jit(solution)/shard_map/ppermute | solution.py:69
  186.4 46.5 %collective-permute-start.57 = (bf16[128,2560]{1,0:T(8,128)(2,1)S(1)}, bf16[128,2560]{1,0:T(8,128)(2,1)S(1)}, u32[]{:S(2)}, u32[]{:S(2)}) collective-permute-start(bf16[128,2560]{1,0:T(8,128)(2,1)S(1)} %copy-done.38), channel_id=1, source_target_pairs={{0,6},{2,0},{4,2},{6,4},{1,7},{3,1},{5,3},{7,5},{8,14},{10,8},{12,... | collective-permute-start | bytes 1966088 | tf_op jit(solution)/shard_map/ppermute | solution.py:69
  192.3 215.4 %collective-permute-start.45 = (s32[128]{0:T(128)}, s32[128]{0:T(128)}, u32[]{:S(2)}, u32[]{:S(2)}) collective-permute-start(s32[128]{0:T(128)} %collective-permute-done.44), channel_id=1, source_target_pairs={{0,1},{1,0},{2,3},{3,2},{4,5},{5,4},{6,7},{7,6},{8,9},{9,8},{10,11... | collective-permute-start | bytes 1544 | tf_op jit(solution)/shard_map/ppermute | solution.py:65
  202.2 206.7 %collective-permute-start.47 = (s32[128]{0:T(128)}, s32[128]{0:T(128)}, u32[]{:S(2)}, u32[]{:S(2)}) collective-permute-start(s32[128]{0:T(128)} %collective-permute-done.46), channel_id=1, source_target_pairs={{0,1},{1,0},{2,3},{3,2},{4,5},{5,4},{6,7},{7,6},{8,9},{9,8},{10,11... | collective-permute-start | bytes 1544 | tf_op jit(solution)/shard_map/ppermute | solution.py:65
  405.3 37.8 %collective-permute-start.32 = (bf16[384,2560]{1,0:T(8,128)(2,1)S(1)}, bf16[384,2560]{1,0:T(8,128)(2,1)}, u32[]{:S(2)}, u32[]{:S(2)}) collective-permute-start(bf16[384,2560]{1,0:T(8,128)(2,1)S(1)} %pad_maximum_fusion.11), channel_id=1, source_target_pairs={{0,1},{1,0},{2,3},{3,2},{4,5},{5,4},{6,7},{7,6},{8,9},{9,8},{10,11... | collective-permute-start | bytes 5898248 | tf_op jit(solution)/shard_map/ppermute | solution.py:65
  567.0 37.4 %collective-permute-start.95 = (bf16[16,8192]{1,0:T(8,128)(2,1)}, bf16[16,8192]{1,0:T(8,128)(2,1)}, u32[]{:S(2)}, u32[]{:S(2)}) collective-permute-start(bf16[16,8192]{1,0:T(8,128)(2,1)} %fusion.150), channel_id=1, source_target_pairs={{0,8},{8,16},{16,24},{24,0},{1,9},{9,17},{17,25},{25,1},{2,10},{10... | collective-permute-start | bytes 786440 | tf_op jit(solution)/shard_map/ppermute | solution.py:69
  567.9 36.5 %collective-permute-start.94 = (bf16[16,8192]{1,0:T(8,128)(2,1)}, bf16[16,8192]{1,0:T(8,128)(2,1)}, u32[]{:S(2)}, u32[]{:S(2)}) collective-permute-start(bf16[16,8192]{1,0:T(8,128)(2,1)} %fusion.150), channel_id=1, source_target_pairs={{0,16},{8,24},{16,0},{24,8},{1,17},{9,25},{17,1},{25,9},{2,18},{10... | collective-permute-start | bytes 786440 | tf_op jit(solution)/shard_map/ppermute | solution.py:69
  568.4 36.0 %collective-permute-start.96 = (bf16[16,8192]{1,0:T(8,128)(2,1)}, bf16[16,8192]{1,0:T(8,128)(2,1)}, u32[]{:S(2)}, u32[]{:S(2)}) collective-permute-start(bf16[16,8192]{1,0:T(8,128)(2,1)} %fusion.150), channel_id=1, source_target_pairs={{0,24},{8,0},{16,8},{24,16},{1,25},{9,1},{17,9},{25,17},{2,26},{10... | collective-permute-start | bytes 786440 | tf_op jit(solution)/shard_map/ppermute | solution.py:69
  584.8 54.5 %collective-permute-start.48 = (bf16[512,2560]{1,0:T(8,128)(2,1)}, bf16[512,2560]{1,0:T(8,128)(2,1)}, u32[]{:S(2)}, u32[]{:S(2)}) collective-permute-start(bf16[512,2560]{1,0:T(8,128)(2,1)} %pad_maximum_fusion.6), channel_id=1, source_target_pairs={{0,1},{1,0},{2,3},{3,2},{4,5},{5,4},{6,7},{7,6},{8,9},{9,8},{10,11... | collective-permute-start | bytes 7864328 | tf_op jit(solution)/shard_map/ppermute | solution.py:65
  632.7 52.5 %collective-permute-start.62 = (bf16[160,2560]{1,0:T(8,128)(2,1)}, bf16[160,2560]{1,0:T(8,128)(2,1)}, u32[]{:S(2)}, u32[]{:S(2)}) collective-permute-start(bf16[160,2560]{1,0:T(8,128)(2,1)} %pad_maximum_fusion.33), channel_id=1, source_target_pairs={{0,2},{2,4},{4,6},{6,0},{1,3},{3,5},{5,7},{7,1},{8,10},{10,12},{12... | collective-permute-start | bytes 2457608 | tf_op jit(solution)/shard_map/ppermute | solution.py:69
  634.0 52.5 %collective-permute-start.60 = (bf16[160,2560]{1,0:T(8,128)(2,1)}, bf16[160,2560]{1,0:T(8,128)(2,1)}, u32[]{:S(2)}, u32[]{:S(2)}) collective-permute-start(bf16[160,2560]{1,0:T(8,128)(2,1)} %pad_maximum_fusion.31), channel_id=1, source_target_pairs={{0,6},{2,0},{4,2},{6,4},{1,7},{3,1},{5,3},{7,5},{8,14},{10,8},{12,... | collective-permute-start | bytes 2457608 | tf_op jit(solution)/shard_map/ppermute | solution.py:69
  644.4 67.4 %collective-permute-start.49 = (bf16[128,2560]{1,0:T(8,128)(2,1)S(1)}, bf16[128,2560]{1,0:T(8,128)(2,1)S(1)}, u32[]{:S(2)}, u32[]{:S(2)}) collective-permute-start(bf16[128,2560]{1,0:T(8,128)(2,1)S(1)} %get-tuple-element.134), channel_id=1, source_target_pairs={{0,6},{2,0},{4,2},{6,4},{1,7},{3,1},{5,3},{7,5},{8,14},{10,8},{12,... | collective-permute-start | bytes 1966088 | tf_op jit(solution)/shard_map/ppermute | solution.py:69
  645.5 70.7 %collective-permute-start.51 = (bf16[128,2560]{1,0:T(8,128)(2,1)S(1)}, bf16[128,2560]{1,0:T(8,128)(2,1)S(1)}, u32[]{:S(2)}, u32[]{:S(2)}) collective-permute-start(bf16[128,2560]{1,0:T(8,128)(2,1)S(1)} %get-tuple-element.135), channel_id=1, source_target_pairs={{0,2},{2,4},{4,6},{6,0},{1,3},{3,5},{5,7},{7,1},{8,10},{10,12},{12... | collective-permute-start | bytes 1966088 | tf_op jit(solution)/shard_map/ppermute | solution.py:69
  650.2 87.0 %collective-permute-start.50 = (bf16[128,2560]{1,0:T(8,128)(2,1)S(1)}, bf16[128,2560]{1,0:T(8,128)(2,1)S(1)}, u32[]{:S(2)}, u32[]{:S(2)}) collective-permute-start(bf16[128,2560]{1,0:T(8,128)(2,1)S(1)} %get-tuple-element.136), channel_id=1, source_target_pairs={{0,4},{2,6},{4,0},{6,2},{1,5},{3,7},{5,1},{7,3},{8,12},{10,14},{12... | collective-permute-start | bytes 1966088 | tf_op jit(solution)/shard_map/ppermute | solution.py:69
  688.9 62.0 %collective-permute-start.66 = (bf16[32,2560]{1,0:T(8,128)(2,1)S(1)}, bf16[32,2560]{1,0:T(8,128)(2,1)S(1)}, u32[]{:S(2)}, u32[]{:S(2)}) collective-permute-start(bf16[32,2560]{1,0:T(8,128)(2,1)S(1)} %fusion.153), channel_id=1, source_target_pairs={{0,2},{2,4},{4,6},{6,0},{1,3},{3,5},{5,7},{7,1},{8,10},{10,12},{12... | collective-permute-start | bytes 491528 | tf_op jit(solution)/shard_map/ppermute | solution.py:69
  689.0 61.9 %collective-permute-start.65 = (bf16[32,2560]{1,0:T(8,128)(2,1)S(1)}, bf16[32,2560]{1,0:T(8,128)(2,1)S(1)}, u32[]{:S(2)}, u32[]{:S(2)}) collective-permute-start(bf16[32,2560]{1,0:T(8,128)(2,1)S(1)} %fusion.153), channel_id=1, source_target_pairs={{0,4},{2,6},{4,0},{6,2},{1,5},{3,7},{5,1},{7,3},{8,12},{10,14},{12... | collective-permute-start | bytes 491528 | tf_op jit(solution)/shard_map/ppermute | solution.py:69
  711.9 38.4 %collective-permute-start.64 = (bf16[32,2560]{1,0:T(8,128)(2,1)S(1)}, bf16[32,2560]{1,0:T(8,128)(2,1)S(1)}, u32[]{:S(2)}, u32[]{:S(2)}) collective-permute-start(bf16[32,2560]{1,0:T(8,128)(2,1)S(1)} %fusion.153), channel_id=1, source_target_pairs={{0,6},{2,0},{4,2},{6,4},{1,7},{3,1},{5,3},{7,5},{8,14},{10,8},{12,... | collective-permute-start | bytes 491528 | tf_op jit(solution)/shard_map/ppermute | solution.py:69
  763.0 78.0 %collective-permute-start.82 = (f32[512,128]{0,1:T(8,128)}, f32[512,128]{0,1:T(8,128)}, u32[]{:S(2)}, u32[]{:S(2)}) collective-permute-start(f32[512,128]{0,1:T(8,128)} %fusion.160), channel_id=1, source_target_pairs={{0,1},{1,0},{2,3},{3,2},{4,5},{5,4},{6,7},{7,6},{8,9},{9,8},{10,11... | collective-permute-start | bytes 786440 | tf_op jit(solution)/shard_map/ppermute | solution.py:65
  862.8 76.2 %collective-permute-start.93 = (bf16[5,128,1280]{2,1,0:T(8,128)(2,1)S(1)}, bf16[5,128,1280]{2,1,0:T(8,128)(2,1)S(1)}, u32[]{:S(2)}, u32[]{:S(2)}) collective-permute-start(bf16[5,128,1280]{2,1,0:T(8,128)(2,1)S(1)} %fusion.69), channel_id=1, source_target_pairs={{0,1},{1,0},{2,3},{3,2},{4,5},{5,4},{6,7},{7,6},{8,9},{9,8},{10,11... | collective-permute-start | bytes 4915208 | tf_op jit(solution)/shard_map/ppermute | solution.py:65
  883.5 74.9 %collective-permute-start.81 = (bf16[5,1280,128]{2,1,0:T(8,128)(2,1)}, bf16[5,1280,128]{2,1,0:T(8,128)(2,1)}, u32[]{:S(2)}, u32[]{:S(2)}) collective-permute-start(bf16[5,1280,128]{2,1,0:T(8,128)(2,1)} %fusion.59), channel_id=1, source_target_pairs={{0,1},{1,0},{2,3},{3,2},{4,5},{5,4},{6,7},{7,6},{8,9},{9,8},{10,11... | collective-permute-start | bytes 4915208 | tf_op jit(solution)/shard_map/ppermute | solution.py:65
  (276 other events, 3676.2 us)
Sparse Core Ops, SparseCore 0:
  15.2 167.8 all-gather.6
  185.8 121.4 all-gather.8
  639.5 143.6 all-gather.10

commit v2 on v1

v2 whole, which is shorter than its diff:
```python
import functools
import jax
import jax.numpy as jnp
from jax import lax
from jax.experimental import pallas as pl
from jax.experimental.pallas import tpu as pltpu
from jax.sharding import Mesh, PartitionSpec as P

HEADS = 10
ADAPTERS = 8
HALO = 16
MIDDLE = 3
AXES = ("z", "x", "v", "u", "c")
SIZES = (4, 4, 2, 2, 2)
YAX = ("v", "u")
RING = ("v", "u", "c")
PLANE = ("z", "x")
QUAD = ("u", "c")
CHIPS = ("z", "x", "v", "u")
VMEM = 56 * 2**20

eps_norm = 1e-06
floor_scale = 0.001
bf16 = jnp.bfloat16
f32 = jnp.float32


def dot(a, b):
    return jnp.dot(a, b, preferred_element_type=f32)


def dot_nt(a, b):
    return lax.dot_general(a, b, (((1,), (1,)), ((), ())), preferred_element_type=f32)


def dot_tn(a, b):
    return lax.dot_general(a, b, (((0,), (0,)), ((), ())), preferred_element_type=f32)


def low(v):
    return lax.reduce_precision(v, 8, 7)


def to_low(v):
    return low(v).astype(bf16)


def norm_scale(values):
    return lax.rsqrt(jnp.mean(values * values, axis=-1, keepdims=True) + eps_norm)


def norm_apply(values, gain):
    return (values * norm_scale(values) * gain).astype(bf16)


def norm_back(values, gain, grad):
    s = norm_scale(values)
    gq = gain * grad
    return s * gq - values * (s * s * s) * jnp.mean(values * gq, axis=-1, keepdims=True)


def sigmoid(v):
    return 1.0 / (1.0 + jnp.exp(-v))


def gelu_parts(a):
    k = 0.7978845608028654
    a2 = a * a
    th = jnp.tanh(k * (a + 0.044715 * a2 * a))
    value = 0.5 * a * (1.0 + th)
    slope = 0.5 * (1.0 + th) + 0.5 * a * (1.0 - th * th) * (k * (1.0 + 3.0 * 0.044715 * a2))
    return value, slope


def swap(v):
    return lax.ppermute(v, "c", [(0, 1), (1, 0)])


def shift4(v, axis, by):
    return lax.ppermute(v, axis, [(i, (i + by) % 4) for i in range(4)])


def chip_shift(v, by, cross=False):
    chips = 64
    pairs = [
        (2 * p + c, 2 * (p + by) + (1 - c if cross else c))
        for p in range(chips)
        for c in range(2)
        if 0 <= p + by < chips
    ]
    return lax.ppermute(v, AXES, pairs)


def both(own, other, c):
    rows = own.shape[0]
    three = jnp.concatenate([own, other, own], axis=0)
    return lax.dynamic_slice_in_dim(three, c * rows, 2 * rows, axis=0)


def half(v, c, axis):
    size = v.shape[axis] // 2
    return lax.dynamic_slice_in_dim(v, c * size, size, axis=axis)


def after(first, *values):
    held = lax.optimization_barrier((first, *values))[1:]
    return held[0] if len(held) == 1 else held


def tied(value, other):
    return value + other[(0,) * other.ndim].astype(f32) * 0.0


def line_order(parts, y):
    back = parts[::-1]
    twice = jnp.stack(back + back)
    return lax.dynamic_slice_in_dim(twice, 3 - y, 4, axis=0)


def call(kernel, grid, ins, outs, scratch, scalars, args, micros, waits=()):
    count = len(args)

    def body(s_ref, *refs):
        kernel(s_ref, *refs[:count], *refs[count + len(waits) :])

    ins = list(ins) + [pl.BlockSpec(memory_space=pl.ANY)] * len(waits)
    args = (*args, *waits)
    return pl.pallas_call(
        body,
        grid_spec=pltpu.PrefetchScalarGridSpec(
            num_scalar_prefetch=1,
            grid=grid,
            in_specs=ins,
            out_specs=[spec for spec, _ in outs],
            scratch_shapes=scratch,
        ),
        out_shape=[jax.ShapeDtypeStruct(*shape) for _, shape in outs],
        compiler_params=pltpu.CompilerParams(vmem_limit_bytes=VMEM),
        cost_estimate=pl.CostEstimate(flops=int(micros * 1e9), bytes_accessed=int(micros * 2e6), transcendentals=0),
    )(scalars, *args)


def fixed(shape):
    return pl.BlockSpec(shape, lambda *_: (0,) * len(shape), pipeline_mode=pl.Buffered(1))


def scan_rows(d_ref, p_ref, s_ref, q_ref):
    rows, width = d_ref.shape
    row = lax.broadcasted_iota(jnp.int32, (8, width), 0)

    def tile(i, carry):
        state, product = carry
        at = pl.ds(pl.multiple_of(i * 8, 8), 8)
        a = d_ref[at, :]
        b = p_ref[at, :]
        for s in (1, 2, 4):
            b = a * jnp.where(row >= s, pltpu.roll(b, s, 0), 0.0) + b
            a = a * jnp.where(row >= s, pltpu.roll(a, s, 0), 1.0)
        value = b + a * state
        through = a * product
        s_ref[at, :] = value
        q_ref[at, :] = through
        return value[7:8, :], through[7:8, :]

    lax.fori_loop(
        0, rows // 8, tile, (jnp.zeros((1, width), f32), jnp.ones((1, width), f32)), unroll=8
    )


def scan_rows_back(d_ref, g_ref, s_ref, q_ref, main):
    rows, width = d_ref.shape
    row = lax.broadcasted_iota(jnp.int32, (8, width), 0)

    def tile(i, carry):
        state, product, after_row = carry
        at = pl.ds(pl.multiple_of(i * 8, 8), 8)
        d = d_ref[at, :]
        b = g_ref[at, :]
        a = jnp.where(row < 7, pltpu.roll(d, 7, 0), after_row)
        for s in (1, 2, 4):
            b = a * jnp.where(row < 8 - s, pltpu.roll(b, 8 - s, 0), 0.0) + b
            a = a * jnp.where(row < 8 - s, pltpu.roll(a, 8 - s, 0), 1.0)
        value = b + a * state
        through = a * product
        s_ref[at, :] = value
        q_ref[at, :] = through
        return value[0:1, :], through[0:1, :], d[0:1, :]

    zero = jnp.zeros((1, width), f32)
    one = jnp.ones((1, width), f32)
    last, cut = rows // 8 - 1, main // 8
    lax.fori_loop(0, last + 1 - cut, lambda k, t: tile(last - k, t), (zero, zero, one), unroll=8)
    lax.fori_loop(0, cut, lambda k, t: tile(cut - 1 - k, t), (zero, one, one), unroll=8)


def tile_of(w, i):
    block = w[:, i]
    return block.reshape(block.shape[0] * block.shape[1], block.shape[2])


def ends_kernel(stretches, s_ref, near_ref, gain_ref, x_ref, normed_ref, down_ref, marks_ref, hold_ref):
    toks = x_ref.shape[0] // 2
    quarter = x_ref.shape[1] // 4
    reach = quarter + marks_ref.shape[1]
    size = 8 * stretches
    for core in range(2):
        for p in range(16):
            for h in range(stretches):
                row = p * size + h * 8
                for y in range(4):
                    block = near_ref[2 * p + y // 2, 2 * (y % 2) + core, :, h * reach : (h + 1) * reach].astype(f32)
                    cols = slice(y * quarter, (y + 1) * quarter)
                    if row < toks:
                        x_ref[core * toks + row : core * toks + row + 8, cols] = block[:, :quarter]
                        if y == 0:
                            marks_ref[core * toks + row : core * toks + row + 8, :] = block[:, quarter:]
                    else:
                        to = core * toks + row - toks
                        hold_ref[to : to + 8, cols] = block[:, :quarter]
    down_ref[...] = hold_ref[...].astype(bf16)
    x = x_ref[...]
    normed_ref[...] = norm_apply(x, gain_ref[...])


def pack_kernel(s_ref, exa_ref, exb_ref, exn_ref, pick_ref, lg_ref, down_ref, n2_ref, mid_ref, out_ref):
    cols, wide = exa_ref.shape
    rank = mid_ref.shape[0]
    lanes = out_ref.shape[1]
    share = down_ref.shape[1]
    for i, ref in enumerate((exa_ref, exb_ref, exn_ref)):
        out_ref[:cols, i * wide : (i + 1) * wide] = ref[...]
    at = 3 * wide
    out_ref[:cols, at : at + share] = dot_tn(pick_ref[...], down_ref[...]).astype(bf16)
    out_ref[:cols, at + share :] = dot_tn(lg_ref[...], n2_ref[...]).astype(bf16)
    total = mid_ref.shape[1]
    for i in range(3):
        lo, hi = i * lanes, min((i + 1) * lanes, total)
        rows = slice(cols + i * rank, cols + (i + 1) * rank)
        out_ref[rows, : hi - lo] = mid_ref[:, lo:hi]
        if hi - lo < lanes:
            out_ref[rows, hi - lo :] = jnp.zeros((rank, lanes - hi + lo), bf16)


def fill_kernel(c_ref, x_ref, w_ref, pick_ref, leave_ref, mask_ref, taps_ref, enter_ref, conv_ref, lat_ref, acc_ref):
    rows, width = conv_ref.shape
    acc_ref[...] = dot(x_ref[...], tile_of(w_ref, 0)) + dot(pick_ref[...], leave_ref[...])
    step = width // 5
    for j in range(5):
        at = slice(j * step, (j + 1) * step)
        total = taps_ref[0:1, at] * acc_ref[HALO : HALO + rows, at]
        for k in range(1, taps_ref.shape[0]):
            total = total + taps_ref[k : k + 1, at] * acc_ref[HALO - k : HALO - k + rows, at] * mask_ref[:, k - 1 : k]
        conv_ref[:, at] = total.astype(bf16)

    @pl.when(pl.program_id(0) == 0)
    def _():
        lat_ref[...] = jnp.zeros_like(lat_ref)

    lat_ref[...] += dot(conv_ref[...], enter_ref[...])


def gate_weights(w_ref, hold_ref):
    @pl.when(pl.program_id(0) == 0)
    def _():
        wide = w_ref.shape[3]
        for i in range(4):
            hold_ref[:, i * wide : (i + 1) * wide] = tile_of(w_ref, i)

    head = 2 * w_ref.shape[3]
    at = pl.ds(pl.multiple_of(pl.program_id(0) * head, head), head)
    return hold_ref[at, :head], hold_ref[at, head:]


def gates_kernel(
    c_ref, conv_ref, own_ref, other_ref, select_ref, w_ref, leave_in_ref, leave_de_ref, mask_ref, rate_ref,
    sin_ref, sde_ref, dec_ref, state_ref, prod_ref, pick_in_ref, pick_de_ref, push_ref, hold_ref,
):
    cols = select_ref.shape[1]
    inner, decay = gate_weights(w_ref, hold_ref)

    @pl.when(pl.program_id(0) == 0)
    def _():
        lat = own_ref[...] + other_ref[...]
        select = select_ref[...]
        pick_in_ref[...] = (lat[:, :cols] * select).astype(bf16)
        pick_de_ref[...] = (lat[:, cols:] * select).astype(bf16)

    retain = mask_ref[:, 0:1]
    conv = conv_ref[...]
    sig_in = sigmoid(dot(conv, inner) + dot(pick_in_ref[...], leave_in_ref[...]))
    sig_de = sigmoid(dot(conv, decay) + dot(pick_de_ref[...], leave_de_ref[...]))
    raw = jnp.exp(-8.0 * rate_ref[...] * sig_de)
    scale = jnp.where(retain > 0.5, jnp.sqrt(jnp.maximum(1.0 - raw * raw, floor_scale)), 1.0)
    sin_ref[...] = sig_in
    sde_ref[...] = sig_de
    dec_ref[...] = raw * retain
    push_ref[...] = conv.astype(f32) * sig_in * scale
    scan_rows(dec_ref, push_ref, state_ref, prod_ref)


def gelu_kernel(c_ref, x_ref, w_ref, pick_ref, leave_ref, value_ref, slope_ref):
    pre = dot(x_ref[...], tile_of(w_ref, 0)) + dot(pick_ref[...], leave_ref[...])
    value, slope = gelu_parts(pre)
    value_ref[...] = value
    slope_ref[...] = slope


def out_kernel(
    c_ref, state_ref, prod_ref, entering_ref, branch_ref, w_ref, enter_ref, leave_ref, select_ref,
    states_ref, mixed_ref, lat_ref, mine_ref, send_ref, extra_ref, acc_ref, hold_ref,
):
    b = pl.program_id(0)
    q = w_ref.shape[3]
    states = state_ref[...] + prod_ref[...] * entering_ref[...]
    states_ref[...] = states
    hold_ref[...] = (branch_ref[...] * states).astype(bf16)
    mixed_ref[...] = hold_ref[...]

    @pl.when(b == 0)
    def _():
        lat_ref[...] = jnp.zeros_like(lat_ref)
        acc_ref[...] = jnp.zeros_like(acc_ref)

    lat_ref[...] += dot(hold_ref[...], enter_ref[...])
    for i in range(4):
        acc_ref[:, i * q : (i + 1) * q] += dot(hold_ref[...], tile_of(w_ref, i))

    @pl.when(b == pl.num_programs(0) - 1)
    def _():
        acc_ref[...] += dot((lat_ref[...] * select_ref[...]).astype(bf16), leave_ref[...])
        rows = mine_ref.shape[0]
        at = pl.multiple_of(c_ref[0] * rows, rows)
        mine_ref[...] = acc_ref[pl.ds(at, rows), :]
        send_ref[:rows, :] = acc_ref[pl.ds(pl.multiple_of(rows - at, rows), rows), :].astype(bf16)
        extra = acc_ref[2 * rows :, :].astype(bf16)
        send_ref[rows:, :] = extra
        extra_ref[...] = extra


def narrow_block(far_ref, j, top):
    wide = far_ref.shape[2]
    tail = wide // 4
    low_rows = (far_ref.shape[1] - top) // 5
    planes = pl.ds(4 * j, 4)
    main = far_ref[planes, top : top + 4 * low_rows, :].reshape(16 * low_rows, wide)
    pieces = []
    for p in range(4):
        rows = far_ref[4 * j + p, top + 4 * low_rows :, :]
        pieces += [rows[:, k * tail : (k + 1) * tail] for k in range(4)]
    return main, jnp.concatenate(pieces, axis=0)


def fetch(refs, hold_ref, sems):
    size = refs[0].shape[0]
    return [pltpu.make_async_copy(r, hold_ref.at[pl.ds(i * size, size), :], sems.at[i]) for i, r in enumerate(refs)]


def ffn_kernel(count, s_ref, *refs):
    n2_refs, gd_refs = refs[: 2 * count], refs[2 * count : 4 * count]
    far_ref, la_ref, lb_ref, en_ref, ew_ref, ln_ref, select_ref = refs[4 * count : 4 * count + 7]
    mine_ref, theirs_ref, ga_ref, gb_ref, hid_ref, lgw_ref, pickn_ref, pickw_ref, lgn_ref = refs[4 * count + 7 : 4 * count + 16]
    n2_hold, gd_hold, n2_sems, gd_sems = refs[4 * count + 16 :]
    side, width = mine_ref.shape
    slotp = hid_ref.shape[1]
    step = slotp // 4
    wide = far_ref.shape[2]
    top = width // 16
    n2_copies = fetch(n2_refs, n2_hold, n2_sems)
    gd_copies = fetch(gd_refs, gd_hold, gd_sems)
    for copy in n2_copies + gd_copies:
        copy.start()
    for copy in n2_copies + gd_copies:
        copy.wait()
    select = select_ref[...]
    pickw_ref[...] = (dot(n2_hold[...], ew_ref[...]) * select).astype(bf16)
    lgn_ref[...] = (dot_nt(gd_hold[...], ln_ref[...]) * select).astype(bf16)

    def hidden(j, _):
        at = pl.ds(pl.multiple_of(j * step, step), step)
        at_b = pl.ds(pl.multiple_of(slotp + j * step, step), step)
        a = dot(n2_hold[...], far_ref[:, :top, at].reshape(width, step)) + dot(pickw_ref[...], la_ref[:, at])
        up = dot(n2_hold[...], far_ref[:, :top, at_b].reshape(width, step)) + dot(pickw_ref[...], lb_ref[:, at])
        main, last = narrow_block(far_ref, j, top)
        grad = dot_nt(gd_hold[:, :wide], main) + dot_nt(gd_hold[:, wide:], last) + dot_nt(lgn_ref[...], en_ref[at, :])
        act, slope = gelu_parts(a)
        hid_ref[:, at] = (act * up).astype(bf16)
        ga_ref[:, at] = (slope * up * grad).astype(bf16)
        gb_ref[:, at] = (act * grad).astype(bf16)
        return 0

    lax.fori_loop(0, 4, hidden, 0)
    lgw_ref[...] = ((dot_nt(ga_ref[...], la_ref[...]) + dot_nt(gb_ref[...], lb_ref[...])) * select).astype(bf16)
    pickn_ref[...] = (dot(hid_ref[...], en_ref[...]) * select).astype(bf16)
    part = width // 4

    def back(q, _):
        at = pl.ds(pl.multiple_of(q * part, part), part)
        planes = pl.ds(4 * q, 4)
        total = dot_nt(ga_ref[...], far_ref[planes, :top, :slotp].reshape(part, slotp))
        total += dot_nt(gb_ref[...], far_ref[planes, :top, slotp:].reshape(part, slotp))
        total += dot_nt(lgw_ref[...], ew_ref[at, :])
        mine_ref[:, at] = total[:side].astype(bf16)
        theirs_ref[:, at] = total[side:].astype(bf16)
        return 0

    lax.fori_loop(0, 4, back, 0)


def down_kernel(s_ref, *refs):
    n2_refs, gd_refs = refs[:8], refs[8:16]
    hid0, hid1, ga0, ga1, gb0, gb1, far_ref, pick0, pick1, lgn0, lgn1, pickn0, pickn1, lgw0, lgw1, ln_ref = refs[16:32]
    down_ref, mida_ref, midb_ref, midn_ref, midl_ref, mide_ref, exa_ref, exb_ref, exn_ref = refs[32:41]
    acc_ref, hold_ref, wide_ref, n2_hold, gd_hold, n2_sems, gd_sems = refs[41:]
    j = pl.program_id(0)
    rank = mida_ref.shape[0]
    piece = n2_refs[0].shape[0]
    here = pl.ds(pl.multiple_of(s_ref[0] * rank, rank), rank)
    main, last = narrow_block(far_ref, 0, far_ref.shape[1] * 2 // 3)
    cut = main.shape[1]
    ring_of = lambda v, w: jnp.concatenate([v[:piece, :], v[2 * piece : 3 * piece, :], w[...]], axis=0)
    rest_of = lambda v: jnp.concatenate([v[piece : 2 * piece, :], v[3 * piece :, :]], axis=0)
    n2_copies = fetch(n2_refs, n2_hold, n2_sems)
    gd_copies = fetch(gd_refs, gd_hold, gd_sems)

    @pl.when(j == 0)
    def _():
        for copy in n2_copies + gd_copies:
            copy.start()
        acc_ref[...] = dot(ring_of(pickn0, pickn1), ln_ref[...])

    hid = ring_of(hid0, hid1)
    acc_ref[:, :cut] += dot(hid, main)
    acc_ref[:, cut:] += dot(hid, last)
    for left0, left1, right0, right1, out_ref, extra_ref in (
        (pick0, pick1, ga0, ga1, mida_ref, exa_ref),
        (pick0, pick1, gb0, gb1, midb_ref, exb_ref),
        (lgn0, lgn1, hid0, hid1, midn_ref, exn_ref),
    ):
        hold_ref[...] = dot_tn(ring_of(left0, left1), ring_of(right0, right1))
        out_ref[...] = hold_ref[here, :].astype(bf16)
        extra_ref[...] = dot_tn(rest_of(left0), rest_of(right0)).astype(bf16)

    @pl.when(j == pl.num_programs(0) - 1)
    def _():
        down_ref[...] = acc_ref[...].astype(bf16)
        for copy in n2_copies + gd_copies:
            copy.wait()
        wide_ref[...] = dot_tn(ring_of(pickn0, pickn1), gd_hold[...])
        midl_ref[...] = wide_ref[here, :].astype(bf16)
        wide_ref[...] = dot_tn(ring_of(lgw0, lgw1), n2_hold[...])
        mide_ref[...] = wide_ref[here, :].astype(bf16)


def outback_kernel(
    main, c_ref, go_ref, w_ref, leave_ref, enter_ref, select_ref, states_ref, branch_ref, slope_ref, dec_ref,
    gg_ref, lg_ref, state_ref, prod_ref, gs_ref,
):
    b = pl.program_id(0)
    q = w_ref.shape[3]

    @pl.when(b == 0)
    def _():
        lg_ref[...] = (dot_nt(go_ref[...], leave_ref[...]) * select_ref[...]).astype(bf16)

    gm = dot_nt(lg_ref[...], enter_ref[...])
    for i in range(4):
        gm += dot_nt(go_ref[:, i * q : (i + 1) * q], tile_of(w_ref, i))
    gg_ref[...] = (slope_ref[...] * (gm * states_ref[...])).astype(bf16)
    gs_ref[...] = gm * branch_ref[...]
    scan_rows_back(dec_ref, gs_ref, state_ref, prod_ref, main)


def geluback_kernel(c_ref, g_ref, w_ref, leave_ref, enter_ref, select_ref, part_ref, lat_ref, lg_ref):
    b = pl.program_id(0)
    q = w_ref.shape[3]

    @pl.when(b == 0)
    def _():
        lat = dot_nt(g_ref[...], leave_ref[...])
        lat_ref[...] = lat
        lg_ref[...] = (lat * select_ref[...]).astype(bf16)

    rows = part_ref.shape[0]
    part = dot_nt(g_ref[:rows, :q], tile_of(w_ref, 0)) + dot_nt(g_ref[:rows, q : 2 * q], tile_of(w_ref, 1))
    part_ref[...] = part + dot_nt(lg_ref[:rows, :], enter_ref[...])


def gateback_kernel(
    c_ref, back_ref, trail_ref, coming_ref, states_ref, entering_ref, conv_ref, sin_ref, sde_ref, dec_ref, mask_ref, rate_ref,
    w_ref, leave_in_ref, leave_de_ref,
    gi_ref, gd_ref, base_ref, lat_ref, hold_ref, gate_ref,
):
    rows = conv_ref.shape[0]
    cols = leave_in_ref.shape[0]
    inner, decay = gate_weights(w_ref, gate_ref)
    retain = mask_ref[:, 0:1]
    hold_ref[7:8, :] = entering_ref[...]
    hold_ref[8:, :] = states_ref[...]
    rate = rate_ref[...]
    sig_in = sin_ref[...]
    sig_de = sde_ref[...]
    conv = conv_ref[...].astype(f32)
    carried = back_ref[...] + trail_ref[...] * coming_ref[...]
    raw = jnp.exp(-8.0 * rate * sig_de)
    grown = 1.0 - raw * raw
    scale = jnp.where(retain > 0.5, jnp.sqrt(jnp.maximum(grown, floor_scale)), 1.0)
    through = carried * conv
    gi = (through * scale * sig_in * (1.0 - sig_in)).astype(bf16)
    grad_grown = jnp.where((grown > floor_scale) & (retain > 0.5), through * sig_in * 0.5 / scale, 0.0)
    grad_log = carried * hold_ref[7 : 7 + rows, :] * dec_ref[...] - 2.0 * raw * raw * grad_grown
    gd = (grad_log * (-8.0 * rate) * sig_de * (1.0 - sig_de)).astype(bf16)
    gi_ref[...] = gi
    gd_ref[...] = gd
    base_ref[...] = carried * sig_in * scale + dot_nt(gi, inner) + dot_nt(gd, decay)

    @pl.when(pl.program_id(0) == 0)
    def _():
        lat_ref[...] = jnp.zeros_like(lat_ref)

    lat_ref[:, :cols] += dot_nt(gi, leave_in_ref[...])
    lat_ref[:, cols:] += dot_nt(gd, leave_de_ref[...])


def fillback_kernel(
    c_ref, base_ref, own_ref, other_ref, hbase_ref, hown_ref, hother_ref, select_ref, mask_ref, taps_ref, enter_in_ref, enter_de_ref, leave_ref,
    w_ref, enter_ref, before_ref,
    gf_ref, lgi_ref, lgd_ref, lat_ref, mine_ref, theirs_ref, gc_ref, hlg_ref, lg_ref, part_ref,
):
    b = pl.program_id(0)
    q = w_ref.shape[3]
    rows, width = base_ref.shape
    main = part_ref.shape[0]
    cols = lgi_ref.shape[1]

    @pl.when(b == 0)
    def _():
        lat = own_ref[...] + other_ref[...]
        hlat = hown_ref[...] + hother_ref[...]
        select = select_ref[:rows, :]
        hselect = select_ref[rows:, :]
        lgi_ref[...] = (lat[:, :cols] * select).astype(bf16)
        lgd_ref[...] = (lat[:, cols:] * select).astype(bf16)
        hlg_ref[:, :cols] = (hlat[:, :cols] * hselect).astype(bf16)
        hlg_ref[:, cols:] = (hlat[:, cols:] * hselect).astype(bf16)
        step = width // 5
        for j in range(5):
            at = slice(j * step, (j + 1) * step)
            ei = enter_in_ref[at, :]
            ed = enter_de_ref[at, :]
            here = base_ref[:, at] + dot_nt(lgi_ref[...], ei) + dot_nt(lgd_ref[...], ed)
            gc_ref[:main, at] = here[:main]
            gc_ref[main : main + HALO, at] = (
                hbase_ref[:, at] + dot_nt(hlg_ref[:, :cols], ei) + dot_nt(hlg_ref[:, cols:], ed)
            )
            gc_ref[main + HALO : rows + HALO, at] = here[main:]
            gc_ref[rows + HALO :, at] = jnp.zeros((HALO, step), f32)
            for lo, hi, to in ((0, main, 0), (main + HALO, rows + HALO, main)):
                total = taps_ref[0:1, at] * gc_ref[lo:hi, at]
                for k in range(1, taps_ref.shape[0]):
                    total = total + taps_ref[k : k + 1, at] * gc_ref[lo + k : hi + k, at] * mask_ref[lo + k : hi + k, k - 1 : k]
                gf_ref[to : to + hi - lo, at] = total.astype(bf16)
        lat = dot_nt(gf_ref[...], leave_ref[...])
        lat_ref[...] = lat
        lg_ref[...] = (lat[:main] * select_ref[:main, :]).astype(bf16)

    part = dot_nt(gf_ref[:main, :q], tile_of(w_ref, 0)) + dot_nt(gf_ref[:main, q : 2 * q], tile_of(w_ref, 1))
    part_ref[...] = before_ref[...] + part + dot_nt(lg_ref[...], enter_ref[...])
    own = mine_ref.shape[0]
    at = pl.multiple_of(c_ref[0] * own, own)
    mine_ref[...] = part_ref[pl.ds(at, own), :]
    theirs_ref[...] = part_ref[pl.ds(pl.multiple_of(own - at, own), own), :].astype(bf16)


def mids_kernel(count, s_ref, *refs):
    out_ref, hold_ref = refs[2 * count :]
    rank = out_ref.shape[0] // count
    here = pl.ds(pl.multiple_of(s_ref[0] * rank, rank), rank)
    for i in range(count):
        hold_ref[...] = dot_tn(refs[2 * i][...], refs[2 * i + 1][...])
        out_ref[i * rank : (i + 1) * rank, :] = hold_ref[here, :].astype(bf16)


def extras_kernel(count, s_ref, *refs):
    enter_ref, leave_ref = refs[4 * count :]
    for i in range(count):
        enter_ref[i] = dot_tn(refs[2 * i][...], refs[2 * i + 1][...]).astype(bf16)
    for i in range(count):
        k = 2 * count + 2 * i
        leave_ref[i] = dot_tn(refs[k][...], refs[k + 1][...]).astype(bf16)


def square_kernel(s_ref, one_ref, own_e_ref, other_e_ref, own_l_ref, other_l_ref, own_me_ref, other_me_ref, own_ml_ref, other_ml_ref, enter_ref, leave_ref):
    size = own_e_ref.shape[1]
    one = one_ref[...]
    for core, e_ref, l_ref, me_ref, ml_ref in (
        (s_ref[0], own_e_ref, own_l_ref, own_me_ref, own_ml_ref),
        (1 - s_ref[0], other_e_ref, other_l_ref, other_me_ref, other_ml_ref),
    ):
        at = pl.ds(pl.multiple_of(core * size, size), size)
        enter_ref[0, at, :] = e_ref[0].astype(f32) + dot_tn(me_ref[...], one)
        leave_ref[0, :, at] = l_ref[0].astype(f32) + dot_tn(one, ml_ref[...])


def unit_parts(one_ref, extra_ref, mid_ref):
    one = one_ref[...]
    return [(extra_ref[m].astype(f32) + dot_tn(one, mid_ref[m])).astype(bf16) for m in range(8)]


def wide_kernel(s_ref, one_ref, spread_ref, extra_ref, mid_ref, out_ref):
    parts = unit_parts(one_ref, extra_ref, mid_ref)
    size = spread_ref.shape[1] // 8
    spread = spread_ref[...]
    done = [
        dot_nt(jnp.concatenate([v[:, p * size : (p + 1) * size] for v in parts], axis=1), spread) for p in range(4)
    ]
    out_ref[...] = jnp.concatenate(done, axis=1)


def enter_kernel(s_ref, one_ref, spread_ref, extra_ref, mid_ref, out_ref):
    parts = unit_parts(one_ref, extra_ref, mid_ref)
    units, size = spread_ref.shape
    size = size // 8
    spread = spread_ref[...]
    for p in range(4):
        some = jnp.concatenate([v[:, p * size : (p + 1) * size] for v in parts], axis=1)
        out_ref[p * units : (p + 1) * units, :] = dot_nt(spread, some)


def shares_kernel(s_ref, one_ref, eye_ref, extra_l_ref, extra_e_ref, mid0_ref, mid1_ref, mid2_ref, leave_ref, enter_ref):
    one = one_ref[...]
    width = leave_ref.shape[1]
    share = extra_l_ref.shape[2]
    start = mid0_ref.shape[2] - 2 * share
    sums = []
    for ref in (mid0_ref, mid1_ref, mid2_ref):
        total = ref[0].astype(f32)
        for m in range(1, 8):
            total = total + ref[m].astype(f32)
        sums.append(total.astype(bf16))
    mid = jnp.concatenate([sums[0][:, start:], sums[1], sums[2]], axis=1)
    leave_ref[...] = dot_tn(one, mid[:, :width])
    enter_ref[...] = dot_tn(mid[:, width : 2 * width], one)
    for m in range(8):
        lo, hi = m * share, min((m + 1) * share, width)
        if lo < hi:
            leave_ref[:, lo:hi] += extra_l_ref[m, :, : hi - lo].astype(f32)
            enter_ref[lo:hi, :] += dot_tn(extra_e_ref[m], eye_ref[...])[: hi - lo]


def linked(former, latter):
    return (former[0] * latter[0], latter[0] * former[1] + latter[1])


def line_carry(value, axis, reverse):
    sign = -1 if reverse else 1
    here = lax.axis_index(axis)
    here = 3 - here if reverse else here
    came = {by: shift4(value, axis, sign * by) for by in (1, 2, 3)}
    unit = (jnp.ones_like(value[0]), jnp.zeros_like(value[0]))

    def take(so_far, by, valid):
        new = linked(so_far, (came[by][0], came[by][1]))
        return tuple(jnp.where(valid, a, b) for a, b in zip(new, so_far))

    enter = unit
    for by in (3, 2, 1):
        enter = take(enter, by, here >= by)
    total = linked(enter, (value[0], value[1]))
    for by in (3, 2, 1):
        total = take(total, by, here < by)
    return enter, jnp.stack(total)


def chips_carry(value, reverse):
    by_y, line = line_carry(value, YAX, reverse)
    by_x, plane = line_carry(line, "x", reverse)
    by_z, _ = line_carry(plane, "z", reverse)
    return linked(linked(by_z, by_x), by_y)[1]


def index_of(place):
    at = 0
    for i, n in zip(place, (4, 4, 4, 2)):
        at = at * n + i
    return at


def scatter_ends(payload, seg_lanes, c):
    reached = {0: [(0, 0, 0)], 1: [(3, 3, 3)]}
    width = payload.shape[1]
    payload = jnp.concatenate([payload, seg_lanes], axis=1)
    for axis in range(3):
        if axis < 2:
            size = payload.shape[0] // 4
            pieces = [payload[k * size : (k + 1) * size] for k in range(4)]
        else:
            size = width // 4
            pieces = [jnp.concatenate([payload[:, k * size : (k + 1) * size], payload[:, width:]], axis=1) for k in range(4)]
        total = jnp.where(c == 0, pieces[0], pieces[3])
        added = {0: [], 1: []}
        for hop in (2, 1, 3):
            pairs = []
            for core in (0, 1):
                for place in reached[core]:
                    to = list(place)
                    to[axis] = hop if core == 0 else 3 - hop
                    added[core].append(tuple(to))
                    pairs.append((index_of((*place, core)), index_of((*to, core))))
            total = total + lax.ppermute(jnp.where(c == 0, pieces[hop], pieces[3 - hop]), AXES, pairs)
        for core in (0, 1):
            reached[core] = reached[core] + added[core]
        payload = total
    return payload


def line_sum(v, axis):
    one, two, three = (shift4(v, axis, by).astype(f32) for by in (1, 2, 3))
    return (v.astype(f32) + two) + (one + three)


def ring_rows(own):
    parts = [own] + [shift4(own, YAX, by) for by in (1, 2, 3)]
    return parts, [swap(part) for part in parts]


def line_back(sums):
    total = sums[0]
    for by in (1, 2, 3):
        total = total + shift4(sums[by].astype(bf16), YAX, -by).astype(f32)
    return total


def per_device(
    block_input,
    cotangent,
    segments,
    adapter_index,
    norm_first,
    norm_second,
    conv_taps,
    decay_rate,
    gelu_proj,
    input_proj,
    inner_gate,
    decay_gate,
    output_proj,
    widen_proj,
    narrow_proj,
    enter_square,
    leave_square,
    enter_widen,
    leave_widen,
    enter_narrow,
    leave_narrow,
):
    c = lax.axis_index("c")
    y = lax.axis_index(YAX)
    member = lax.axis_index(RING)
    plane = lax.axis_index(PLANE)
    chip = lax.axis_index(("z", "x", "v", "u"))
    place = lax.axis_index(AXES)
    toks, width = block_input.shape
    halfw = width // 2
    quarter = width // 4
    heads = HEADS // 2
    head = width // HEADS
    cols = enter_square.shape[-1]
    rank = cols // ADAPTERS
    main = 2 * toks
    per = gelu_proj.shape[0]
    per4 = 4 * per
    ff = widen_proj.shape[1] // 2
    slot = ff // 8
    slotp = slot * 16 // 15
    wide2 = 2 * slotp
    hcol = slotp // 4
    per_n = narrow_proj.shape[0]
    chunk = slotp // 16
    glane = 2 * head // 4

    grad_down_own = cotangent.astype(bf16)
    seg_lanes = jnp.broadcast_to(jnp.tile(segments, 2).astype(bf16)[:, None], (2 * toks, cols))
    payload = jnp.concatenate([block_input.astype(bf16), grad_down_own], axis=0)
    is_end = (place == 0) | (place == 127)
    piece = scatter_ends(jnp.where(is_end, payload, jnp.zeros_like(payload)), jnp.where(is_end, seg_lanes, jnp.zeros_like(seg_lanes)), c)

    gates = jnp.concatenate([inner_gate, decay_gate], axis=1)
    quads = jnp.stack(
        [
            jnp.concatenate(
                [v[:, q * (v.shape[1] // 4) : (q + 1) * (v.shape[1] // 4)] for v in (gelu_proj, input_proj, output_proj, gates)],
                axis=1,
            )
            for q in range(4)
        ]
    )
    lanes = quads.shape[2]
    quads = lax.all_to_all(quads, QUAD, 0, 0, tiled=True).reshape(per4, lanes)
    reach = piece.shape[1]
    stretches = piece.shape[0] // 8
    piece = jnp.concatenate([piece[k * 8 : (k + 1) * 8] for k in range(stretches)], axis=1)
    piece = jnp.pad(piece, ((0, 0), (0, lanes - stretches * reach)))
    quads = jnp.concatenate([quads, piece], axis=0)
    near = lax.all_gather(quads[None], AXES, axis=0, tiled=True).reshape(32, 4, per4 + 8, lanes)

    block_input, segments, widen_proj, narrow_proj = after(quads, block_input, segments, widen_proj, narrow_proj)

    block = 4 * 8 * per_n
    bcols = 4 * 8 * chunk
    at_col = jnp.arange(bcols)
    unit = at_col % (4 * chunk) % chunk
    from_row = at_col % (4 * chunk) // chunk * (8 * per_n) + at_col // (4 * chunk) * per_n + unit
    spread = ((jnp.arange(block)[:, None] == from_row[None, :]) & (unit < per_n)[None, :]).astype(bf16)
    units = 8 * per_n
    at_unit = jnp.arange(8 * chunk)
    spread_one = (jnp.arange(units)[:, None] == (at_unit // chunk * per_n + at_unit % chunk)[None, :]) & (at_unit % chunk < per_n)[None, :]
    spread_one = spread_one.astype(bf16)
    pieces = widen_proj.reshape(per, 8, block).transpose(1, 0, 2).reshape(8 * per, block)
    pieces = dot(pieces, spread).astype(bf16).reshape(8, per, 8, hcol).transpose(2, 1, 0, 3)
    pieces = lax.all_to_all(pieces.reshape(8 * per, wide2), RING, 0, 0, tiled=True)
    rows_n = jnp.pad(narrow_proj, ((0, chunk - per_n), (0, 0)))
    tail_n = rows_n[:, wide2:].reshape(4, chunk // 4, width - wide2).transpose(1, 0, 2).reshape(chunk // 4, wide2)
    shard_far = jnp.concatenate([pieces, rows_n[:, :wide2], tail_n], axis=0)
    far = lax.all_gather(shard_far[None], PLANE, axis=0, tiled=True)

    middle_owner = adapter_index[MIDDLE]
    column_owner = jnp.arange(cols) // rank
    owner_of = jnp.arange(adapter_index.shape[0])
    one_hot = (jnp.arange(cols)[None, :] == (middle_owner * rank + jnp.arange(rank))[:, None]).astype(bf16)
    core_at = c.astype(jnp.int32).reshape(1)
    middle_at = middle_owner.reshape(1)

    def select_of(segs):
        owners = jnp.sum((segs[:, None] == owner_of[None, :]).astype(jnp.int32) * adapter_index[None, :], axis=1)
        return (owners[:, None] == column_owner[None, :]).astype(f32)

    taps = half(conv_taps, c, 1)
    rate = half(decay_rate, c, 0)[None, :]
    enter_half = half(enter_square, c, 1)
    leave_half = half(leave_square, c, 2)
    enter_gates = jnp.concatenate([enter_half[2], enter_half[3]], axis=1)

    rows = 2 * main
    normed_own = norm_apply(block_input, norm_first)
    normed_main = both(normed_own, swap(normed_own), c)
    normed_halo = chip_shift(normed_main[main - HALO :], 1)
    normed_long = jnp.concatenate([normed_halo, normed_main], axis=0)
    seg_main = both(segments, swap(segments), c)
    halo_seg = jnp.broadcast_to(jnp.where(chip > 0, MIDDLE, -1), (HALO,))
    select_main = select_of(seg_main)
    select_halo = jnp.broadcast_to((column_owner == middle_owner).astype(f32)[None, :], (HALO, cols))
    ring_segs = [jnp.concatenate(v) for v in ring_rows(segments)]
    ring_selects = [select_of(v) for v in ring_segs]

    my_spread = lax.dynamic_slice_in_dim(spread, member * hcol, hcol, axis=1)
    leave_wide = leave_widen.reshape(cols, 8, block).transpose(1, 0, 2).reshape(8 * cols, block)
    leave_wide = dot(leave_wide, my_spread).astype(bf16).reshape(8, cols, hcol).transpose(1, 0, 2).reshape(cols, wide2)
    leave_a, leave_b = leave_wide[:, :slotp], leave_wide[:, slotp:]
    enter_down = lax.dot_general(
        my_spread, enter_narrow.reshape(4, block, cols), (((0,), (1,)), ((), ())), preferred_element_type=f32
    )
    enter_down = enter_down.transpose(1, 0, 2).reshape(slotp, cols).astype(bf16)

    near = after((shard_far, normed_long, select_main, ring_selects, leave_a, leave_b, enter_down, enter_gates), near)
    x_extra, normed_extra, down_extra, marks_extra = call(
        functools.partial(ends_kernel, stretches), (1,),
        [pl.BlockSpec((32, 4, 8, lanes), lambda *_: (0, 0, per4 // 8, 0), pipeline_mode=pl.Buffered(1)), fixed((1, width))],
        [(fixed((main, width)), ((main, width), f32)), (fixed((main, width)), ((main, width), bf16)),
         (fixed((main, width)), ((main, width), bf16)), (fixed((main, cols)), ((main, cols), f32))],
        [pltpu.VMEM((main, width), f32)],
        core_at, (near, norm_first[None, :]), 5,
    )
    seg_first = marks_extra[:toks, 0].astype(jnp.int32)
    seg_last = marks_extra[toks:, 0].astype(jnp.int32)
    seg_extra = jnp.concatenate([seg_first, seg_last])
    normed_long = jnp.concatenate([normed_long, normed_extra], axis=0)
    normed = normed_long[HALO:]
    marks = jnp.concatenate([halo_seg, seg_main, seg_first + 100, seg_last + 200])
    same = [(marks[HALO - k : -k] == marks[HALO:]).astype(f32)[:, None] for k in range(1, 4)]
    mask = jnp.concatenate(same + [jnp.zeros((rows, 5), f32)], axis=1)
    mask_long = jnp.concatenate([mask[:main], jnp.ones((HALO, 8), f32), mask[main:], jnp.zeros((HALO, 8), f32)], axis=0)
    select_extra = select_of(seg_extra) * (seg_extra != MIDDLE).astype(f32)[:, None]
    select = jnp.concatenate([select_main, select_extra], axis=0)
    select_long = jnp.concatenate([select_halo, select], axis=0)
    select_after = jnp.concatenate([select, select_halo], axis=0)
    pick_fill = (dot(normed_long, enter_square[1]) * select_long).astype(bf16)
    pick_gelu = (dot(normed, enter_square[0]) * select).astype(bf16)

    col_spec = lambda i: pl.BlockSpec((8, 2, per4, quarter), lambda b, s: (b, s[0], 0, i))
    out_spec = pl.BlockSpec((8, 4, per4, quarter), lambda b, s: (2 * s[0] + b, 0, 0, 2))
    gate_spec = pl.BlockSpec((16, 4, per4, glane), lambda b, s: (s[0], 0, 0, 3 * quarter // glane), pipeline_mode=pl.Buffered(1))
    side_col_spec = lambda i: pl.BlockSpec((32, 1, per4, quarter), lambda b, s: (0, 2 * s[0] + b, 0, i))
    rows_spec = lambda n: pl.BlockSpec((n, quarter), lambda b, s: (0, b))
    head_spec = lambda n: pl.BlockSpec((n, head), lambda h, s: (0, h))
    enter_spec = pl.BlockSpec((quarter, cols), lambda b, s: (b, 0))
    hidden_spec = lambda n: pl.BlockSpec((n, hcol), lambda j, s: (0, j))
    wide_block = (rows, halfw)
    small_block = (rows, cols)
    F = lambda *shape: (fixed(shape), (shape, f32))
    B = lambda *shape: (fixed(shape), (shape, bf16))
    layer = 2 * rows * halfw * width
    mib = 2**20

    gd_rows = ring_rows(grad_down_own)
    long = rows + HALO
    convolved, lat_gates = call(
        fill_kernel, (2,),
        [fixed((long, width)), side_col_spec(1), fixed((long, cols)), rows_spec(cols), fixed((rows, 8)), rows_spec(4),
         pl.BlockSpec((quarter, 2 * cols), lambda b, s: (b, 0))],
        [(rows_spec(rows), (wide_block, bf16)), F(rows, 2 * cols)],
        [pltpu.VMEM((long, quarter), f32)],
        core_at, (normed_long, near, pick_fill, leave_half[1], mask, taps, enter_gates), 12, (shard_far, *gd_rows[0][1:]),
    )
    pick_fill = pick_fill[HALO:]

    sides = lambda v: [half(v, c, 0), half(v, 1 - c, 0)]
    feed_select = [
        jnp.concatenate([ring_selects[0][:toks], sides(select_extra)[0], ring_selects[1][:toks], sides(select_extra)[1]], axis=0),
        jnp.concatenate([ring_selects[0][toks:], ring_selects[1][toks:]], axis=0),
    ]
    sig_in, sig_de, decays, state, prod, pick_in, pick_de = call(
        gates_kernel, (heads,),
        [head_spec(rows), fixed((rows, 2 * cols)), fixed((rows, 2 * cols)), fixed(small_block), gate_spec,
         head_spec(cols), head_spec(cols), fixed((rows, 8)), head_spec(1)],
        [(head_spec(rows), (wide_block, f32))] * 5 + [B(*small_block)] * 2,
        [pltpu.VMEM((rows, head), f32), pltpu.VMEM((halfw, 2 * head), bf16)],
        core_at, (convolved, lat_gates, swap(lat_gates), select, near, leave_half[2], leave_half[3], mask, rate), 12,
    )
    entering = chips_carry(jnp.stack([prod[main - 1], state[main - 1]]), False)[None, :]
    branch, slope = call(
        gelu_kernel, (2,),
        [fixed((rows, width)), side_col_spec(0), fixed(small_block), rows_spec(cols)],
        [(rows_spec(rows), (wide_block, f32))] * 2,
        [],
        core_at, (normed, near, pick_gelu, leave_half[0]), 12,
    )
    states, mixed, lat_out, out_mine, out_send, out_extra = call(
        out_kernel, (2,),
        [rows_spec(rows), rows_spec(rows), rows_spec(1), rows_spec(rows), out_spec, enter_spec, fixed((cols, width)), fixed(small_block)],
        [(rows_spec(rows), (wide_block, f32)), (rows_spec(rows), (wide_block, bf16)), F(*small_block),
         F(toks, width), B(toks + main, width), B(main, width)],
        [pltpu.VMEM((rows, width), f32), pltpu.VMEM((rows, quarter), bf16)],
        core_at, (state, prod, entering, branch, near, enter_half[4], leave_square[4], select), 15,
    )
    got = swap(out_send).astype(f32)
    residual = block_input + out_mine + got[:toks]
    residual_extra = x_extra + (out_extra.astype(f32) + got[toks:])
    n2_extra = norm_apply(residual_extra, norm_second)

    n2_rows = ring_rows(norm_apply(residual, norm_second))
    ring = 8 * toks
    anywhere = pl.BlockSpec(memory_space=pl.ANY)
    far_rows = far.shape[1]

    def feed(n2_pieces, gd_pieces, select, micros, waits=()):
        count = len(n2_pieces) // 2
        n = 2 * count * toks
        return call(
            functools.partial(ffn_kernel, count), (1,),
            [anywhere] * (4 * count)
            + [fixed(far.shape), fixed((cols, slotp)), fixed((cols, slotp)), fixed((slotp, cols)), fixed((width, cols)), fixed((cols, width)),
               fixed((n, cols))],
            [B(n // 2, width)] * 2 + [B(n, slotp)] * 3 + [B(n, cols)] * 4,
            [pltpu.VMEM((n, width), bf16), pltpu.VMEM((n, width), bf16), pltpu.SemaphoreType.DMA((2 * count,)), pltpu.SemaphoreType.DMA((2 * count,))],
            core_at,
            (*n2_pieces, *gd_pieces, far, leave_a, leave_b, enter_down, enter_widen, leave_narrow, select),
            micros, waits,
        )

    mix = lambda rows, extra: [rows[0][0], sides(extra)[0], rows[1][0], sides(extra)[1]]
    mine0, theirs0, *near_parts = feed(mix(n2_rows, n2_extra), mix(gd_rows, down_extra), feed_select[0], 25)
    mine1, theirs1, *far_parts = feed(n2_rows[0][1:] + n2_rows[1][1:], gd_rows[0][1:] + gd_rows[1][1:], feed_select[1], 37, (theirs0,))
    add = lambda a, b: a.astype(f32) + b.astype(f32)
    sums0 = add(mine0, swap(theirs0))

    eighth = main // 8
    extra_mine = sums0[toks:]
    extra_of = lambda k: lax.dynamic_slice_in_dim(extra_mine, jnp.remainder(y - k, 4) * eighth, eighth, axis=0)
    extra_total = line_back([extra_of(k) for k in range(4)]).astype(bf16)
    extra_half = line_order([extra_total] + [shift4(extra_total, YAX, by) for by in (1, 2, 3)], y).reshape(main // 2, -1)
    grad_n2_extra = both(extra_half, swap(extra_half), c).astype(f32)
    lat_side = jnp.concatenate([near_parts[3], near_parts[4]], axis=1)
    lat_sum = to_low(add(lat_side[toks : 2 * toks], swap(lat_side[3 * toks :])))
    lat_sum = line_sum(lat_sum, YAX).astype(bf16)
    lat_extra = both(lat_sum, swap(lat_sum), c)
    lgw_extra = lat_extra[:, :cols]
    pick_n_extra = lat_extra[:, cols:]

    sums1 = add(mine1, swap(theirs1)).astype(bf16)
    sums = [sums0[:toks]] + [sums1[k * toks : (k + 1) * toks] for k in range(3)]
    mid_spec = (pl.BlockSpec((rank, hcol), lambda j, s: (0, j)), ((rank, slotp), bf16))
    extra_spec = (pl.BlockSpec((cols, hcol), lambda j, s: (0, j)), ((cols, slotp), bf16))
    down, mid_a, mid_b, mid_n, mid_l, mid_e, ex_a, ex_b, ex_n = call(
        down_kernel, (4,),
        [anywhere] * 16 + [hidden_spec(4 * toks), hidden_spec(6 * toks)] * 3
        + [pl.BlockSpec((4, far_rows, wide2), lambda j, s: (j, 0, 0))]
        + [fixed((4 * toks, cols)), fixed((6 * toks, cols))] * 4 + [fixed((cols, width))],
        [B(ring, width)] + [mid_spec] * 3 + [B(rank, width)] * 2 + [extra_spec] * 3,
        [pltpu.VMEM((ring, width), f32), pltpu.VMEM((cols, hcol), f32), pltpu.VMEM((cols, width), f32),
         pltpu.VMEM((ring, width), bf16), pltpu.VMEM((ring, width), bf16), pltpu.SemaphoreType.DMA((8,)), pltpu.SemaphoreType.DMA((8,))],
        middle_at,
        (n2_rows[0][0], n2_rows[1][0], *n2_rows[0][1:], *n2_rows[1][1:], gd_rows[0][0], gd_rows[1][0], *gd_rows[0][1:], *gd_rows[1][1:],
         near_parts[2], far_parts[2], near_parts[0], far_parts[0], near_parts[1], far_parts[1], far,
         near_parts[5], far_parts[5], near_parts[6], far_parts[6], near_parts[4], far_parts[4], near_parts[3], far_parts[3], leave_narrow),
        19, (*sums[1:], extra_total),
    )
    ffn_mid = jnp.concatenate([mid_a, mid_b, mid_n, mid_l, mid_e], axis=1)
    mid_shape = ffn_mid.shape
    ffn_mid = lax.all_to_all(ffn_mid.reshape(16, -1, cols), PLANE, 0, 0, tiled=True)
    ffn_mid = to_low(jnp.sum(ffn_mid.astype(f32), axis=0))
    grad_n2 = tied(line_back(sums), ffn_mid)
    ffn_mid = lax.all_to_all(jnp.broadcast_to(ffn_mid[None], (16, *ffn_mid.shape)), PLANE, 0, 0, tiled=True).reshape(mid_shape)

    grad_residual = cotangent + norm_back(residual, norm_second, grad_n2)
    grad_residual_extra = down_extra.astype(f32) + norm_back(residual_extra, norm_second, grad_n2_extra)
    grad_out_own = grad_residual.astype(bf16)
    grad_out = jnp.concatenate([both(grad_out_own, swap(grad_out_own), c), grad_residual_extra.astype(bf16)], axis=0)
    down_mine = jnp.concatenate([down[:toks], down[2 * toks : 5 * toks]], axis=0)
    down_theirs = jnp.concatenate([down[toks : 2 * toks], down[5 * toks :]], axis=0)
    down_total = tied(add(down_mine, swap(down_theirs)), grad_out)
    down_sums = [down_total[k * toks : (k + 1) * toks] for k in range(4)]
    block_output = residual + line_back(down_sums)
    grad_gelu, lg_out, back, trail = call(
        functools.partial(outback_kernel, main), (2,),
        [fixed((rows, width)), out_spec, fixed((cols, width)), enter_spec, fixed(small_block)] + [rows_spec(rows)] * 4,
        [(rows_spec(rows), (wide_block, bf16)), B(*small_block)] + [(rows_spec(rows), (wide_block, f32))] * 2,
        [pltpu.VMEM((rows, quarter), f32)],
        core_at, (grad_out, near, leave_square[4], enter_half[4], select, states, branch, slope, decays), 18,
    )
    coming = chips_carry(jnp.stack([decays[0] * trail[0], decays[0] * back[0]]), True)[None, :]
    gelu_part, lat_gelu = call(
        geluback_kernel, (4,),
        [fixed(wide_block), col_spec(0), fixed((cols, halfw)), enter_spec, fixed(small_block)],
        [(rows_spec(main), ((main, width), f32)), F(*small_block)],
        [pltpu.VMEM(small_block, bf16)],
        core_at, (grad_gelu, near, leave_half[0], enter_square[0], select), 12,
    )

    grad_in, grad_de, base, lat_gates = call(
        gateback_kernel, (heads,),
        [head_spec(rows), head_spec(rows), head_spec(1), head_spec(rows), head_spec(1)] + [head_spec(rows)] * 4
        + [fixed((rows, 8)), head_spec(1), gate_spec, head_spec(cols), head_spec(cols)],
        [(head_spec(rows), (wide_block, bf16))] * 2 + [(head_spec(rows), (wide_block, f32)), F(rows, 2 * cols)],
        [pltpu.VMEM((rows + 8, head), f32), pltpu.VMEM((halfw, 2 * head), bf16)],
        core_at, (back, trail, coming, states, entering, convolved, sig_in, sig_de, decays, mask, rate, near, leave_half[2], leave_half[3]),
        8,
    )

    share = -(-width // 7 // 128) * 128
    share_of = lambda v: lax.dynamic_slice_in_dim(jnp.pad(v, ((0, 0), (0, 8 * share - width))), member * share, share, axis=1)
    lanes_all = 3 * slotp + 2 * share
    (packed,) = call(
        pack_kernel, (1,),
        [fixed((cols, slotp))] * 3 + [fixed((main, cols))] * 2 + [fixed((main, share))] * 2 + [fixed((rank, 3 * slotp + 2 * width))],
        [B(cols + 3 * rank, lanes_all)], [], core_at,
        (ex_a, ex_b, ex_n, pick_n_extra, lgw_extra, share_of(down_extra), share_of(n2_extra), ffn_mid), 3, (base,),
    )
    ffn_all = lax.all_gather(packed, RING, axis=0)

    halo_base = chip_shift(base[:HALO], -1)
    halo_lat = chip_shift(lat_gates[:HALO], -1)
    halo_other = chip_shift(lat_gates[:HALO], -1, cross=True)
    grad_fill, lg_in, lg_de, lat_fill, normed_mine, normed_theirs = call(
        fillback_kernel, (4,),
        [fixed(wide_block), fixed((rows, 2 * cols)), fixed((rows, 2 * cols)), fixed((HALO, halfw)), fixed((HALO, 2 * cols)), fixed((HALO, 2 * cols)),
         fixed((rows + HALO, cols)), fixed((rows + 2 * HALO, 8)), fixed((4, halfw)), fixed((halfw, cols)), fixed((halfw, cols)), fixed((cols, halfw)),
         col_spec(1), enter_spec, rows_spec(main)],
        [B(*wide_block), B(*small_block), B(*small_block), F(*small_block),
         (rows_spec(toks), ((toks, width), f32)), (rows_spec(toks), ((toks, width), bf16))],
        [pltpu.VMEM((rows + 2 * HALO, halfw), f32), pltpu.VMEM((HALO, 2 * cols), bf16), pltpu.VMEM((main, cols), bf16), pltpu.VMEM((main, quarter), f32)],
        core_at,
        (base, lat_gates, swap(lat_gates), halo_base, halo_lat, halo_other, select_after, mask_long, taps, enter_half[2], enter_half[3],
         leave_half[1], near, enter_square[1], gelu_part),
        12,
    )

    lat_all = jnp.concatenate([lat_gelu, lat_fill, lat_out], axis=1)
    lat_all = lat_all + swap(lat_all)
    lg_gelu = (lat_all[:, :cols] * select).astype(bf16)
    lg_fill = (lat_all[:, cols : 2 * cols] * select).astype(bf16)
    pick_out = (lat_all[:, 2 * cols :] * select).astype(bf16)
    normed_half = half(normed, c, 1)
    pairs = [
        (lg_gelu, normed_half), (lg_fill, normed_half), (lg_in, convolved), (lg_de, convolved), (lg_out, mixed),
        (pick_gelu, grad_gelu), (pick_fill, grad_fill), (pick_in, grad_in), (pick_de, grad_de), (pick_out, half(grad_out, c, 1)),
    ]
    part_spec = lambda n, i: pl.BlockSpec((main, n), lambda *_: (i, 0), pipeline_mode=pl.Buffered(1))
    operands = [v for pair in pairs for v in pair]
    (mid,) = call(
        functools.partial(mids_kernel, 10), (1,),
        [part_spec(cols, 0), part_spec(halfw, 0)] * 10,
        [B(10 * rank, halfw)],
        [pltpu.VMEM((cols, halfw), f32)],
        middle_at, operands, 6,
    )
    mid_own = mid
    shape = mid.shape
    mid = lax.all_to_all(mid.reshape(64, -1, cols), CHIPS, 0, 0, tiled=True)
    mid = to_low(jnp.sum(mid.astype(f32), axis=0))
    mid = lax.all_to_all(jnp.broadcast_to(mid[None], (64, *mid.shape)), CHIPS, 0, 0, tiled=True).reshape(shape)

    operands = [*[v for pair in pairs[:5] for v in pair[::-1]], *[v for pair in pairs[5:] for v in pair]]
    enter_extra, leave_extra = call(
        functools.partial(extras_kernel, 5), (1,),
        [part_spec(halfw, 1), part_spec(cols, 1)] * 5 + [part_spec(cols, 1), part_spec(halfw, 1)] * 5,
        [B(5, halfw, cols), B(5, cols, halfw)],
        [],
        core_at, operands, 6, (mid_own,),
    )
    (grad_leave_widen,) = call(
        wide_kernel, (8,),
        [fixed((rank, cols)), fixed((units, 8 * chunk)), pl.BlockSpec((8, cols, hcol), lambda i, s: (0, 0, i)), pl.BlockSpec((8, rank, hcol), lambda i, s: (0, cols // rank, i))],
        [(pl.BlockSpec((cols, block), lambda i, s: (0, i)), ((cols, 2 * ff), f32))],
        [], core_at, (one_hot, spread_one, ffn_all, ffn_all), 12, (mid_own,),
    )
    (grad_enter_narrow,) = call(
        enter_kernel, (4,),
        [fixed((rank, cols)), fixed((units, 8 * chunk)), pl.BlockSpec((8, cols, hcol), lambda i, s: (0, 0, 8 + i)), pl.BlockSpec((8, rank, hcol), lambda i, s: (0, cols // rank, 8 + i))],
        [(pl.BlockSpec((block, cols), lambda i, s: (i, 0)), ((ff, cols), f32))],
        [], core_at, (one_hot, spread_one, ffn_all, ffn_all), 7, (mid_own,),
    )
    grad_normed = normed_mine + swap(normed_theirs).astype(f32)
    input_grad = grad_residual + norm_back(block_input, norm_first, grad_normed)
    eye = jnp.eye(cols, dtype=bf16)
    share_spec = lambda i: pl.BlockSpec((8, cols, share), lambda *_: (0, 0, 3 * slotp // share + i))
    mid_rows = lambda i: pl.BlockSpec((8, rank, lanes_all), lambda *_: (0, cols // rank + i, 0))
    grad_leave_narrow, grad_enter_widen = call(
        shares_kernel, (1,),
        [fixed((rank, cols)), fixed((cols, cols)), share_spec(0), share_spec(1)] + [mid_rows(i) for i in range(3)],
        [F(cols, width), F(width, cols)],
        [], core_at, (one_hot, eye) + (ffn_all,) * 5, 4, (mid_own,),
    )
    per_k = lambda *shape: pl.BlockSpec((1,) + shape, lambda k, s: (k,) + (0,) * len(shape))
    mid_e_spec = pl.BlockSpec((rank, halfw), lambda k, s: (k, 0))
    mid_l_spec = pl.BlockSpec((rank, halfw), lambda k, s: (5 + k, 0))
    mid_other = swap(mid)
    grad_enter_square, grad_leave_square = call(
        square_kernel, (5,),
        [fixed((rank, cols)), per_k(halfw, cols), per_k(halfw, cols), per_k(cols, halfw), per_k(cols, halfw),
         mid_e_spec, mid_e_spec, mid_l_spec, mid_l_spec],
        [(per_k(width, cols), ((5, width, cols), f32)), (per_k(cols, width), ((5, cols, width), f32))],
        [], core_at, (one_hot, enter_extra, swap(enter_extra), leave_extra, swap(leave_extra), mid, mid_other, mid, mid_other), 9,
    )
    return (
        block_output,
        input_grad,
        grad_enter_square,
        grad_leave_square,
        grad_enter_widen,
        grad_leave_widen,
        grad_enter_narrow,
        grad_leave_narrow,
    )


def solution(mesh):
    split = Mesh(mesh.devices.reshape(SIZES), AXES)
    by_row = P(AXES, None)
    return jax.shard_map(
        per_device,
        mesh=split,
        in_specs=(by_row, by_row, P(AXES), P(), P(), P(), P(), P()) + (by_row,) * 7 + (P(),) * 6,
        out_specs=(by_row, by_row, P(), P(), P(), P(), P(), P()),
        check_vma=False,
    )
```

time: 1050 us -> 765 us (0.73)
  Pallas kernels: 11.5 us -> 237 us
  matrix products: 211 us -> 15.9 us
  local copies, waits for them, and re-layouts: 228 us -> 93 us
  other arithmetic: 141 us -> 73.9 us
  waiting for transfers between devices: 206 us -> 146 us
  starting transfers between devices: 223 us -> 169 us
    pallas_call x2 -> x19, Pallas kernels: 11.5 us -> 237 us  [call(): pl.pallas_call(body, grid_spec=pltpu.PrefetchScalarGridSpec(num_scalar_pr...]
    ppermute x51 -> x42, waiting for transfers between devices: 174 us -> 21.3 us  [shift4(): return lax.ppermute(v, axis, [(i, (i + by) % 4) for i in range(4)])]
    dot_general x51 -> x1, matrix products: 121 us -> 2.64 us  [per_device(): lax.dot_general(my_spread, enter_narrow.reshape(4, block, cols), (((0,),...]
    all_gather x3, waiting for transfers between devices: 0.01 us -> 85.5 us  [the longest x1 76.9 us: per_device(): lax.all_gather(quads[None], AXES, axis=0, tiled=True)]
    dot_general x19 -> x4, matrix products: 90.9 us -> 13.2 us  [dot(): return jnp.dot(a, b, preferred_element_type=f32)]
    reshape x15 -> x9, local copies, waits for them, and re-layouts: 62.3 us -> 12.3 us  [the longest x3 3.05 us: per_device(): widen_proj.reshape(per, 8, block).transpose(1, 0, 2).reshape(8 * per, block)]
    ppermute x27 -> x28, starting transfers between devices: 97 us -> 50.2 us  [swap(): return lax.ppermute(v, 'c', [(0, 1), (1, 0)])]
    all_to_all x1 -> x6, starting transfers between devices: 6.69 us -> 48.2 us  [the longest x1 19.2 us: per_device(): quads = lax.all_to_all(quads, QUAD, 0, 0, tiled=True).reshape(per4, lanes)]
  transfers between devices with their start and end apart: 104 -> 92, of which waited for: 28 -> 19; matrix products, arithmetic and copies ran while one was open for 38% -> 21% of each run, Pallas kernels for 1% -> 22%
where the time goes in v2:
time: 765 us; the launch traced here: 753 us
  Pallas kernels  237 us (31%)
  starting transfers between devices  169 us (22%)
  waiting for transfers between devices  146 us (19%)
  local copies, waits for them, and re-layouts  93 us (12%)
  other arithmetic  73.9 us (10%)
  between operations  17.9 us (2%)
  matrix products  15.9 us (2%)
    pallas_call x19, Pallas kernels, call(): pl.pallas_call(body, grid_spec=pltpu.PrefetchScalarGridSpec(num_scalar_pr...  237 us
    all_gather x1, waiting for transfers between devices, per_device(): lax.all_gather(quads[None], AXES, axis=0, tiled=True)  76.9 us
    ppermute x42, starting transfers between devices, shift4(): return lax.ppermute(v, axis, [(i, (i + by) % 4) for i in range(4)])  57.2 us
    ppermute x28, starting transfers between devices, swap(): return lax.ppermute(v, 'c', [(0, 1), (1, 0)])  50.2 us
    unnamed x198, local copies, waits for them, and re-layouts  27.4 us
    ppermute x42, waiting for transfers between devices, shift4(): return lax.ppermute(v, axis, [(i, (i + by) % 4) for i in range(4)])  21.3 us
    all_to_all x1, starting transfers between devices, per_device(): quads = lax.all_to_all(quads, QUAD, 0, 0, tiled=True).reshape(per4, lanes)  19.2 us
  transfers between devices with their start and end apart: 92, of which 19 were waited for; matrix products, arithmetic and copies ran while one was open for 21% of the time, Pallas kernels for 22%

profile of v2, /device:TPU:1, one launch (start us, length us, event | category | flops | bytes accessed | tf_op | source)
XLA Modules:
  0.0 752.7 jit_solution(9930795691491992990)
XLA Ops:
  19.7 19.2 %all-to-all-start = ((bf16[4,20,2048]{2,1,0:T(8,128)(2,1)}), bf16[4,20,2048]{2,1,0:T(8,128)(2,1)}, u32[]{:S(2)}, u32[]{:S(2)}) async-start(bf16[4,20,2048]{2,1,0:T(8,128)(2,1)} %pad_maximum_fusion.6), calls=%async_computation | async-start | bytes 786432 | tf_op jit(solution)/shard_map/all_to_all | solution.py:798
  55.6 6.2 convolution_convert_fusion
  74.4 8.5 %all-to-all-done.1 = bf16[8,20,2048]{2,1,0:T(8,128)(2,1)} async-done(((bf16[8,20,2048]{2,1,0:T(8,128)(2,1)}), bf16[8,20,2048]{2,1,0:T(8,128)(2,1)}, u32[]{:S(2)}, u32[]{:S(2)}) %all-to-all-start.1) | async-done | bytes 655392 | tf_op jit(solution)/shard_map/all_to_all | solution.py:820
  91.4 6.3 copy.65
  97.7 6.3 copy.66
  143.2 76.9 %all-gather.7.cloned.1.call-done = bf16[11264,2048]{1,0:T(8,128)(2,1)} async-done(((bf16[88,2048]{1,0:T(8,128)(2,1)}), bf16[11264,2048]{1,0:T(8,128)(2,1)}) %all-gather.7.cloned.1.call-update) | async-done | bytes 46137360 | tf_op jit(solution)/shard_map/all_gather | solution.py:804
  232.4 11.5 %shard_map.261 = (bf16[512,1280]{1,0:T(8,128)(2,1)}, f32[512,256]{1,0:T(8,128)}) custom-call(s32[1]{0:T(128)} %bitcast.5.s_ref, bf16[528,2560]{1,0:T(8,128)(2,1)} %pad_maximum_fusion.2.refs_0_, bf16[32,4,88,2048]{3,2,1,0:T(8,128)(2,1)} %bitcast.108, bf16[528,128]{1,0:T(8,128)(2,1)} %fusion.31.refs_2_, bf16[128,1280]{1,0:T(8,128)(2,1)} %get-tuple-element.194.refs_3_.refs_11_, ...), custom_call_target="tpu_custom_call" | custom-call | flops 12000000000 | bytes 24000000 | tf_op jit(solution)/shard_map/pallas_call | solution.py:128
  247.7 10.9 %shard_map.262 = (f32[512,1280]{1,0:T(8,128)}, f32[512,1280]{1,0:T(8,128)}, f32[512,1280]{1,0:T(8,128)}, f32[512,1280]{1,0:T(8,128)}, f32[512,1280]{1,0:T(8,128)...) custom-call(s32[1]{0:T(128)} %bitcast.5.s_ref, ...), custom_call_target="tpu_custom_call" | custom-call | flops 12000000000 | bytes 24000000 | tf_op jit(solution)/shard_map/pallas_call | solution.py:128
  277.9 10.0 %shard_map.263 = (f32[512,1280]{1,0:T(8,128)}, f32[512,1280]{1,0:T(8,128)}) custom-call(s32[1]{0:T(128)} %bitcast.5.s_ref, bf16[512,2560]{1,0:T(8,128)(2,1)} %pad_maximum_fusion.refs_0_, bf16[32,4,88,2048]{3,2,1,0:T(8,128)(2,1)} %bitcast.110, bf16[512,128]{1,0:T(8,128)(2,1)} %fusion.32.refs_2_.refs_10_, bf16[128,1280]{1,0:T(8,128)(2,1)} %get-tuple-element.191.refs_3_.refs_2_), custom_call_target="tpu_custom_call" | custom-call | flops 12000000000 | bytes 24000000 | tf_op jit(solution)/shard_map/pallas_call | solution.py:128
  288.6 14.0 %shard_map.264 = (f32[512,1280]{1,0:T(8,128)}, bf16[512,1280]{1,0:T(8,128)(2,1)}, f32[512,128]{1,0:T(8,128)}, f32[128,2560]{1,0:T(8,128)}, bf16[384,2560]{1,0:T(8,128)(2,1)}, /*index=5*/bf16[256,2560]{1,0:T(8,128)(2,1)}) custom-call(s32[1]{0:T(128)} %bitcast.5.s_ref, f32[512,1280]{1,0:T(8,128)} %get-tuple-element.92.refs_0_, ...), custom_call_target="tpu_custom_call" | custom-call | flops 15000000512 | bytes 30000000 | tf_op jit(solution)/shard_map/pallas_call | solution.py:128
  319.0 8.5 %all-gather.9.cloned.1.call-done = bf16[3840,2048]{1,0:T(8,128)(2,1)} async-done(((bf16[240,2048]{1,0:T(8,128)(2,1)}), bf16[3840,2048]{1,0:T(8,128)(2,1)}) %all-gather.9.cloned.1.call-update) | async-done | bytes 15728656 | tf_op jit(solution)/shard_map/all_gather | solution.py:824
  327.5 30.7 %shard_map.265 = (bf16[256,2560]{1,0:T(8,128)(2,1)}, bf16[256,2560]{1,0:T(8,128)(2,1)}, bf16[512,1024]{1,0:T(8,128)(2,1)}, bf16[512,1024]{1,0:T(8,128)(2,1)}, bf...) custom-call(s32[1]{0:T(128)} %bitcast.5.s_ref, ...), custom_call_target="tpu_custom_call" | custom-call | flops 24999999488 | bytes 50000000 | tf_op jit(solution)/shard_map/pallas_call | solution.py:128
  381.2 18.5 %collective-permute-start.41 = (bf16[128,2560]{1,0:T(8,128)(2,1)}, bf16[128,2560]{1,0:T(8,128)(2,1)S(1)}, u32[]{:S(2)}, u32[]{:S(2)}) collective-permute-start(bf16[128,2560]{1,0:T(8,128)(2,1)} %collective-permute-done.19.refs_9_.refs_7_.refs_11_), channel_id=1, source_target_pairs={{0,1},{1,0},{2,3},{3,2},{4,5},{5,4},{6,7},{7,6},{8,9},{9,8},{10,11... | collective-permute-start | bytes 1966088 | tf_op jit(solution)/shard_map/ppermute | solution.py:76
  408.3 41.3 %shard_map.266 = (bf16[384,2560]{1,0:T(8,128)(2,1)}, bf16[384,2560]{1,0:T(8,128)(2,1)}, bf16[768,1024]{1,0:T(8,128)(2,1)}, bf16[768,1024]{1,0:T(8,128)(2,1)}, bf...) custom-call(s32[1]{0:T(128)} %bitcast.5.s_ref, ...), custom_call_target="tpu_custom_call" | custom-call | flops 36999999488 | bytes 74000000 | tf_op jit(solution)/shard_map/pallas_call | solution.py:128
  452.2 7.8 %collective-permute-done.57 = bf16[32,2560]{1,0:T(8,128)(2,1)S(1)} collective-permute-done((bf16[32,2560]{1,0:T(8,128)(2,1)S(1)}, bf16[32,2560]{1,0:T(8,128)(2,1)S(1)}, u32[]{:S(2)}, u32[]{:S(2)}) %collective-permute-start.57) | collective-permute-done | bytes 163872 | tf_op jit(solution)/shard_map/ppermute | solution.py:80
  465.8 19.4 %shard_map.267 = (bf16[1024,2560]{1,0:T(8,128)(2,1)}, bf16[16,1024]{1,0:T(8,128)(2,1)}, bf16[16,1024]{1,0:T(8,128)(2,1)}, bf16[16,1024]{1,0:T(8,128)(2,1)}, bf16...) custom-call(s32[1]{0:T(128)} %slice.463.s_ref, ...), custom_call_target="tpu_custom_call" | custom-call | flops 19000000512 | bytes 38000000 | tf_op jit(solution)/shard_map/pallas_call | solution.py:128
  506.8 5.4 collective-permute-done.49
  526.1 15.2 %shard_map.268 = (bf16[512,1280]{1,0:T(8,128)(2,1)}, bf16[512,128]{1,0:T(8,128)(2,1)}, f32[512,1280]{1,0:T(8,128)}, f32[512,1280]{1,0:T(8,128)}) custom-call(s32[1]{0:T(128)} %bitcast.5.s_ref, bf16[512,2560]{1,0:T(8,128)(2,1)} %pad_maximum_fusion.1.refs_0_, bf16[32,4,88,2048]{3,2,1,0:T(8,128)(2,1)} %bitcast.112, ...), custom_call_target="tpu_custom_call" | custom-call | flops 17999998976 | bytes 36000000 | tf_op jit(solution)/shard_map/pallas_call | solution.py:128
  554.9 5.9 all-to-all-start.5
  569.9 12.0 %shard_map.269 = (bf16[512,1280]{1,0:T(8,128)(2,1)}, bf16[512,1280]{1,0:T(8,128)(2,1)}, f32[512,1280]{1,0:T(8,128)}, f32[512,256]{1,0:T(8,128)}) custom-call(s32[1]{0:T(128)} %bitcast.5.s_ref, f32[512,1280]{1,0:T(8,128)} %get-tuple-element.127.refs_0_, f32[512,1280]{1,0:T(8,128)} %get-tuple-element.128.refs_1_, f32[1,1280]{1,0:T(1,128)} %fusion.72.refs_2_, ...), custom_call_target="tpu_custom_call" | custom-call | flops 8000000000 | bytes 16000000 | tf_op jit(solution)/shard_map/pallas_call | solution.py:128
  608.7 8.1 %shard_map.270 = (f32[256,2560]{1,0:T(8,128)}, f32[512,128]{1,0:T(8,128)}) custom-call(s32[1]{0:T(128)} %bitcast.5.s_ref, bf16[512,1280]{1,0:T(8,128)(2,1)} %get-tuple-element.133.refs_0_.refs_11_, bf16[32,4,88,2048]{3,2,1,0:T(8,128)(2,1)} %bitcast.114, bf16[128,1280]{1,0:T(8,128)(2,1)} %get-tuple-element.191.refs_3_.refs_2_, ...), custom_call_target="tpu_custom_call" | custom-call | flops 12000000000 | bytes 24000000 | tf_op jit(solution)/shard_map/pallas_call | solution.py:128
  618.0 12.1 %shard_map.271 = (bf16[512,1280]{1,0:T(8,128)(2,1)}, bf16[512,128]{1,0:T(8,128)(2,1)}, bf16[512,128]{1,0:T(8,128)(2,1)}, f32[512,128]{1,0:T(8,128)}, f32[128,2560]{1,0:T(8,128)}, /*index=5*/bf16[128,2560]{1,0:T(8,128)(2,1)}) custom-call(s32[1]{0:T(128)} %bitcast.5.s_ref, f32[512,1280]{1,0:T(8,128)} %get-tuple-element.131.refs_0_.refs_8_, ...), custom_call_target="tpu_custom_call" | custom-call | flops 12000000000 | bytes 24000000 | tf_op jit(solution)/shard_map/pallas_call | solution.py:128
  643.3 5.4 collective-permute-start.53
  651.0 5.6 shard_map.272.refs_20_.refs_7_.refs_4_
  658.8 7.8 %all-to-all-start.3 = ((bf16[64,25,128]{2,1,0:T(8,128)(2,1)}), bf16[64,25,128]{2,1,0:T(8,128)(2,1)S(1)}, u32[]{:S(2)}, u32[]{:S(2)}) async-start(bf16[64,25,128]{2,1,0:T(8,128)(2,1)} %reshape.295), calls=%async_computation.3 | async-start | bytes 1048576 | tf_op jit(solution)/shard_map/all_to_all | solution.py:1098
  666.6 6.1 shard_map.273
  674.2 12.1 %all-to-all-done.3 = bf16[64,25,128]{2,1,0:T(8,128)(2,1)S(1)} async-done(((bf16[64,25,128]{2,1,0:T(8,128)(2,1)}), bf16[64,25,128]{2,1,0:T(8,128)(2,1)S(1)}, u32[]{:S(2)}, u32[]{:S(2)}) %all-to-all-start.3) | async-done | bytes 409632 | tf_op jit(solution)/shard_map/all_to_all | solution.py:1098
  687.3 6.2 all-to-all-start.4
  696.9 8.0 %all-to-all-done.4 = bf16[64,25,128]{2,1,0:T(8,128)(2,1)} async-done(((bf16[64,25,128]{2,1,0:T(8,128)(2,1)}), bf16[64,25,128]{2,1,0:T(8,128)(2,1)}, u32[]{:S(2)}, u32[]{:S(2)}) %all-to-all-start.4) | async-done | bytes 409632 | tf_op jit(solution)/shard_map/all_to_all | solution.py:1100
  713.3 9.4 %shard_map.274 = (f32[5,2560,128]{2,1,0:T(8,128)}, f32[5,128,2560]{2,1,0:T(8,128)}) custom-call(s32[1]{0:T(128)} %bitcast.5.s_ref, bf16[16,128]{1,0:T(8,128)(2,1)} %fusion.64.refs_0_, bf16[5,1280,128]{2,1,0:T(8,128)(2,1)} %get-tuple-element.149.refs_1_, bf16[5,1280,128]{2,1,0:T(8,128)(2,1)} %collective-permute-done.75.refs_2_, ...), custom_call_target="tpu_custom_call" | custom-call | flops 8999999488 | bytes 18000000 | tf_op jit(solution)/shard_map/pallas_call | solution.py:128
  722.6 6.6 shard_map.278
  729.3 12.2 %shard_map.277 = f32[128,15360]{1,0:T(8,128)} custom-call(s32[1]{0:T(128)} %bitcast.5.s_ref, bf16[16,128]{1,0:T(8,128)(2,1)} %fusion.64.refs_0_, bf16[480,512]{1,0:T(8,128)(2,1)} %fusion.34.refs_1_, bf16[8,176,3840]{2,1,0:T(8,128)(2,1)} %bitcast.118, bf16[8,176,3840]{2,1,0:T(8,128)(2,1)} %bitcast.119, bf16[160,1280]{1,0:T(8,128)(2,1)} %shard_map.272.refs_20_.refs_7_.refs_4_), custom_call_target="tpu_custom_call" | custom-call | flops 12000000000 | bytes 24000000 | tf_op jit(solution)/shard_map/pallas_call | solution.py:128
  (562 shorter events, 300.9 us)
Async XLA Ops:
  16.3 22.6 %collective-permute-start.3 = (bf16[16,2688]{1,0:T(8,128)(2,1)}, bf16[16,2688]{1,0:T(8,128)(2,1)S(1)}, u32[]{:S(2)}, u32[]{:S(2)}) collective-permute-start(bf16[16,2688]{1,0:T(8,128)(2,1)} %get-tuple-element.218), channel_id=1, source_target_pairs={{0,16},{64,80},{32,48},{96,112},{127,111},{63,47},{95,79},{31,15}} | collective-permute-start | bytes 258056 | tf_op jit(solution)/shard_map/ppermute | solution.py:709
  16.9 22.0 %collective-permute-start.4 = (bf16[16,2688]{1,0:T(8,128)(2,1)}, bf16[16,2688]{1,0:T(8,128)(2,1)S(1)}, u32[]{:S(2)}, u32[]{:S(2)}) collective-permute-start(bf16[16,2688]{1,0:T(8,128)(2,1)} %get-tuple-element.219), channel_id=1, source_target_pairs={{0,8},{64,72},{32,40},{96,104},{127,119},{63,55},{95,87},{31,23}} | collective-permute-start | bytes 258056 | tf_op jit(solution)/shard_map/ppermute | solution.py:709
  17.6 21.3 %collective-permute-start.5 = (bf16[16,2688]{1,0:T(8,128)(2,1)S(1)}, bf16[16,2688]{1,0:T(8,128)(2,1)}, u32[]{:S(2)}, u32[]{:S(2)}) collective-permute-start(bf16[16,2688]{1,0:T(8,128)(2,1)S(1)} %get-tuple-element.220), channel_id=1, source_target_pairs={{0,24},{64,88},{32,56},{96,120},{127,103},{63,39},{95,71},{31,7}} | collective-permute-start | bytes 258056 | tf_op jit(solution)/shard_map/ppermute | solution.py:709
  19.7 25.9 %all-to-all-start = ((bf16[4,20,2048]{2,1,0:T(8,128)(2,1)}), bf16[4,20,2048]{2,1,0:T(8,128)(2,1)}, u32[]{:S(2)}, u32[]{:S(2)}) async-start(bf16[4,20,2048]{2,1,0:T(8,128)(2,1)} %pad_maximum_fusion.6), calls=%async_computation | async-start | bytes 786432 | tf_op jit(solution)/shard_map/all_to_all | solution.py:798
  38.9 181.3 %all-gather.7.cloned.1.call-start = ((), (), s32[]{:S(2)}) async-start(), calls=%async_computation.6 | async-start | bytes 46497792 | tf_op jit(solution)/shard_map/all_gather | solution.py:804
  71.8 255.7 %all-gather.9.cloned.1.call-start = ((), (), s32[]{:S(2)}) async-start(), calls=%async_computation.7 | async-start | bytes 16711680 | tf_op jit(solution)/shard_map/all_gather | solution.py:824
  87.2 145.2 %collective-permute-start.20 = (bf16[128,2560]{1,0:T(8,128)(2,1)}, bf16[128,2560]{1,0:T(8,128)(2,1)}, u32[]{:S(2)}, u32[]{:S(2)}) collective-permute-start(bf16[128,2560]{1,0:T(8,128)(2,1)} %convert_element_type.256.refs_4_.refs_8_), channel_id=1, source_target_pairs={{0,6},{2,0},{4,2},{6,4},{1,7},{3,1},{5,3},{7,5},{8,14},{10,8},{12,... | collective-permute-start | bytes 1966088 | tf_op jit(solution)/shard_map/ppermute | solution.py:80
  136.0 96.4 %collective-permute-start.19 = (bf16[128,2560]{1,0:T(8,128)(2,1)}, bf16[128,2560]{1,0:T(8,128)(2,1)}, u32[]{:S(2)}, u32[]{:S(2)}) collective-permute-start(bf16[128,2560]{1,0:T(8,128)(2,1)} %convert_element_type.256.refs_4_.refs_8_), channel_id=1, source_target_pairs={{0,4},{2,6},{4,0},{6,2},{1,5},{3,7},{5,1},{7,3},{8,12},{10,14},{12... | collective-permute-start | bytes 1966088 | tf_op jit(solution)/shard_map/ppermute | solution.py:80
  138.6 93.8 %collective-permute-start.18 = (bf16[128,2560]{1,0:T(8,128)(2,1)}, bf16[128,2560]{1,0:T(8,128)(2,1)}, u32[]{:S(2)}, u32[]{:S(2)}) collective-permute-start(bf16[128,2560]{1,0:T(8,128)(2,1)} %convert_element_type.256.refs_4_.refs_8_), channel_id=1, source_target_pairs={{0,2},{2,4},{4,6},{6,0},{1,3},{3,5},{5,7},{7,1},{8,10},{10,12},{12... | collective-permute-start | bytes 1966088 | tf_op jit(solution)/shard_map/ppermute | solution.py:80
  141.3 86.2 %collective-permute-start.10 = (bf16[16,2560]{1,0:T(8,128)(2,1)S(1)}, bf16[16,2560]{1,0:T(8,128)(2,1)S(1)}, u32[]{:S(2)}, u32[]{:S(2)}) collective-permute-start(bf16[16,2560]{1,0:T(8,128)(2,1)S(1)} %slice.566), channel_id=1, source_target_pairs={{0,2},{1,3},{2,4},{3,5},{4,6},{5,7},{6,8},{7,9},{8,10},{9,11},{10,... | collective-permute-start | bytes 245768 | tf_op jit(solution)/shard_map/ppermute | solution.py:91
  363.2 18.0 %collective-permute-start.34 = (bf16[128,2560]{1,0:T(8,128)(2,1)S(1)}, bf16[128,2560]{1,0:T(8,128)(2,1)S(1)}, u32[]{:S(2)}, u32[]{:S(2)}) collective-permute-start(bf16[128,2560]{1,0:T(8,128)(2,1)S(1)} %copy-done.40), channel_id=1, source_target_pairs={{0,4},{2,6},{4,0},{6,2},{1,5},{3,7},{5,1},{7,3},{8,12},{10,14},{12... | collective-permute-start | bytes 1966088 | tf_op jit(solution)/shard_map/ppermute | solution.py:80
  364.7 35.0 %collective-permute-start.33 = (bf16[128,2560]{1,0:T(8,128)(2,1)S(1)}, bf16[128,2560]{1,0:T(8,128)(2,1)S(1)}, u32[]{:S(2)}, u32[]{:S(2)}) collective-permute-start(bf16[128,2560]{1,0:T(8,128)(2,1)S(1)} %copy-done.40), channel_id=1, source_target_pairs={{0,2},{2,4},{4,6},{6,0},{1,3},{3,5},{5,7},{7,1},{8,10},{10,12},{12... | collective-permute-start | bytes 1966088 | tf_op jit(solution)/shard_map/ppermute | solution.py:80
  370.8 29.0 %collective-permute-start.45 = (bf16[32,2560]{1,0:T(8,128)(2,1)S(1)}, bf16[32,2560]{1,0:T(8,128)(2,1)S(1)}, u32[]{:S(2)}, u32[]{:S(2)}) collective-permute-start(bf16[32,2560]{1,0:T(8,128)(2,1)S(1)} %get-tuple-element.206), channel_id=1, source_target_pairs={{0,6},{2,0},{4,2},{6,4},{1,7},{3,1},{5,3},{7,5},{8,14},{10,8},{12,... | collective-permute-start | bytes 491528 | tf_op jit(solution)/shard_map/ppermute | solution.py:80
  377.8 22.5 %collective-permute-start.47 = (bf16[32,2560]{1,0:T(8,128)(2,1)S(1)}, bf16[32,2560]{1,0:T(8,128)(2,1)S(1)}, u32[]{:S(2)}, u32[]{:S(2)}) collective-permute-start(bf16[32,2560]{1,0:T(8,128)(2,1)S(1)} %get-tuple-element.207), channel_id=1, source_target_pairs={{0,2},{2,4},{4,6},{6,0},{1,3},{3,5},{5,7},{7,1},{8,10},{10,12},{12... | collective-permute-start | bytes 491528 | tf_op jit(solution)/shard_map/ppermute | solution.py:80
  379.0 22.2 %collective-permute-start.46 = (bf16[32,2560]{1,0:T(8,128)(2,1)S(1)}, bf16[32,2560]{1,0:T(8,128)(2,1)S(1)}, u32[]{:S(2)}, u32[]{:S(2)}) collective-permute-start(bf16[32,2560]{1,0:T(8,128)(2,1)S(1)} %get-tuple-element.208), channel_id=1, source_target_pairs={{0,4},{2,6},{4,0},{6,2},{1,5},{3,7},{5,1},{7,3},{8,12},{10,14},{12... | collective-permute-start | bytes 491528 | tf_op jit(solution)/shard_map/ppermute | solution.py:80
  381.2 23.0 %collective-permute-start.41 = (bf16[128,2560]{1,0:T(8,128)(2,1)}, bf16[128,2560]{1,0:T(8,128)(2,1)S(1)}, u32[]{:S(2)}, u32[]{:S(2)}) collective-permute-start(bf16[128,2560]{1,0:T(8,128)(2,1)} %collective-permute-done.19.refs_9_.refs_7_.refs_11_), channel_id=1, source_target_pairs={{0,1},{1,0},{2,3},{3,2},{4,5},{5,4},{6,7},{7,6},{8,9},{9,8},{10,11... | collective-permute-start | bytes 1966088 | tf_op jit(solution)/shard_map/ppermute | solution.py:76
  404.2 141.9 %collective-permute-start.81 = (bf16[128,256]{1,0:T(8,128)(2,1)}, bf16[128,256]{1,0:T(8,128)(2,1)}, u32[]{:S(2)}, u32[]{:S(2)}) collective-permute-start(bf16[128,256]{1,0:T(8,128)(2,1)} %reduce-precision_convert_fusion), channel_id=1, source_target_pairs={{0,6},{2,0},{4,2},{6,4},{1,7},{3,1},{5,3},{7,5},{8,14},{10,8},{12,... | collective-permute-start | bytes 196616 | tf_op jit(solution)/shard_map/ppermute | solution.py:80
  404.4 141.7 %collective-permute-start.80 = (bf16[128,256]{1,0:T(8,128)(2,1)}, bf16[128,256]{1,0:T(8,128)(2,1)}, u32[]{:S(2)}, u32[]{:S(2)}) collective-permute-start(bf16[128,256]{1,0:T(8,128)(2,1)} %reduce-precision_convert_fusion), channel_id=1, source_target_pairs={{0,2},{2,4},{4,6},{6,0},{1,3},{3,5},{5,7},{7,1},{8,10},{10,12},{12... | collective-permute-start | bytes 196616 | tf_op jit(solution)/shard_map/ppermute | solution.py:80
  405.8 44.9 %collective-permute-start.56 = (bf16[32,2560]{1,0:T(8,128)(2,1)S(1)}, bf16[32,2560]{1,0:T(8,128)(2,1)S(1)}, u32[]{:S(2)}, u32[]{:S(2)}) collective-permute-start(bf16[32,2560]{1,0:T(8,128)(2,1)S(1)} %add_convert_fusion.2.refs_35_), channel_id=1, source_target_pairs={{0,6},{2,0},{4,2},{6,4},{1,7},{3,1},{5,3},{7,5},{8,14},{10,8},{12,... | collective-permute-start | bytes 491528 | tf_op jit(solution)/shard_map/ppermute | solution.py:80
  462.1 32.9 %collective-permute-start.59 = (bf16[128,2560]{1,0:T(8,128)(2,1)}, bf16[128,2560]{1,0:T(8,128)(2,1)}, u32[]{:S(2)}, u32[]{:S(2)}) collective-permute-start(bf16[128,2560]{1,0:T(8,128)(2,1)} %bitcast.42), channel_id=1, source_target_pairs={{0,1},{1,0},{2,3},{3,2},{4,5},{5,4},{6,7},{7,6},{8,9},{9,8},{10,11... | collective-permute-start | bytes 1966088 | tf_op jit(solution)/shard_map/ppermute | solution.py:76
  464.7 39.4 %collective-permute-start.51 = (bf16[128,2560]{1,0:T(8,128)(2,1)}, bf16[128,2560]{1,0:T(8,128)(2,1)S(1)}, u32[]{:S(2)}, u32[]{:S(2)}) collective-permute-start(bf16[128,2560]{1,0:T(8,128)(2,1)} %get-tuple-element.201.refs_34_), channel_id=1, source_target_pairs={{0,2},{2,4},{4,6},{6,0},{1,3},{3,5},{5,7},{7,1},{8,10},{10,12},{12... | collective-permute-start | bytes 1966088 | tf_op jit(solution)/shard_map/ppermute | solution.py:80
  464.7 42.1 %collective-permute-start.50 = (bf16[128,2560]{1,0:T(8,128)(2,1)}, bf16[128,2560]{1,0:T(8,128)(2,1)}, u32[]{:S(2)}, u32[]{:S(2)}) collective-permute-start(bf16[128,2560]{1,0:T(8,128)(2,1)} %get-tuple-element.202.refs_33_), channel_id=1, source_target_pairs={{0,4},{2,6},{4,0},{6,2},{1,5},{3,7},{5,1},{7,3},{8,12},{10,14},{12... | collective-permute-start | bytes 1966088 | tf_op jit(solution)/shard_map/ppermute | solution.py:80
  504.2 42.0 %collective-permute-start.79 = (bf16[128,256]{1,0:T(8,128)(2,1)}, bf16[128,256]{1,0:T(8,128)(2,1)S(1)}, u32[]{:S(2)}, u32[]{:S(2)}) collective-permute-start(bf16[128,256]{1,0:T(8,128)(2,1)} %reduce-precision_convert_fusion), channel_id=1, source_target_pairs={{0,4},{2,6},{4,0},{6,2},{1,5},{3,7},{5,1},{7,3},{8,12},{10,14},{12... | collective-permute-start | bytes 196616 | tf_op jit(solution)/shard_map/ppermute | solution.py:80
  560.8 161.8 %all-gather.11.cloned.1.call-start = ((), (), s32[]{:S(2)}) async-start(), calls=%async_computation.8 | async-start | bytes 12165120 | tf_op jit(solution)/shard_map/all_gather | solution.py:1058
  598.9 37.6 %collective-permute-start.48 = (bf16[512,2560]{1,0:T(8,128)(2,1)}, bf16[512,2560]{1,0:T(8,128)(2,1)}, u32[]{:S(2)}, u32[]{:S(2)}) collective-permute-start(bf16[512,2560]{1,0:T(8,128)(2,1)} %pad_maximum_fusion.3), channel_id=1, source_target_pairs={{0,1},{1,0},{2,3},{3,2},{4,5},{5,4},{6,7},{7,6},{8,9},{9,8},{10,11... | collective-permute-start | bytes 7864328 | tf_op jit(solution)/shard_map/ppermute | solution.py:76
  643.3 63.1 %collective-permute-start.53 = (bf16[128,2560]{1,0:T(8,128)(2,1)}, bf16[128,2560]{1,0:T(8,128)(2,1)}, u32[]{:S(2)}, u32[]{:S(2)}) collective-permute-start(bf16[128,2560]{1,0:T(8,128)(2,1)} %get-tuple-element.198), channel_id=1, source_target_pairs={{0,6},{2,0},{4,2},{6,4},{1,7},{3,1},{5,3},{7,5},{8,14},{10,8},{12,... | collective-permute-start | bytes 1966088 | tf_op jit(solution)/shard_map/ppermute | solution.py:80
  648.7 60.5 %collective-permute-start.55 = (bf16[128,2560]{1,0:T(8,128)(2,1)}, bf16[128,2560]{1,0:T(8,128)(2,1)}, u32[]{:S(2)}, u32[]{:S(2)}) collective-permute-start(bf16[128,2560]{1,0:T(8,128)(2,1)} %get-tuple-element.199), channel_id=1, source_target_pairs={{0,2},{2,4},{4,6},{6,0},{1,3},{3,5},{5,7},{7,1},{8,10},{10,12},{12... | collective-permute-start | bytes 1966088 | tf_op jit(solution)/shard_map/ppermute | solution.py:80
  648.7 60.5 %collective-permute-start.54 = (bf16[128,2560]{1,0:T(8,128)(2,1)}, bf16[128,2560]{1,0:T(8,128)(2,1)}, u32[]{:S(2)}, u32[]{:S(2)}) collective-permute-start(bf16[128,2560]{1,0:T(8,128)(2,1)} %get-tuple-element.200), channel_id=1, source_target_pairs={{0,4},{2,6},{4,0},{6,2},{1,5},{3,7},{5,1},{7,3},{8,12},{10,14},{12... | collective-permute-start | bytes 1966088 | tf_op jit(solution)/shard_map/ppermute | solution.py:80
  658.8 27.5 %all-to-all-start.3 = ((bf16[64,25,128]{2,1,0:T(8,128)(2,1)}), bf16[64,25,128]{2,1,0:T(8,128)(2,1)S(1)}, u32[]{:S(2)}, u32[]{:S(2)}) async-start(bf16[64,25,128]{2,1,0:T(8,128)(2,1)} %reshape.295), calls=%async_computation.3 | async-start | bytes 1048576 | tf_op jit(solution)/shard_map/all_to_all | solution.py:1098
  672.7 39.8 %collective-permute-start.75 = (bf16[5,1280,128]{2,1,0:T(8,128)(2,1)}, bf16[5,1280,128]{2,1,0:T(8,128)(2,1)}, u32[]{:S(2)}, u32[]{:S(2)}) collective-permute-start(bf16[5,1280,128]{2,1,0:T(8,128)(2,1)} %get-tuple-element.149.refs_1_), channel_id=1, source_target_pairs={{0,1},{1,0},{2,3},{3,2},{4,5},{5,4},{6,7},{7,6},{8,9},{9,8},{10,11... | collective-permute-start | bytes 4915208 | tf_op jit(solution)/shard_map/ppermute | solution.py:76
  674.1 38.4 %collective-permute-start.76 = (bf16[5,128,1280]{2,1,0:T(8,128)(2,1)}, bf16[5,128,1280]{2,1,0:T(8,128)(2,1)}, u32[]{:S(2)}, u32[]{:S(2)}) collective-permute-start(bf16[5,128,1280]{2,1,0:T(8,128)(2,1)} %get-tuple-element.150.refs_3_), channel_id=1, source_target_pairs={{0,1},{1,0},{2,3},{3,2},{4,5},{5,4},{6,7},{7,6},{8,9},{9,8},{10,11... | collective-permute-start | bytes 4915208 | tf_op jit(solution)/shard_map/ppermute | solution.py:76
  687.3 17.6 %all-to-all-start.4 = ((bf16[64,25,128]{2,1,0:T(8,128)(2,1)}), bf16[64,25,128]{2,1,0:T(8,128)(2,1)}, u32[]{:S(2)}, u32[]{:S(2)}) async-start(bf16[64,25,128]{2,1,0:T(8,128)(2,1)} %broadcast_in_dim.61), calls=%async_computation.4 | async-start | bytes 1048576 | tf_op jit(solution)/shard_map/all_to_all | solution.py:1100
  (148 other events, 1515.6 us)
Sparse Core Ops, SparseCore 0:
  51.4 168.7 all-gather.6
  222.3 105.1 all-gather.8
  584.8 63.1 all-gather.10

commit v3 on v2

--- a/solution.py
+++ b/solution.py
@@ -241,8 +241,13 @@
             out_ref[rows, hi - lo :] = jnp.zeros((rank, lanes - hi + lo), bf16)
 
 
-def fill_kernel(c_ref, x_ref, w_ref, pick_ref, leave_ref, mask_ref, taps_ref, enter_ref, conv_ref, lat_ref, acc_ref):
+def fill_kernel(c_ref, x_ref, w_ref, first_ref, select_ref, leave_ref, mask_ref, taps_ref, enter_ref, conv_ref, lat_ref, pick_ref, acc_ref):
     rows, width = conv_ref.shape
+
+    @pl.when(pl.program_id(0) == 0)
+    def _():
+        pick_ref[...] = (dot(x_ref[...], first_ref[...]) * select_ref[...]).astype(bf16)
+
     acc_ref[...] = dot(x_ref[...], tile_of(w_ref, 0)) + dot(pick_ref[...], leave_ref[...])
     step = width // 5
     for j in range(5):
@@ -298,8 +303,12 @@
     scan_rows(dec_ref, push_ref, state_ref, prod_ref)
 
 
-def gelu_kernel(c_ref, x_ref, w_ref, pick_ref, leave_ref, value_ref, slope_ref):
-    pre = dot(x_ref[...], tile_of(w_ref, 0)) + dot(pick_ref[...], leave_ref[...])
+def gelu_kernel(c_ref, x_ref, w_ref, first_ref, select_ref, leave_ref, value_ref, slope_ref, pick_ref):
+    @pl.when(pl.program_id(0) == 0)
+    def _():
+        pick_ref[...] = (dot(x_ref[HALO:, :], first_ref[...]) * select_ref[...]).astype(bf16)
+
+    pre = dot(x_ref[HALO:, :], tile_of(w_ref, 0)) + dot(pick_ref[...], leave_ref[...])
     value, slope = gelu_parts(pre)
     value_ref[...] = value
     slope_ref[...] = slope
@@ -356,19 +365,30 @@
 
 
 def ffn_kernel(count, s_ref, *refs):
-    n2_refs, gd_refs = refs[: 2 * count], refs[2 * count : 4 * count]
-    far_ref, la_ref, lb_ref, en_ref, ew_ref, ln_ref, select_ref = refs[4 * count : 4 * count + 7]
-    mine_ref, theirs_ref, ga_ref, gb_ref, hid_ref, lgw_ref, pickn_ref, pickw_ref, lgn_ref = refs[4 * count + 7 : 4 * count + 16]
-    n2_hold, gd_hold, n2_sems, gd_sems = refs[4 * count + 16 :]
-    side, width = mine_ref.shape
+    n2_refs, gd_refs = refs[:count], refs[count : 2 * count]
+    far_hbm, la_ref, lb_ref, en_ref, ew_ref, ln_ref, select_ref = refs[2 * count : 2 * count + 7]
+    gn_ref, ga_ref, gb_ref, hid_ref, lgw_ref, pickn_ref, pickw_ref, lgn_ref = refs[2 * count + 7 : 2 * count + 15]
+    n2_hold, gd_hold, far_ref, n2_sems, gd_sems, far_sems = refs[2 * count + 15 :]
+    width = gn_ref.shape[1]
     slotp = hid_ref.shape[1]
     step = slotp // 4
     wide = far_ref.shape[2]
     top = width // 16
+
+    def far_copies(j):
+        at = pl.ds(pl.multiple_of(j * step, step), step)
+        at_b = pl.ds(pl.multiple_of(slotp + j * step, step), step)
+        planes = pl.ds(4 * j, 4)
+        places = [(slice(None), pl.ds(0, top), at), (slice(None), pl.ds(0, top), at_b), (planes, pl.ds(top, far_ref.shape[1] - top), slice(None))]
+        return [pltpu.make_async_copy(far_hbm.at[p], far_ref.at[p], far_sems.at[j, i]) for i, p in enumerate(places)]
+
     n2_copies = fetch(n2_refs, n2_hold, n2_sems)
     gd_copies = fetch(gd_refs, gd_hold, gd_sems)
     for copy in n2_copies + gd_copies:
         copy.start()
+    for j in range(4):
+        for copy in far_copies(j):
+            copy.start()
     for copy in n2_copies + gd_copies:
         copy.wait()
     select = select_ref[...]
@@ -376,6 +396,8 @@
     lgn_ref[...] = (dot_nt(gd_hold[...], ln_ref[...]) * select).astype(bf16)
 
     def hidden(j, _):
+        for copy in far_copies(j):
+            copy.wait()
         at = pl.ds(pl.multiple_of(j * step, step), step)
         at_b = pl.ds(pl.multiple_of(slotp + j * step, step), step)
         a = dot(n2_hold[...], far_ref[:, :top, at].reshape(width, step)) + dot(pickw_ref[...], la_ref[:, at])
@@ -398,9 +420,7 @@
         planes = pl.ds(4 * q, 4)
         total = dot_nt(ga_ref[...], far_ref[planes, :top, :slotp].reshape(part, slotp))
         total += dot_nt(gb_ref[...], far_ref[planes, :top, slotp:].reshape(part, slotp))
-        total += dot_nt(lgw_ref[...], ew_ref[at, :])
-        mine_ref[:, at] = total[:side].astype(bf16)
-        theirs_ref[:, at] = total[side:].astype(bf16)
+        gn_ref[:, at] = (total + dot_nt(lgw_ref[...], ew_ref[at, :])).astype(bf16)
         return 0
 
     lax.fori_loop(0, 4, back, 0)
@@ -408,17 +428,18 @@
 
 def down_kernel(s_ref, *refs):
     n2_refs, gd_refs = refs[:8], refs[8:16]
-    hid0, hid1, ga0, ga1, gb0, gb1, far_ref, pick0, pick1, lgn0, lgn1, pickn0, pickn1, lgw0, lgw1, ln_ref = refs[16:32]
-    down_ref, mida_ref, midb_ref, midn_ref, midl_ref, mide_ref, exa_ref, exb_ref, exn_ref = refs[32:41]
-    acc_ref, hold_ref, wide_ref, n2_hold, gd_hold, n2_sems, gd_sems = refs[41:]
+    hid, ga, gb, pick, lgn, pickn, lgw = [refs[16 + 3 * i : 19 + 3 * i] for i in range(7)]
+    far_ref, ln_ref = refs[37:39]
+    down_ref, mida_ref, midb_ref, midn_ref, midl_ref, mide_ref, exa_ref, exb_ref, exn_ref = refs[39:48]
+    acc_ref, hold_ref, wide_ref, n2_hold, gd_hold, n2_sems, gd_sems = refs[48:]
     j = pl.program_id(0)
     rank = mida_ref.shape[0]
     piece = n2_refs[0].shape[0]
     here = pl.ds(pl.multiple_of(s_ref[0] * rank, rank), rank)
     main, last = narrow_block(far_ref, 0, far_ref.shape[1] * 2 // 3)
     cut = main.shape[1]
-    ring_of = lambda v, w: jnp.concatenate([v[:piece, :], v[2 * piece : 3 * piece, :], w[...]], axis=0)
-    rest_of = lambda v: jnp.concatenate([v[piece : 2 * piece, :], v[3 * piece :, :]], axis=0)
+    ring_of = lambda v: jnp.concatenate([v[0][:piece, :], v[0][2 * piece : 3 * piece, :], v[1][...], v[2][...]], axis=0)
+    rest_of = lambda v: jnp.concatenate([v[0][piece : 2 * piece, :], v[0][3 * piece :, :]], axis=0)
     n2_copies = fetch(n2_refs, n2_hold, n2_sems)
     gd_copies = fetch(gd_refs, gd_hold, gd_sems)
 
@@ -426,28 +447,24 @@
     def _():
         for copy in n2_copies + gd_copies:
             copy.start()
-        acc_ref[...] = dot(ring_of(pickn0, pickn1), ln_ref[...])
-
-    hid = ring_of(hid0, hid1)
-    acc_ref[:, :cut] += dot(hid, main)
-    acc_ref[:, cut:] += dot(hid, last)
-    for left0, left1, right0, right1, out_ref, extra_ref in (
-        (pick0, pick1, ga0, ga1, mida_ref, exa_ref),
-        (pick0, pick1, gb0, gb1, midb_ref, exb_ref),
-        (lgn0, lgn1, hid0, hid1, midn_ref, exn_ref),
-    ):
-        hold_ref[...] = dot_tn(ring_of(left0, left1), ring_of(right0, right1))
+        acc_ref[...] = dot(ring_of(pickn), ln_ref[...])
+
+    hidden = ring_of(hid)
+    acc_ref[:, :cut] += dot(hidden, main)
+    acc_ref[:, cut:] += dot(hidden, last)
+    for left, right, out_ref, extra_ref in ((pick, ga, mida_ref, exa_ref), (pick, gb, midb_ref, exb_ref), (lgn, hid, midn_ref, exn_ref)):
+        hold_ref[...] = dot_tn(ring_of(left), ring_of(right))
         out_ref[...] = hold_ref[here, :].astype(bf16)
-        extra_ref[...] = dot_tn(rest_of(left0), rest_of(right0)).astype(bf16)
+        extra_ref[...] = dot_tn(rest_of(left), rest_of(right)).astype(bf16)
 
     @pl.when(j == pl.num_programs(0) - 1)
     def _():
         down_ref[...] = acc_ref[...].astype(bf16)
         for copy in n2_copies + gd_copies:
             copy.wait()
-        wide_ref[...] = dot_tn(ring_of(pickn0, pickn1), gd_hold[...])
+        wide_ref[...] = dot_tn(ring_of(pickn), gd_hold[...])
         midl_ref[...] = wide_ref[here, :].astype(bf16)
-        wide_ref[...] = dot_tn(ring_of(lgw0, lgw1), n2_hold[...])
+        wide_ref[...] = dot_tn(ring_of(lgw), n2_hold[...])
         mide_ref[...] = wide_ref[here, :].astype(bf16)
 
 
@@ -601,29 +618,27 @@
         leave_ref[0, :, at] = l_ref[0].astype(f32) + dot_tn(one, ml_ref[...])
 
 
-def unit_parts(one_ref, extra_ref, mid_ref):
-    one = one_ref[...]
-    return [(extra_ref[m].astype(f32) + dot_tn(one, mid_ref[m])).astype(bf16) for m in range(8)]
+def unit_parts(one_ref, extra_ref, mid_ref, size):
+    count = extra_ref.shape[0]
+    cut = lambda ref, p: jnp.concatenate([ref[m, :, p * size : (p + 1) * size] for m in range(count)], axis=1)
+    mid = jnp.concatenate([cut(mid_ref, p) for p in range(4)], axis=1)
+    placed = dot_tn(one_ref[...], mid).astype(bf16)
+    wide = count * size
+    return jnp.concatenate([cut(extra_ref, p) + placed[:, p * wide : (p + 1) * wide] for p in range(4)], axis=0)
 
 
 def wide_kernel(s_ref, one_ref, spread_ref, extra_ref, mid_ref, out_ref):
-    parts = unit_parts(one_ref, extra_ref, mid_ref)
-    size = spread_ref.shape[1] // 8
-    spread = spread_ref[...]
-    done = [
-        dot_nt(jnp.concatenate([v[:, p * size : (p + 1) * size] for v in parts], axis=1), spread) for p in range(4)
-    ]
-    out_ref[...] = jnp.concatenate(done, axis=1)
+    cols = out_ref.shape[0]
+    done = dot_nt(unit_parts(one_ref, extra_ref, mid_ref, spread_ref.shape[1] // 8), spread_ref[...])
+    out_ref[...] = jnp.concatenate([done[p * cols : (p + 1) * cols] for p in range(4)], axis=1)
 
 
 def enter_kernel(s_ref, one_ref, spread_ref, extra_ref, mid_ref, out_ref):
-    parts = unit_parts(one_ref, extra_ref, mid_ref)
     units, size = spread_ref.shape
-    size = size // 8
-    spread = spread_ref[...]
+    cols = out_ref.shape[1]
+    done = dot_nt(spread_ref[...], unit_parts(one_ref, extra_ref, mid_ref, size // 8))
     for p in range(4):
-        some = jnp.concatenate([v[:, p * size : (p + 1) * size] for v in parts], axis=1)
-        out_ref[p * units : (p + 1) * units, :] = dot_nt(spread, some)
+        out_ref[p * units : (p + 1) * units, :] = done[:, p * cols : (p + 1) * cols]
 
 
 def shares_kernel(s_ref, one_ref, eye_ref, extra_l_ref, extra_e_ref, mid0_ref, mid1_ref, mid2_ref, leave_ref, enter_ref):
@@ -868,7 +883,7 @@
         [(fixed((main, width)), ((main, width), f32)), (fixed((main, width)), ((main, width), bf16)),
          (fixed((main, width)), ((main, width), bf16)), (fixed((main, cols)), ((main, cols), f32))],
         [pltpu.VMEM((main, width), f32)],
-        core_at, (near, norm_first[None, :]), 5,
+        core_at, (near, norm_first[None, :]), 1,
     )
     seg_first = marks_extra[:toks, 0].astype(jnp.int32)
     seg_last = marks_extra[toks:, 0].astype(jnp.int32)
@@ -883,8 +898,6 @@
     select = jnp.concatenate([select_main, select_extra], axis=0)
     select_long = jnp.concatenate([select_halo, select], axis=0)
     select_after = jnp.concatenate([select, select_halo], axis=0)
-    pick_fill = (dot(normed_long, enter_square[1]) * select_long).astype(bf16)
-    pick_gelu = (dot(normed, enter_square[0]) * select).astype(bf16)
 
     col_spec = lambda i: pl.BlockSpec((8, 2, per4, quarter), lambda b, s: (b, s[0], 0, i))
     out_spec = pl.BlockSpec((8, 4, per4, quarter), lambda b, s: (2 * s[0] + b, 0, 0, 2))
@@ -901,22 +914,23 @@
     layer = 2 * rows * halfw * width
     mib = 2**20
 
-    gd_rows = ring_rows(grad_down_own)
+    gd_rows = ring_rows(tied(cotangent, near).astype(bf16))
     long = rows + HALO
-    convolved, lat_gates = call(
+    convolved, lat_gates, pick_fill = call(
         fill_kernel, (2,),
-        [fixed((long, width)), side_col_spec(1), fixed((long, cols)), rows_spec(cols), fixed((rows, 8)), rows_spec(4),
+        [fixed((long, width)), side_col_spec(1), fixed((width, cols)), fixed((long, cols)), rows_spec(cols), fixed((rows, 8)), rows_spec(4),
          pl.BlockSpec((quarter, 2 * cols), lambda b, s: (b, 0))],
-        [(rows_spec(rows), (wide_block, bf16)), F(rows, 2 * cols)],
+        [(rows_spec(rows), (wide_block, bf16)), F(rows, 2 * cols), B(long, cols)],
         [pltpu.VMEM((long, quarter), f32)],
-        core_at, (normed_long, near, pick_fill, leave_half[1], mask, taps, enter_gates), 12, (shard_far, *gd_rows[0][1:]),
+        core_at, (normed_long, near, enter_square[1], select_long, leave_half[1], mask, taps, enter_gates), 1, (shard_far,),
     )
     pick_fill = pick_fill[HALO:]
 
-    sides = lambda v: [half(v, c, 0), half(v, 1 - c, 0)]
+    sides = lambda v: [v[:toks], v[toks:]]
     feed_select = [
         jnp.concatenate([ring_selects[0][:toks], sides(select_extra)[0], ring_selects[1][:toks], sides(select_extra)[1]], axis=0),
-        jnp.concatenate([ring_selects[0][toks:], ring_selects[1][toks:]], axis=0),
+        ring_selects[0][toks:],
+        ring_selects[1][toks:],
     ]
     sig_in, sig_de, decays, state, prod, pick_in, pick_de = call(
         gates_kernel, (heads,),
@@ -924,15 +938,15 @@
          head_spec(cols), head_spec(cols), fixed((rows, 8)), head_spec(1)],
         [(head_spec(rows), (wide_block, f32))] * 5 + [B(*small_block)] * 2,
         [pltpu.VMEM((rows, head), f32), pltpu.VMEM((halfw, 2 * head), bf16)],
-        core_at, (convolved, lat_gates, swap(lat_gates), select, near, leave_half[2], leave_half[3], mask, rate), 12,
+        core_at, (convolved, lat_gates, swap(lat_gates), select, near, leave_half[2], leave_half[3], mask, rate), 4, tuple(gd_rows[0][1:]),
     )
     entering = chips_carry(jnp.stack([prod[main - 1], state[main - 1]]), False)[None, :]
-    branch, slope = call(
+    branch, slope, pick_gelu = call(
         gelu_kernel, (2,),
-        [fixed((rows, width)), side_col_spec(0), fixed(small_block), rows_spec(cols)],
-        [(rows_spec(rows), (wide_block, f32))] * 2,
+        [fixed((long, width)), side_col_spec(0), fixed((width, cols)), fixed(small_block), rows_spec(cols)],
+        [(rows_spec(rows), (wide_block, f32))] * 2 + [B(*small_block)],
         [],
-        core_at, (normed, near, pick_gelu, leave_half[0]), 12,
+        core_at, (normed_long, near, enter_square[0], select, leave_half[0]), 12,
     )
     states, mixed, lat_out, out_mine, out_send, out_extra = call(
         out_kernel, (2,),
@@ -942,6 +956,7 @@
         [pltpu.VMEM((rows, width), f32), pltpu.VMEM((rows, quarter), bf16)],
         core_at, (state, prod, entering, branch, near, enter_half[4], leave_square[4], select), 15,
     )
+    pick_out = ((lat_out + swap(lat_out)) * select).astype(bf16)
     got = swap(out_send).astype(f32)
     residual = block_input + out_mine + got[:toks]
     residual_extra = x_extra + (out_extra.astype(f32) + got[toks:])
@@ -953,73 +968,66 @@
     far_rows = far.shape[1]
 
     def feed(n2_pieces, gd_pieces, select, micros, waits=()):
-        count = len(n2_pieces) // 2
-        n = 2 * count * toks
+        count = len(n2_pieces)
+        n = count * toks
         return call(
             functools.partial(ffn_kernel, count), (1,),
-            [anywhere] * (4 * count)
-            + [fixed(far.shape), fixed((cols, slotp)), fixed((cols, slotp)), fixed((slotp, cols)), fixed((width, cols)), fixed((cols, width)),
-               fixed((n, cols))],
-            [B(n // 2, width)] * 2 + [B(n, slotp)] * 3 + [B(n, cols)] * 4,
-            [pltpu.VMEM((n, width), bf16), pltpu.VMEM((n, width), bf16), pltpu.SemaphoreType.DMA((2 * count,)), pltpu.SemaphoreType.DMA((2 * count,))],
+            [anywhere] * (2 * count + 1)
+            + [fixed((cols, slotp)), fixed((cols, slotp)), fixed((slotp, cols)), fixed((width, cols)), fixed((cols, width)), fixed((n, cols))],
+            [B(n, width)] + [B(n, slotp)] * 3 + [B(n, cols)] * 4,
+            [pltpu.VMEM((n, width), bf16), pltpu.VMEM((n, width), bf16), pltpu.VMEM(far.shape, bf16),
+             pltpu.SemaphoreType.DMA((count,)), pltpu.SemaphoreType.DMA((count,)), pltpu.SemaphoreType.DMA((4, 3))],
             core_at,
             (*n2_pieces, *gd_pieces, far, leave_a, leave_b, enter_down, enter_widen, leave_narrow, select),
             micros, waits,
         )
 
     mix = lambda rows, extra: [rows[0][0], sides(extra)[0], rows[1][0], sides(extra)[1]]
-    mine0, theirs0, *near_parts = feed(mix(n2_rows, n2_extra), mix(gd_rows, down_extra), feed_select[0], 25)
-    mine1, theirs1, *far_parts = feed(n2_rows[0][1:] + n2_rows[1][1:], gd_rows[0][1:] + gd_rows[1][1:], feed_select[1], 37, (theirs0,))
+    gn0, *parts0 = feed(mix(n2_rows, n2_extra), mix(gd_rows, down_extra), feed_select[0], 60)
+    gn1, *parts1 = feed(n2_rows[0][1:], gd_rows[0][1:], feed_select[1], 40, (gn0,))
+    gn2, *parts2 = feed(n2_rows[1][1:], gd_rows[1][1:], feed_select[2], 60, (gn1,))
     add = lambda a, b: a.astype(f32) + b.astype(f32)
-    sums0 = add(mine0, swap(theirs0))
 
     eighth = main // 8
-    extra_mine = sums0[toks:]
-    extra_of = lambda k: lax.dynamic_slice_in_dim(extra_mine, jnp.remainder(y - k, 4) * eighth, eighth, axis=0)
-    extra_total = line_back([extra_of(k) for k in range(4)]).astype(bf16)
-    extra_half = line_order([extra_total] + [shift4(extra_total, YAX, by) for by in (1, 2, 3)], y).reshape(main // 2, -1)
-    grad_n2_extra = both(extra_half, swap(extra_half), c).astype(f32)
-    lat_side = jnp.concatenate([near_parts[3], near_parts[4]], axis=1)
-    lat_sum = to_low(add(lat_side[toks : 2 * toks], swap(lat_side[3 * toks :])))
-    lat_sum = line_sum(lat_sum, YAX).astype(bf16)
-    lat_extra = both(lat_sum, swap(lat_sum), c)
+    side0 = jnp.concatenate([tied(gn0, gn1).astype(bf16), parts0[3], parts0[4]], axis=1)
+    extra_part = jnp.concatenate([side0[toks : 2 * toks], side0[3 * toks :]], axis=0)
+    extra_total = lax.all_to_all(extra_part, RING, 0, 0, tiled=True).reshape(8, eighth, -1)
+    extra_total = to_low(tied(jnp.sum(extra_total.astype(f32), axis=0), gn2))
+    extra_all = lax.all_to_all(jnp.broadcast_to(extra_total[None], (8, *extra_total.shape)), RING, 0, 0, tiled=True).reshape(main, -1)
+    grad_n2_extra = extra_all[:, :width].astype(f32)
+    lat_extra = extra_all[:, width:]
     lgw_extra = lat_extra[:, :cols]
     pick_n_extra = lat_extra[:, cols:]
 
-    sums1 = add(mine1, swap(theirs1)).astype(bf16)
-    sums = [sums0[:toks]] + [sums1[k * toks : (k + 1) * toks] for k in range(3)]
+    sums0 = add(gn0[:toks], swap(gn0[2 * toks : 3 * toks]))
+    sums1 = add(gn1, swap(gn2)).astype(bf16)
+    sums = [sums0] + [sums1[k * toks : (k + 1) * toks] for k in range(3)]
     mid_spec = (pl.BlockSpec((rank, hcol), lambda j, s: (0, j)), ((rank, slotp), bf16))
     extra_spec = (pl.BlockSpec((cols, hcol), lambda j, s: (0, j)), ((cols, slotp), bf16))
     down, mid_a, mid_b, mid_n, mid_l, mid_e, ex_a, ex_b, ex_n = call(
         down_kernel, (4,),
-        [anywhere] * 16 + [hidden_spec(4 * toks), hidden_spec(6 * toks)] * 3
-        + [pl.BlockSpec((4, far_rows, wide2), lambda j, s: (j, 0, 0))]
-        + [fixed((4 * toks, cols)), fixed((6 * toks, cols))] * 4 + [fixed((cols, width))],
+        [anywhere] * 16 + [hidden_spec(4 * toks), hidden_spec(3 * toks), hidden_spec(3 * toks)] * 3
+        + [fixed((4 * toks, cols)), fixed((3 * toks, cols)), fixed((3 * toks, cols))] * 4
+        + [pl.BlockSpec((4, far_rows, wide2), lambda j, s: (j, 0, 0)), fixed((cols, width))],
         [B(ring, width)] + [mid_spec] * 3 + [B(rank, width)] * 2 + [extra_spec] * 3,
         [pltpu.VMEM((ring, width), f32), pltpu.VMEM((cols, hcol), f32), pltpu.VMEM((cols, width), f32),
          pltpu.VMEM((ring, width), bf16), pltpu.VMEM((ring, width), bf16), pltpu.SemaphoreType.DMA((8,)), pltpu.SemaphoreType.DMA((8,))],
         middle_at,
         (n2_rows[0][0], n2_rows[1][0], *n2_rows[0][1:], *n2_rows[1][1:], gd_rows[0][0], gd_rows[1][0], *gd_rows[0][1:], *gd_rows[1][1:],
-         near_parts[2], far_parts[2], near_parts[0], far_parts[0], near_parts[1], far_parts[1], far,
-         near_parts[5], far_parts[5], near_parts[6], far_parts[6], near_parts[4], far_parts[4], near_parts[3], far_parts[3], leave_narrow),
-        19, (*sums[1:], extra_total),
-    )
-    ffn_mid = jnp.concatenate([mid_a, mid_b, mid_n, mid_l, mid_e], axis=1)
+         *[v[i] for i in (2, 0, 1, 5, 6, 4, 3) for v in (parts0, parts1, parts2)], far, leave_narrow),
+        60, (*sums[1:], extra_total),
+    )
+    grad_n2 = tied(tied(line_back(sums), down), extra_all)
+    ffn_mid = tied(jnp.concatenate([mid_a, mid_b, mid_n, mid_l, mid_e], axis=1), grad_n2).astype(bf16)
     mid_shape = ffn_mid.shape
     ffn_mid = lax.all_to_all(ffn_mid.reshape(16, -1, cols), PLANE, 0, 0, tiled=True)
     ffn_mid = to_low(jnp.sum(ffn_mid.astype(f32), axis=0))
-    grad_n2 = tied(line_back(sums), ffn_mid)
     ffn_mid = lax.all_to_all(jnp.broadcast_to(ffn_mid[None], (16, *ffn_mid.shape)), PLANE, 0, 0, tiled=True).reshape(mid_shape)
 
     grad_residual = cotangent + norm_back(residual, norm_second, grad_n2)
     grad_residual_extra = down_extra.astype(f32) + norm_back(residual_extra, norm_second, grad_n2_extra)
     grad_out_own = grad_residual.astype(bf16)
     grad_out = jnp.concatenate([both(grad_out_own, swap(grad_out_own), c), grad_residual_extra.astype(bf16)], axis=0)
-    down_mine = jnp.concatenate([down[:toks], down[2 * toks : 5 * toks]], axis=0)
-    down_theirs = jnp.concatenate([down[toks : 2 * toks], down[5 * toks :]], axis=0)
-    down_total = tied(add(down_mine, swap(down_theirs)), grad_out)
-    down_sums = [down_total[k * toks : (k + 1) * toks] for k in range(4)]
-    block_output = residual + line_back(down_sums)
     grad_gelu, lg_out, back, trail = call(
         functools.partial(outback_kernel, main), (2,),
         [fixed((rows, width)), out_spec, fixed((cols, width)), enter_spec, fixed(small_block)] + [rows_spec(rows)] * 4,
@@ -1057,8 +1065,8 @@
     )
     ffn_all = lax.all_gather(packed, RING, axis=0)
 
-    halo_base = chip_shift(base[:HALO], -1)
-    halo_lat = chip_shift(lat_gates[:HALO], -1)
+    halo_both = chip_shift(jnp.concatenate([base[:HALO], lat_gates[:HALO]], axis=1), -1)
+    halo_base, halo_lat = halo_both[:, :halfw], halo_both[:, halfw:]
     halo_other = chip_shift(lat_gates[:HALO], -1, cross=True)
     grad_fill, lg_in, lg_de, lat_fill, normed_mine, normed_theirs = call(
         fillback_kernel, (4,),
@@ -1074,11 +1082,8 @@
         12,
     )
 
-    lat_all = jnp.concatenate([lat_gelu, lat_fill, lat_out], axis=1)
-    lat_all = lat_all + swap(lat_all)
-    lg_gelu = (lat_all[:, :cols] * select).astype(bf16)
-    lg_fill = (lat_all[:, cols : 2 * cols] * select).astype(bf16)
-    pick_out = (lat_all[:, 2 * cols :] * select).astype(bf16)
+    lg_gelu = ((lat_gelu + swap(lat_gelu)) * select).astype(bf16)
+    lg_fill = ((lat_fill + swap(lat_fill)) * select).astype(bf16)
     normed_half = half(normed, c, 1)
     pairs = [
         (lg_gelu, normed_half), (lg_fill, normed_half), (lg_in, convolved), (lg_de, convolved), (lg_out, mixed),
@@ -1097,8 +1102,12 @@
     shape = mid.shape
     mid = lax.all_to_all(mid.reshape(64, -1, cols), CHIPS, 0, 0, tiled=True)
     mid = to_low(jnp.sum(mid.astype(f32), axis=0))
-    mid = lax.all_to_all(jnp.broadcast_to(mid[None], (64, *mid.shape)), CHIPS, 0, 0, tiled=True).reshape(shape)
-
+
+    down_mine = jnp.concatenate([down[:toks], down[2 * toks : 5 * toks]], axis=0)
+    down_theirs = jnp.concatenate([down[toks : 2 * toks], down[5 * toks :]], axis=0)
+    down_total = tied(add(down_mine, swap(down_theirs)), base)
+    down_sums = [down_total[k * toks : (k + 1) * toks] for k in range(4)]
+    block_output = residual + line_back(down_sums)
     operands = [*[v for pair in pairs[:5] for v in pair[::-1]], *[v for pair in pairs[5:] for v in pair]]
     enter_extra, leave_extra = call(
         functools.partial(extras_kernel, 5), (1,),
@@ -1113,6 +1122,8 @@
         [(pl.BlockSpec((cols, block), lambda i, s: (0, i)), ((cols, 2 * ff), f32))],
         [], core_at, (one_hot, spread_one, ffn_all, ffn_all), 12, (mid_own,),
     )
+    mid = tied(mid, grad_leave_widen).astype(bf16)
+    mid = lax.all_to_all(jnp.broadcast_to(mid[None], (64, *mid.shape)), CHIPS, 0, 0, tiled=True).reshape(shape)
     (grad_enter_narrow,) = call(
         enter_kernel, (4,),
         [fixed((rank, cols)), fixed((units, 8 * chunk)), pl.BlockSpec((8, cols, hcol), lambda i, s: (0, 0, 8 + i)), pl.BlockSpec((8, rank, hcol), lambda i, s: (0, cols // rank, 8 + i))],

time: 765 us -> 686 us (0.90)
  starting transfers between devices: 169 us -> 137 us
  waiting for transfers between devices: 146 us -> 123 us
  local copies, waits for them, and re-layouts: 93 us -> 78.6 us
    all_gather x1, waiting for transfers between devices: 76.9 us -> 53.3 us  [per_device(): lax.all_gather(quads[None], AXES, axis=0, tiled=True)]
    ppermute x28 -> x27, starting transfers between devices: 50.2 us -> 27.1 us  [swap(): return lax.ppermute(v, 'c', [(0, 1), (1, 0)])]
    ppermute x42 -> x33, starting transfers between devices: 57.2 us -> 36.2 us  [shift4(): return lax.ppermute(v, axis, [(i, (i + by) % 4) for i in range(4)])]
    all_to_all x0 -> x2, waiting for transfers between devices: none -> 14.4 us  [the longest x1 14.4 us: per_device(): lax.all_to_all(jnp.broadcast_to(extra_total[None], (8, *extra_total.shape...]
    all_to_all x1, waiting for transfers between devices: 12.1 us -> 3.46 us  [per_device(): mid = lax.all_to_all(mid.reshape(64, -1, cols), CHIPS, 0, 0, tiled=True)]
    all_to_all x0 -> x2, starting transfers between devices: none -> 8.54 us  [the longest x1 4.95 us: per_device(): lax.all_to_all(jnp.broadcast_to(extra_total[None], (8, *extra_total.shape...]
    all_gather x1, waiting for transfers between devices: 8.52 us -> 0.01 us  [per_device(): far = lax.all_gather(shard_far[None], PLANE, axis=0, tiled=True)]
    unnamed x198 -> x186, local copies, waits for them, and re-layouts: 27.4 us -> 19.1 us
  transfers between devices with their start and end apart: 92 -> 83, of which waited for: 19 -> 20; matrix products, arithmetic and copies ran while one was open for 21% -> 21% of each run, Pallas kernels for 22% -> 31%
where the time goes in v3:
time: 686 us; the launch traced here: 674 us
  Pallas kernels  234 us (34%)
  starting transfers between devices  137 us (20%)
  waiting for transfers between devices  123 us (18%)
  local copies, waits for them, and re-layouts  78.6 us (11%)
  other arithmetic  71.9 us (10%)
  between operations  21.5 us (3%)
  matrix products  8.89 us (1%)
    pallas_call x20, Pallas kernels, call(): pl.pallas_call(body, grid_spec=pltpu.PrefetchScalarGridSpec(num_scalar_pr...  234 us
    all_gather x1, waiting for transfers between devices, per_device(): lax.all_gather(quads[None], AXES, axis=0, tiled=True)  53.3 us
    ppermute x33, starting transfers between devices, shift4(): return lax.ppermute(v, axis, [(i, (i + by) % 4) for i in range(4)])  36.2 us
    ppermute x33, waiting for transfers between devices, shift4(): return lax.ppermute(v, axis, [(i, (i + by) % 4) for i in range(4)])  27.4 us
    ppermute x27, starting transfers between devices, swap(): return lax.ppermute(v, 'c', [(0, 1), (1, 0)])  27.1 us
    unnamed x186, local copies, waits for them, and re-layouts  19.1 us
    all_to_all x1, starting transfers between devices, per_device(): quads = lax.all_to_all(quads, QUAD, 0, 0, tiled=True).reshape(per4, lanes)  18.7 us
    all_to_all x1, waiting for transfers between devices, per_device(): lax.all_to_all(jnp.broadcast_to(extra_total[None], (8, *extra_total.shape...  14.4 us
  transfers between devices with their start and end apart: 83, of which 20 were waited for; matrix products, arithmetic and copies ran while one was open for 21% of the time, Pallas kernels for 31%

profile of v3, /device:TPU:1, one launch (start us, length us, event | category | flops | bytes accessed | tf_op | source)
XLA Modules:
  0.0 674.4 jit_solution(10843922828085144298)
XLA Ops:
  17.7 18.7 %all-to-all-start = ((bf16[4,20,2048]{2,1,0:T(8,128)(2,1)}), bf16[4,20,2048]{2,1,0:T(8,128)(2,1)S(1)}, u32[]{:S(2)}, u32[]{:S(2)}) async-start(bf16[4,20,2048]{2,1,0:T(8,128)(2,1)} %pad_maximum_fusion.5), calls=%async_computation | async-start | bytes 786432 | tf_op jit(solution)/shard_map/all_to_all | solution.py:813
  43.1 6.6 collective-permute-done.8
  51.7 5.1 convolution_convert_fusion
  64.3 12.3 %all-to-all-done.1 = bf16[8,20,2048]{2,1,0:T(8,128)(2,1)S(1)} async-done(((bf16[8,20,2048]{2,1,0:T(8,128)(2,1)}), bf16[8,20,2048]{2,1,0:T(8,128)(2,1)S(1)}, u32[]{:S(2)}, u32[]{:S(2)}) %all-to-all-start.1) | async-done | bytes 655392 | tf_op jit(solution)/shard_map/all_to_all | solution.py:835
  80.0 6.0 copy.65
  86.0 6.3 copy.66
  125.8 53.3 %all-gather.7.cloned.1.call-done = bf16[11264,2048]{1,0:T(8,128)(2,1)} async-done(((bf16[88,2048]{1,0:T(8,128)(2,1)}), bf16[11264,2048]{1,0:T(8,128)(2,1)}) %all-gather.7.cloned.1.call-update) | async-done | bytes 46137360 | tf_op jit(solution)/shard_map/all_gather | solution.py:819
  197.9 12.6 %shard_map.261 = (bf16[512,1280]{1,0:T(8,128)(2,1)}, f32[512,256]{1,0:T(8,128)}, bf16[528,128]{1,0:T(8,128)(2,1)}) custom-call(s32[1]{0:T(128)} %bitcast.5.s_ref, bf16[528,2560]{1,0:T(8,128)(2,1)} %pad_maximum_fusion.1.refs_0_, bf16[32,4,88,2048]{3,2,1,0:T(8,128)(2,1)} %bitcast.103, bf16[2560,128]{1,0:T(8,128)(2,1)} %get-tuple-element.210.refs_2_.refs_13_, ...), custom_call_target="tpu_custom_call" | custom-call | flops 1000000000 | bytes 2000000 | tf_op jit(solution)/shard_map/pallas_call | solution.py:128
  218.2 11.6 %shard_map.262 = (f32[512,1280]{1,0:T(8,128)}, f32[512,1280]{1,0:T(8,128)}, f32[512,1280]{1,0:T(8,128)}, f32[512,1280]{1,0:T(8,128)}, f32[512,1280]{1,0:T(8,128)...) custom-call(s32[1]{0:T(128)} %bitcast.5.s_ref, ...), custom_call_target="tpu_custom_call" | custom-call | flops 4000000000 | bytes 8000000 | tf_op jit(solution)/shard_map/pallas_call | solution.py:128
  245.7 11.2 %shard_map.263 = (f32[512,1280]{1,0:T(8,128)}, f32[512,1280]{1,0:T(8,128)}, bf16[512,128]{1,0:T(8,128)(2,1)}) custom-call(s32[1]{0:T(128)} %bitcast.5.s_ref, bf16[528,2560]{1,0:T(8,128)(2,1)} %pad_maximum_fusion.1.refs_0_, bf16[32,4,88,2048]{3,2,1,0:T(8,128)(2,1)} %bitcast.105, bf16[2560,128]{1,0:T(8,128)(2,1)} %get-tuple-element.209.refs_2_.refs_3_, ...), custom_call_target="tpu_custom_call" | custom-call | flops 12000000000 | bytes 24000000 | tf_op jit(solution)/shard_map/pallas_call | solution.py:128
  257.6 13.9 %shard_map.264 = (f32[512,1280]{1,0:T(8,128)}, bf16[512,1280]{1,0:T(8,128)(2,1)}, f32[512,128]{1,0:T(8,128)}, f32[128,2560]{1,0:T(8,128)}, bf16[384,2560]{1,0:T(8,128)(2,1)}, /*index=5*/bf16[256,2560]{1,0:T(8,128)(2,1)}) custom-call(s32[1]{0:T(128)} %bitcast.5.s_ref, f32[512,1280]{1,0:T(8,128)} %get-tuple-element.100.refs_0_, ...), custom_call_target="tpu_custom_call" | custom-call | flops 15000000512 | bytes 30000000 | tf_op jit(solution)/shard_map/pallas_call | solution.py:128
  290.8 26.0 %shard_map.265 = (bf16[512,2560]{1,0:T(8,128)(2,1)}, bf16[512,1024]{1,0:T(8,128)(2,1)}, bf16[512,1024]{1,0:T(8,128)(2,1)}, bf16[512,1024]{1,0:T(8,128)(2,1)}, bf...) custom-call(s32[1]{0:T(128)} %bitcast.5.s_ref, ...), custom_call_target="tpu_custom_call" | custom-call | flops 60000002048 | bytes 120000000 | tf_op jit(solution)/shard_map/pallas_call | solution.py:128
  321.0 21.1 %shard_map.266 = (bf16[384,2560]{1,0:T(8,128)(2,1)}, bf16[384,1024]{1,0:T(8,128)(2,1)}, bf16[384,1024]{1,0:T(8,128)(2,1)}, bf16[384,1024]{1,0:T(8,128)(2,1)}, bf...) custom-call(s32[1]{0:T(128)} %bitcast.5.s_ref, ...), custom_call_target="tpu_custom_call" | custom-call | flops 40000000000 | bytes 80000000 | tf_op jit(solution)/shard_map/pallas_call | solution.py:128
  353.4 20.9 %shard_map.267 = (bf16[384,2560]{1,0:T(8,128)(2,1)}, bf16[384,1024]{1,0:T(8,128)(2,1)}, bf16[384,1024]{1,0:T(8,128)(2,1)}, bf16[384,1024]{1,0:T(8,128)(2,1)}, bf...) custom-call(s32[1]{0:T(128)} %bitcast.5.s_ref, ...), custom_call_target="tpu_custom_call" | custom-call | flops 60000002048 | bytes 120000000 | tf_op jit(solution)/shard_map/pallas_call | solution.py:128
  378.0 5.0 all-to-all-start.3
  387.9 14.4 %all-to-all-done.3 = bf16[8,32,2816]{2,1,0:T(8,128)(2,1)S(1)} async-done(((bf16[8,32,2816]{2,1,0:T(8,128)(2,1)}), bf16[8,32,2816]{2,1,0:T(8,128)(2,1)S(1)}, u32[]{:S(2)}, u32[]{:S(2)}) %all-to-all-start.3) | async-done | bytes 1441824 | tf_op jit(solution)/shard_map/all_to_all | solution.py:996
  413.7 19.6 %shard_map.268 = (bf16[1024,2560]{1,0:T(8,128)(2,1)}, bf16[16,1024]{1,0:T(8,128)(2,1)}, bf16[16,1024]{1,0:T(8,128)(2,1)}, bf16[16,1024]{1,0:T(8,128)(2,1)}, bf16...) custom-call(s32[1]{0:T(128)} %slice.502.s_ref, ...), custom_call_target="tpu_custom_call" | custom-call | flops 60000002048 | bytes 120000000 | tf_op jit(solution)/shard_map/pallas_call | solution.py:128
  449.5 6.3 all-to-all-start.5
  460.1 15.2 %shard_map.269 = (bf16[512,1280]{1,0:T(8,128)(2,1)}, bf16[512,128]{1,0:T(8,128)(2,1)}, f32[512,1280]{1,0:T(8,128)}, f32[512,1280]{1,0:T(8,128)}) custom-call(s32[1]{0:T(128)} %bitcast.5.s_ref, bf16[512,2560]{1,0:T(8,128)(2,1)} %pad_maximum_fusion.refs_0_, bf16[32,4,88,2048]{3,2,1,0:T(8,128)(2,1)} %bitcast.107, ...), custom_call_target="tpu_custom_call" | custom-call | flops 17999998976 | bytes 36000000 | tf_op jit(solution)/shard_map/pallas_call | solution.py:128
  487.4 5.9 all-to-all-start.6
  502.5 12.1 %shard_map.270 = (bf16[512,1280]{1,0:T(8,128)(2,1)}, bf16[512,1280]{1,0:T(8,128)(2,1)}, f32[512,1280]{1,0:T(8,128)}, f32[512,256]{1,0:T(8,128)}) custom-call(s32[1]{0:T(128)} %bitcast.5.s_ref, f32[512,1280]{1,0:T(8,128)} %get-tuple-element.136.refs_0_, f32[512,1280]{1,0:T(8,128)} %get-tuple-element.137.refs_1_, f32[1,1280]{1,0:T(1,128)} %fusion.71.refs_2_, ...), custom_call_target="tpu_custom_call" | custom-call | flops 8000000000 | bytes 16000000 | tf_op jit(solution)/shard_map/pallas_call | solution.py:128
  539.8 8.0 %shard_map.271 = (f32[256,2560]{1,0:T(8,128)}, f32[512,128]{1,0:T(8,128)}) custom-call(s32[1]{0:T(128)} %bitcast.5.s_ref, bf16[512,1280]{1,0:T(8,128)(2,1)} %get-tuple-element.142.refs_0_.refs_11_, bf16[32,4,88,2048]{3,2,1,0:T(8,128)(2,1)} %bitcast.109, bf16[128,1280]{1,0:T(8,128)(2,1)} %get-tuple-element.205.refs_4_.refs_2_, ...), custom_call_target="tpu_custom_call" | custom-call | flops 12000000000 | bytes 24000000 | tf_op jit(solution)/shard_map/pallas_call | solution.py:128
  550.8 12.1 %shard_map.272 = (bf16[512,1280]{1,0:T(8,128)(2,1)}, bf16[512,128]{1,0:T(8,128)(2,1)}, bf16[512,128]{1,0:T(8,128)(2,1)}, f32[512,128]{1,0:T(8,128)}, f32[128,2560]{1,0:T(8,128)}, /*index=5*/bf16[128,2560]{1,0:T(8,128)(2,1)}) custom-call(s32[1]{0:T(128)} %bitcast.5.s_ref, f32[512,1280]{1,0:T(8,128)} %get-tuple-element.140.refs_0_.refs_8_, ...), custom_call_target="tpu_custom_call" | custom-call | flops 12000000000 | bytes 24000000 | tf_op jit(solution)/shard_map/pallas_call | solution.py:128
  567.6 5.6 shard_map.273.refs_20_.refs_4_.refs_7_
  575.5 10.1 %all-to-all-start.4 = ((bf16[64,25,128]{2,1,0:T(8,128)(2,1)}), bf16[64,25,128]{2,1,0:T(8,128)(2,1)S(1)}, u32[]{:S(2)}, u32[]{:S(2)}) async-start(bf16[64,25,128]{2,1,0:T(8,128)(2,1)} %reshape.324), calls=%async_computation.4 | async-start | bytes 1048576 | tf_op jit(solution)/shard_map/all_to_all | solution.py:1103
  585.7 6.2 shard_map.274
  598.4 5.6 fusion.87
  607.4 10.8 %shard_map.276 = f32[128,15360]{1,0:T(8,128)} custom-call(s32[1]{0:T(128)} %bitcast.5.s_ref, bf16[16,128]{1,0:T(8,128)(2,1)} %fusion.61.refs_0_, bf16[480,512]{1,0:T(8,128)(2,1)} %fusion.37.refs_1_, bf16[8,176,3840]{2,1,0:T(8,128)(2,1)} %bitcast.111, bf16[8,176,3840]{2,1,0:T(8,128)(2,1)} %bitcast.112, bf16[160,1280]{1,0:T(8,128)(2,1)} %shard_map.273.refs_20_.refs_4_.refs_7_), custom_call_target="tpu_custom_call" | custom-call | flops 12000000000 | bytes 24000000 | tf_op jit(solution)/shard_map/pallas_call | solution.py:128
  621.0 7.0 %all-to-all-start.7 = ((bf16[64,25,128]{2,1,0:T(8,128)(2,1)}), bf16[64,25,128]{2,1,0:T(8,128)(2,1)S(1)}, u32[]{:S(2)}, u32[]{:S(2)}) async-start(bf16[64,25,128]{2,1,0:T(8,128)(2,1)} %broadcast_in_dim.65), calls=%async_computation.7 | async-start | bytes 1048576 | tf_op jit(solution)/shard_map/all_to_all | solution.py:1126
  628.0 10.5 %collective-permute-done.60 = bf16[128,2560]{1,0:T(8,128)(2,1)} collective-permute-done((bf16[128,2560]{1,0:T(8,128)(2,1)S(1)}, bf16[128,2560]{1,0:T(8,128)(2,1)}, u32[]{:S(2)}, u32[]{:S(2)}) %collective-permute-start.60) | collective-permute-done | bytes 655392 | tf_op jit(solution)/shard_map/ppermute | solution.py:80
  647.4 5.8 shard_map.279
  658.2 9.5 %shard_map.277 = (f32[5,2560,128]{2,1,0:T(8,128)}, f32[5,128,2560]{2,1,0:T(8,128)}) custom-call(s32[1]{0:T(128)} %bitcast.5.s_ref, bf16[16,128]{1,0:T(8,128)(2,1)} %fusion.61.refs_0_, bf16[5,1280,128]{2,1,0:T(8,128)(2,1)} %get-tuple-element.160.refs_1_, bf16[5,1280,128]{2,1,0:T(8,128)(2,1)} %collective-permute-done.69.refs_2_, ...), custom_call_target="tpu_custom_call" | custom-call | flops 8999999488 | bytes 18000000 | tf_op jit(solution)/shard_map/pallas_call | solution.py:128
  (533 shorter events, 257.6 us)
Async XLA Ops:
  13.6 22.7 %collective-permute-start.3 = (bf16[16,2688]{1,0:T(8,128)(2,1)}, bf16[16,2688]{1,0:T(8,128)(2,1)S(1)}, u32[]{:S(2)}, u32[]{:S(2)}) collective-permute-start(bf16[16,2688]{1,0:T(8,128)(2,1)} %get-tuple-element.230), channel_id=1, source_target_pairs={{0,16},{64,80},{32,48},{96,112},{127,111},{63,47},{95,79},{31,15}} | collective-permute-start | bytes 258056 | tf_op jit(solution)/shard_map/ppermute | solution.py:724
  17.7 25.3 %all-to-all-start = ((bf16[4,20,2048]{2,1,0:T(8,128)(2,1)}), bf16[4,20,2048]{2,1,0:T(8,128)(2,1)S(1)}, u32[]{:S(2)}, u32[]{:S(2)}) async-start(bf16[4,20,2048]{2,1,0:T(8,128)(2,1)} %pad_maximum_fusion.5), calls=%async_computation | async-start | bytes 786432 | tf_op jit(solution)/shard_map/all_to_all | solution.py:813
  36.4 142.7 %all-gather.7.cloned.1.call-start = ((), (), s32[]{:S(2)}) async-start(), calls=%async_computation.8 | async-start | bytes 46497792 | tf_op jit(solution)/shard_map/all_gather | solution.py:819
  62.5 228.3 %all-gather.9.cloned.1.call-start = ((), (), s32[]{:S(2)}) async-start(), calls=%async_computation.9 | async-start | bytes 16711680 | tf_op jit(solution)/shard_map/all_gather | solution.py:839
  124.4 68.8 %collective-permute-start.10 = (bf16[16,2560]{1,0:T(8,128)(2,1)S(1)}, bf16[16,2560]{1,0:T(8,128)(2,1)S(1)}, u32[]{:S(2)}, u32[]{:S(2)}) collective-permute-start(bf16[16,2560]{1,0:T(8,128)(2,1)S(1)} %slice.617), channel_id=1, source_target_pairs={{0,2},{1,3},{2,4},{3,5},{4,6},{5,7},{6,8},{7,9},{8,10},{9,11},{10,... | collective-permute-start | bytes 245768 | tf_op jit(solution)/shard_map/ppermute | solution.py:91
  183.1 30.9 %collective-permute-start.21 = (bf16[128,2560]{1,0:T(8,128)(2,1)}, bf16[128,2560]{1,0:T(8,128)(2,1)}, u32[]{:S(2)}, u32[]{:S(2)}) collective-permute-start(bf16[128,2560]{1,0:T(8,128)(2,1)} %add_convert_fusion.3.refs_4_.refs_8_), channel_id=1, source_target_pairs={{0,6},{2,0},{4,2},{6,4},{1,7},{3,1},{5,3},{7,5},{8,14},{10,8},{12,... | collective-permute-start | bytes 1966088 | tf_op jit(solution)/shard_map/ppermute | solution.py:80
  186.0 28.1 %collective-permute-start.20 = (bf16[128,2560]{1,0:T(8,128)(2,1)}, bf16[128,2560]{1,0:T(8,128)(2,1)}, u32[]{:S(2)}, u32[]{:S(2)}) collective-permute-start(bf16[128,2560]{1,0:T(8,128)(2,1)} %add_convert_fusion.3.refs_4_.refs_8_), channel_id=1, source_target_pairs={{0,4},{2,6},{4,0},{6,2},{1,5},{3,7},{5,1},{7,3},{8,12},{10,14},{12... | collective-permute-start | bytes 1966088 | tf_op jit(solution)/shard_map/ppermute | solution.py:80
  186.1 32.1 %collective-permute-start.19 = (bf16[128,2560]{1,0:T(8,128)(2,1)}, bf16[128,2560]{1,0:T(8,128)(2,1)}, u32[]{:S(2)}, u32[]{:S(2)}) collective-permute-start(bf16[128,2560]{1,0:T(8,128)(2,1)} %add_convert_fusion.3.refs_4_.refs_8_), channel_id=1, source_target_pairs={{0,2},{2,4},{4,6},{6,0},{1,3},{3,5},{5,7},{7,1},{8,10},{10,12},{12... | collective-permute-start | bytes 1966088 | tf_op jit(solution)/shard_map/ppermute | solution.py:80
  279.3 65.1 %collective-permute-start.42 = (bf16[128,2560]{1,0:T(8,128)(2,1)}, bf16[128,2560]{1,0:T(8,128)(2,1)S(1)}, u32[]{:S(2)}, u32[]{:S(2)}) collective-permute-start(bf16[128,2560]{1,0:T(8,128)(2,1)} %collective-permute-done.21.refs_11_.refs_5_.refs_12_), channel_id=1, source_target_pairs={{0,1},{1,0},{2,3},{3,2},{4,5},{5,4},{6,7},{7,6},{8,9},{9,8},{10,11... | collective-permute-start | bytes 1966088 | tf_op jit(solution)/shard_map/ppermute | solution.py:76
  279.8 72.7 %collective-permute-start.41 = (bf16[128,2560]{1,0:T(8,128)(2,1)}, bf16[128,2560]{1,0:T(8,128)(2,1)}, u32[]{:S(2)}, u32[]{:S(2)}) collective-permute-start(bf16[128,2560]{1,0:T(8,128)(2,1)} %collective-permute-done.20.refs_10_.refs_4_.refs_11_), channel_id=1, source_target_pairs={{0,1},{1,0},{2,3},{3,2},{4,5},{5,4},{6,7},{7,6},{8,9},{9,8},{10,11... | collective-permute-start | bytes 1966088 | tf_op jit(solution)/shard_map/ppermute | solution.py:76
  281.7 35.1 %collective-permute-start.35 = (bf16[128,2560]{1,0:T(8,128)(2,1)S(1)}, bf16[128,2560]{1,0:T(8,128)(2,1)}, u32[]{:S(2)}, u32[]{:S(2)}) collective-permute-start(bf16[128,2560]{1,0:T(8,128)(2,1)S(1)} %multiply_convert_fusion.1.refs_0_), channel_id=1, source_target_pairs={{0,6},{2,0},{4,2},{6,4},{1,7},{3,1},{5,3},{7,5},{8,14},{10,8},{12,... | collective-permute-start | bytes 1966088 | tf_op jit(solution)/shard_map/ppermute | solution.py:80
  288.6 29.1 %collective-permute-start.34 = (bf16[128,2560]{1,0:T(8,128)(2,1)S(1)}, bf16[128,2560]{1,0:T(8,128)(2,1)}, u32[]{:S(2)}, u32[]{:S(2)}) collective-permute-start(bf16[128,2560]{1,0:T(8,128)(2,1)S(1)} %multiply_convert_fusion.1.refs_0_), channel_id=1, source_target_pairs={{0,4},{2,6},{4,0},{6,2},{1,5},{3,7},{5,1},{7,3},{8,12},{10,14},{12... | collective-permute-start | bytes 1966088 | tf_op jit(solution)/shard_map/ppermute | solution.py:80
  290.8 30.1 %collective-permute-start.33 = (bf16[128,2560]{1,0:T(8,128)(2,1)S(1)}, bf16[128,2560]{1,0:T(8,128)(2,1)}, u32[]{:S(2)}, u32[]{:S(2)}) collective-permute-start(bf16[128,2560]{1,0:T(8,128)(2,1)S(1)} %multiply_convert_fusion.1.refs_0_), channel_id=1, source_target_pairs={{0,2},{2,4},{4,6},{6,0},{1,3},{3,5},{5,7},{7,1},{8,10},{10,12},{12... | collective-permute-start | bytes 1966088 | tf_op jit(solution)/shard_map/ppermute | solution.py:80
  316.9 35.7 %collective-permute-start.40 = (bf16[128,2560]{1,0:T(8,128)(2,1)}, bf16[128,2560]{1,0:T(8,128)(2,1)S(1)}, u32[]{:S(2)}, u32[]{:S(2)}) collective-permute-start(bf16[128,2560]{1,0:T(8,128)(2,1)} %collective-permute-done.19.refs_9_.refs_3_.refs_10_), channel_id=1, source_target_pairs={{0,1},{1,0},{2,3},{3,2},{4,5},{5,4},{6,7},{7,6},{8,9},{9,8},{10,11... | collective-permute-start | bytes 1966088 | tf_op jit(solution)/shard_map/ppermute | solution.py:76
  348.9 27.0 %all-to-all-start.2 = ((bf16[8,32,2816]{2,1,0:T(8,128)(2,1)}), bf16[8,32,2816]{2,1,0:T(8,128)(2,1)S(1)}, u32[]{:S(2)}, u32[]{:S(2)}) async-start(bf16[8,32,2816]{2,1,0:T(8,128)(2,1)} %bitcast.38), calls=%async_computation.2 | async-start | bytes 2883584 | tf_op jit(solution)/shard_map/all_to_all | solution.py:994
  378.0 24.3 %all-to-all-start.3 = ((bf16[8,32,2816]{2,1,0:T(8,128)(2,1)}), bf16[8,32,2816]{2,1,0:T(8,128)(2,1)S(1)}, u32[]{:S(2)}, u32[]{:S(2)}) async-start(bf16[8,32,2816]{2,1,0:T(8,128)(2,1)} %broadcast_in_dim.61), calls=%async_computation.3 | async-start | bytes 2883584 | tf_op jit(solution)/shard_map/all_to_all | solution.py:996
  383.0 25.5 %collective-permute-start.43 = (bf16[384,2560]{1,0:T(8,128)(2,1)}, bf16[384,2560]{1,0:T(8,128)(2,1)}, u32[]{:S(2)}, u32[]{:S(2)}) collective-permute-start(bf16[384,2560]{1,0:T(8,128)(2,1)} %get-tuple-element.131), channel_id=1, source_target_pairs={{0,1},{1,0},{2,3},{3,2},{4,5},{5,4},{6,7},{7,6},{8,9},{9,8},{10,11... | collective-permute-start | bytes 5898248 | tf_op jit(solution)/shard_map/ppermute | solution.py:76
  387.4 50.1 %collective-permute-start.45 = (bf16[128,2560]{1,0:T(8,128)(2,1)}, bf16[128,2560]{1,0:T(8,128)(2,1)}, u32[]{:S(2)}, u32[]{:S(2)}) collective-permute-start(bf16[128,2560]{1,0:T(8,128)(2,1)} %slice.560), channel_id=1, source_target_pairs={{0,1},{1,0},{2,3},{3,2},{4,5},{5,4},{6,7},{7,6},{8,9},{9,8},{10,11... | collective-permute-start | bytes 1966088 | tf_op jit(solution)/shard_map/ppermute | solution.py:76
  410.7 26.8 %collective-permute-start.48 = (bf16[128,2560]{1,0:T(8,128)(2,1)S(1)}, bf16[128,2560]{1,0:T(8,128)(2,1)S(1)}, u32[]{:S(2)}, u32[]{:S(2)}) collective-permute-start(bf16[128,2560]{1,0:T(8,128)(2,1)S(1)} %get-tuple-element.217.refs_41_), channel_id=1, source_target_pairs={{0,2},{2,4},{4,6},{6,0},{1,3},{3,5},{5,7},{7,1},{8,10},{10,12},{12... | collective-permute-start | bytes 1966088 | tf_op jit(solution)/shard_map/ppermute | solution.py:80
  411.0 29.8 %collective-permute-start.47 = (bf16[128,2560]{1,0:T(8,128)(2,1)S(1)}, bf16[128,2560]{1,0:T(8,128)(2,1)S(1)}, u32[]{:S(2)}, u32[]{:S(2)}) collective-permute-start(bf16[128,2560]{1,0:T(8,128)(2,1)S(1)} %get-tuple-element.218.refs_40_), channel_id=1, source_target_pairs={{0,4},{2,6},{4,0},{6,2},{1,5},{3,7},{5,1},{7,3},{8,12},{10,14},{12... | collective-permute-start | bytes 1966088 | tf_op jit(solution)/shard_map/ppermute | solution.py:80
  412.8 29.4 %collective-permute-start.46 = (bf16[128,2560]{1,0:T(8,128)(2,1)S(1)}, bf16[128,2560]{1,0:T(8,128)(2,1)S(1)}, u32[]{:S(2)}, u32[]{:S(2)}) collective-permute-start(bf16[128,2560]{1,0:T(8,128)(2,1)S(1)} %get-tuple-element.219.refs_39_), channel_id=1, source_target_pairs={{0,6},{2,0},{4,2},{6,4},{1,7},{3,1},{5,3},{7,5},{8,14},{10,8},{12,... | collective-permute-start | bytes 1966088 | tf_op jit(solution)/shard_map/ppermute | solution.py:80
  449.5 30.2 %all-to-all-start.5 = ((bf16[16,64,128]{2,1,0:T(8,128)(2,1)}), bf16[16,64,128]{2,1,0:T(8,128)(2,1)}, u32[]{:S(2)}, u32[]{:S(2)}) async-start(bf16[16,64,128]{2,1,0:T(8,128)(2,1)} %bitcast.134), calls=%async_computation.5 | async-start | bytes 524288 | tf_op jit(solution)/shard_map/all_to_all | solution.py:1023
  493.3 114.2 %all-gather.11.cloned.1.call-start = ((), (), s32[]{:S(2)}) async-start(), calls=%async_computation.10 | async-start | bytes 12165120 | tf_op jit(solution)/shard_map/all_gather | solution.py:1066
  524.3 42.4 %collective-permute-start.68 = (f32[512,128]{1,0:T(8,128)S(1)}, f32[512,128]{1,0:T(8,128)S(1)}, u32[]{:S(2)}, u32[]{:S(2)}) collective-permute-start(f32[512,128]{1,0:T(8,128)S(1)} %copy-done.50), channel_id=1, source_target_pairs={{0,1},{1,0},{2,3},{3,2},{4,5},{5,4},{6,7},{7,6},{8,9},{9,8},{10,11... | collective-permute-start | bytes 786440 | tf_op jit(solution)/shard_map/ppermute | solution.py:76
  535.7 62.6 %collective-permute-start.44 = (bf16[512,2560]{1,0:T(8,128)(2,1)}, bf16[512,2560]{1,0:T(8,128)(2,1)}, u32[]{:S(2)}, u32[]{:S(2)}) collective-permute-start(bf16[512,2560]{1,0:T(8,128)(2,1)} %pad_maximum_fusion.2), channel_id=1, source_target_pairs={{0,1},{1,0},{2,3},{3,2},{4,5},{5,4},{6,7},{7,6},{8,9},{9,8},{10,11... | collective-permute-start | bytes 7864328 | tf_op jit(solution)/shard_map/ppermute | solution.py:76
  566.2 26.3 %collective-permute-start.65 = (bf16[128,2560]{1,0:T(8,128)(2,1)}, bf16[128,2560]{1,0:T(8,128)(2,1)S(1)}, u32[]{:S(2)}, u32[]{:S(2)}) collective-permute-start(bf16[128,2560]{1,0:T(8,128)(2,1)} %get-tuple-element.145), channel_id=1, source_target_pairs={{0,1},{1,0},{2,3},{3,2},{4,5},{5,4},{6,7},{7,6},{8,9},{9,8},{10,11... | collective-permute-start | bytes 1966088 | tf_op jit(solution)/shard_map/ppermute | solution.py:76
  575.5 22.7 %all-to-all-start.4 = ((bf16[64,25,128]{2,1,0:T(8,128)(2,1)}), bf16[64,25,128]{2,1,0:T(8,128)(2,1)S(1)}, u32[]{:S(2)}, u32[]{:S(2)}) async-start(bf16[64,25,128]{2,1,0:T(8,128)(2,1)} %reshape.324), calls=%async_computation.4 | async-start | bytes 1048576 | tf_op jit(solution)/shard_map/all_to_all | solution.py:1103
  591.9 65.5 %collective-permute-start.69 = (bf16[5,1280,128]{2,1,0:T(8,128)(2,1)}, bf16[5,1280,128]{2,1,0:T(8,128)(2,1)}, u32[]{:S(2)}, u32[]{:S(2)}) collective-permute-start(bf16[5,1280,128]{2,1,0:T(8,128)(2,1)} %get-tuple-element.160.refs_1_), channel_id=1, source_target_pairs={{0,1},{1,0},{2,3},{3,2},{4,5},{5,4},{6,7},{7,6},{8,9},{9,8},{10,11... | collective-permute-start | bytes 4915208 | tf_op jit(solution)/shard_map/ppermute | solution.py:76
  592.3 65.1 %collective-permute-start.70 = (bf16[5,128,1280]{2,1,0:T(8,128)(2,1)}, bf16[5,128,1280]{2,1,0:T(8,128)(2,1)}, u32[]{:S(2)}, u32[]{:S(2)}) collective-permute-start(bf16[5,128,1280]{2,1,0:T(8,128)(2,1)} %get-tuple-element.161.refs_3_), channel_id=1, source_target_pairs={{0,1},{1,0},{2,3},{3,2},{4,5},{5,4},{6,7},{7,6},{8,9},{9,8},{10,11... | collective-permute-start | bytes 4915208 | tf_op jit(solution)/shard_map/ppermute | solution.py:76
  605.2 22.8 %collective-permute-start.59 = (bf16[128,2560]{1,0:T(8,128)(2,1)}, bf16[128,2560]{1,0:T(8,128)(2,1)S(1)}, u32[]{:S(2)}, u32[]{:S(2)}) collective-permute-start(bf16[128,2560]{1,0:T(8,128)(2,1)} %get-tuple-element.212), channel_id=1, source_target_pairs={{0,6},{2,0},{4,2},{6,4},{1,7},{3,1},{5,3},{7,5},{8,14},{10,8},{12,... | collective-permute-start | bytes 1966088 | tf_op jit(solution)/shard_map/ppermute | solution.py:80
  606.6 31.9 %collective-permute-start.60 = (bf16[128,2560]{1,0:T(8,128)(2,1)S(1)}, bf16[128,2560]{1,0:T(8,128)(2,1)}, u32[]{:S(2)}, u32[]{:S(2)}) collective-permute-start(bf16[128,2560]{1,0:T(8,128)(2,1)S(1)} %get-tuple-element.214), channel_id=1, source_target_pairs={{0,4},{2,6},{4,0},{6,2},{1,5},{3,7},{5,1},{7,3},{8,12},{10,14},{12... | collective-permute-start | bytes 1966088 | tf_op jit(solution)/shard_map/ppermute | solution.py:80
  621.0 22.4 %all-to-all-start.7 = ((bf16[64,25,128]{2,1,0:T(8,128)(2,1)}), bf16[64,25,128]{2,1,0:T(8,128)(2,1)S(1)}, u32[]{:S(2)}, u32[]{:S(2)}) async-start(bf16[64,25,128]{2,1,0:T(8,128)(2,1)} %broadcast_in_dim.65), calls=%async_computation.7 | async-start | bytes 1048576 | tf_op jit(solution)/shard_map/all_to_all | solution.py:1126
  (138 other events, 1222.0 us)
Sparse Core Ops, SparseCore 0:
  51.4 127.6 all-gather.6
  181.2 105.3 all-gather.8
  517.4 64.5 all-gather.10

commit v4 on v3

--- a/solution.py
+++ b/solution.py
@@ -222,23 +222,14 @@
     normed_ref[...] = norm_apply(x, gain_ref[...])
 
 
-def pack_kernel(s_ref, exa_ref, exb_ref, exn_ref, pick_ref, lg_ref, down_ref, n2_ref, mid_ref, out_ref):
-    cols, wide = exa_ref.shape
-    rank = mid_ref.shape[0]
-    lanes = out_ref.shape[1]
+def pack_kernel(s_ref, exa_ref, exb_ref, exn_ref, pick_ref, lg_ref, down_ref, n2_ref, out_ref):
+    wide = exa_ref.shape[1]
     share = down_ref.shape[1]
     for i, ref in enumerate((exa_ref, exb_ref, exn_ref)):
-        out_ref[:cols, i * wide : (i + 1) * wide] = ref[...]
+        out_ref[:, i * wide : (i + 1) * wide] = ref[...]
     at = 3 * wide
-    out_ref[:cols, at : at + share] = dot_tn(pick_ref[...], down_ref[...]).astype(bf16)
-    out_ref[:cols, at + share :] = dot_tn(lg_ref[...], n2_ref[...]).astype(bf16)
-    total = mid_ref.shape[1]
-    for i in range(3):
-        lo, hi = i * lanes, min((i + 1) * lanes, total)
-        rows = slice(cols + i * rank, cols + (i + 1) * rank)
-        out_ref[rows, : hi - lo] = mid_ref[:, lo:hi]
-        if hi - lo < lanes:
-            out_ref[rows, hi - lo :] = jnp.zeros((rank, lanes - hi + lo), bf16)
+    out_ref[:, at : at + share] = dot_tn(pick_ref[...], down_ref[...]).astype(bf16)
+    out_ref[:, at + share :] = dot_tn(lg_ref[...], n2_ref[...]).astype(bf16)
 
 
 def fill_kernel(c_ref, x_ref, w_ref, first_ref, select_ref, leave_ref, mask_ref, taps_ref, enter_ref, conv_ref, lat_ref, pick_ref, acc_ref):
@@ -621,7 +612,7 @@
 def unit_parts(one_ref, extra_ref, mid_ref, size):
     count = extra_ref.shape[0]
     cut = lambda ref, p: jnp.concatenate([ref[m, :, p * size : (p + 1) * size] for m in range(count)], axis=1)
-    mid = jnp.concatenate([cut(mid_ref, p) for p in range(4)], axis=1)
+    mid = jnp.concatenate([mid_ref[0, m, :, p * size : (p + 1) * size] for p in range(4) for m in range(count)], axis=1)
     placed = dot_tn(one_ref[...], mid).astype(bf16)
     wide = count * size
     return jnp.concatenate([cut(extra_ref, p) + placed[:, p * wide : (p + 1) * wide] for p in range(4)], axis=0)
@@ -641,18 +632,18 @@
         out_ref[p * units : (p + 1) * units, :] = done[:, p * cols : (p + 1) * cols]
 
 
-def shares_kernel(s_ref, one_ref, eye_ref, extra_l_ref, extra_e_ref, mid0_ref, mid1_ref, mid2_ref, leave_ref, enter_ref):
+def shares_kernel(s_ref, one_ref, eye_ref, extra_l_ref, extra_e_ref, mid_ref, leave_ref, enter_ref):
     one = one_ref[...]
     width = leave_ref.shape[1]
     share = extra_l_ref.shape[2]
-    start = mid0_ref.shape[2] - 2 * share
+    per = mid_ref.shape[3]
     sums = []
-    for ref in (mid0_ref, mid1_ref, mid2_ref):
-        total = ref[0].astype(f32)
+    for p in range(16 - 2 * width // per, 16):
+        total = mid_ref[p, 0].astype(f32)
         for m in range(1, 8):
-            total = total + ref[m].astype(f32)
+            total = total + mid_ref[p, m].astype(f32)
         sums.append(total.astype(bf16))
-    mid = jnp.concatenate([sums[0][:, start:], sums[1], sums[2]], axis=1)
+    mid = jnp.concatenate(sums, axis=1)
     leave_ref[...] = dot_tn(one, mid[:, :width])
     enter_ref[...] = dot_tn(mid[:, width : 2 * width], one)
     for m in range(8):
@@ -994,11 +985,6 @@
     extra_total = lax.all_to_all(extra_part, RING, 0, 0, tiled=True).reshape(8, eighth, -1)
     extra_total = to_low(tied(jnp.sum(extra_total.astype(f32), axis=0), gn2))
     extra_all = lax.all_to_all(jnp.broadcast_to(extra_total[None], (8, *extra_total.shape)), RING, 0, 0, tiled=True).reshape(main, -1)
-    grad_n2_extra = extra_all[:, :width].astype(f32)
-    lat_extra = extra_all[:, width:]
-    lgw_extra = lat_extra[:, :cols]
-    pick_n_extra = lat_extra[:, cols:]
-
     sums0 = add(gn0[:toks], swap(gn0[2 * toks : 3 * toks]))
     sums1 = add(gn1, swap(gn2)).astype(bf16)
     sums = [sums0] + [sums1[k * toks : (k + 1) * toks] for k in range(3)]
@@ -1017,12 +1003,15 @@
          *[v[i] for i in (2, 0, 1, 5, 6, 4, 3) for v in (parts0, parts1, parts2)], far, leave_narrow),
         60, (*sums[1:], extra_total),
     )
-    grad_n2 = tied(tied(line_back(sums), down), extra_all)
+    grad_n2 = tied(line_back(sums), down)
+    grad_n2_extra = tied(extra_all[:, :width].astype(f32), down)
+    lat_extra = extra_all[:, width:]
+    lgw_extra = lat_extra[:, :cols]
+    pick_n_extra = lat_extra[:, cols:]
     ffn_mid = tied(jnp.concatenate([mid_a, mid_b, mid_n, mid_l, mid_e], axis=1), grad_n2).astype(bf16)
-    mid_shape = ffn_mid.shape
-    ffn_mid = lax.all_to_all(ffn_mid.reshape(16, -1, cols), PLANE, 0, 0, tiled=True)
+    ffn_mid = lax.all_to_all(ffn_mid.reshape(rank, 16, -1).transpose(1, 0, 2), PLANE, 0, 0, tiled=True)
     ffn_mid = to_low(jnp.sum(ffn_mid.astype(f32), axis=0))
-    ffn_mid = lax.all_to_all(jnp.broadcast_to(ffn_mid[None], (16, *ffn_mid.shape)), PLANE, 0, 0, tiled=True).reshape(mid_shape)
+    ffn_mid = lax.all_gather(ffn_mid[None], AXES, axis=0, tiled=True).reshape(16, 8, rank, -1)
 
     grad_residual = cotangent + norm_back(residual, norm_second, grad_n2)
     grad_residual_extra = down_extra.astype(f32) + norm_back(residual_extra, norm_second, grad_n2_extra)
@@ -1036,12 +1025,17 @@
         core_at, (grad_out, near, leave_square[4], enter_half[4], select, states, branch, slope, decays), 18,
     )
     coming = chips_carry(jnp.stack([decays[0] * trail[0], decays[0] * back[0]]), True)[None, :]
+    down_mine = jnp.concatenate([down[:toks], down[2 * toks : 5 * toks]], axis=0)
+    down_theirs = jnp.concatenate([down[toks : 2 * toks], down[5 * toks :]], axis=0)
+    down_total = tied(add(down_mine, swap(down_theirs)), coming)
+    down_sums = [down_total[k * toks : (k + 1) * toks] for k in range(4)]
+    block_output = residual + line_back(down_sums)
     gelu_part, lat_gelu = call(
         geluback_kernel, (4,),
         [fixed(wide_block), col_spec(0), fixed((cols, halfw)), enter_spec, fixed(small_block)],
         [(rows_spec(main), ((main, width), f32)), F(*small_block)],
         [pltpu.VMEM(small_block, bf16)],
-        core_at, (grad_gelu, near, leave_half[0], enter_square[0], select), 12,
+        core_at, (grad_gelu, near, leave_half[0], enter_square[0], select), 1,
     )
 
     grad_in, grad_de, base, lat_gates = call(
@@ -1059,9 +1053,9 @@
     lanes_all = 3 * slotp + 2 * share
     (packed,) = call(
         pack_kernel, (1,),
-        [fixed((cols, slotp))] * 3 + [fixed((main, cols))] * 2 + [fixed((main, share))] * 2 + [fixed((rank, 3 * slotp + 2 * width))],
-        [B(cols + 3 * rank, lanes_all)], [], core_at,
-        (ex_a, ex_b, ex_n, pick_n_extra, lgw_extra, share_of(down_extra), share_of(n2_extra), ffn_mid), 3, (base,),
+        [fixed((cols, slotp))] * 3 + [fixed((main, cols))] * 2 + [fixed((main, share))] * 2,
+        [B(cols, lanes_all)], [], core_at,
+        (ex_a, ex_b, ex_n, pick_n_extra, lgw_extra, share_of(down_extra), share_of(n2_extra)), 3, (base,),
     )
     ffn_all = lax.all_gather(packed, RING, axis=0)
 
@@ -1079,7 +1073,7 @@
         core_at,
         (base, lat_gates, swap(lat_gates), halo_base, halo_lat, halo_other, select_after, mask_long, taps, enter_half[2], enter_half[3],
          leave_half[1], near, enter_square[1], gelu_part),
-        12,
+        1,
     )
 
     lg_gelu = ((lat_gelu + swap(lat_gelu)) * select).astype(bf16)
@@ -1096,18 +1090,13 @@
         [part_spec(cols, 0), part_spec(halfw, 0)] * 10,
         [B(10 * rank, halfw)],
         [pltpu.VMEM((cols, halfw), f32)],
-        middle_at, operands, 6,
+        middle_at, operands, 6, (block_output,),
     )
     mid_own = mid
     shape = mid.shape
     mid = lax.all_to_all(mid.reshape(64, -1, cols), CHIPS, 0, 0, tiled=True)
     mid = to_low(jnp.sum(mid.astype(f32), axis=0))
 
-    down_mine = jnp.concatenate([down[:toks], down[2 * toks : 5 * toks]], axis=0)
-    down_theirs = jnp.concatenate([down[toks : 2 * toks], down[5 * toks :]], axis=0)
-    down_total = tied(add(down_mine, swap(down_theirs)), base)
-    down_sums = [down_total[k * toks : (k + 1) * toks] for k in range(4)]
-    block_output = residual + line_back(down_sums)
     operands = [*[v for pair in pairs[:5] for v in pair[::-1]], *[v for pair in pairs[5:] for v in pair]]
     enter_extra, leave_extra = call(
         functools.partial(extras_kernel, 5), (1,),
@@ -1118,32 +1107,32 @@
     )
     (grad_leave_widen,) = call(
         wide_kernel, (8,),
-        [fixed((rank, cols)), fixed((units, 8 * chunk)), pl.BlockSpec((8, cols, hcol), lambda i, s: (0, 0, i)), pl.BlockSpec((8, rank, hcol), lambda i, s: (0, cols // rank, i))],
+        [fixed((rank, cols)), fixed((units, 8 * chunk)), pl.BlockSpec((8, cols, hcol), lambda i, s: (0, 0, i)), pl.BlockSpec((1, 8, rank, hcol), lambda i, s: (i // 2, 0, 0, i % 2))],
         [(pl.BlockSpec((cols, block), lambda i, s: (0, i)), ((cols, 2 * ff), f32))],
-        [], core_at, (one_hot, spread_one, ffn_all, ffn_all), 12, (mid_own,),
+        [], core_at, (one_hot, spread_one, ffn_all, ffn_mid), 12, (mid_own,),
     )
     mid = tied(mid, grad_leave_widen).astype(bf16)
     mid = lax.all_to_all(jnp.broadcast_to(mid[None], (64, *mid.shape)), CHIPS, 0, 0, tiled=True).reshape(shape)
     (grad_enter_narrow,) = call(
         enter_kernel, (4,),
-        [fixed((rank, cols)), fixed((units, 8 * chunk)), pl.BlockSpec((8, cols, hcol), lambda i, s: (0, 0, 8 + i)), pl.BlockSpec((8, rank, hcol), lambda i, s: (0, cols // rank, 8 + i))],
+        [fixed((rank, cols)), fixed((units, 8 * chunk)), pl.BlockSpec((8, cols, hcol), lambda i, s: (0, 0, 8 + i)), pl.BlockSpec((1, 8, rank, hcol), lambda i, s: (4 + i // 2, 0, 0, i % 2))],
         [(pl.BlockSpec((block, cols), lambda i, s: (i, 0)), ((ff, cols), f32))],
-        [], core_at, (one_hot, spread_one, ffn_all, ffn_all), 7, (mid_own,),
+        [], core_at, (one_hot, spread_one, ffn_all, ffn_mid), 7, (mid_own,),
     )
     grad_normed = normed_mine + swap(normed_theirs).astype(f32)
     input_grad = grad_residual + norm_back(block_input, norm_first, grad_normed)
     eye = jnp.eye(cols, dtype=bf16)
     share_spec = lambda i: pl.BlockSpec((8, cols, share), lambda *_: (0, 0, 3 * slotp // share + i))
-    mid_rows = lambda i: pl.BlockSpec((8, rank, lanes_all), lambda *_: (0, cols // rank + i, 0))
     grad_leave_narrow, grad_enter_widen = call(
         shares_kernel, (1,),
-        [fixed((rank, cols)), fixed((cols, cols)), share_spec(0), share_spec(1)] + [mid_rows(i) for i in range(3)],
+        [fixed((rank, cols)), fixed((cols, cols)), share_spec(0), share_spec(1), fixed(ffn_mid.shape)],
         [F(cols, width), F(width, cols)],
-        [], core_at, (one_hot, eye) + (ffn_all,) * 5, 4, (mid_own,),
+        [], core_at, (one_hot, eye, ffn_all, ffn_all, ffn_mid), 4, (mid_own,),
     )
     per_k = lambda *shape: pl.BlockSpec((1,) + shape, lambda k, s: (k,) + (0,) * len(shape))
     mid_e_spec = pl.BlockSpec((rank, halfw), lambda k, s: (k, 0))
     mid_l_spec = pl.BlockSpec((rank, halfw), lambda k, s: (5 + k, 0))
+    mid = tied(tied(mid, grad_enter_narrow), grad_leave_narrow).astype(bf16)
     mid_other = swap(mid)
     grad_enter_square, grad_leave_square = call(
         square_kernel, (5,),

time: 686 us -> 695 us (1.013)
  waiting for transfers between devices: 123 us -> 136 us
  starting transfers between devices: 137 us -> 126 us
    ppermute x33, waiting for transfers between devices: 27.4 us -> 54 us  [shift4(): return lax.ppermute(v, axis, [(i, (i + by) % 4) for i in range(4)])]
    all_to_all x1, waiting for transfers between devices: 14.4 us -> 0.01 us  [per_device(): lax.all_to_all(jnp.broadcast_to(extra_total[None], (8, *extra_total.shape...]
    all_to_all x2 -> x1, starting transfers between devices: 12.2 us -> 4.19 us  [per_device(): lax.all_to_all(ffn_mid.reshape(rank, 16, -1).transpose(1, 0, 2), PLANE, 0...]
    unnamed x186 -> x188, local copies, waits for them, and re-layouts: 19.1 us -> 17.2 us
  transfers between devices with their start and end apart: 83 -> 83, of which waited for: 20 -> 25; matrix products, arithmetic and copies ran while one was open for 21% -> 21% of each run, Pallas kernels for 31% -> 33%
where the time goes in v4:
time: 695 us; the launch traced here: 683 us
  Pallas kernels  234 us (34%)
  waiting for transfers between devices  136 us (20%)
  starting transfers between devices  126 us (18%)
  local copies, waits for them, and re-layouts  79.3 us (11%)
  other arithmetic  77.5 us (11%)
  between operations  22.2 us (3%)
  matrix products  8.89 us (1%)
    pallas_call x20, Pallas kernels, call(): pl.pallas_call(body, grid_spec=pltpu.PrefetchScalarGridSpec(num_scalar_pr...  234 us
    ppermute x33, waiting for transfers between devices, shift4(): return lax.ppermute(v, axis, [(i, (i + by) % 4) for i in range(4)])  54 us
    all_gather x1, waiting for transfers between devices, per_device(): lax.all_gather(quads[None], AXES, axis=0, tiled=True)  53.8 us
    ppermute x33, starting transfers between devices, shift4(): return lax.ppermute(v, axis, [(i, (i + by) % 4) for i in range(4)])  42.1 us
    ppermute x27, starting transfers between devices, swap(): return lax.ppermute(v, 'c', [(0, 1), (1, 0)])  22.6 us
    all_to_all x1, starting transfers between devices, per_device(): quads = lax.all_to_all(quads, QUAD, 0, 0, tiled=True).reshape(per4, lanes)  17.4 us
    unnamed x188, local copies, waits for them, and re-layouts  17.2 us
  transfers between devices with their start and end apart: 83, of which 25 were waited for; matrix products, arithmetic and copies ran while one was open for 21% of the time, Pallas kernels for 33%

profile of v4, /device:TPU:1, one launch (start us, length us, event | category | flops | bytes accessed | tf_op | source)
XLA Modules:
  0.0 683.2 jit_solution(12423824500845638374)
XLA Ops:
  19.8 17.4 %all-to-all-start = ((bf16[4,20,2048]{2,1,0:T(8,128)(2,1)}), bf16[4,20,2048]{2,1,0:T(8,128)(2,1)S(1)}, u32[]{:S(2)}, u32[]{:S(2)}) async-start(bf16[4,20,2048]{2,1,0:T(8,128)(2,1)} %pad_maximum_fusion.5), calls=%async_computation | async-start | bytes 786432 | tf_op jit(solution)/shard_map/all_to_all | solution.py:804
  43.8 6.6 collective-permute-done.8
  52.4 5.1 convolution_convert_fusion
  65.0 12.5 %all-to-all-done.1 = bf16[8,20,2048]{2,1,0:T(8,128)(2,1)S(1)} async-done(((bf16[8,20,2048]{2,1,0:T(8,128)(2,1)}), bf16[8,20,2048]{2,1,0:T(8,128)(2,1)S(1)}, u32[]{:S(2)}, u32[]{:S(2)}) %all-to-all-start.1) | async-done | bytes 655392 | tf_op jit(solution)/shard_map/all_to_all | solution.py:826
  79.7 6.3 copy.66
  86.0 6.3 copy.67
  127.2 53.8 %all-gather.9.cloned.1.call-done = bf16[11264,2048]{1,0:T(8,128)(2,1)} async-done(((bf16[88,2048]{1,0:T(8,128)(2,1)}), bf16[11264,2048]{1,0:T(8,128)(2,1)}) %all-gather.9.cloned.1.call-update) | async-done | bytes 46137360 | tf_op jit(solution)/shard_map/all_gather | solution.py:810
  189.9 5.0 shard_map.260
  201.3 12.6 %shard_map.261 = (bf16[512,1280]{1,0:T(8,128)(2,1)}, f32[512,256]{1,0:T(8,128)}, bf16[528,128]{1,0:T(8,128)(2,1)}) custom-call(s32[1]{0:T(128)} %bitcast.5.s_ref, bf16[528,2560]{1,0:T(8,128)(2,1)} %pad_maximum_fusion.1.refs_0_, bf16[32,4,88,2048]{3,2,1,0:T(8,128)(2,1)} %bitcast.105, bf16[2560,128]{1,0:T(8,128)(2,1)} %get-tuple-element.210.refs_2_.refs_13_, ...), custom_call_target="tpu_custom_call" | custom-call | flops 1000000000 | bytes 2000000 | tf_op jit(solution)/shard_map/pallas_call | solution.py:128
  218.1 11.0 %shard_map.262 = (f32[512,1280]{1,0:T(8,128)}, f32[512,1280]{1,0:T(8,128)}, f32[512,1280]{1,0:T(8,128)}, f32[512,1280]{1,0:T(8,128)}, f32[512,1280]{1,0:T(8,128)...) custom-call(s32[1]{0:T(128)} %bitcast.5.s_ref, ...), custom_call_target="tpu_custom_call" | custom-call | flops 4000000000 | bytes 8000000 | tf_op jit(solution)/shard_map/pallas_call | solution.py:128
  250.3 11.3 %shard_map.263 = (f32[512,1280]{1,0:T(8,128)}, f32[512,1280]{1,0:T(8,128)}, bf16[512,128]{1,0:T(8,128)(2,1)}) custom-call(s32[1]{0:T(128)} %bitcast.5.s_ref, bf16[528,2560]{1,0:T(8,128)(2,1)} %pad_maximum_fusion.1.refs_0_, bf16[32,4,88,2048]{3,2,1,0:T(8,128)(2,1)} %bitcast.107, bf16[2560,128]{1,0:T(8,128)(2,1)} %get-tuple-element.209.refs_2_.refs_3_, ...), custom_call_target="tpu_custom_call" | custom-call | flops 12000000000 | bytes 24000000 | tf_op jit(solution)/shard_map/pallas_call | solution.py:128
  262.2 14.2 %shard_map.264 = (f32[512,1280]{1,0:T(8,128)}, bf16[512,1280]{1,0:T(8,128)(2,1)}, f32[512,128]{1,0:T(8,128)}, f32[128,2560]{1,0:T(8,128)}, bf16[384,2560]{1,0:T(8,128)(2,1)}, /*index=5*/bf16[256,2560]{1,0:T(8,128)(2,1)}) custom-call(s32[1]{0:T(128)} %bitcast.5.s_ref, f32[512,1280]{1,0:T(8,128)} %get-tuple-element.100.refs_0_, ...), custom_call_target="tpu_custom_call" | custom-call | flops 15000000512 | bytes 30000000 | tf_op jit(solution)/shard_map/pallas_call | solution.py:128
  295.0 26.0 %shard_map.265 = (bf16[512,2560]{1,0:T(8,128)(2,1)}, bf16[512,1024]{1,0:T(8,128)(2,1)}, bf16[512,1024]{1,0:T(8,128)(2,1)}, bf16[512,1024]{1,0:T(8,128)(2,1)}, bf...) custom-call(s32[1]{0:T(128)} %bitcast.5.s_ref, ...), custom_call_target="tpu_custom_call" | custom-call | flops 60000002048 | bytes 120000000 | tf_op jit(solution)/shard_map/pallas_call | solution.py:128
  322.1 21.0 %shard_map.266 = (bf16[384,2560]{1,0:T(8,128)(2,1)}, bf16[384,1024]{1,0:T(8,128)(2,1)}, bf16[384,1024]{1,0:T(8,128)(2,1)}, bf16[384,1024]{1,0:T(8,128)(2,1)}, bf...) custom-call(s32[1]{0:T(128)} %bitcast.5.s_ref, ...), custom_call_target="tpu_custom_call" | custom-call | flops 40000000000 | bytes 80000000 | tf_op jit(solution)/shard_map/pallas_call | solution.py:128
  356.0 20.9 %shard_map.267 = (bf16[384,2560]{1,0:T(8,128)(2,1)}, bf16[384,1024]{1,0:T(8,128)(2,1)}, bf16[384,1024]{1,0:T(8,128)(2,1)}, bf16[384,1024]{1,0:T(8,128)(2,1)}, bf...) custom-call(s32[1]{0:T(128)} %bitcast.5.s_ref, ...), custom_call_target="tpu_custom_call" | custom-call | flops 60000002048 | bytes 120000000 | tf_op jit(solution)/shard_map/pallas_call | solution.py:128
  382.7 4.8 all-to-all-start.3
  395.4 19.5 %shard_map.268 = (bf16[1024,2560]{1,0:T(8,128)(2,1)}, bf16[16,1024]{1,0:T(8,128)(2,1)}, bf16[16,1024]{1,0:T(8,128)(2,1)}, bf16[16,1024]{1,0:T(8,128)(2,1)}, bf16...) custom-call(s32[1]{0:T(128)} %slice.506.s_ref, ...), custom_call_target="tpu_custom_call" | custom-call | flops 60000002048 | bytes 120000000 | tf_op jit(solution)/shard_map/pallas_call | solution.py:128
  421.0 13.9 %collective-permute-done.48 = bf16[128,2560]{1,0:T(8,128)(2,1)} collective-permute-done((bf16[128,2560]{1,0:T(8,128)(2,1)}, bf16[128,2560]{1,0:T(8,128)(2,1)}, u32[]{:S(2)}, u32[]{:S(2)}) %collective-permute-start.48) | collective-permute-done | bytes 655392 | tf_op jit(solution)/shard_map/ppermute | solution.py:80
  458.7 15.3 %shard_map.269 = (bf16[512,1280]{1,0:T(8,128)(2,1)}, bf16[512,128]{1,0:T(8,128)(2,1)}, f32[512,1280]{1,0:T(8,128)}, f32[512,1280]{1,0:T(8,128)}) custom-call(s32[1]{0:T(128)} %bitcast.5.s_ref, bf16[512,2560]{1,0:T(8,128)(2,1)} %pad_maximum_fusion.refs_0_, bf16[32,4,88,2048]{3,2,1,0:T(8,128)(2,1)} %bitcast.109, ...), custom_call_target="tpu_custom_call" | custom-call | flops 17999998976 | bytes 36000000 | tf_op jit(solution)/shard_map/pallas_call | solution.py:128
  492.7 12.5 %shard_map.270 = (bf16[512,1280]{1,0:T(8,128)(2,1)}, bf16[512,1280]{1,0:T(8,128)(2,1)}, f32[512,1280]{1,0:T(8,128)}, f32[512,256]{1,0:T(8,128)}) custom-call(s32[1]{0:T(128)} %bitcast.5.s_ref, f32[512,1280]{1,0:T(8,128)} %get-tuple-element.137.refs_0_, f32[512,1280]{1,0:T(8,128)} %get-tuple-element.136.refs_1_, f32[1,1280]{1,0:T(1,128)} %fusion.70.refs_2_, ...), custom_call_target="tpu_custom_call" | custom-call | flops 8000000000 | bytes 16000000 | tf_op jit(solution)/shard_map/pallas_call | solution.py:128
  532.0 8.0 %shard_map.271 = (f32[256,2560]{1,0:T(8,128)}, f32[512,128]{1,0:T(8,128)}) custom-call(s32[1]{0:T(128)} %bitcast.5.s_ref, bf16[512,1280]{1,0:T(8,128)(2,1)} %get-tuple-element.142.refs_0_.refs_11_, bf16[32,4,88,2048]{3,2,1,0:T(8,128)(2,1)} %bitcast.111, bf16[128,1280]{1,0:T(8,128)(2,1)} %get-tuple-element.205.refs_4_.refs_2_, ...), custom_call_target="tpu_custom_call" | custom-call | flops 1000000000 | bytes 2000000 | tf_op jit(solution)/shard_map/pallas_call | solution.py:128
  544.0 12.0 %shard_map.272 = (bf16[512,1280]{1,0:T(8,128)(2,1)}, bf16[512,128]{1,0:T(8,128)(2,1)}, bf16[512,128]{1,0:T(8,128)(2,1)}, f32[512,128]{1,0:T(8,128)}, f32[128,2560]{1,0:T(8,128)}, /*index=5*/bf16[128,2560]{1,0:T(8,128)(2,1)}) custom-call(s32[1]{0:T(128)} %bitcast.5.s_ref, f32[512,1280]{1,0:T(8,128)} %get-tuple-element.140.refs_0_.refs_7_, ...), custom_call_target="tpu_custom_call" | custom-call | flops 1000000000 | bytes 2000000 | tf_op jit(solution)/shard_map/pallas_call | solution.py:128
  559.7 4.7 collective-permute-start.59
  567.8 24.2 %collective-permute-done.59 = bf16[128,2560]{1,0:T(8,128)(2,1)S(1)} collective-permute-done((bf16[128,2560]{1,0:T(8,128)(2,1)S(1)}, bf16[128,2560]{1,0:T(8,128)(2,1)S(1)}, u32[]{:S(2)}, u32[]{:S(2)}) %collective-permute-start.59) | collective-permute-done | bytes 655392 | tf_op jit(solution)/shard_map/ppermute | solution.py:80
  598.0 5.6 shard_map.273.refs_20_.refs_4_.refs_5_
  605.8 6.1 all-to-all-start.4
  612.0 6.1 shard_map.274
  619.0 5.1 all-to-all-done.4
  624.3 10.8 %shard_map.276 = f32[128,15360]{1,0:T(8,128)} custom-call(s32[1]{0:T(128)} %bitcast.5.s_ref, bf16[16,128]{1,0:T(8,128)(2,1)} %fusion.60.refs_0_, bf16[480,512]{1,0:T(8,128)(2,1)} %fusion.37.refs_1_, bf16[8,128,3840]{2,1,0:T(8,128)(2,1)} %bitcast.113, bf16[16,8,16,512]{3,2,1,0:T(8,128)(2,1)} %bitcast.126, bf16[160,1280]{1,0:T(8,128)(2,1)} %shard_map.273.refs_20_.refs_4_.refs_5_), custom_call_target="tpu_custom_call" | custom-call | flops 12000000000 | bytes 24000000 | tf_op jit(solution)/shard_map/pallas_call | solution.py:128
  637.8 5.5 all-to-all-start.6
  643.3 5.9 shard_map.277
  667.0 9.5 %shard_map.279 = (f32[5,2560,128]{2,1,0:T(8,128)}, f32[5,128,2560]{2,1,0:T(8,128)}) custom-call(s32[1]{0:T(128)} %bitcast.5.s_ref, bf16[16,128]{1,0:T(8,128)(2,1)} %fusion.60.refs_0_, bf16[5,1280,128]{2,1,0:T(8,128)(2,1)} %get-tuple-element.160.refs_1_, bf16[5,1280,128]{2,1,0:T(8,128)(2,1)} %collective-permute-done.69.refs_2_, ...), custom_call_target="tpu_custom_call" | custom-call | flops 8999999488 | bytes 18000000 | tf_op jit(solution)/shard_map/pallas_call | solution.py:128
  (538 shorter events, 261.6 us)
Async XLA Ops:
  15.7 21.4 %collective-permute-start.3 = (bf16[16,2688]{1,0:T(8,128)(2,1)}, bf16[16,2688]{1,0:T(8,128)(2,1)S(1)}, u32[]{:S(2)}, u32[]{:S(2)}) collective-permute-start(bf16[16,2688]{1,0:T(8,128)(2,1)} %get-tuple-element.230), channel_id=1, source_target_pairs={{0,16},{64,80},{32,48},{96,112},{127,111},{63,47},{95,79},{31,15}} | collective-permute-start | bytes 258056 | tf_op jit(solution)/shard_map/ppermute | solution.py:715
  16.4 20.8 %collective-permute-start.4 = (bf16[16,2688]{1,0:T(8,128)(2,1)}, bf16[16,2688]{1,0:T(8,128)(2,1)}, u32[]{:S(2)}, u32[]{:S(2)}) collective-permute-start(bf16[16,2688]{1,0:T(8,128)(2,1)} %get-tuple-element.231), channel_id=1, source_target_pairs={{0,8},{64,72},{32,40},{96,104},{127,119},{63,55},{95,87},{31,23}} | collective-permute-start | bytes 258056 | tf_op jit(solution)/shard_map/ppermute | solution.py:715
  17.7 20.1 %collective-permute-start.5 = (bf16[16,2688]{1,0:T(8,128)(2,1)}, bf16[16,2688]{1,0:T(8,128)(2,1)}, u32[]{:S(2)}, u32[]{:S(2)}) collective-permute-start(bf16[16,2688]{1,0:T(8,128)(2,1)} %get-tuple-element.232), channel_id=1, source_target_pairs={{0,24},{64,88},{32,56},{96,120},{127,103},{63,39},{95,71},{31,7}} | collective-permute-start | bytes 258056 | tf_op jit(solution)/shard_map/ppermute | solution.py:715
  19.8 23.9 %all-to-all-start = ((bf16[4,20,2048]{2,1,0:T(8,128)(2,1)}), bf16[4,20,2048]{2,1,0:T(8,128)(2,1)S(1)}, u32[]{:S(2)}, u32[]{:S(2)}) async-start(bf16[4,20,2048]{2,1,0:T(8,128)(2,1)} %pad_maximum_fusion.5), calls=%async_computation | async-start | bytes 786432 | tf_op jit(solution)/shard_map/all_to_all | solution.py:804
  37.2 143.9 %all-gather.9.cloned.1.call-start = ((), (), s32[]{:S(2)}) async-start(), calls=%async_computation.7 | async-start | bytes 46497792 | tf_op jit(solution)/shard_map/all_gather | solution.py:810
  63.3 231.7 %all-gather.11.cloned.1.call-start = ((), (), s32[]{:S(2)}) async-start(), calls=%async_computation.8 | async-start | bytes 16711680 | tf_op jit(solution)/shard_map/all_gather | solution.py:830
  124.1 72.5 %collective-permute-start.10 = (bf16[16,2560]{1,0:T(8,128)(2,1)S(1)}, bf16[16,2560]{1,0:T(8,128)(2,1)S(1)}, u32[]{:S(2)}, u32[]{:S(2)}) collective-permute-start(bf16[16,2560]{1,0:T(8,128)(2,1)S(1)} %slice.622), channel_id=1, source_target_pairs={{0,2},{1,3},{2,4},{3,5},{4,6},{5,7},{6,8},{7,9},{8,10},{9,11},{10,... | collective-permute-start | bytes 245768 | tf_op jit(solution)/shard_map/ppermute | solution.py:91
  185.1 31.9 %collective-permute-start.19 = (bf16[128,2560]{1,0:T(8,128)(2,1)}, bf16[128,2560]{1,0:T(8,128)(2,1)}, u32[]{:S(2)}, u32[]{:S(2)}) collective-permute-start(bf16[128,2560]{1,0:T(8,128)(2,1)} %add_convert_fusion.3.refs_4_.refs_8_), channel_id=1, source_target_pairs={{0,2},{2,4},{4,6},{6,0},{1,3},{3,5},{5,7},{7,1},{8,10},{10,12},{12... | collective-permute-start | bytes 1966088 | tf_op jit(solution)/shard_map/ppermute | solution.py:80
  186.3 31.8 %collective-permute-start.20 = (bf16[128,2560]{1,0:T(8,128)(2,1)}, bf16[128,2560]{1,0:T(8,128)(2,1)}, u32[]{:S(2)}, u32[]{:S(2)}) collective-permute-start(bf16[128,2560]{1,0:T(8,128)(2,1)} %add_convert_fusion.3.refs_4_.refs_8_), channel_id=1, source_target_pairs={{0,4},{2,6},{4,0},{6,2},{1,5},{3,7},{5,1},{7,3},{8,12},{10,14},{12... | collective-permute-start | bytes 1966088 | tf_op jit(solution)/shard_map/ppermute | solution.py:80
  189.1 29.0 %collective-permute-start.21 = (bf16[128,2560]{1,0:T(8,128)(2,1)}, bf16[128,2560]{1,0:T(8,128)(2,1)}, u32[]{:S(2)}, u32[]{:S(2)}) collective-permute-start(bf16[128,2560]{1,0:T(8,128)(2,1)} %add_convert_fusion.3.refs_4_.refs_8_), channel_id=1, source_target_pairs={{0,6},{2,0},{4,2},{6,4},{1,7},{3,1},{5,3},{7,5},{8,14},{10,8},{12,... | collective-permute-start | bytes 1966088 | tf_op jit(solution)/shard_map/ppermute | solution.py:80
  283.5 62.9 %collective-permute-start.40 = (bf16[128,2560]{1,0:T(8,128)(2,1)}, bf16[128,2560]{1,0:T(8,128)(2,1)S(1)}, u32[]{:S(2)}, u32[]{:S(2)}) collective-permute-start(bf16[128,2560]{1,0:T(8,128)(2,1)} %collective-permute-done.19.refs_9_.refs_3_.refs_10_), channel_id=1, source_target_pairs={{0,1},{1,0},{2,3},{3,2},{4,5},{5,4},{6,7},{7,6},{8,9},{9,8},{10,11... | collective-permute-start | bytes 1966088 | tf_op jit(solution)/shard_map/ppermute | solution.py:76
  284.0 71.1 %collective-permute-start.41 = (bf16[128,2560]{1,0:T(8,128)(2,1)}, bf16[128,2560]{1,0:T(8,128)(2,1)}, u32[]{:S(2)}, u32[]{:S(2)}) collective-permute-start(bf16[128,2560]{1,0:T(8,128)(2,1)} %collective-permute-done.20.refs_10_.refs_4_.refs_11_), channel_id=1, source_target_pairs={{0,1},{1,0},{2,3},{3,2},{4,5},{5,4},{6,7},{7,6},{8,9},{9,8},{10,11... | collective-permute-start | bytes 1966088 | tf_op jit(solution)/shard_map/ppermute | solution.py:76
  286.5 34.5 %collective-permute-start.33 = (bf16[128,2560]{1,0:T(8,128)(2,1)S(1)}, bf16[128,2560]{1,0:T(8,128)(2,1)}, u32[]{:S(2)}, u32[]{:S(2)}) collective-permute-start(bf16[128,2560]{1,0:T(8,128)(2,1)S(1)} %multiply_convert_fusion.1.refs_0_), channel_id=1, source_target_pairs={{0,2},{2,4},{4,6},{6,0},{1,3},{3,5},{5,7},{7,1},{8,10},{10,12},{12... | collective-permute-start | bytes 1966088 | tf_op jit(solution)/shard_map/ppermute | solution.py:80
  291.1 30.9 %collective-permute-start.34 = (bf16[128,2560]{1,0:T(8,128)(2,1)S(1)}, bf16[128,2560]{1,0:T(8,128)(2,1)}, u32[]{:S(2)}, u32[]{:S(2)}) collective-permute-start(bf16[128,2560]{1,0:T(8,128)(2,1)S(1)} %multiply_convert_fusion.1.refs_0_), channel_id=1, source_target_pairs={{0,4},{2,6},{4,0},{6,2},{1,5},{3,7},{5,1},{7,3},{8,12},{10,14},{12... | collective-permute-start | bytes 1966088 | tf_op jit(solution)/shard_map/ppermute | solution.py:80
  293.9 28.2 %collective-permute-start.35 = (bf16[128,2560]{1,0:T(8,128)(2,1)S(1)}, bf16[128,2560]{1,0:T(8,128)(2,1)}, u32[]{:S(2)}, u32[]{:S(2)}) collective-permute-start(bf16[128,2560]{1,0:T(8,128)(2,1)S(1)} %multiply_convert_fusion.1.refs_0_), channel_id=1, source_target_pairs={{0,6},{2,0},{4,2},{6,4},{1,7},{3,1},{5,3},{7,5},{8,14},{10,8},{12,... | collective-permute-start | bytes 1966088 | tf_op jit(solution)/shard_map/ppermute | solution.py:80
  321.0 34.1 %collective-permute-start.42 = (bf16[128,2560]{1,0:T(8,128)(2,1)}, bf16[128,2560]{1,0:T(8,128)(2,1)S(1)}, u32[]{:S(2)}, u32[]{:S(2)}) collective-permute-start(bf16[128,2560]{1,0:T(8,128)(2,1)} %collective-permute-done.21.refs_11_.refs_5_.refs_12_), channel_id=1, source_target_pairs={{0,1},{1,0},{2,3},{3,2},{4,5},{5,4},{6,7},{7,6},{8,9},{9,8},{10,11... | collective-permute-start | bytes 1966088 | tf_op jit(solution)/shard_map/ppermute | solution.py:76
  351.1 30.2 %all-to-all-start.2 = ((bf16[8,32,2816]{2,1,0:T(8,128)(2,1)}), bf16[8,32,2816]{2,1,0:T(8,128)(2,1)S(1)}, u32[]{:S(2)}, u32[]{:S(2)}) async-start(bf16[8,32,2816]{2,1,0:T(8,128)(2,1)} %bitcast.38), calls=%async_computation.2 | async-start | bytes 2883584 | tf_op jit(solution)/shard_map/all_to_all | solution.py:985
  379.0 41.5 %collective-permute-start.45 = (bf16[128,2560]{1,0:T(8,128)(2,1)}, bf16[128,2560]{1,0:T(8,128)(2,1)}, u32[]{:S(2)}, u32[]{:S(2)}) collective-permute-start(bf16[128,2560]{1,0:T(8,128)(2,1)} %slice.565), channel_id=1, source_target_pairs={{0,1},{1,0},{2,3},{3,2},{4,5},{5,4},{6,7},{7,6},{8,9},{9,8},{10,11... | collective-permute-start | bytes 1966088 | tf_op jit(solution)/shard_map/ppermute | solution.py:76
  382.7 35.3 %all-to-all-start.3 = ((bf16[8,32,2816]{2,1,0:T(8,128)(2,1)}), bf16[8,32,2816]{2,1,0:T(8,128)(2,1)S(1)}, u32[]{:S(2)}, u32[]{:S(2)}) async-start(bf16[8,32,2816]{2,1,0:T(8,128)(2,1)} %broadcast_in_dim.59), calls=%async_computation.3 | async-start | bytes 2883584 | tf_op jit(solution)/shard_map/all_to_all | solution.py:987
  391.5 29.1 %collective-permute-start.46 = (bf16[128,2560]{1,0:T(8,128)(2,1)}, bf16[128,2560]{1,0:T(8,128)(2,1)S(1)}, u32[]{:S(2)}, u32[]{:S(2)}) collective-permute-start(bf16[128,2560]{1,0:T(8,128)(2,1)} %get-tuple-element.219.refs_39_), channel_id=1, source_target_pairs={{0,6},{2,0},{4,2},{6,4},{1,7},{3,1},{5,3},{7,5},{8,14},{10,8},{12,... | collective-permute-start | bytes 1966088 | tf_op jit(solution)/shard_map/ppermute | solution.py:80
  394.1 26.9 %collective-permute-start.47 = (bf16[128,2560]{1,0:T(8,128)(2,1)}, bf16[128,2560]{1,0:T(8,128)(2,1)}, u32[]{:S(2)}, u32[]{:S(2)}) collective-permute-start(bf16[128,2560]{1,0:T(8,128)(2,1)} %get-tuple-element.218.refs_40_), channel_id=1, source_target_pairs={{0,4},{2,6},{4,0},{6,2},{1,5},{3,7},{5,1},{7,3},{8,12},{10,14},{12... | collective-permute-start | bytes 1966088 | tf_op jit(solution)/shard_map/ppermute | solution.py:80
  394.7 40.2 %collective-permute-start.48 = (bf16[128,2560]{1,0:T(8,128)(2,1)}, bf16[128,2560]{1,0:T(8,128)(2,1)}, u32[]{:S(2)}, u32[]{:S(2)}) collective-permute-start(bf16[128,2560]{1,0:T(8,128)(2,1)} %get-tuple-element.217.refs_41_), channel_id=1, source_target_pairs={{0,2},{2,4},{4,6},{6,0},{1,3},{3,5},{5,7},{7,1},{8,10},{10,12},{12... | collective-permute-start | bytes 1966088 | tf_op jit(solution)/shard_map/ppermute | solution.py:80
  444.5 179.7 %all-gather.15.cloned.1.call-start = ((), (), s32[]{:S(2)}) async-start(), calls=%async_computation.10 | async-start | bytes 2113536 | tf_op jit(solution)/shard_map/all_gather | solution.py:1014
  454.2 170.1 %all-gather.13.cloned.1.call-start = ((), (), s32[]{:S(2)}) async-start(), calls=%async_computation.9 | async-start | bytes 8847360 | tf_op jit(solution)/shard_map/all_gather | solution.py:1060
  514.8 42.0 %collective-permute-start.44 = (bf16[512,2560]{1,0:T(8,128)(2,1)}, bf16[512,2560]{1,0:T(8,128)(2,1)}, u32[]{:S(2)}, u32[]{:S(2)}) collective-permute-start(bf16[512,2560]{1,0:T(8,128)(2,1)} %pad_maximum_fusion.2), channel_id=1, source_target_pairs={{0,1},{1,0},{2,3},{3,2},{4,5},{5,4},{6,7},{7,6},{8,9},{9,8},{10,11... | collective-permute-start | bytes 7864328 | tf_op jit(solution)/shard_map/ppermute | solution.py:76
  526.3 38.0 %collective-permute-start.68 = (f32[512,128]{1,0:T(8,128)S(1)}, f32[512,128]{1,0:T(8,128)}, u32[]{:S(2)}, u32[]{:S(2)}) collective-permute-start(f32[512,128]{1,0:T(8,128)S(1)} %copy-done.50), channel_id=1, source_target_pairs={{0,1},{1,0},{2,3},{3,2},{4,5},{5,4},{6,7},{7,6},{8,9},{9,8},{10,11... | collective-permute-start | bytes 786440 | tf_op jit(solution)/shard_map/ppermute | solution.py:76
  541.8 22.9 %collective-permute-start.66 = (f32[512,128]{1,0:T(8,128)}, f32[512,128]{1,0:T(8,128)}, u32[]{:S(2)}, u32[]{:S(2)}) collective-permute-start(f32[512,128]{1,0:T(8,128)} %get-tuple-element.146), channel_id=1, source_target_pairs={{0,1},{1,0},{2,3},{3,2},{4,5},{5,4},{6,7},{7,6},{8,9},{9,8},{10,11... | collective-permute-start | bytes 786440 | tf_op jit(solution)/shard_map/ppermute | solution.py:76
  559.7 32.3 %collective-permute-start.59 = (bf16[128,2560]{1,0:T(8,128)(2,1)S(1)}, bf16[128,2560]{1,0:T(8,128)(2,1)S(1)}, u32[]{:S(2)}, u32[]{:S(2)}) collective-permute-start(bf16[128,2560]{1,0:T(8,128)(2,1)S(1)} %get-tuple-element.212), channel_id=1, source_target_pairs={{0,6},{2,0},{4,2},{6,4},{1,7},{3,1},{5,3},{7,5},{8,14},{10,8},{12,... | collective-permute-start | bytes 1966088 | tf_op jit(solution)/shard_map/ppermute | solution.py:80
  564.3 27.6 %collective-permute-start.60 = (bf16[128,2560]{1,0:T(8,128)(2,1)S(1)}, bf16[128,2560]{1,0:T(8,128)(2,1)S(1)}, u32[]{:S(2)}, u32[]{:S(2)}) collective-permute-start(bf16[128,2560]{1,0:T(8,128)(2,1)S(1)} %get-tuple-element.214), channel_id=1, source_target_pairs={{0,4},{2,6},{4,0},{6,2},{1,5},{3,7},{5,1},{7,3},{8,12},{10,14},{12... | collective-permute-start | bytes 1966088 | tf_op jit(solution)/shard_map/ppermute | solution.py:80
  564.7 31.8 %collective-permute-start.61 = (bf16[128,2560]{1,0:T(8,128)(2,1)S(1)}, bf16[128,2560]{1,0:T(8,128)(2,1)S(1)}, u32[]{:S(2)}, u32[]{:S(2)}) collective-permute-start(bf16[128,2560]{1,0:T(8,128)(2,1)S(1)} %get-tuple-element.213), channel_id=1, source_target_pairs={{0,2},{2,4},{4,6},{6,0},{1,3},{3,5},{5,7},{7,1},{8,10},{10,12},{12... | collective-permute-start | bytes 1966088 | tf_op jit(solution)/shard_map/ppermute | solution.py:80
  618.1 48.2 %collective-permute-start.69 = (bf16[5,1280,128]{2,1,0:T(8,128)(2,1)}, bf16[5,1280,128]{2,1,0:T(8,128)(2,1)}, u32[]{:S(2)}, u32[]{:S(2)}) collective-permute-start(bf16[5,1280,128]{2,1,0:T(8,128)(2,1)} %get-tuple-element.160.refs_1_), channel_id=1, source_target_pairs={{0,1},{1,0},{2,3},{3,2},{4,5},{5,4},{6,7},{7,6},{8,9},{9,8},{10,11... | collective-permute-start | bytes 4915208 | tf_op jit(solution)/shard_map/ppermute | solution.py:76
  618.9 47.4 %collective-permute-start.70 = (bf16[5,128,1280]{2,1,0:T(8,128)(2,1)}, bf16[5,128,1280]{2,1,0:T(8,128)(2,1)}, u32[]{:S(2)}, u32[]{:S(2)}) collective-permute-start(bf16[5,128,1280]{2,1,0:T(8,128)(2,1)} %get-tuple-element.161.refs_3_), channel_id=1, source_target_pairs={{0,1},{1,0},{2,3},{3,2},{4,5},{5,4},{6,7},{7,6},{8,9},{9,8},{10,11... | collective-permute-start | bytes 4915208 | tf_op jit(solution)/shard_map/ppermute | solution.py:76
  (140 other events, 1271.8 us)
Sparse Core Ops, SparseCore 0:
  52.2 128.8 all-gather.8
  183.2 105.3 all-gather.10
  454.3 63.3 all-gather.14
  519.3 46.5 all-gather.12

commit v5 on v4

--- a/solution.py
+++ b/solution.py
@@ -421,8 +421,8 @@
     n2_refs, gd_refs = refs[:8], refs[8:16]
     hid, ga, gb, pick, lgn, pickn, lgw = [refs[16 + 3 * i : 19 + 3 * i] for i in range(7)]
     far_ref, ln_ref = refs[37:39]
-    down_ref, mida_ref, midb_ref, midn_ref, midl_ref, mide_ref, exa_ref, exb_ref, exn_ref = refs[39:48]
-    acc_ref, hold_ref, wide_ref, n2_hold, gd_hold, n2_sems, gd_sems = refs[48:]
+    mine_ref, theirs_ref, mida_ref, midb_ref, midn_ref, midl_ref, mide_ref, exa_ref, exb_ref, exn_ref = refs[39:49]
+    acc_ref, hold_ref, wide_ref, n2_hold, gd_hold, n2_sems, gd_sems = refs[49:]
     j = pl.program_id(0)
     rank = mida_ref.shape[0]
     piece = n2_refs[0].shape[0]
@@ -450,7 +450,11 @@
 
     @pl.when(j == pl.num_programs(0) - 1)
     def _():
-        down_ref[...] = acc_ref[...].astype(bf16)
+        for k in range(4):
+            to = pl.ds(pl.multiple_of(lax.rem(s_ref[1] - k + 4, 4) * piece, piece), piece)
+            own, other = (0, 1) if k == 0 else (k + 1, k + 4)
+            mine_ref[to, :] = acc_ref[own * piece : (own + 1) * piece, :].astype(bf16)
+            theirs_ref[to, :] = acc_ref[other * piece : (other + 1) * piece, :].astype(bf16)
         for copy in n2_copies + gd_copies:
             copy.wait()
         wide_ref[...] = dot_tn(ring_of(pickn), gd_hold[...])
@@ -579,13 +583,18 @@
     theirs_ref[...] = part_ref[pl.ds(pl.multiple_of(own - at, own), own), :].astype(bf16)
 
 
-def mids_kernel(count, s_ref, *refs):
+def mids_kernel(count, rank, s_ref, *refs):
     out_ref, hold_ref = refs[2 * count :]
-    rank = out_ref.shape[0] // count
     here = pl.ds(pl.multiple_of(s_ref[0] * rank, rank), rank)
+    lanes = out_ref.shape[1]
+    parts = hold_ref.shape[1] // lanes
     for i in range(count):
         hold_ref[...] = dot_tn(refs[2 * i][...], refs[2 * i + 1][...])
-        out_ref[i * rank : (i + 1) * rank, :] = hold_ref[here, :].astype(bf16)
+        for j in range(parts):
+            at = (i * parts + j) * rank
+            out_ref[at : at + rank, :] = hold_ref[here, j * lanes : (j + 1) * lanes].astype(bf16)
+    filled = count * parts * rank
+    out_ref[filled:, :] = jnp.zeros((out_ref.shape[0] - filled, lanes), bf16)
 
 
 def extras_kernel(count, s_ref, *refs):
@@ -600,13 +609,15 @@
 def square_kernel(s_ref, one_ref, own_e_ref, other_e_ref, own_l_ref, other_l_ref, own_me_ref, other_me_ref, own_ml_ref, other_ml_ref, enter_ref, leave_ref):
     size = own_e_ref.shape[1]
     one = one_ref[...]
+    rank = one.shape[0]
+    whole = lambda ref: jnp.concatenate([ref[j * rank : (j + 1) * rank, :] for j in range(ref.shape[0] // rank)], axis=1)
     for core, e_ref, l_ref, me_ref, ml_ref in (
         (s_ref[0], own_e_ref, own_l_ref, own_me_ref, own_ml_ref),
         (1 - s_ref[0], other_e_ref, other_l_ref, other_me_ref, other_ml_ref),
     ):
         at = pl.ds(pl.multiple_of(core * size, size), size)
-        enter_ref[0, at, :] = e_ref[0].astype(f32) + dot_tn(me_ref[...], one)
-        leave_ref[0, :, at] = l_ref[0].astype(f32) + dot_tn(one, ml_ref[...])
+        enter_ref[0, at, :] = e_ref[0].astype(f32) + dot_tn(whole(me_ref), one)
+        leave_ref[0, :, at] = l_ref[0].astype(f32) + dot_tn(one, whole(ml_ref))
 
 
 def unit_parts(one_ref, extra_ref, mid_ref, size):
@@ -932,12 +943,16 @@
         core_at, (convolved, lat_gates, swap(lat_gates), select, near, leave_half[2], leave_half[3], mask, rate), 4, tuple(gd_rows[0][1:]),
     )
     entering = chips_carry(jnp.stack([prod[main - 1], state[main - 1]]), False)[None, :]
+    normed_half = half(normed, c, 1)
+    share = -(-width // 7 // 128) * 128
+    share_of = lambda v: lax.dynamic_slice_in_dim(jnp.pad(v, ((0, 0), (0, 8 * share - width))), member * share, share, axis=1)
+    down_share = share_of(down_extra)
     branch, slope, pick_gelu = call(
         gelu_kernel, (2,),
         [fixed((long, width)), side_col_spec(0), fixed((width, cols)), fixed(small_block), rows_spec(cols)],
         [(rows_spec(rows), (wide_block, f32))] * 2 + [B(*small_block)],
         [],
-        core_at, (normed_long, near, enter_square[0], select, leave_half[0]), 12,
+        core_at, (normed_long, near, enter_square[0], select, leave_half[0]), 12, (normed_half, down_share),
     )
     states, mixed, lat_out, out_mine, out_send, out_extra = call(
         out_kernel, (2,),
@@ -990,21 +1005,21 @@
     sums = [sums0] + [sums1[k * toks : (k + 1) * toks] for k in range(3)]
     mid_spec = (pl.BlockSpec((rank, hcol), lambda j, s: (0, j)), ((rank, slotp), bf16))
     extra_spec = (pl.BlockSpec((cols, hcol), lambda j, s: (0, j)), ((cols, slotp), bf16))
-    down, mid_a, mid_b, mid_n, mid_l, mid_e, ex_a, ex_b, ex_n = call(
+    down_mine, down_theirs, mid_a, mid_b, mid_n, mid_l, mid_e, ex_a, ex_b, ex_n = call(
         down_kernel, (4,),
         [anywhere] * 16 + [hidden_spec(4 * toks), hidden_spec(3 * toks), hidden_spec(3 * toks)] * 3
         + [fixed((4 * toks, cols)), fixed((3 * toks, cols)), fixed((3 * toks, cols))] * 4
         + [pl.BlockSpec((4, far_rows, wide2), lambda j, s: (j, 0, 0)), fixed((cols, width))],
-        [B(ring, width)] + [mid_spec] * 3 + [B(rank, width)] * 2 + [extra_spec] * 3,
+        [B(ring // 2, width)] * 2 + [mid_spec] * 3 + [B(rank, width)] * 2 + [extra_spec] * 3,
         [pltpu.VMEM((ring, width), f32), pltpu.VMEM((cols, hcol), f32), pltpu.VMEM((cols, width), f32),
          pltpu.VMEM((ring, width), bf16), pltpu.VMEM((ring, width), bf16), pltpu.SemaphoreType.DMA((8,)), pltpu.SemaphoreType.DMA((8,))],
-        middle_at,
+        jnp.concatenate([middle_at, y.astype(jnp.int32).reshape(1)]),
         (n2_rows[0][0], n2_rows[1][0], *n2_rows[0][1:], *n2_rows[1][1:], gd_rows[0][0], gd_rows[1][0], *gd_rows[0][1:], *gd_rows[1][1:],
          *[v[i] for i in (2, 0, 1, 5, 6, 4, 3) for v in (parts0, parts1, parts2)], far, leave_narrow),
         60, (*sums[1:], extra_total),
     )
-    grad_n2 = tied(line_back(sums), down)
-    grad_n2_extra = tied(extra_all[:, :width].astype(f32), down)
+    grad_n2 = tied(line_back(sums), mid_l)
+    grad_n2_extra = tied(extra_all[:, :width].astype(f32), mid_l)
     lat_extra = extra_all[:, width:]
     lgw_extra = lat_extra[:, :cols]
     pick_n_extra = lat_extra[:, cols:]
@@ -1025,17 +1040,15 @@
         core_at, (grad_out, near, leave_square[4], enter_half[4], select, states, branch, slope, decays), 18,
     )
     coming = chips_carry(jnp.stack([decays[0] * trail[0], decays[0] * back[0]]), True)[None, :]
-    down_mine = jnp.concatenate([down[:toks], down[2 * toks : 5 * toks]], axis=0)
-    down_theirs = jnp.concatenate([down[toks : 2 * toks], down[5 * toks :]], axis=0)
-    down_total = tied(add(down_mine, swap(down_theirs)), coming)
-    down_sums = [down_total[k * toks : (k + 1) * toks] for k in range(4)]
-    block_output = residual + line_back(down_sums)
+    down_total = tied(add(down_mine, swap(down_theirs)), coming).astype(bf16)
+    down_total = lax.all_to_all(down_total, YAX, 0, 0, tiled=True).reshape(4, toks, width)
+    block_output = residual + jnp.sum(down_total.astype(f32), axis=0)
     gelu_part, lat_gelu = call(
         geluback_kernel, (4,),
         [fixed(wide_block), col_spec(0), fixed((cols, halfw)), enter_spec, fixed(small_block)],
         [(rows_spec(main), ((main, width), f32)), F(*small_block)],
         [pltpu.VMEM(small_block, bf16)],
-        core_at, (grad_gelu, near, leave_half[0], enter_square[0], select), 1,
+        core_at, (grad_gelu, near, leave_half[0], enter_square[0], select), 12,
     )
 
     grad_in, grad_de, base, lat_gates = call(
@@ -1048,14 +1061,12 @@
         8,
     )
 
-    share = -(-width // 7 // 128) * 128
-    share_of = lambda v: lax.dynamic_slice_in_dim(jnp.pad(v, ((0, 0), (0, 8 * share - width))), member * share, share, axis=1)
     lanes_all = 3 * slotp + 2 * share
     (packed,) = call(
         pack_kernel, (1,),
         [fixed((cols, slotp))] * 3 + [fixed((main, cols))] * 2 + [fixed((main, share))] * 2,
         [B(cols, lanes_all)], [], core_at,
-        (ex_a, ex_b, ex_n, pick_n_extra, lgw_extra, share_of(down_extra), share_of(n2_extra)), 3, (base,),
+        (ex_a, ex_b, ex_n, pick_n_extra, lgw_extra, down_share, share_of(n2_extra)), 3, (base,),
     )
     ffn_all = lax.all_gather(packed, RING, axis=0)
 
@@ -1073,28 +1084,27 @@
         core_at,
         (base, lat_gates, swap(lat_gates), halo_base, halo_lat, halo_other, select_after, mask_long, taps, enter_half[2], enter_half[3],
          leave_half[1], near, enter_square[1], gelu_part),
-        1,
+        12,
     )
 
     lg_gelu = ((lat_gelu + swap(lat_gelu)) * select).astype(bf16)
     lg_fill = ((lat_fill + swap(lat_fill)) * select).astype(bf16)
-    normed_half = half(normed, c, 1)
     pairs = [
         (lg_gelu, normed_half), (lg_fill, normed_half), (lg_in, convolved), (lg_de, convolved), (lg_out, mixed),
         (pick_gelu, grad_gelu), (pick_fill, grad_fill), (pick_in, grad_in), (pick_de, grad_de), (pick_out, half(grad_out, c, 1)),
     ]
     part_spec = lambda n, i: pl.BlockSpec((main, n), lambda *_: (i, 0), pipeline_mode=pl.Buffered(1))
     operands = [v for pair in pairs for v in pair]
+    mid_rows = -(-10 * rank * halfw // cols // 64 // 16) * 16
     (mid,) = call(
-        functools.partial(mids_kernel, 10), (1,),
+        functools.partial(mids_kernel, 10, rank), (1,),
         [part_spec(cols, 0), part_spec(halfw, 0)] * 10,
-        [B(10 * rank, halfw)],
+        [B(64 * mid_rows, cols)],
         [pltpu.VMEM((cols, halfw), f32)],
-        middle_at, operands, 6, (block_output,),
+        middle_at, operands, 6,
     )
     mid_own = mid
-    shape = mid.shape
-    mid = lax.all_to_all(mid.reshape(64, -1, cols), CHIPS, 0, 0, tiled=True)
+    mid = lax.all_to_all(mid, CHIPS, 0, 0, tiled=True).reshape(64, mid_rows, cols)
     mid = to_low(jnp.sum(mid.astype(f32), axis=0))
 
     operands = [*[v for pair in pairs[:5] for v in pair[::-1]], *[v for pair in pairs[5:] for v in pair]]
@@ -1112,7 +1122,7 @@
         [], core_at, (one_hot, spread_one, ffn_all, ffn_mid), 12, (mid_own,),
     )
     mid = tied(mid, grad_leave_widen).astype(bf16)
-    mid = lax.all_to_all(jnp.broadcast_to(mid[None], (64, *mid.shape)), CHIPS, 0, 0, tiled=True).reshape(shape)
+    mid = lax.all_to_all(jnp.broadcast_to(mid[None], (64, *mid.shape)).reshape(-1, cols), CHIPS, 0, 0, tiled=True)
     (grad_enter_narrow,) = call(
         enter_kernel, (4,),
         [fixed((rank, cols)), fixed((units, 8 * chunk)), pl.BlockSpec((8, cols, hcol), lambda i, s: (0, 0, 8 + i)), pl.BlockSpec((1, 8, rank, hcol), lambda i, s: (4 + i // 2, 0, 0, i % 2))],
@@ -1130,8 +1140,8 @@
         [], core_at, (one_hot, eye, ffn_all, ffn_all, ffn_mid), 4, (mid_own,),
     )
     per_k = lambda *shape: pl.BlockSpec((1,) + shape, lambda k, s: (k,) + (0,) * len(shape))
-    mid_e_spec = pl.BlockSpec((rank, halfw), lambda k, s: (k, 0))
-    mid_l_spec = pl.BlockSpec((rank, halfw), lambda k, s: (5 + k, 0))
+    mid_e_spec = pl.BlockSpec((rank * halfw // cols, cols), lambda k, s: (k, 0))
+    mid_l_spec = pl.BlockSpec((rank * halfw // cols, cols), lambda k, s: (5 + k, 0))
     mid = tied(tied(mid, grad_enter_narrow), grad_leave_narrow).astype(bf16)
     mid_other = swap(mid)
     grad_enter_square, grad_leave_square = call(

time: 695 us -> 678 us (0.976)
  waiting for transfers between devices: 136 us -> 122 us
  local copies, waits for them, and re-layouts: 79.3 us -> 70.2 us
    ppermute x33 -> x30, waiting for transfers between devices: 54 us -> 24.4 us  [shift4(): return lax.ppermute(v, axis, [(i, (i + by) % 4) for i in range(4)])]
    all_to_all x2 -> x3, waiting for transfers between devices: 5.13 us -> 22.3 us  [the longest x1 10.7 us: per_device(): lax.all_to_all(down_total, YAX, 0, 0, tiled=True).reshape(4, toks, width)]
    all_to_all x2 -> x3, starting transfers between devices: 11.6 us -> 21.2 us  [the longest x1 10.7 us: per_device(): lax.all_to_all(mid, CHIPS, 0, 0, tiled=True).reshape(64, mid_rows, cols)]
    ppermute x33 -> x30, starting transfers between devices: 42.1 us -> 35.6 us  [shift4(): return lax.ppermute(v, axis, [(i, (i + by) % 4) for i in range(4)])]
    unnamed x188 -> x176, local copies, waits for them, and re-layouts: 17.2 us -> 17.3 us
  transfers between devices with their start and end apart: 83 -> 81, of which waited for: 25 -> 23; matrix products, arithmetic and copies ran while one was open for 21% -> 21% of each run, Pallas kernels for 33% -> 34%
where the time goes in v5:
time: 678 us; the launch traced here: 665 us
  Pallas kernels  234 us (35%)
  starting transfers between devices  128 us (19%)
  waiting for transfers between devices  122 us (18%)
  other arithmetic  78.6 us (12%)
  local copies, waits for them, and re-layouts  70.2 us (10%)
  between operations  22.2 us (3%)
  matrix products  8.89 us (1%)
    pallas_call x20, Pallas kernels, call(): pl.pallas_call(body, grid_spec=pltpu.PrefetchScalarGridSpec(num_scalar_pr...  234 us
    all_gather x1, waiting for transfers between devices, per_device(): lax.all_gather(quads[None], AXES, axis=0, tiled=True)  53.2 us
    ppermute x30, starting transfers between devices, shift4(): return lax.ppermute(v, axis, [(i, (i + by) % 4) for i in range(4)])  35.6 us
    ppermute x30, waiting for transfers between devices, shift4(): return lax.ppermute(v, axis, [(i, (i + by) % 4) for i in range(4)])  24.4 us
    ppermute x27, starting transfers between devices, swap(): return lax.ppermute(v, 'c', [(0, 1), (1, 0)])  22.3 us
    all_to_all x1, starting transfers between devices, per_device(): quads = lax.all_to_all(quads, QUAD, 0, 0, tiled=True).reshape(per4, lanes)  17.4 us
    unnamed x176, local copies, waits for them, and re-layouts  17.3 us
  transfers between devices with their start and end apart: 81, of which 23 were waited for; matrix products, arithmetic and copies ran while one was open for 21% of the time, Pallas kernels for 34%

profile of v5, /device:TPU:1, one launch (start us, length us, event | category | flops | bytes accessed | tf_op | source)
XLA Modules:
  0.0 664.8 jit_solution(7582984341899517627)
XLA Ops:
  19.8 17.4 %all-to-all-start = ((bf16[4,20,2048]{2,1,0:T(8,128)(2,1)}), bf16[4,20,2048]{2,1,0:T(8,128)(2,1)S(1)}, u32[]{:S(2)}, u32[]{:S(2)}) async-start(bf16[4,20,2048]{2,1,0:T(8,128)(2,1)} %pad_maximum_fusion.4), calls=%async_computation | async-start | bytes 786432 | tf_op jit(solution)/shard_map/all_to_all | solution.py:815
  43.8 6.6 collective-permute-done.8
  52.4 5.1 convolution_convert_fusion
  65.0 12.5 %all-to-all-done.1 = bf16[8,20,2048]{2,1,0:T(8,128)(2,1)S(1)} async-done(((bf16[8,20,2048]{2,1,0:T(8,128)(2,1)}), bf16[8,20,2048]{2,1,0:T(8,128)(2,1)S(1)}, u32[]{:S(2)}, u32[]{:S(2)}) %all-to-all-start.1) | async-done | bytes 655392 | tf_op jit(solution)/shard_map/all_to_all | solution.py:837
  79.7 6.3 copy.66
  86.0 6.3 copy.67
  127.8 53.2 %all-gather.9.cloned.1.call-done = bf16[11264,2048]{1,0:T(8,128)(2,1)} async-done(((bf16[88,2048]{1,0:T(8,128)(2,1)}), bf16[11264,2048]{1,0:T(8,128)(2,1)}) %all-gather.9.cloned.1.call-update) | async-done | bytes 46137360 | tf_op jit(solution)/shard_map/all_gather | solution.py:821
  190.0 5.1 shard_map.260
  201.3 12.5 %shard_map.261 = (bf16[512,1280]{1,0:T(8,128)(2,1)}, f32[512,256]{1,0:T(8,128)}, bf16[528,128]{1,0:T(8,128)(2,1)}) custom-call(s32[1]{0:T(128)} %bitcast.5.s_ref, bf16[528,2560]{1,0:T(8,128)(2,1)} %pad_maximum_fusion.1.refs_0_, bf16[32,4,88,2048]{3,2,1,0:T(8,128)(2,1)} %bitcast.109, bf16[2560,128]{1,0:T(8,128)(2,1)} %get-tuple-element.206.refs_2_.refs_13_, ...), custom_call_target="tpu_custom_call" | custom-call | flops 1000000000 | bytes 2000000 | tf_op jit(solution)/shard_map/pallas_call | solution.py:128
  218.8 10.9 %shard_map.262 = (f32[512,1280]{1,0:T(8,128)}, f32[512,1280]{1,0:T(8,128)}, f32[512,1280]{1,0:T(8,128)}, f32[512,1280]{1,0:T(8,128)}, f32[512,1280]{1,0:T(8,128)...) custom-call(s32[1]{0:T(128)} %bitcast.5.s_ref, ...), custom_call_target="tpu_custom_call" | custom-call | flops 4000000000 | bytes 8000000 | tf_op jit(solution)/shard_map/pallas_call | solution.py:128
  250.4 11.3 %shard_map.263 = (f32[512,1280]{1,0:T(8,128)}, f32[512,1280]{1,0:T(8,128)}, bf16[512,128]{1,0:T(8,128)(2,1)}) custom-call(s32[1]{0:T(128)} %bitcast.5.s_ref, bf16[528,2560]{1,0:T(8,128)(2,1)} %pad_maximum_fusion.1.refs_0_, bf16[32,4,88,2048]{3,2,1,0:T(8,128)(2,1)} %bitcast.111, bf16[2560,128]{1,0:T(8,128)(2,1)} %get-tuple-element.205.refs_2_.refs_3_, ...), custom_call_target="tpu_custom_call" | custom-call | flops 12000000000 | bytes 24000000 | tf_op jit(solution)/shard_map/pallas_call | solution.py:128
  262.4 14.2 %shard_map.264 = (f32[512,1280]{1,0:T(8,128)}, bf16[512,1280]{1,0:T(8,128)(2,1)}, f32[512,128]{1,0:T(8,128)}, f32[128,2560]{1,0:T(8,128)}, bf16[384,2560]{1,0:T(8,128)(2,1)}, /*index=5*/bf16[256,2560]{1,0:T(8,128)(2,1)}) custom-call(s32[1]{0:T(128)} %bitcast.5.s_ref, f32[512,1280]{1,0:T(8,128)} %get-tuple-element.101.refs_0_, ...), custom_call_target="tpu_custom_call" | custom-call | flops 15000000512 | bytes 30000000 | tf_op jit(solution)/shard_map/pallas_call | solution.py:128
  295.4 26.0 %shard_map.265 = (bf16[512,2560]{1,0:T(8,128)(2,1)}, bf16[512,1024]{1,0:T(8,128)(2,1)}, bf16[512,1024]{1,0:T(8,128)(2,1)}, bf16[512,1024]{1,0:T(8,128)(2,1)}, bf...) custom-call(s32[1]{0:T(128)} %bitcast.5.s_ref, ...), custom_call_target="tpu_custom_call" | custom-call | flops 60000002048 | bytes 120000000 | tf_op jit(solution)/shard_map/pallas_call | solution.py:128
  322.5 21.0 %shard_map.266 = (bf16[384,2560]{1,0:T(8,128)(2,1)}, bf16[384,1024]{1,0:T(8,128)(2,1)}, bf16[384,1024]{1,0:T(8,128)(2,1)}, bf16[384,1024]{1,0:T(8,128)(2,1)}, bf...) custom-call(s32[1]{0:T(128)} %bitcast.5.s_ref, ...), custom_call_target="tpu_custom_call" | custom-call | flops 40000000000 | bytes 80000000 | tf_op jit(solution)/shard_map/pallas_call | solution.py:128
  356.4 20.9 %shard_map.267 = (bf16[384,2560]{1,0:T(8,128)(2,1)}, bf16[384,1024]{1,0:T(8,128)(2,1)}, bf16[384,1024]{1,0:T(8,128)(2,1)}, bf16[384,1024]{1,0:T(8,128)(2,1)}, bf...) custom-call(s32[1]{0:T(128)} %bitcast.5.s_ref, ...), custom_call_target="tpu_custom_call" | custom-call | flops 60000002048 | bytes 120000000 | tf_op jit(solution)/shard_map/pallas_call | solution.py:128
  384.4 4.8 all-to-all-start.3
  397.1 19.5 %shard_map.268 = (bf16[512,2560]{1,0:T(8,128)(2,1)}, bf16[512,2560]{1,0:T(8,128)(2,1)}, bf16[16,1024]{1,0:T(8,128)(2,1)}, bf16[16,1024]{1,0:T(8,128)(2,1)}, bf16...) custom-call(s32[2]{0:T(128)} %pad_add_fusion.6.s_ref, ...), custom_call_target="tpu_custom_call" | custom-call | flops 60000002048 | bytes 120000000 | tf_op jit(solution)/shard_map/pallas_call | solution.py:128
  422.8 13.9 %collective-permute-done.48 = bf16[128,2560]{1,0:T(8,128)(2,1)} collective-permute-done((bf16[128,2560]{1,0:T(8,128)(2,1)}, bf16[128,2560]{1,0:T(8,128)(2,1)}, u32[]{:S(2)}, u32[]{:S(2)}) %collective-permute-start.48) | collective-permute-done | bytes 655392 | tf_op jit(solution)/shard_map/ppermute | solution.py:80
  460.4 15.2 %shard_map.269 = (bf16[512,1280]{1,0:T(8,128)(2,1)}, bf16[512,128]{1,0:T(8,128)(2,1)}, f32[512,1280]{1,0:T(8,128)}, f32[512,1280]{1,0:T(8,128)}) custom-call(s32[1]{0:T(128)} %bitcast.5.s_ref, bf16[512,2560]{1,0:T(8,128)(2,1)} %pad_maximum_fusion.refs_0_, bf16[32,4,88,2048]{3,2,1,0:T(8,128)(2,1)} %bitcast.113, ...), custom_call_target="tpu_custom_call" | custom-call | flops 17999998976 | bytes 36000000 | tf_op jit(solution)/shard_map/pallas_call | solution.py:128
  494.3 12.5 %shard_map.270 = (bf16[512,1280]{1,0:T(8,128)(2,1)}, bf16[512,1280]{1,0:T(8,128)(2,1)}, f32[512,1280]{1,0:T(8,128)}, f32[512,256]{1,0:T(8,128)}) custom-call(s32[1]{0:T(128)} %bitcast.5.s_ref, f32[512,1280]{1,0:T(8,128)} %get-tuple-element.140.refs_0_, f32[512,1280]{1,0:T(8,128)} %get-tuple-element.139.refs_1_, f32[1,1280]{1,0:T(1,128)} %fusion.67.refs_2_, ...), custom_call_target="tpu_custom_call" | custom-call | flops 8000000000 | bytes 16000000 | tf_op jit(solution)/shard_map/pallas_call | solution.py:128
  522.6 8.0 %shard_map.271 = (f32[256,2560]{1,0:T(8,128)}, f32[512,128]{1,0:T(8,128)}) custom-call(s32[1]{0:T(128)} %bitcast.5.s_ref, bf16[512,1280]{1,0:T(8,128)(2,1)} %get-tuple-element.145.refs_0_.refs_11_, bf16[32,4,88,2048]{3,2,1,0:T(8,128)(2,1)} %bitcast.115, bf16[128,1280]{1,0:T(8,128)(2,1)} %get-tuple-element.201.refs_4_.refs_2_, ...), custom_call_target="tpu_custom_call" | custom-call | flops 12000000000 | bytes 24000000 | tf_op jit(solution)/shard_map/pallas_call | solution.py:128
  533.0 12.2 %shard_map.272 = (bf16[512,1280]{1,0:T(8,128)(2,1)}, bf16[512,128]{1,0:T(8,128)(2,1)}, bf16[512,128]{1,0:T(8,128)(2,1)}, f32[512,128]{1,0:T(8,128)}, f32[128,2560]{1,0:T(8,128)}, /*index=5*/bf16[128,2560]{1,0:T(8,128)(2,1)}) custom-call(s32[1]{0:T(128)} %bitcast.5.s_ref, f32[512,1280]{1,0:T(8,128)} %get-tuple-element.143.refs_0_.refs_7_, ...), custom_call_target="tpu_custom_call" | custom-call | flops 12000000000 | bytes 24000000 | tf_op jit(solution)/shard_map/pallas_call | solution.py:128
  549.7 5.7 shard_map.273.refs_20_.refs_4_.refs_5_
  555.5 10.7 %all-to-all-start.5 = ((bf16[64,32,128]{2,1,0:T(8,128)(2,1)}), bf16[64,32,128]{2,1,0:T(8,128)(2,1)S(1)}, u32[]{:S(2)}, u32[]{:S(2)}) async-start(bf16[64,32,128]{2,1,0:T(8,128)(2,1)} %bitcast.134), calls=%async_computation.5 | async-start | bytes 1048576 | tf_op jit(solution)/shard_map/all_to_all | solution.py:1107
  566.2 6.4 shard_map.274
  578.8 10.8 %shard_map.276 = f32[128,15360]{1,0:T(8,128)} custom-call(s32[1]{0:T(128)} %bitcast.5.s_ref, bf16[16,128]{1,0:T(8,128)(2,1)} %fusion.57.refs_0_, bf16[480,512]{1,0:T(8,128)(2,1)} %fusion.34.refs_1_, bf16[8,128,3840]{2,1,0:T(8,128)(2,1)} %bitcast.117, bf16[16,8,16,512]{3,2,1,0:T(8,128)(2,1)} %bitcast.131, bf16[2048,128]{1,0:T(8,128)(2,1)} %shard_map.273.refs_20_.refs_4_.refs_5_), custom_call_target="tpu_custom_call" | custom-call | flops 12000000000 | bytes 24000000 | tf_op jit(solution)/shard_map/pallas_call | solution.py:128
  592.4 5.8 all-to-all-start.7
  598.2 4.8 add_convert_fusion
  603.0 7.4 %all-to-all-done.7 = bf16[64,32,128]{2,1,0:T(8,128)(2,1)S(1)} async-done(((bf16[64,32,128]{2,1,0:T(8,128)(2,1)}), bf16[64,32,128]{2,1,0:T(8,128)(2,1)S(1)}, u32[]{:S(2)}, u32[]{:S(2)}) %all-to-all-start.7) | async-done | bytes 524320 | tf_op jit(solution)/shard_map/all_to_all | solution.py:1125
  615.1 5.9 shard_map.277
  634.5 10.7 %all-to-all-done.4 = bf16[4,128,2560]{2,1,0:T(8,128)(2,1)} async-done(((bf16[4,128,2560]{2,1,0:T(8,128)(2,1)}), bf16[4,128,2560]{2,1,0:T(8,128)(2,1)}, u32[]{:S(2)}, u32[]{:S(2)}) %all-to-all-start.4) | async-done | bytes 2621472 | tf_op jit(solution)/shard_map/all_to_all | solution.py:1044
  648.7 9.4 %shard_map.279 = (f32[5,2560,128]{2,1,0:T(8,128)}, f32[5,128,2560]{2,1,0:T(8,128)}) custom-call(s32[1]{0:T(128)} %bitcast.5.s_ref, bf16[16,128]{1,0:T(8,128)(2,1)} %fusion.57.refs_0_, bf16[5,1280,128]{2,1,0:T(8,128)(2,1)} %get-tuple-element.163.refs_1_, bf16[5,1280,128]{2,1,0:T(8,128)(2,1)} %collective-permute-done.66.refs_2_, ...), custom_call_target="tpu_custom_call" | custom-call | flops 8999999488 | bytes 18000000 | tf_op jit(solution)/shard_map/pallas_call | solution.py:128
  (518 shorter events, 249.6 us)
Async XLA Ops:
  15.7 21.4 %collective-permute-start.3 = (bf16[16,2688]{1,0:T(8,128)(2,1)}, bf16[16,2688]{1,0:T(8,128)(2,1)S(1)}, u32[]{:S(2)}, u32[]{:S(2)}) collective-permute-start(bf16[16,2688]{1,0:T(8,128)(2,1)} %get-tuple-element.223), channel_id=1, source_target_pairs={{0,16},{64,80},{32,48},{96,112},{127,111},{63,47},{95,79},{31,15}} | collective-permute-start | bytes 258056 | tf_op jit(solution)/shard_map/ppermute | solution.py:726
  16.4 20.8 %collective-permute-start.4 = (bf16[16,2688]{1,0:T(8,128)(2,1)}, bf16[16,2688]{1,0:T(8,128)(2,1)}, u32[]{:S(2)}, u32[]{:S(2)}) collective-permute-start(bf16[16,2688]{1,0:T(8,128)(2,1)} %get-tuple-element.224), channel_id=1, source_target_pairs={{0,8},{64,72},{32,40},{96,104},{127,119},{63,55},{95,87},{31,23}} | collective-permute-start | bytes 258056 | tf_op jit(solution)/shard_map/ppermute | solution.py:726
  17.7 20.1 %collective-permute-start.5 = (bf16[16,2688]{1,0:T(8,128)(2,1)}, bf16[16,2688]{1,0:T(8,128)(2,1)}, u32[]{:S(2)}, u32[]{:S(2)}) collective-permute-start(bf16[16,2688]{1,0:T(8,128)(2,1)} %get-tuple-element.225), channel_id=1, source_target_pairs={{0,24},{64,88},{32,56},{96,120},{127,103},{63,39},{95,71},{31,7}} | collective-permute-start | bytes 258056 | tf_op jit(solution)/shard_map/ppermute | solution.py:726
  19.8 23.9 %all-to-all-start = ((bf16[4,20,2048]{2,1,0:T(8,128)(2,1)}), bf16[4,20,2048]{2,1,0:T(8,128)(2,1)S(1)}, u32[]{:S(2)}, u32[]{:S(2)}) async-start(bf16[4,20,2048]{2,1,0:T(8,128)(2,1)} %pad_maximum_fusion.4), calls=%async_computation | async-start | bytes 786432 | tf_op jit(solution)/shard_map/all_to_all | solution.py:815
  37.2 143.9 %all-gather.9.cloned.1.call-start = ((), (), s32[]{:S(2)}) async-start(), calls=%async_computation.8 | async-start | bytes 46497792 | tf_op jit(solution)/shard_map/all_gather | solution.py:821
  63.3 232.1 %all-gather.11.cloned.1.call-start = ((), (), s32[]{:S(2)}) async-start(), calls=%async_computation.9 | async-start | bytes 16711680 | tf_op jit(solution)/shard_map/all_gather | solution.py:841
  124.6 73.7 %collective-permute-start.10 = (bf16[16,2560]{1,0:T(8,128)(2,1)S(1)}, bf16[16,2560]{1,0:T(8,128)(2,1)S(1)}, u32[]{:S(2)}, u32[]{:S(2)}) collective-permute-start(bf16[16,2560]{1,0:T(8,128)(2,1)S(1)} %slice.587), channel_id=1, source_target_pairs={{0,2},{1,3},{2,4},{3,5},{4,6},{5,7},{6,8},{7,9},{8,10},{9,11},{10,... | collective-permute-start | bytes 245768 | tf_op jit(solution)/shard_map/ppermute | solution.py:91
  185.2 32.9 %collective-permute-start.19 = (bf16[128,2560]{1,0:T(8,128)(2,1)}, bf16[128,2560]{1,0:T(8,128)(2,1)}, u32[]{:S(2)}, u32[]{:S(2)}) collective-permute-start(bf16[128,2560]{1,0:T(8,128)(2,1)} %add_convert_fusion.4.refs_4_.refs_8_), channel_id=1, source_target_pairs={{0,2},{2,4},{4,6},{6,0},{1,3},{3,5},{5,7},{7,1},{8,10},{10,12},{12... | collective-permute-start | bytes 1966088 | tf_op jit(solution)/shard_map/ppermute | solution.py:80
  186.4 31.8 %collective-permute-start.20 = (bf16[128,2560]{1,0:T(8,128)(2,1)}, bf16[128,2560]{1,0:T(8,128)(2,1)}, u32[]{:S(2)}, u32[]{:S(2)}) collective-permute-start(bf16[128,2560]{1,0:T(8,128)(2,1)} %add_convert_fusion.4.refs_4_.refs_8_), channel_id=1, source_target_pairs={{0,4},{2,6},{4,0},{6,2},{1,5},{3,7},{5,1},{7,3},{8,12},{10,14},{12... | collective-permute-start | bytes 1966088 | tf_op jit(solution)/shard_map/ppermute | solution.py:80
  189.1 29.0 %collective-permute-start.21 = (bf16[128,2560]{1,0:T(8,128)(2,1)}, bf16[128,2560]{1,0:T(8,128)(2,1)}, u32[]{:S(2)}, u32[]{:S(2)}) collective-permute-start(bf16[128,2560]{1,0:T(8,128)(2,1)} %add_convert_fusion.4.refs_4_.refs_8_), channel_id=1, source_target_pairs={{0,6},{2,0},{4,2},{6,4},{1,7},{3,1},{5,3},{7,5},{8,14},{10,8},{12,... | collective-permute-start | bytes 1966088 | tf_op jit(solution)/shard_map/ppermute | solution.py:80
  283.7 63.0 %collective-permute-start.40 = (bf16[128,2560]{1,0:T(8,128)(2,1)}, bf16[128,2560]{1,0:T(8,128)(2,1)S(1)}, u32[]{:S(2)}, u32[]{:S(2)}) collective-permute-start(bf16[128,2560]{1,0:T(8,128)(2,1)} %collective-permute-done.19.refs_9_.refs_3_.refs_10_), channel_id=1, source_target_pairs={{0,1},{1,0},{2,3},{3,2},{4,5},{5,4},{6,7},{7,6},{8,9},{9,8},{10,11... | collective-permute-start | bytes 1966088 | tf_op jit(solution)/shard_map/ppermute | solution.py:76
  284.2 71.3 %collective-permute-start.41 = (bf16[128,2560]{1,0:T(8,128)(2,1)}, bf16[128,2560]{1,0:T(8,128)(2,1)}, u32[]{:S(2)}, u32[]{:S(2)}) collective-permute-start(bf16[128,2560]{1,0:T(8,128)(2,1)} %collective-permute-done.20.refs_10_.refs_4_.refs_11_), channel_id=1, source_target_pairs={{0,1},{1,0},{2,3},{3,2},{4,5},{5,4},{6,7},{7,6},{8,9},{9,8},{10,11... | collective-permute-start | bytes 1966088 | tf_op jit(solution)/shard_map/ppermute | solution.py:76
  286.8 34.7 %collective-permute-start.33 = (bf16[128,2560]{1,0:T(8,128)(2,1)S(1)}, bf16[128,2560]{1,0:T(8,128)(2,1)}, u32[]{:S(2)}, u32[]{:S(2)}) collective-permute-start(bf16[128,2560]{1,0:T(8,128)(2,1)S(1)} %multiply_convert_fusion.1.refs_0_), channel_id=1, source_target_pairs={{0,2},{2,4},{4,6},{6,0},{1,3},{3,5},{5,7},{7,1},{8,10},{10,12},{12... | collective-permute-start | bytes 1966088 | tf_op jit(solution)/shard_map/ppermute | solution.py:80
  291.5 31.0 %collective-permute-start.34 = (bf16[128,2560]{1,0:T(8,128)(2,1)S(1)}, bf16[128,2560]{1,0:T(8,128)(2,1)}, u32[]{:S(2)}, u32[]{:S(2)}) collective-permute-start(bf16[128,2560]{1,0:T(8,128)(2,1)S(1)} %multiply_convert_fusion.1.refs_0_), channel_id=1, source_target_pairs={{0,4},{2,6},{4,0},{6,2},{1,5},{3,7},{5,1},{7,3},{8,12},{10,14},{12... | collective-permute-start | bytes 1966088 | tf_op jit(solution)/shard_map/ppermute | solution.py:80
  294.2 28.3 %collective-permute-start.35 = (bf16[128,2560]{1,0:T(8,128)(2,1)S(1)}, bf16[128,2560]{1,0:T(8,128)(2,1)}, u32[]{:S(2)}, u32[]{:S(2)}) collective-permute-start(bf16[128,2560]{1,0:T(8,128)(2,1)S(1)} %multiply_convert_fusion.1.refs_0_), channel_id=1, source_target_pairs={{0,6},{2,0},{4,2},{6,4},{1,7},{3,1},{5,3},{7,5},{8,14},{10,8},{12,... | collective-permute-start | bytes 1966088 | tf_op jit(solution)/shard_map/ppermute | solution.py:80
  321.4 34.1 %collective-permute-start.42 = (bf16[128,2560]{1,0:T(8,128)(2,1)}, bf16[128,2560]{1,0:T(8,128)(2,1)S(1)}, u32[]{:S(2)}, u32[]{:S(2)}) collective-permute-start(bf16[128,2560]{1,0:T(8,128)(2,1)} %collective-permute-done.21.refs_11_.refs_5_.refs_12_), channel_id=1, source_target_pairs={{0,1},{1,0},{2,3},{3,2},{4,5},{5,4},{6,7},{7,6},{8,9},{9,8},{10,11... | collective-permute-start | bytes 1966088 | tf_op jit(solution)/shard_map/ppermute | solution.py:76
  351.5 31.5 %all-to-all-start.2 = ((bf16[8,32,2816]{2,1,0:T(8,128)(2,1)}), bf16[8,32,2816]{2,1,0:T(8,128)(2,1)S(1)}, u32[]{:S(2)}, u32[]{:S(2)}) async-start(bf16[8,32,2816]{2,1,0:T(8,128)(2,1)} %bitcast.39), calls=%async_computation.2 | async-start | bytes 2883584 | tf_op jit(solution)/shard_map/all_to_all | solution.py:1000
  380.6 41.8 %collective-permute-start.45 = (bf16[128,2560]{1,0:T(8,128)(2,1)}, bf16[128,2560]{1,0:T(8,128)(2,1)}, u32[]{:S(2)}, u32[]{:S(2)}) collective-permute-start(bf16[128,2560]{1,0:T(8,128)(2,1)} %slice.534), channel_id=1, source_target_pairs={{0,1},{1,0},{2,3},{3,2},{4,5},{5,4},{6,7},{7,6},{8,9},{9,8},{10,11... | collective-permute-start | bytes 1966088 | tf_op jit(solution)/shard_map/ppermute | solution.py:76
  384.4 35.4 %all-to-all-start.3 = ((bf16[8,32,2816]{2,1,0:T(8,128)(2,1)}), bf16[8,32,2816]{2,1,0:T(8,128)(2,1)S(1)}, u32[]{:S(2)}, u32[]{:S(2)}) async-start(bf16[8,32,2816]{2,1,0:T(8,128)(2,1)} %broadcast_in_dim.59), calls=%async_computation.3 | async-start | bytes 2883584 | tf_op jit(solution)/shard_map/all_to_all | solution.py:1002
  393.2 29.2 %collective-permute-start.46 = (bf16[128,2560]{1,0:T(8,128)(2,1)}, bf16[128,2560]{1,0:T(8,128)(2,1)S(1)}, u32[]{:S(2)}, u32[]{:S(2)}) collective-permute-start(bf16[128,2560]{1,0:T(8,128)(2,1)} %get-tuple-element.212.refs_39_), channel_id=1, source_target_pairs={{0,6},{2,0},{4,2},{6,4},{1,7},{3,1},{5,3},{7,5},{8,14},{10,8},{12,... | collective-permute-start | bytes 1966088 | tf_op jit(solution)/shard_map/ppermute | solution.py:80
  395.8 26.9 %collective-permute-start.47 = (bf16[128,2560]{1,0:T(8,128)(2,1)}, bf16[128,2560]{1,0:T(8,128)(2,1)}, u32[]{:S(2)}, u32[]{:S(2)}) collective-permute-start(bf16[128,2560]{1,0:T(8,128)(2,1)} %get-tuple-element.211.refs_40_), channel_id=1, source_target_pairs={{0,4},{2,6},{4,0},{6,2},{1,5},{3,7},{5,1},{7,3},{8,12},{10,14},{12... | collective-permute-start | bytes 1966088 | tf_op jit(solution)/shard_map/ppermute | solution.py:80
  396.4 40.2 %collective-permute-start.48 = (bf16[128,2560]{1,0:T(8,128)(2,1)}, bf16[128,2560]{1,0:T(8,128)(2,1)}, u32[]{:S(2)}, u32[]{:S(2)}) collective-permute-start(bf16[128,2560]{1,0:T(8,128)(2,1)} %get-tuple-element.210.refs_41_), channel_id=1, source_target_pairs={{0,2},{2,4},{4,6},{6,0},{1,3},{3,5},{5,7},{7,1},{8,10},{10,12},{12... | collective-permute-start | bytes 1966088 | tf_op jit(solution)/shard_map/ppermute | solution.py:80
  446.1 132.6 %all-gather.15.cloned.1.call-start = ((), (), s32[]{:S(2)}) async-start(), calls=%async_computation.11 | async-start | bytes 2113536 | tf_op jit(solution)/shard_map/all_gather | solution.py:1029
  455.8 123.0 %all-gather.13.cloned.1.call-start = ((), (), s32[]{:S(2)}) async-start(), calls=%async_computation.10 | async-start | bytes 8847360 | tf_op jit(solution)/shard_map/all_gather | solution.py:1071
  514.1 34.8 %collective-permute-start.65 = (f32[512,128]{1,0:T(8,128)S(1)}, f32[512,128]{1,0:T(8,128)S(1)}, u32[]{:S(2)}, u32[]{:S(2)}) collective-permute-start(f32[512,128]{1,0:T(8,128)S(1)} %copy-done.45), channel_id=1, source_target_pairs={{0,1},{1,0},{2,3},{3,2},{4,5},{5,4},{6,7},{7,6},{8,9},{9,8},{10,11... | collective-permute-start | bytes 786440 | tf_op jit(solution)/shard_map/ppermute | solution.py:76
  518.5 79.7 %collective-permute-start.44 = (bf16[512,2560]{1,0:T(8,128)(2,1)}, bf16[512,2560]{1,0:T(8,128)(2,1)}, u32[]{:S(2)}, u32[]{:S(2)}) collective-permute-start(bf16[512,2560]{1,0:T(8,128)(2,1)} %get-tuple-element.134), channel_id=1, source_target_pairs={{0,1},{1,0},{2,3},{3,2},{4,5},{5,4},{6,7},{7,6},{8,9},{9,8},{10,11... | collective-permute-start | bytes 7864328 | tf_op jit(solution)/shard_map/ppermute | solution.py:76
  548.7 24.3 %collective-permute-start.62 = (bf16[128,2560]{1,0:T(8,128)(2,1)}, bf16[128,2560]{1,0:T(8,128)(2,1)}, u32[]{:S(2)}, u32[]{:S(2)}) collective-permute-start(bf16[128,2560]{1,0:T(8,128)(2,1)} %get-tuple-element.148), channel_id=1, source_target_pairs={{0,1},{1,0},{2,3},{3,2},{4,5},{5,4},{6,7},{7,6},{8,9},{9,8},{10,11... | collective-permute-start | bytes 1966088 | tf_op jit(solution)/shard_map/ppermute | solution.py:76
  555.5 23.2 %all-to-all-start.5 = ((bf16[64,32,128]{2,1,0:T(8,128)(2,1)}), bf16[64,32,128]{2,1,0:T(8,128)(2,1)S(1)}, u32[]{:S(2)}, u32[]{:S(2)}) async-start(bf16[64,32,128]{2,1,0:T(8,128)(2,1)} %bitcast.134), calls=%async_computation.5 | async-start | bytes 1048576 | tf_op jit(solution)/shard_map/all_to_all | solution.py:1107
  572.5 76.1 %collective-permute-start.66 = (bf16[5,1280,128]{2,1,0:T(8,128)(2,1)}, bf16[5,1280,128]{2,1,0:T(8,128)(2,1)}, u32[]{:S(2)}, u32[]{:S(2)}) collective-permute-start(bf16[5,1280,128]{2,1,0:T(8,128)(2,1)} %get-tuple-element.163.refs_1_), channel_id=1, source_target_pairs={{0,1},{1,0},{2,3},{3,2},{4,5},{5,4},{6,7},{7,6},{8,9},{9,8},{10,11... | collective-permute-start | bytes 4915208 | tf_op jit(solution)/shard_map/ppermute | solution.py:76
  572.9 75.7 %collective-permute-start.67 = (bf16[5,128,1280]{2,1,0:T(8,128)(2,1)}, bf16[5,128,1280]{2,1,0:T(8,128)(2,1)}, u32[]{:S(2)}, u32[]{:S(2)}) collective-permute-start(bf16[5,128,1280]{2,1,0:T(8,128)(2,1)} %get-tuple-element.164.refs_3_), channel_id=1, source_target_pairs={{0,1},{1,0},{2,3},{3,2},{4,5},{5,4},{6,7},{7,6},{8,9},{9,8},{10,11... | collective-permute-start | bytes 4915208 | tf_op jit(solution)/shard_map/ppermute | solution.py:76
  610.4 34.7 %all-to-all-start.4 = ((bf16[4,128,2560]{2,1,0:T(8,128)(2,1)}), bf16[4,128,2560]{2,1,0:T(8,128)(2,1)}, u32[]{:S(2)}, u32[]{:S(2)}) async-start(bf16[4,128,2560]{2,1,0:T(8,128)(2,1)} %bitcast.125), calls=%async_computation.4 | async-start | bytes 5242880 | tf_op jit(solution)/shard_map/all_to_all | solution.py:1044
  629.8 18.9 %collective-permute-start.68 = (bf16[2048,128]{1,0:T(8,128)(2,1)}, bf16[2048,128]{1,0:T(8,128)(2,1)}, u32[]{:S(2)}, u32[]{:S(2)}) collective-permute-start(bf16[2048,128]{1,0:T(8,128)(2,1)} %bitcast.53.refs_5_.refs_7_), channel_id=1, source_target_pairs={{0,1},{1,0},{2,3},{3,2},{4,5},{5,4},{6,7},{7,6},{8,9},{9,8},{10,11... | collective-permute-start | bytes 1572872 | tf_op jit(solution)/shard_map/ppermute | solution.py:76
  (132 other events, 1099.0 us)
Sparse Core Ops, SparseCore 0:
  52.1 128.8 all-gather.8
  183.2 105.3 all-gather.10
  455.9 63.2 all-gather.14
  521.4 48.1 all-gather.12

commit v6 on v5

--- a/solution.py
+++ b/solution.py
@@ -1042,7 +1042,6 @@
     coming = chips_carry(jnp.stack([decays[0] * trail[0], decays[0] * back[0]]), True)[None, :]
     down_total = tied(add(down_mine, swap(down_theirs)), coming).astype(bf16)
     down_total = lax.all_to_all(down_total, YAX, 0, 0, tiled=True).reshape(4, toks, width)
-    block_output = residual + jnp.sum(down_total.astype(f32), axis=0)
     gelu_part, lat_gelu = call(
         geluback_kernel, (4,),
         [fixed(wide_block), col_spec(0), fixed((cols, halfw)), enter_spec, fixed(small_block)],
@@ -1142,15 +1141,15 @@
     per_k = lambda *shape: pl.BlockSpec((1,) + shape, lambda k, s: (k,) + (0,) * len(shape))
     mid_e_spec = pl.BlockSpec((rank * halfw // cols, cols), lambda k, s: (k, 0))
     mid_l_spec = pl.BlockSpec((rank * halfw // cols, cols), lambda k, s: (5 + k, 0))
-    mid = tied(tied(mid, grad_enter_narrow), grad_leave_narrow).astype(bf16)
     mid_other = swap(mid)
     grad_enter_square, grad_leave_square = call(
         square_kernel, (5,),
         [fixed((rank, cols)), per_k(halfw, cols), per_k(halfw, cols), per_k(cols, halfw), per_k(cols, halfw),
          mid_e_spec, mid_e_spec, mid_l_spec, mid_l_spec],
         [(per_k(width, cols), ((5, width, cols), f32)), (per_k(cols, width), ((5, cols, width), f32))],
-        [], core_at, (one_hot, enter_extra, swap(enter_extra), leave_extra, swap(leave_extra), mid, mid_other, mid, mid_other), 9,
-    )
+        [], core_at, (one_hot, enter_extra, swap(enter_extra), leave_extra, swap(leave_extra), mid, mid_other, mid, mid_other), 9, (grad_enter_narrow, grad_leave_narrow),
+    )
+    block_output = tied(residual + jnp.sum(down_total.astype(f32), axis=0), grad_leave_square)
     return (
         block_output,
         input_grad,

time: 678 us -> 676 us (level)
  transfers between devices with their start and end apart: 81 -> 81, of which waited for: 23 -> 26; matrix products, arithmetic and copies ran while one was open for 21% -> 20% of each run, Pallas kernels for 34% -> 34%
where the time goes in v6:
time: 676 us; the launch traced here: 665 us
  Pallas kernels  234 us (35%)
  starting transfers between devices  129 us (19%)
  waiting for transfers between devices  124 us (18%)
  other arithmetic  78.6 us (12%)
  local copies, waits for them, and re-layouts  68.9 us (10%)
  between operations  21.5 us (3%)
  matrix products  8.88 us (1%)
    pallas_call x20, Pallas kernels, call(): pl.pallas_call(body, grid_spec=pltpu.PrefetchScalarGridSpec(num_scalar_pr...  234 us
    all_gather x1, waiting for transfers between devices, per_device(): lax.all_gather(quads[None], AXES, axis=0, tiled=True)  53.3 us
    ppermute x30, starting transfers between devices, shift4(): return lax.ppermute(v, axis, [(i, (i + by) % 4) for i in range(4)])  32.4 us
    ppermute x30, waiting for transfers between devices, shift4(): return lax.ppermute(v, axis, [(i, (i + by) % 4) for i in range(4)])  27.2 us
    ppermute x27, starting transfers between devices, swap(): return lax.ppermute(v, 'c', [(0, 1), (1, 0)])  24 us
    all_to_all x1, starting transfers between devices, per_device(): quads = lax.all_to_all(quads, QUAD, 0, 0, tiled=True).reshape(per4, lanes)  17.4 us
    unnamed x176, local copies, waits for them, and re-layouts  17.2 us
    all_to_all x1, waiting for transfers between devices, per_device(): lax.all_to_all(down_total, YAX, 0, 0, tiled=True).reshape(4, toks, width)  14.2 us
  transfers between devices with their start and end apart: 81, of which 26 were waited for; matrix products, arithmetic and copies ran while one was open for 20% of the time, Pallas kernels for 34%

profile of v6, /device:TPU:1, one launch (start us, length us, event | category | flops | bytes accessed | tf_op | source)
XLA Modules:
  0.0 664.7 jit_solution(4786986853440537503)
XLA Ops:
  19.8 17.4 %all-to-all-start = ((bf16[4,20,2048]{2,1,0:T(8,128)(2,1)}), bf16[4,20,2048]{2,1,0:T(8,128)(2,1)S(1)}, u32[]{:S(2)}, u32[]{:S(2)}) async-start(bf16[4,20,2048]{2,1,0:T(8,128)(2,1)} %pad_maximum_fusion.4), calls=%async_computation | async-start | bytes 786432 | tf_op jit(solution)/shard_map/all_to_all | solution.py:815
  43.8 6.6 collective-permute-done.8
  52.4 5.1 convolution_convert_fusion
  65.0 12.5 %all-to-all-done.1 = bf16[8,20,2048]{2,1,0:T(8,128)(2,1)S(1)} async-done(((bf16[8,20,2048]{2,1,0:T(8,128)(2,1)}), bf16[8,20,2048]{2,1,0:T(8,128)(2,1)S(1)}, u32[]{:S(2)}, u32[]{:S(2)}) %all-to-all-start.1) | async-done | bytes 655392 | tf_op jit(solution)/shard_map/all_to_all | solution.py:837
  79.7 6.3 copy.66
  86.0 6.3 copy.67
  127.7 53.3 %all-gather.9.cloned.1.call-done = bf16[11264,2048]{1,0:T(8,128)(2,1)} async-done(((bf16[88,2048]{1,0:T(8,128)(2,1)}), bf16[11264,2048]{1,0:T(8,128)(2,1)}) %all-gather.9.cloned.1.call-update) | async-done | bytes 46137360 | tf_op jit(solution)/shard_map/all_gather | solution.py:821
  190.0 5.1 shard_map.260
  201.4 12.5 %shard_map.261 = (bf16[512,1280]{1,0:T(8,128)(2,1)}, f32[512,256]{1,0:T(8,128)}, bf16[528,128]{1,0:T(8,128)(2,1)}) custom-call(s32[1]{0:T(128)} %bitcast.5.s_ref, bf16[528,2560]{1,0:T(8,128)(2,1)} %pad_maximum_fusion.1.refs_0_, bf16[32,4,88,2048]{3,2,1,0:T(8,128)(2,1)} %bitcast.108, bf16[2560,128]{1,0:T(8,128)(2,1)} %get-tuple-element.206.refs_2_.refs_13_, ...), custom_call_target="tpu_custom_call" | custom-call | flops 1000000000 | bytes 2000000 | tf_op jit(solution)/shard_map/pallas_call | solution.py:128
  218.8 10.9 %shard_map.262 = (f32[512,1280]{1,0:T(8,128)}, f32[512,1280]{1,0:T(8,128)}, f32[512,1280]{1,0:T(8,128)}, f32[512,1280]{1,0:T(8,128)}, f32[512,1280]{1,0:T(8,128)...) custom-call(s32[1]{0:T(128)} %bitcast.5.s_ref, ...), custom_call_target="tpu_custom_call" | custom-call | flops 4000000000 | bytes 8000000 | tf_op jit(solution)/shard_map/pallas_call | solution.py:128
  250.4 11.3 %shard_map.263 = (f32[512,1280]{1,0:T(8,128)}, f32[512,1280]{1,0:T(8,128)}, bf16[512,128]{1,0:T(8,128)(2,1)}) custom-call(s32[1]{0:T(128)} %bitcast.5.s_ref, bf16[528,2560]{1,0:T(8,128)(2,1)} %pad_maximum_fusion.1.refs_0_, bf16[32,4,88,2048]{3,2,1,0:T(8,128)(2,1)} %bitcast.110, bf16[2560,128]{1,0:T(8,128)(2,1)} %get-tuple-element.205.refs_2_.refs_3_, ...), custom_call_target="tpu_custom_call" | custom-call | flops 12000000000 | bytes 24000000 | tf_op jit(solution)/shard_map/pallas_call | solution.py:128
  262.4 14.2 %shard_map.264 = (f32[512,1280]{1,0:T(8,128)}, bf16[512,1280]{1,0:T(8,128)(2,1)}, f32[512,128]{1,0:T(8,128)}, f32[128,2560]{1,0:T(8,128)}, bf16[384,2560]{1,0:T(8,128)(2,1)}, /*index=5*/bf16[256,2560]{1,0:T(8,128)(2,1)}) custom-call(s32[1]{0:T(128)} %bitcast.5.s_ref, f32[512,1280]{1,0:T(8,128)} %get-tuple-element.101.refs_0_, ...), custom_call_target="tpu_custom_call" | custom-call | flops 15000000512 | bytes 30000000 | tf_op jit(solution)/shard_map/pallas_call | solution.py:128
  295.3 26.0 %shard_map.265 = (bf16[512,2560]{1,0:T(8,128)(2,1)}, bf16[512,1024]{1,0:T(8,128)(2,1)}, bf16[512,1024]{1,0:T(8,128)(2,1)}, bf16[512,1024]{1,0:T(8,128)(2,1)}, bf...) custom-call(s32[1]{0:T(128)} %bitcast.5.s_ref, ...), custom_call_target="tpu_custom_call" | custom-call | flops 60000002048 | bytes 120000000 | tf_op jit(solution)/shard_map/pallas_call | solution.py:128
  323.2 21.0 %shard_map.266 = (bf16[384,2560]{1,0:T(8,128)(2,1)}, bf16[384,1024]{1,0:T(8,128)(2,1)}, bf16[384,1024]{1,0:T(8,128)(2,1)}, bf16[384,1024]{1,0:T(8,128)(2,1)}, bf...) custom-call(s32[1]{0:T(128)} %bitcast.5.s_ref, ...), custom_call_target="tpu_custom_call" | custom-call | flops 40000000000 | bytes 80000000 | tf_op jit(solution)/shard_map/pallas_call | solution.py:128
  356.3 20.9 %shard_map.267 = (bf16[384,2560]{1,0:T(8,128)(2,1)}, bf16[384,1024]{1,0:T(8,128)(2,1)}, bf16[384,1024]{1,0:T(8,128)(2,1)}, bf16[384,1024]{1,0:T(8,128)(2,1)}, bf...) custom-call(s32[1]{0:T(128)} %bitcast.5.s_ref, ...), custom_call_target="tpu_custom_call" | custom-call | flops 60000002048 | bytes 120000000 | tf_op jit(solution)/shard_map/pallas_call | solution.py:128
  384.3 4.8 all-to-all-start.3
  396.9 19.5 %shard_map.268 = (bf16[512,2560]{1,0:T(8,128)(2,1)}, bf16[512,2560]{1,0:T(8,128)(2,1)}, bf16[16,1024]{1,0:T(8,128)(2,1)}, bf16[16,1024]{1,0:T(8,128)(2,1)}, bf16...) custom-call(s32[2]{0:T(128)} %pad_add_fusion.6.s_ref, ...), custom_call_target="tpu_custom_call" | custom-call | flops 60000002048 | bytes 120000000 | tf_op jit(solution)/shard_map/pallas_call | solution.py:128
  422.6 13.9 %collective-permute-done.48 = bf16[128,2560]{1,0:T(8,128)(2,1)} collective-permute-done((bf16[128,2560]{1,0:T(8,128)(2,1)}, bf16[128,2560]{1,0:T(8,128)(2,1)}, u32[]{:S(2)}, u32[]{:S(2)}) %collective-permute-start.48) | collective-permute-done | bytes 655392 | tf_op jit(solution)/shard_map/ppermute | solution.py:80
  461.0 15.2 %shard_map.269 = (bf16[512,1280]{1,0:T(8,128)(2,1)}, bf16[512,128]{1,0:T(8,128)(2,1)}, f32[512,1280]{1,0:T(8,128)}, f32[512,1280]{1,0:T(8,128)}) custom-call(s32[1]{0:T(128)} %bitcast.5.s_ref, bf16[512,2560]{1,0:T(8,128)(2,1)} %pad_maximum_fusion.refs_0_, bf16[32,4,88,2048]{3,2,1,0:T(8,128)(2,1)} %bitcast.112, ...), custom_call_target="tpu_custom_call" | custom-call | flops 17999998976 | bytes 36000000 | tf_op jit(solution)/shard_map/pallas_call | solution.py:128
  493.1 12.4 %shard_map.271 = (bf16[512,1280]{1,0:T(8,128)(2,1)}, bf16[512,1280]{1,0:T(8,128)(2,1)}, f32[512,1280]{1,0:T(8,128)}, f32[512,256]{1,0:T(8,128)}) custom-call(s32[1]{0:T(128)} %bitcast.5.s_ref, f32[512,1280]{1,0:T(8,128)} %get-tuple-element.140.refs_0_, f32[512,1280]{1,0:T(8,128)} %get-tuple-element.139.refs_1_, f32[1,1280]{1,0:T(1,128)} %fusion.67.refs_2_, ...), custom_call_target="tpu_custom_call" | custom-call | flops 8000000000 | bytes 16000000 | tf_op jit(solution)/shard_map/pallas_call | solution.py:128
  512.7 5.8 collective-permute-start.64
  522.6 8.1 %shard_map.270 = (f32[256,2560]{1,0:T(8,128)}, f32[512,128]{1,0:T(8,128)}) custom-call(s32[1]{0:T(128)} %bitcast.5.s_ref, bf16[512,1280]{1,0:T(8,128)(2,1)} %get-tuple-element.141.refs_0_.refs_11_, bf16[32,4,88,2048]{3,2,1,0:T(8,128)(2,1)} %bitcast.114, bf16[128,1280]{1,0:T(8,128)(2,1)} %get-tuple-element.201.refs_4_.refs_2_, ...), custom_call_target="tpu_custom_call" | custom-call | flops 12000000000 | bytes 24000000 | tf_op jit(solution)/shard_map/pallas_call | solution.py:128
  533.3 12.1 %shard_map.272 = (bf16[512,1280]{1,0:T(8,128)(2,1)}, bf16[512,128]{1,0:T(8,128)(2,1)}, bf16[512,128]{1,0:T(8,128)(2,1)}, f32[512,128]{1,0:T(8,128)}, f32[128,2560]{1,0:T(8,128)}, /*index=5*/bf16[128,2560]{1,0:T(8,128)(2,1)}) custom-call(s32[1]{0:T(128)} %bitcast.5.s_ref, f32[512,1280]{1,0:T(8,128)} %get-tuple-element.145.refs_0_.refs_7_, ...), custom_call_target="tpu_custom_call" | custom-call | flops 12000000000 | bytes 24000000 | tf_op jit(solution)/shard_map/pallas_call | solution.py:128
  549.8 5.6 shard_map.273.refs_20_.refs_4_.refs_5_
  555.4 10.9 %all-to-all-start.5 = ((bf16[64,32,128]{2,1,0:T(8,128)(2,1)}), bf16[64,32,128]{2,1,0:T(8,128)(2,1)S(1)}, u32[]{:S(2)}, u32[]{:S(2)}) async-start(bf16[64,32,128]{2,1,0:T(8,128)(2,1)} %bitcast.133), calls=%async_computation.5 | async-start | bytes 1048576 | tf_op jit(solution)/shard_map/all_to_all | solution.py:1106
  566.4 6.3 shard_map.274
  579.0 4.7 all-to-all-start.4
  587.2 10.8 %shard_map.276 = f32[128,15360]{1,0:T(8,128)} custom-call(s32[1]{0:T(128)} %bitcast.5.s_ref, bf16[16,128]{1,0:T(8,128)(2,1)} %fusion.57.refs_0_, bf16[480,512]{1,0:T(8,128)(2,1)} %fusion.34.refs_1_, bf16[8,128,3840]{2,1,0:T(8,128)(2,1)} %bitcast.116, bf16[16,8,16,512]{3,2,1,0:T(8,128)(2,1)} %bitcast.130, bf16[2048,128]{1,0:T(8,128)(2,1)} %shard_map.273.refs_20_.refs_4_.refs_5_), custom_call_target="tpu_custom_call" | custom-call | flops 12000000000 | bytes 24000000 | tf_op jit(solution)/shard_map/pallas_call | solution.py:128
  599.9 14.2 %all-to-all-done.4 = bf16[4,128,2560]{2,1,0:T(8,128)(2,1)} async-done(((bf16[4,128,2560]{2,1,0:T(8,128)(2,1)}), bf16[4,128,2560]{2,1,0:T(8,128)(2,1)}, u32[]{:S(2)}, u32[]{:S(2)}) %all-to-all-start.4) | async-done | bytes 2621472 | tf_op jit(solution)/shard_map/all_to_all | solution.py:1044
  615.0 8.8 %all-to-all-start.7 = ((bf16[64,32,128]{2,1,0:T(8,128)(2,1)}), bf16[64,32,128]{2,1,0:T(8,128)(2,1)S(1)}, u32[]{:S(2)}, u32[]{:S(2)}) async-start(bf16[64,32,128]{2,1,0:T(8,128)(2,1)} %broadcast_in_dim.62), calls=%async_computation.7 | async-start | bytes 1048576 | tf_op jit(solution)/shard_map/all_to_all | solution.py:1124
  638.0 5.8 shard_map.277.refs_9_
  644.7 9.3 %shard_map.279 = (f32[5,2560,128]{2,1,0:T(8,128)}, f32[5,128,2560]{2,1,0:T(8,128)}) custom-call(s32[1]{0:T(128)} %bitcast.5.s_ref, bf16[16,128]{1,0:T(8,128)(2,1)} %fusion.57.refs_0_, bf16[5,1280,128]{2,1,0:T(8,128)(2,1)} %get-tuple-element.161.refs_1_, bf16[5,1280,128]{2,1,0:T(8,128)(2,1)} %collective-permute-done.65.refs_2_, ...), custom_call_target="tpu_custom_call" | custom-call | flops 8999999488 | bytes 18000000 | tf_op jit(solution)/shard_map/pallas_call | solution.py:128
  (516 shorter events, 245.7 us)
Async XLA Ops:
  15.7 21.4 %collective-permute-start.3 = (bf16[16,2688]{1,0:T(8,128)(2,1)}, bf16[16,2688]{1,0:T(8,128)(2,1)S(1)}, u32[]{:S(2)}, u32[]{:S(2)}) collective-permute-start(bf16[16,2688]{1,0:T(8,128)(2,1)} %get-tuple-element.223), channel_id=1, source_target_pairs={{0,16},{64,80},{32,48},{96,112},{127,111},{63,47},{95,79},{31,15}} | collective-permute-start | bytes 258056 | tf_op jit(solution)/shard_map/ppermute | solution.py:726
  16.4 20.8 %collective-permute-start.4 = (bf16[16,2688]{1,0:T(8,128)(2,1)}, bf16[16,2688]{1,0:T(8,128)(2,1)}, u32[]{:S(2)}, u32[]{:S(2)}) collective-permute-start(bf16[16,2688]{1,0:T(8,128)(2,1)} %get-tuple-element.224), channel_id=1, source_target_pairs={{0,8},{64,72},{32,40},{96,104},{127,119},{63,55},{95,87},{31,23}} | collective-permute-start | bytes 258056 | tf_op jit(solution)/shard_map/ppermute | solution.py:726
  17.7 20.1 %collective-permute-start.5 = (bf16[16,2688]{1,0:T(8,128)(2,1)}, bf16[16,2688]{1,0:T(8,128)(2,1)}, u32[]{:S(2)}, u32[]{:S(2)}) collective-permute-start(bf16[16,2688]{1,0:T(8,128)(2,1)} %get-tuple-element.225), channel_id=1, source_target_pairs={{0,24},{64,88},{32,56},{96,120},{127,103},{63,39},{95,71},{31,7}} | collective-permute-start | bytes 258056 | tf_op jit(solution)/shard_map/ppermute | solution.py:726
  19.8 23.9 %all-to-all-start = ((bf16[4,20,2048]{2,1,0:T(8,128)(2,1)}), bf16[4,20,2048]{2,1,0:T(8,128)(2,1)S(1)}, u32[]{:S(2)}, u32[]{:S(2)}) async-start(bf16[4,20,2048]{2,1,0:T(8,128)(2,1)} %pad_maximum_fusion.4), calls=%async_computation | async-start | bytes 786432 | tf_op jit(solution)/shard_map/all_to_all | solution.py:815
  37.2 143.9 %all-gather.9.cloned.1.call-start = ((), (), s32[]{:S(2)}) async-start(), calls=%async_computation.8 | async-start | bytes 46497792 | tf_op jit(solution)/shard_map/all_gather | solution.py:821
  63.3 232.0 %all-gather.11.cloned.1.call-start = ((), (), s32[]{:S(2)}) async-start(), calls=%async_computation.9 | async-start | bytes 16711680 | tf_op jit(solution)/shard_map/all_gather | solution.py:841
  124.5 73.8 %collective-permute-start.10 = (bf16[16,2560]{1,0:T(8,128)(2,1)S(1)}, bf16[16,2560]{1,0:T(8,128)(2,1)S(1)}, u32[]{:S(2)}, u32[]{:S(2)}) collective-permute-start(bf16[16,2560]{1,0:T(8,128)(2,1)S(1)} %slice.583), channel_id=1, source_target_pairs={{0,2},{1,3},{2,4},{3,5},{4,6},{5,7},{6,8},{7,9},{8,10},{9,11},{10,... | collective-permute-start | bytes 245768 | tf_op jit(solution)/shard_map/ppermute | solution.py:91
  185.1 32.9 %collective-permute-start.19 = (bf16[128,2560]{1,0:T(8,128)(2,1)}, bf16[128,2560]{1,0:T(8,128)(2,1)}, u32[]{:S(2)}, u32[]{:S(2)}) collective-permute-start(bf16[128,2560]{1,0:T(8,128)(2,1)} %add_convert_fusion.4.refs_4_.refs_8_), channel_id=1, source_target_pairs={{0,2},{2,4},{4,6},{6,0},{1,3},{3,5},{5,7},{7,1},{8,10},{10,12},{12... | collective-permute-start | bytes 1966088 | tf_op jit(solution)/shard_map/ppermute | solution.py:80
  186.4 31.8 %collective-permute-start.20 = (bf16[128,2560]{1,0:T(8,128)(2,1)}, bf16[128,2560]{1,0:T(8,128)(2,1)}, u32[]{:S(2)}, u32[]{:S(2)}) collective-permute-start(bf16[128,2560]{1,0:T(8,128)(2,1)} %add_convert_fusion.4.refs_4_.refs_8_), channel_id=1, source_target_pairs={{0,4},{2,6},{4,0},{6,2},{1,5},{3,7},{5,1},{7,3},{8,12},{10,14},{12... | collective-permute-start | bytes 1966088 | tf_op jit(solution)/shard_map/ppermute | solution.py:80
  189.1 29.0 %collective-permute-start.21 = (bf16[128,2560]{1,0:T(8,128)(2,1)}, bf16[128,2560]{1,0:T(8,128)(2,1)}, u32[]{:S(2)}, u32[]{:S(2)}) collective-permute-start(bf16[128,2560]{1,0:T(8,128)(2,1)} %add_convert_fusion.4.refs_4_.refs_8_), channel_id=1, source_target_pairs={{0,6},{2,0},{4,2},{6,4},{1,7},{3,1},{5,3},{7,5},{8,14},{10,8},{12,... | collective-permute-start | bytes 1966088 | tf_op jit(solution)/shard_map/ppermute | solution.py:80
  283.7 63.0 %collective-permute-start.40 = (bf16[128,2560]{1,0:T(8,128)(2,1)}, bf16[128,2560]{1,0:T(8,128)(2,1)}, u32[]{:S(2)}, u32[]{:S(2)}) collective-permute-start(bf16[128,2560]{1,0:T(8,128)(2,1)} %collective-permute-done.19.refs_9_.refs_3_.refs_10_), channel_id=1, source_target_pairs={{0,1},{1,0},{2,3},{3,2},{4,5},{5,4},{6,7},{7,6},{8,9},{9,8},{10,11... | collective-permute-start | bytes 1966088 | tf_op jit(solution)/shard_map/ppermute | solution.py:76
  284.2 71.2 %collective-permute-start.41 = (bf16[128,2560]{1,0:T(8,128)(2,1)}, bf16[128,2560]{1,0:T(8,128)(2,1)}, u32[]{:S(2)}, u32[]{:S(2)}) collective-permute-start(bf16[128,2560]{1,0:T(8,128)(2,1)} %collective-permute-done.20.refs_10_.refs_4_.refs_11_), channel_id=1, source_target_pairs={{0,1},{1,0},{2,3},{3,2},{4,5},{5,4},{6,7},{7,6},{8,9},{9,8},{10,11... | collective-permute-start | bytes 1966088 | tf_op jit(solution)/shard_map/ppermute | solution.py:76
  286.7 34.6 %collective-permute-start.33 = (bf16[128,2560]{1,0:T(8,128)(2,1)S(1)}, bf16[128,2560]{1,0:T(8,128)(2,1)}, u32[]{:S(2)}, u32[]{:S(2)}) collective-permute-start(bf16[128,2560]{1,0:T(8,128)(2,1)S(1)} %multiply_convert_fusion.1.refs_0_), channel_id=1, source_target_pairs={{0,2},{2,4},{4,6},{6,0},{1,3},{3,5},{5,7},{7,1},{8,10},{10,12},{12... | collective-permute-start | bytes 1966088 | tf_op jit(solution)/shard_map/ppermute | solution.py:80
  291.5 30.9 %collective-permute-start.34 = (bf16[128,2560]{1,0:T(8,128)(2,1)S(1)}, bf16[128,2560]{1,0:T(8,128)(2,1)S(1)}, u32[]{:S(2)}, u32[]{:S(2)}) collective-permute-start(bf16[128,2560]{1,0:T(8,128)(2,1)S(1)} %multiply_convert_fusion.1.refs_0_), channel_id=1, source_target_pairs={{0,4},{2,6},{4,0},{6,2},{1,5},{3,7},{5,1},{7,3},{8,12},{10,14},{12... | collective-permute-start | bytes 1966088 | tf_op jit(solution)/shard_map/ppermute | solution.py:80
  294.2 28.2 %collective-permute-start.35 = (bf16[128,2560]{1,0:T(8,128)(2,1)S(1)}, bf16[128,2560]{1,0:T(8,128)(2,1)}, u32[]{:S(2)}, u32[]{:S(2)}) collective-permute-start(bf16[128,2560]{1,0:T(8,128)(2,1)S(1)} %multiply_convert_fusion.1.refs_0_), channel_id=1, source_target_pairs={{0,6},{2,0},{4,2},{6,4},{1,7},{3,1},{5,3},{7,5},{8,14},{10,8},{12,... | collective-permute-start | bytes 1966088 | tf_op jit(solution)/shard_map/ppermute | solution.py:80
  321.4 34.1 %collective-permute-start.42 = (bf16[128,2560]{1,0:T(8,128)(2,1)}, bf16[128,2560]{1,0:T(8,128)(2,1)S(1)}, u32[]{:S(2)}, u32[]{:S(2)}) collective-permute-start(bf16[128,2560]{1,0:T(8,128)(2,1)} %collective-permute-done.21.refs_11_.refs_5_.refs_12_), channel_id=1, source_target_pairs={{0,1},{1,0},{2,3},{3,2},{4,5},{5,4},{6,7},{7,6},{8,9},{9,8},{10,11... | collective-permute-start | bytes 1966088 | tf_op jit(solution)/shard_map/ppermute | solution.py:76
  351.4 31.4 %all-to-all-start.2 = ((bf16[8,32,2816]{2,1,0:T(8,128)(2,1)}), bf16[8,32,2816]{2,1,0:T(8,128)(2,1)S(1)}, u32[]{:S(2)}, u32[]{:S(2)}) async-start(bf16[8,32,2816]{2,1,0:T(8,128)(2,1)} %bitcast.39), calls=%async_computation.2 | async-start | bytes 2883584 | tf_op jit(solution)/shard_map/all_to_all | solution.py:1000
  380.5 40.4 %collective-permute-start.45 = (bf16[128,2560]{1,0:T(8,128)(2,1)}, bf16[128,2560]{1,0:T(8,128)(2,1)}, u32[]{:S(2)}, u32[]{:S(2)}) collective-permute-start(bf16[128,2560]{1,0:T(8,128)(2,1)} %slice.531), channel_id=1, source_target_pairs={{0,1},{1,0},{2,3},{3,2},{4,5},{5,4},{6,7},{7,6},{8,9},{9,8},{10,11... | collective-permute-start | bytes 1966088 | tf_op jit(solution)/shard_map/ppermute | solution.py:76
  384.3 34.0 %all-to-all-start.3 = ((bf16[8,32,2816]{2,1,0:T(8,128)(2,1)}), bf16[8,32,2816]{2,1,0:T(8,128)(2,1)S(1)}, u32[]{:S(2)}, u32[]{:S(2)}) async-start(bf16[8,32,2816]{2,1,0:T(8,128)(2,1)} %broadcast_in_dim.59), calls=%async_computation.3 | async-start | bytes 2883584 | tf_op jit(solution)/shard_map/all_to_all | solution.py:1002
  393.0 28.1 %collective-permute-start.46 = (bf16[128,2560]{1,0:T(8,128)(2,1)}, bf16[128,2560]{1,0:T(8,128)(2,1)}, u32[]{:S(2)}, u32[]{:S(2)}) collective-permute-start(bf16[128,2560]{1,0:T(8,128)(2,1)} %get-tuple-element.212.refs_39_), channel_id=1, source_target_pairs={{0,6},{2,0},{4,2},{6,4},{1,7},{3,1},{5,3},{7,5},{8,14},{10,8},{12,... | collective-permute-start | bytes 1966088 | tf_op jit(solution)/shard_map/ppermute | solution.py:80
  395.6 27.0 %collective-permute-start.47 = (bf16[128,2560]{1,0:T(8,128)(2,1)}, bf16[128,2560]{1,0:T(8,128)(2,1)}, u32[]{:S(2)}, u32[]{:S(2)}) collective-permute-start(bf16[128,2560]{1,0:T(8,128)(2,1)} %get-tuple-element.211.refs_40_), channel_id=1, source_target_pairs={{0,4},{2,6},{4,0},{6,2},{1,5},{3,7},{5,1},{7,3},{8,12},{10,14},{12... | collective-permute-start | bytes 1966088 | tf_op jit(solution)/shard_map/ppermute | solution.py:80
  396.2 40.3 %collective-permute-start.48 = (bf16[128,2560]{1,0:T(8,128)(2,1)}, bf16[128,2560]{1,0:T(8,128)(2,1)}, u32[]{:S(2)}, u32[]{:S(2)}) collective-permute-start(bf16[128,2560]{1,0:T(8,128)(2,1)} %get-tuple-element.210.refs_41_), channel_id=1, source_target_pairs={{0,2},{2,4},{4,6},{6,0},{1,3},{3,5},{5,7},{7,1},{8,10},{10,12},{12... | collective-permute-start | bytes 1966088 | tf_op jit(solution)/shard_map/ppermute | solution.py:80
  447.1 140.1 %all-gather.15.cloned.1.call-start = ((), (), s32[]{:S(2)}) async-start(), calls=%async_computation.11 | async-start | bytes 2113536 | tf_op jit(solution)/shard_map/all_gather | solution.py:1029
  456.3 130.9 %all-gather.13.cloned.1.call-start = ((), (), s32[]{:S(2)}) async-start(), calls=%async_computation.10 | async-start | bytes 8847360 | tf_op jit(solution)/shard_map/all_gather | solution.py:1070
  512.7 36.2 %collective-permute-start.64 = (f32[512,128]{1,0:T(8,128)S(1)}, f32[512,128]{1,0:T(8,128)S(1)}, u32[]{:S(2)}, u32[]{:S(2)}) collective-permute-start(f32[512,128]{1,0:T(8,128)S(1)} %copy-done.43), channel_id=1, source_target_pairs={{0,1},{1,0},{2,3},{3,2},{4,5},{5,4},{6,7},{7,6},{8,9},{9,8},{10,11... | collective-permute-start | bytes 786440 | tf_op jit(solution)/shard_map/ppermute | solution.py:76
  518.5 56.3 %collective-permute-start.44 = (bf16[512,2560]{1,0:T(8,128)(2,1)}, bf16[512,2560]{1,0:T(8,128)(2,1)}, u32[]{:S(2)}, u32[]{:S(2)}) collective-permute-start(bf16[512,2560]{1,0:T(8,128)(2,1)} %get-tuple-element.134), channel_id=1, source_target_pairs={{0,1},{1,0},{2,3},{3,2},{4,5},{5,4},{6,7},{7,6},{8,9},{9,8},{10,11... | collective-permute-start | bytes 7864328 | tf_op jit(solution)/shard_map/ppermute | solution.py:76
  548.7 24.5 %collective-permute-start.68 = (bf16[128,2560]{1,0:T(8,128)(2,1)}, bf16[128,2560]{1,0:T(8,128)(2,1)}, u32[]{:S(2)}, u32[]{:S(2)}) collective-permute-start(bf16[128,2560]{1,0:T(8,128)(2,1)} %get-tuple-element.173), channel_id=1, source_target_pairs={{0,1},{1,0},{2,3},{3,2},{4,5},{5,4},{6,7},{7,6},{8,9},{9,8},{10,11... | collective-permute-start | bytes 1966088 | tf_op jit(solution)/shard_map/ppermute | solution.py:76
  555.4 23.6 %all-to-all-start.5 = ((bf16[64,32,128]{2,1,0:T(8,128)(2,1)}), bf16[64,32,128]{2,1,0:T(8,128)(2,1)S(1)}, u32[]{:S(2)}, u32[]{:S(2)}) async-start(bf16[64,32,128]{2,1,0:T(8,128)(2,1)} %bitcast.133), calls=%async_computation.5 | async-start | bytes 1048576 | tf_op jit(solution)/shard_map/all_to_all | solution.py:1106
  572.7 71.2 %collective-permute-start.65 = (bf16[5,1280,128]{2,1,0:T(8,128)(2,1)}, bf16[5,1280,128]{2,1,0:T(8,128)(2,1)}, u32[]{:S(2)}, u32[]{:S(2)}) collective-permute-start(bf16[5,1280,128]{2,1,0:T(8,128)(2,1)} %get-tuple-element.161.refs_1_), channel_id=1, source_target_pairs={{0,1},{1,0},{2,3},{3,2},{4,5},{5,4},{6,7},{7,6},{8,9},{9,8},{10,11... | collective-permute-start | bytes 4915208 | tf_op jit(solution)/shard_map/ppermute | solution.py:76
  573.0 70.8 %collective-permute-start.66 = (bf16[5,128,1280]{2,1,0:T(8,128)(2,1)}, bf16[5,128,1280]{2,1,0:T(8,128)(2,1)}, u32[]{:S(2)}, u32[]{:S(2)}) collective-permute-start(bf16[5,128,1280]{2,1,0:T(8,128)(2,1)} %get-tuple-element.162.refs_3_), channel_id=1, source_target_pairs={{0,1},{1,0},{2,3},{3,2},{4,5},{5,4},{6,7},{7,6},{8,9},{9,8},{10,11... | collective-permute-start | bytes 4915208 | tf_op jit(solution)/shard_map/ppermute | solution.py:76
  579.0 35.1 %all-to-all-start.4 = ((bf16[4,128,2560]{2,1,0:T(8,128)(2,1)}), bf16[4,128,2560]{2,1,0:T(8,128)(2,1)}, u32[]{:S(2)}, u32[]{:S(2)}) async-start(bf16[4,128,2560]{2,1,0:T(8,128)(2,1)} %bitcast.124), calls=%async_computation.4 | async-start | bytes 5242880 | tf_op jit(solution)/shard_map/all_to_all | solution.py:1044
  615.0 20.2 %all-to-all-start.7 = ((bf16[64,32,128]{2,1,0:T(8,128)(2,1)}), bf16[64,32,128]{2,1,0:T(8,128)(2,1)S(1)}, u32[]{:S(2)}, u32[]{:S(2)}) async-start(bf16[64,32,128]{2,1,0:T(8,128)(2,1)} %broadcast_in_dim.62), calls=%async_computation.7 | async-start | bytes 1048576 | tf_op jit(solution)/shard_map/all_to_all | solution.py:1124
  (132 other events, 1092.1 us)
Sparse Core Ops, SparseCore 0:
  52.1 128.8 all-gather.8
  183.2 105.3 all-gather.10
  456.4 62.0 all-gather.14
  520.1 45.1 all-gather.12

commit v7 on v6

--- a/solution.py
+++ b/solution.py
@@ -1047,7 +1047,7 @@
         [fixed(wide_block), col_spec(0), fixed((cols, halfw)), enter_spec, fixed(small_block)],
         [(rows_spec(main), ((main, width), f32)), F(*small_block)],
         [pltpu.VMEM(small_block, bf16)],
-        core_at, (grad_gelu, near, leave_half[0], enter_square[0], select), 12,
+        core_at, (grad_gelu, near, leave_half[0], enter_square[0], select), 2,
     )
 
     grad_in, grad_de, base, lat_gates = call(
@@ -1057,7 +1057,7 @@
         [(head_spec(rows), (wide_block, bf16))] * 2 + [(head_spec(rows), (wide_block, f32)), F(rows, 2 * cols)],
         [pltpu.VMEM((rows + 8, head), f32), pltpu.VMEM((halfw, 2 * head), bf16)],
         core_at, (back, trail, coming, states, entering, convolved, sig_in, sig_de, decays, mask, rate, near, leave_half[2], leave_half[3]),
-        8,
+        60,
     )
 
     lanes_all = 3 * slotp + 2 * share
@@ -1083,7 +1083,7 @@
         core_at,
         (base, lat_gates, swap(lat_gates), halo_base, halo_lat, halo_other, select_after, mask_long, taps, enter_half[2], enter_half[3],
          leave_half[1], near, enter_square[1], gelu_part),
-        12,
+        2,
     )
 
     lg_gelu = ((lat_gelu + swap(lat_gelu)) * select).astype(bf16)
@@ -1100,7 +1100,7 @@
         [part_spec(cols, 0), part_spec(halfw, 0)] * 10,
         [B(64 * mid_rows, cols)],
         [pltpu.VMEM((cols, halfw), f32)],
-        middle_at, operands, 6,
+        middle_at, operands, 6, (down_total,),
     )
     mid_own = mid
     mid = lax.all_to_all(mid, CHIPS, 0, 0, tiled=True).reshape(64, mid_rows, cols)

time: 676 us -> 702 us (1.038)
  waiting for transfers between devices: 124 us -> 152 us
  other arithmetic: 78.6 us -> 71 us
    all_to_all x1, waiting for transfers between devices: 14.2 us -> 37.9 us  [per_device(): lax.all_to_all(down_total, YAX, 0, 0, tiled=True).reshape(4, toks, width)]
    all_to_all x1, waiting for transfers between devices: 0.01 us -> 15.4 us  [per_device(): lax.all_to_all(jnp.broadcast_to(extra_total[None], (8, *extra_total.shape...]
    ppermute x30, waiting for transfers between devices: 27.2 us -> 14.4 us  [shift4(): return lax.ppermute(v, axis, [(i, (i + by) % 4) for i in range(4)])]
    unnamed x176 -> x174, local copies, waits for them, and re-layouts: 17.2 us -> 19.1 us
  transfers between devices with their start and end apart: 81 -> 81, of which waited for: 26 -> 20; matrix products, arithmetic and copies ran while one was open for 20% -> 18% of each run, Pallas kernels for 34% -> 30%
where the time goes in v7:
time: 702 us; the launch traced here: 690 us
  Pallas kernels  233 us (33%)
  waiting for transfers between devices  152 us (22%)
  starting transfers between devices  133 us (19%)
  other arithmetic  71 us (10%)
  local copies, waits for them, and re-layouts  70.6 us (10%)
  between operations  21.4 us (3%)
  matrix products  8.9 us (1%)
    pallas_call x20, Pallas kernels, call(): pl.pallas_call(body, grid_spec=pltpu.PrefetchScalarGridSpec(num_scalar_pr...  233 us
    all_gather x1, waiting for transfers between devices, per_device(): lax.all_gather(quads[None], AXES, axis=0, tiled=True)  53.2 us
    all_to_all x1, waiting for transfers between devices, per_device(): lax.all_to_all(down_total, YAX, 0, 0, tiled=True).reshape(4, toks, width)  37.9 us
    ppermute x30, starting transfers between devices, shift4(): return lax.ppermute(v, axis, [(i, (i + by) % 4) for i in range(4)])  34.7 us
    ppermute x27, starting transfers between devices, swap(): return lax.ppermute(v, 'c', [(0, 1), (1, 0)])  24 us
    unnamed x174, local copies, waits for them, and re-layouts  19.1 us
    all_to_all x1, starting transfers between devices, per_device(): quads = lax.all_to_all(quads, QUAD, 0, 0, tiled=True).reshape(per4, lanes)  17.4 us
    all_to_all x1, waiting for transfers between devices, per_device(): lax.all_to_all(jnp.broadcast_to(extra_total[None], (8, *extra_total.shape...  15.4 us
  transfers between devices with their start and end apart: 81, of which 20 were waited for; matrix products, arithmetic and copies ran while one was open for 18% of the time, Pallas kernels for 30%

profile of v7, /device:TPU:1, one launch (start us, length us, event | category | flops | bytes accessed | tf_op | source)
XLA Modules:
  0.0 690.3 jit_solution(10300897305817106496)
XLA Ops:
  19.8 17.4 %all-to-all-start = ((bf16[4,20,2048]{2,1,0:T(8,128)(2,1)}), bf16[4,20,2048]{2,1,0:T(8,128)(2,1)S(1)}, u32[]{:S(2)}, u32[]{:S(2)}) async-start(bf16[4,20,2048]{2,1,0:T(8,128)(2,1)} %pad_maximum_fusion.4), calls=%async_computation | async-start | bytes 786432 | tf_op jit(solution)/shard_map/all_to_all | solution.py:815
  43.8 6.6 collective-permute-done.8
  52.4 5.1 convolution_convert_fusion
  65.0 12.5 %all-to-all-done.1 = bf16[8,20,2048]{2,1,0:T(8,128)(2,1)S(1)} async-done(((bf16[8,20,2048]{2,1,0:T(8,128)(2,1)}), bf16[8,20,2048]{2,1,0:T(8,128)(2,1)S(1)}, u32[]{:S(2)}, u32[]{:S(2)}) %all-to-all-start.1) | async-done | bytes 655392 | tf_op jit(solution)/shard_map/all_to_all | solution.py:837
  79.8 6.3 copy.66
  86.0 6.3 copy.67
  127.9 53.2 %all-gather.9.cloned.1.call-done = bf16[11264,2048]{1,0:T(8,128)(2,1)} async-done(((bf16[88,2048]{1,0:T(8,128)(2,1)}), bf16[11264,2048]{1,0:T(8,128)(2,1)}) %all-gather.9.cloned.1.call-update) | async-done | bytes 46137360 | tf_op jit(solution)/shard_map/all_gather | solution.py:821
  190.0 5.1 shard_map.260
  201.4 12.5 %shard_map.261 = (bf16[512,1280]{1,0:T(8,128)(2,1)}, f32[512,256]{1,0:T(8,128)}, bf16[528,128]{1,0:T(8,128)(2,1)}) custom-call(s32[1]{0:T(128)} %bitcast.5.s_ref, bf16[528,2560]{1,0:T(8,128)(2,1)} %pad_maximum_fusion.1.refs_0_, bf16[32,4,88,2048]{3,2,1,0:T(8,128)(2,1)} %bitcast.108, bf16[2560,128]{1,0:T(8,128)(2,1)} %get-tuple-element.206.refs_2_.refs_13_, ...), custom_call_target="tpu_custom_call" | custom-call | flops 1000000000 | bytes 2000000 | tf_op jit(solution)/shard_map/pallas_call | solution.py:128
  218.8 11.0 %shard_map.262 = (f32[512,1280]{1,0:T(8,128)}, f32[512,1280]{1,0:T(8,128)}, f32[512,1280]{1,0:T(8,128)}, f32[512,1280]{1,0:T(8,128)}, f32[512,1280]{1,0:T(8,128)...) custom-call(s32[1]{0:T(128)} %bitcast.5.s_ref, ...), custom_call_target="tpu_custom_call" | custom-call | flops 4000000000 | bytes 8000000 | tf_op jit(solution)/shard_map/pallas_call | solution.py:128
  250.5 11.3 %shard_map.263 = (f32[512,1280]{1,0:T(8,128)}, f32[512,1280]{1,0:T(8,128)}, bf16[512,128]{1,0:T(8,128)(2,1)}) custom-call(s32[1]{0:T(128)} %bitcast.5.s_ref, bf16[528,2560]{1,0:T(8,128)(2,1)} %pad_maximum_fusion.1.refs_0_, bf16[32,4,88,2048]{3,2,1,0:T(8,128)(2,1)} %bitcast.110, bf16[2560,128]{1,0:T(8,128)(2,1)} %get-tuple-element.205.refs_2_.refs_3_, ...), custom_call_target="tpu_custom_call" | custom-call | flops 12000000000 | bytes 24000000 | tf_op jit(solution)/shard_map/pallas_call | solution.py:128
  262.5 14.2 %shard_map.264 = (f32[512,1280]{1,0:T(8,128)}, bf16[512,1280]{1,0:T(8,128)(2,1)}, f32[512,128]{1,0:T(8,128)}, f32[128,2560]{1,0:T(8,128)}, bf16[384,2560]{1,0:T(8,128)(2,1)}, /*index=5*/bf16[256,2560]{1,0:T(8,128)(2,1)}) custom-call(s32[1]{0:T(128)} %bitcast.5.s_ref, f32[512,1280]{1,0:T(8,128)} %get-tuple-element.101.refs_0_, ...), custom_call_target="tpu_custom_call" | custom-call | flops 15000000512 | bytes 30000000 | tf_op jit(solution)/shard_map/pallas_call | solution.py:128
  295.7 26.0 %shard_map.265 = (bf16[512,2560]{1,0:T(8,128)(2,1)}, bf16[512,1024]{1,0:T(8,128)(2,1)}, bf16[512,1024]{1,0:T(8,128)(2,1)}, bf16[512,1024]{1,0:T(8,128)(2,1)}, bf...) custom-call(s32[1]{0:T(128)} %bitcast.5.s_ref, ...), custom_call_target="tpu_custom_call" | custom-call | flops 60000002048 | bytes 120000000 | tf_op jit(solution)/shard_map/pallas_call | solution.py:128
  322.7 21.0 %shard_map.266 = (bf16[384,2560]{1,0:T(8,128)(2,1)}, bf16[384,1024]{1,0:T(8,128)(2,1)}, bf16[384,1024]{1,0:T(8,128)(2,1)}, bf16[384,1024]{1,0:T(8,128)(2,1)}, bf...) custom-call(s32[1]{0:T(128)} %bitcast.5.s_ref, ...), custom_call_target="tpu_custom_call" | custom-call | flops 40000000000 | bytes 80000000 | tf_op jit(solution)/shard_map/pallas_call | solution.py:128
  356.2 20.9 %shard_map.267 = (bf16[384,2560]{1,0:T(8,128)(2,1)}, bf16[384,1024]{1,0:T(8,128)(2,1)}, bf16[384,1024]{1,0:T(8,128)(2,1)}, bf16[384,1024]{1,0:T(8,128)(2,1)}, bf...) custom-call(s32[1]{0:T(128)} %bitcast.5.s_ref, ...), custom_call_target="tpu_custom_call" | custom-call | flops 60000002048 | bytes 120000000 | tf_op jit(solution)/shard_map/pallas_call | solution.py:128
  390.0 15.4 %all-to-all-done.3 = bf16[8,32,2816]{2,1,0:T(8,128)(2,1)S(1)} async-done(((bf16[8,32,2816]{2,1,0:T(8,128)(2,1)}), bf16[8,32,2816]{2,1,0:T(8,128)(2,1)S(1)}, u32[]{:S(2)}, u32[]{:S(2)}) %all-to-all-start.3) | async-done | bytes 1441824 | tf_op jit(solution)/shard_map/all_to_all | solution.py:1002
  412.0 19.5 %shard_map.268 = (bf16[512,2560]{1,0:T(8,128)(2,1)}, bf16[512,2560]{1,0:T(8,128)(2,1)}, bf16[16,1024]{1,0:T(8,128)(2,1)}, bf16[16,1024]{1,0:T(8,128)(2,1)}, bf16...) custom-call(s32[2]{0:T(128)} %pad_add_fusion.6.s_ref, ...), custom_call_target="tpu_custom_call" | custom-call | flops 60000002048 | bytes 120000000 | tf_op jit(solution)/shard_map/pallas_call | solution.py:128
  437.4 5.9 collective-permute-done.48
  453.1 15.3 %shard_map.269 = (bf16[512,1280]{1,0:T(8,128)(2,1)}, bf16[512,128]{1,0:T(8,128)(2,1)}, f32[512,1280]{1,0:T(8,128)}, f32[512,1280]{1,0:T(8,128)}) custom-call(s32[1]{0:T(128)} %bitcast.5.s_ref, bf16[512,2560]{1,0:T(8,128)(2,1)} %pad_maximum_fusion.refs_0_, bf16[32,4,88,2048]{3,2,1,0:T(8,128)(2,1)} %bitcast.112, ...), custom_call_target="tpu_custom_call" | custom-call | flops 17999998976 | bytes 36000000 | tf_op jit(solution)/shard_map/pallas_call | solution.py:128
  492.2 12.1 %shard_map.271 = (bf16[512,1280]{1,0:T(8,128)(2,1)}, bf16[512,1280]{1,0:T(8,128)(2,1)}, f32[512,1280]{1,0:T(8,128)}, f32[512,256]{1,0:T(8,128)}) custom-call(s32[1]{0:T(128)} %bitcast.5.s_ref, f32[512,1280]{1,0:T(8,128)} %get-tuple-element.140.refs_0_, f32[512,1280]{1,0:T(8,128)} %get-tuple-element.139.refs_1_, f32[1,1280]{1,0:T(1,128)} %fusion.67.refs_2_, ...), custom_call_target="tpu_custom_call" | custom-call | flops 60000002048 | bytes 120000000 | tf_op jit(solution)/shard_map/pallas_call | solution.py:128
  518.6 8.0 %shard_map.270 = (f32[256,2560]{1,0:T(8,128)}, f32[512,128]{1,0:T(8,128)}) custom-call(s32[1]{0:T(128)} %bitcast.5.s_ref, bf16[512,1280]{1,0:T(8,128)(2,1)} %get-tuple-element.141.refs_0_.refs_11_, bf16[32,4,88,2048]{3,2,1,0:T(8,128)(2,1)} %bitcast.114, bf16[128,1280]{1,0:T(8,128)(2,1)} %get-tuple-element.201.refs_4_.refs_2_, ...), custom_call_target="tpu_custom_call" | custom-call | flops 2000000000 | bytes 4000000 | tf_op jit(solution)/shard_map/pallas_call | solution.py:128
  530.3 11.9 %shard_map.272 = (bf16[512,1280]{1,0:T(8,128)(2,1)}, bf16[512,128]{1,0:T(8,128)(2,1)}, bf16[512,128]{1,0:T(8,128)(2,1)}, f32[512,128]{1,0:T(8,128)}, f32[128,2560]{1,0:T(8,128)}, /*index=5*/bf16[128,2560]{1,0:T(8,128)(2,1)}) custom-call(s32[1]{0:T(128)} %bitcast.5.s_ref, f32[512,1280]{1,0:T(8,128)} %get-tuple-element.145.refs_0_.refs_7_, ...), custom_call_target="tpu_custom_call" | custom-call | flops 2000000000 | bytes 4000000 | tf_op jit(solution)/shard_map/pallas_call | solution.py:128
  546.8 6.3 all-to-all-start.4
  562.3 37.9 %all-to-all-done.4.refs_20_ = bf16[4,128,2560]{2,1,0:T(8,128)(2,1)} async-done(((bf16[4,128,2560]{2,1,0:T(8,128)(2,1)}), bf16[4,128,2560]{2,1,0:T(8,128)(2,1)}, u32[]{:S(2)}, u32[]{:S(2)}) %all-to-all-start.4) | async-done | bytes 2621472 | tf_op jit(solution)/shard_map/all_to_all | solution.py:1044
  600.2 5.7 shard_map.273.refs_20_.refs_4_.refs_5_
  606.0 10.6 %all-to-all-start.5 = ((bf16[64,32,128]{2,1,0:T(8,128)(2,1)}), bf16[64,32,128]{2,1,0:T(8,128)(2,1)S(1)}, u32[]{:S(2)}, u32[]{:S(2)}) async-start(bf16[64,32,128]{2,1,0:T(8,128)(2,1)} %bitcast.133), calls=%async_computation.5 | async-start | bytes 1048576 | tf_op jit(solution)/shard_map/all_to_all | solution.py:1106
  616.5 6.2 shard_map.274
  627.6 10.8 %shard_map.276 = f32[128,15360]{1,0:T(8,128)} custom-call(s32[1]{0:T(128)} %bitcast.5.s_ref, bf16[16,128]{1,0:T(8,128)(2,1)} %fusion.57.refs_0_, bf16[480,512]{1,0:T(8,128)(2,1)} %fusion.34.refs_1_, bf16[8,128,3840]{2,1,0:T(8,128)(2,1)} %bitcast.116, bf16[16,8,16,512]{3,2,1,0:T(8,128)(2,1)} %bitcast.130, bf16[2048,128]{1,0:T(8,128)(2,1)} %shard_map.273.refs_20_.refs_4_.refs_5_), custom_call_target="tpu_custom_call" | custom-call | flops 12000000000 | bytes 24000000 | tf_op jit(solution)/shard_map/pallas_call | solution.py:128
  641.1 8.3 %all-to-all-start.7 = ((bf16[64,32,128]{2,1,0:T(8,128)(2,1)}), bf16[64,32,128]{2,1,0:T(8,128)(2,1)S(1)}, u32[]{:S(2)}, u32[]{:S(2)}) async-start(bf16[64,32,128]{2,1,0:T(8,128)(2,1)} %broadcast_in_dim.62), calls=%async_computation.7 | async-start | bytes 1048576 | tf_op jit(solution)/shard_map/all_to_all | solution.py:1124
  655.7 6.0 all-to-all-done.7
  663.7 5.8 shard_map.277.refs_9_
  670.3 9.3 %shard_map.279 = (f32[5,2560,128]{2,1,0:T(8,128)}, f32[5,128,2560]{2,1,0:T(8,128)}) custom-call(s32[1]{0:T(128)} %bitcast.5.s_ref, bf16[16,128]{1,0:T(8,128)(2,1)} %fusion.57.refs_0_, bf16[5,1280,128]{2,1,0:T(8,128)(2,1)} %get-tuple-element.161.refs_1_, bf16[5,1280,128]{2,1,0:T(8,128)(2,1)} %collective-permute-done.65.refs_2_, ...), custom_call_target="tpu_custom_call" | custom-call | flops 8999999488 | bytes 18000000 | tf_op jit(solution)/shard_map/pallas_call | solution.py:128
  (514 shorter events, 244.7 us)
Async XLA Ops:
  15.7 21.4 %collective-permute-start.3 = (bf16[16,2688]{1,0:T(8,128)(2,1)}, bf16[16,2688]{1,0:T(8,128)(2,1)S(1)}, u32[]{:S(2)}, u32[]{:S(2)}) collective-permute-start(bf16[16,2688]{1,0:T(8,128)(2,1)} %get-tuple-element.223), channel_id=1, source_target_pairs={{0,16},{64,80},{32,48},{96,112},{127,111},{63,47},{95,79},{31,15}} | collective-permute-start | bytes 258056 | tf_op jit(solution)/shard_map/ppermute | solution.py:726
  16.4 20.8 %collective-permute-start.4 = (bf16[16,2688]{1,0:T(8,128)(2,1)}, bf16[16,2688]{1,0:T(8,128)(2,1)}, u32[]{:S(2)}, u32[]{:S(2)}) collective-permute-start(bf16[16,2688]{1,0:T(8,128)(2,1)} %get-tuple-element.224), channel_id=1, source_target_pairs={{0,8},{64,72},{32,40},{96,104},{127,119},{63,55},{95,87},{31,23}} | collective-permute-start | bytes 258056 | tf_op jit(solution)/shard_map/ppermute | solution.py:726
  17.7 20.1 %collective-permute-start.5 = (bf16[16,2688]{1,0:T(8,128)(2,1)}, bf16[16,2688]{1,0:T(8,128)(2,1)}, u32[]{:S(2)}, u32[]{:S(2)}) collective-permute-start(bf16[16,2688]{1,0:T(8,128)(2,1)} %get-tuple-element.225), channel_id=1, source_target_pairs={{0,24},{64,88},{32,56},{96,120},{127,103},{63,39},{95,71},{31,7}} | collective-permute-start | bytes 258056 | tf_op jit(solution)/shard_map/ppermute | solution.py:726
  19.8 23.9 %all-to-all-start = ((bf16[4,20,2048]{2,1,0:T(8,128)(2,1)}), bf16[4,20,2048]{2,1,0:T(8,128)(2,1)S(1)}, u32[]{:S(2)}, u32[]{:S(2)}) async-start(bf16[4,20,2048]{2,1,0:T(8,128)(2,1)} %pad_maximum_fusion.4), calls=%async_computation | async-start | bytes 786432 | tf_op jit(solution)/shard_map/all_to_all | solution.py:815
  37.2 143.9 %all-gather.9.cloned.1.call-start = ((), (), s32[]{:S(2)}) async-start(), calls=%async_computation.8 | async-start | bytes 46497792 | tf_op jit(solution)/shard_map/all_gather | solution.py:821
  59.7 17.9 %all-to-all-start.1 = ((bf16[8,20,2048]{2,1,0:T(8,128)(2,1)}), bf16[8,20,2048]{2,1,0:T(8,128)(2,1)S(1)}, u32[]{:S(2)}, u32[]{:S(2)}) async-start(bf16[8,20,2048]{2,1,0:T(8,128)(2,1)} %copy.64), calls=%async_computation.1 | async-start | bytes 1572864 | tf_op jit(solution)/shard_map/all_to_all | solution.py:837
  63.3 232.4 %all-gather.11.cloned.1.call-start = ((), (), s32[]{:S(2)}) async-start(), calls=%async_computation.9 | async-start | bytes 16711680 | tf_op jit(solution)/shard_map/all_gather | solution.py:841
  124.5 73.9 %collective-permute-start.10 = (bf16[16,2560]{1,0:T(8,128)(2,1)S(1)}, bf16[16,2560]{1,0:T(8,128)(2,1)S(1)}, u32[]{:S(2)}, u32[]{:S(2)}) collective-permute-start(bf16[16,2560]{1,0:T(8,128)(2,1)S(1)} %slice.583), channel_id=1, source_target_pairs={{0,2},{1,3},{2,4},{3,5},{4,6},{5,7},{6,8},{7,9},{8,10},{9,11},{10,... | collective-permute-start | bytes 245768 | tf_op jit(solution)/shard_map/ppermute | solution.py:91
  185.2 32.9 %collective-permute-start.19 = (bf16[128,2560]{1,0:T(8,128)(2,1)}, bf16[128,2560]{1,0:T(8,128)(2,1)}, u32[]{:S(2)}, u32[]{:S(2)}) collective-permute-start(bf16[128,2560]{1,0:T(8,128)(2,1)} %add_convert_fusion.4.refs_4_.refs_8_), channel_id=1, source_target_pairs={{0,2},{2,4},{4,6},{6,0},{1,3},{3,5},{5,7},{7,1},{8,10},{10,12},{12... | collective-permute-start | bytes 1966088 | tf_op jit(solution)/shard_map/ppermute | solution.py:80
  186.4 31.8 %collective-permute-start.20 = (bf16[128,2560]{1,0:T(8,128)(2,1)}, bf16[128,2560]{1,0:T(8,128)(2,1)}, u32[]{:S(2)}, u32[]{:S(2)}) collective-permute-start(bf16[128,2560]{1,0:T(8,128)(2,1)} %add_convert_fusion.4.refs_4_.refs_8_), channel_id=1, source_target_pairs={{0,4},{2,6},{4,0},{6,2},{1,5},{3,7},{5,1},{7,3},{8,12},{10,14},{12... | collective-permute-start | bytes 1966088 | tf_op jit(solution)/shard_map/ppermute | solution.py:80
  189.2 29.0 %collective-permute-start.21 = (bf16[128,2560]{1,0:T(8,128)(2,1)}, bf16[128,2560]{1,0:T(8,128)(2,1)}, u32[]{:S(2)}, u32[]{:S(2)}) collective-permute-start(bf16[128,2560]{1,0:T(8,128)(2,1)} %add_convert_fusion.4.refs_4_.refs_8_), channel_id=1, source_target_pairs={{0,6},{2,0},{4,2},{6,4},{1,7},{3,1},{5,3},{7,5},{8,14},{10,8},{12,... | collective-permute-start | bytes 1966088 | tf_op jit(solution)/shard_map/ppermute | solution.py:80
  283.7 63.1 %collective-permute-start.40 = (bf16[128,2560]{1,0:T(8,128)(2,1)}, bf16[128,2560]{1,0:T(8,128)(2,1)S(1)}, u32[]{:S(2)}, u32[]{:S(2)}) collective-permute-start(bf16[128,2560]{1,0:T(8,128)(2,1)} %collective-permute-done.19.refs_9_.refs_3_.refs_10_), channel_id=1, source_target_pairs={{0,1},{1,0},{2,3},{3,2},{4,5},{5,4},{6,7},{7,6},{8,9},{9,8},{10,11... | collective-permute-start | bytes 1966088 | tf_op jit(solution)/shard_map/ppermute | solution.py:76
  284.2 71.2 %collective-permute-start.41 = (bf16[128,2560]{1,0:T(8,128)(2,1)}, bf16[128,2560]{1,0:T(8,128)(2,1)}, u32[]{:S(2)}, u32[]{:S(2)}) collective-permute-start(bf16[128,2560]{1,0:T(8,128)(2,1)} %collective-permute-done.20.refs_10_.refs_4_.refs_11_), channel_id=1, source_target_pairs={{0,1},{1,0},{2,3},{3,2},{4,5},{5,4},{6,7},{7,6},{8,9},{9,8},{10,11... | collective-permute-start | bytes 1966088 | tf_op jit(solution)/shard_map/ppermute | solution.py:76
  286.7 35.0 %collective-permute-start.33 = (bf16[128,2560]{1,0:T(8,128)(2,1)S(1)}, bf16[128,2560]{1,0:T(8,128)(2,1)}, u32[]{:S(2)}, u32[]{:S(2)}) collective-permute-start(bf16[128,2560]{1,0:T(8,128)(2,1)S(1)} %multiply_convert_fusion.1.refs_0_), channel_id=1, source_target_pairs={{0,2},{2,4},{4,6},{6,0},{1,3},{3,5},{5,7},{7,1},{8,10},{10,12},{12... | collective-permute-start | bytes 1966088 | tf_op jit(solution)/shard_map/ppermute | solution.py:80
  291.5 31.3 %collective-permute-start.34 = (bf16[128,2560]{1,0:T(8,128)(2,1)S(1)}, bf16[128,2560]{1,0:T(8,128)(2,1)}, u32[]{:S(2)}, u32[]{:S(2)}) collective-permute-start(bf16[128,2560]{1,0:T(8,128)(2,1)S(1)} %multiply_convert_fusion.1.refs_0_), channel_id=1, source_target_pairs={{0,4},{2,6},{4,0},{6,2},{1,5},{3,7},{5,1},{7,3},{8,12},{10,14},{12... | collective-permute-start | bytes 1966088 | tf_op jit(solution)/shard_map/ppermute | solution.py:80
  294.3 28.4 %collective-permute-start.35 = (bf16[128,2560]{1,0:T(8,128)(2,1)S(1)}, bf16[128,2560]{1,0:T(8,128)(2,1)}, u32[]{:S(2)}, u32[]{:S(2)}) collective-permute-start(bf16[128,2560]{1,0:T(8,128)(2,1)S(1)} %multiply_convert_fusion.1.refs_0_), channel_id=1, source_target_pairs={{0,6},{2,0},{4,2},{6,4},{1,7},{3,1},{5,3},{7,5},{8,14},{10,8},{12,... | collective-permute-start | bytes 1966088 | tf_op jit(solution)/shard_map/ppermute | solution.py:80
  321.7 33.7 %collective-permute-start.42 = (bf16[128,2560]{1,0:T(8,128)(2,1)}, bf16[128,2560]{1,0:T(8,128)(2,1)S(1)}, u32[]{:S(2)}, u32[]{:S(2)}) collective-permute-start(bf16[128,2560]{1,0:T(8,128)(2,1)} %collective-permute-done.21.refs_11_.refs_5_.refs_12_), channel_id=1, source_target_pairs={{0,1},{1,0},{2,3},{3,2},{4,5},{5,4},{6,7},{7,6},{8,9},{9,8},{10,11... | collective-permute-start | bytes 1966088 | tf_op jit(solution)/shard_map/ppermute | solution.py:76
  351.3 27.6 %all-to-all-start.2 = ((bf16[8,32,2816]{2,1,0:T(8,128)(2,1)}), bf16[8,32,2816]{2,1,0:T(8,128)(2,1)S(1)}, u32[]{:S(2)}, u32[]{:S(2)}) async-start(bf16[8,32,2816]{2,1,0:T(8,128)(2,1)} %bitcast.39), calls=%async_computation.2 | async-start | bytes 2883584 | tf_op jit(solution)/shard_map/all_to_all | solution.py:1000
  378.4 27.7 %collective-permute-start.43 = (bf16[384,2560]{1,0:T(8,128)(2,1)}, bf16[384,2560]{1,0:T(8,128)(2,1)}, u32[]{:S(2)}, u32[]{:S(2)}) collective-permute-start(bf16[384,2560]{1,0:T(8,128)(2,1)} %get-tuple-element.132), channel_id=1, source_target_pairs={{0,1},{1,0},{2,3},{3,2},{4,5},{5,4},{6,7},{7,6},{8,9},{9,8},{10,11... | collective-permute-start | bytes 5898248 | tf_op jit(solution)/shard_map/ppermute | solution.py:76
  381.1 24.3 %all-to-all-start.3 = ((bf16[8,32,2816]{2,1,0:T(8,128)(2,1)}), bf16[8,32,2816]{2,1,0:T(8,128)(2,1)S(1)}, u32[]{:S(2)}, u32[]{:S(2)}) async-start(bf16[8,32,2816]{2,1,0:T(8,128)(2,1)} %broadcast_in_dim.59), calls=%async_computation.3 | async-start | bytes 2883584 | tf_op jit(solution)/shard_map/all_to_all | solution.py:1002
  390.0 47.4 %collective-permute-start.45 = (bf16[128,2560]{1,0:T(8,128)(2,1)}, bf16[128,2560]{1,0:T(8,128)(2,1)}, u32[]{:S(2)}, u32[]{:S(2)}) collective-permute-start(bf16[128,2560]{1,0:T(8,128)(2,1)} %slice.531), channel_id=1, source_target_pairs={{0,1},{1,0},{2,3},{3,2},{4,5},{5,4},{6,7},{7,6},{8,9},{9,8},{10,11... | collective-permute-start | bytes 1966088 | tf_op jit(solution)/shard_map/ppermute | solution.py:76
  409.9 27.5 %collective-permute-start.46 = (bf16[128,2560]{1,0:T(8,128)(2,1)}, bf16[128,2560]{1,0:T(8,128)(2,1)S(1)}, u32[]{:S(2)}, u32[]{:S(2)}) collective-permute-start(bf16[128,2560]{1,0:T(8,128)(2,1)} %get-tuple-element.212.refs_39_), channel_id=1, source_target_pairs={{0,6},{2,0},{4,2},{6,4},{1,7},{3,1},{5,3},{7,5},{8,14},{10,8},{12,... | collective-permute-start | bytes 1966088 | tf_op jit(solution)/shard_map/ppermute | solution.py:80
  410.8 26.6 %collective-permute-start.47 = (bf16[128,2560]{1,0:T(8,128)(2,1)}, bf16[128,2560]{1,0:T(8,128)(2,1)S(1)}, u32[]{:S(2)}, u32[]{:S(2)}) collective-permute-start(bf16[128,2560]{1,0:T(8,128)(2,1)} %get-tuple-element.211.refs_40_), channel_id=1, source_target_pairs={{0,4},{2,6},{4,0},{6,2},{1,5},{3,7},{5,1},{7,3},{8,12},{10,14},{12... | collective-permute-start | bytes 1966088 | tf_op jit(solution)/shard_map/ppermute | solution.py:80
  412.0 31.3 %collective-permute-start.48 = (bf16[128,2560]{1,0:T(8,128)(2,1)}, bf16[128,2560]{1,0:T(8,128)(2,1)}, u32[]{:S(2)}, u32[]{:S(2)}) collective-permute-start(bf16[128,2560]{1,0:T(8,128)(2,1)} %get-tuple-element.210.refs_41_), channel_id=1, source_target_pairs={{0,2},{2,4},{4,6},{6,0},{1,3},{3,5},{5,7},{7,1},{8,10},{10,12},{12... | collective-permute-start | bytes 1966088 | tf_op jit(solution)/shard_map/ppermute | solution.py:80
  477.9 149.7 %all-gather.15.cloned.1.call-start = ((), (), s32[]{:S(2)}) async-start(), calls=%async_computation.11 | async-start | bytes 2113536 | tf_op jit(solution)/shard_map/all_gather | solution.py:1029
  489.0 138.5 %all-gather.13.cloned.1.call-start = ((), (), s32[]{:S(2)}) async-start(), calls=%async_computation.10 | async-start | bytes 8847360 | tf_op jit(solution)/shard_map/all_gather | solution.py:1070
  506.9 35.9 %collective-permute-start.44 = (bf16[512,2560]{1,0:T(8,128)(2,1)}, bf16[512,2560]{1,0:T(8,128)(2,1)}, u32[]{:S(2)}, u32[]{:S(2)}) collective-permute-start(bf16[512,2560]{1,0:T(8,128)(2,1)} %get-tuple-element.134), channel_id=1, source_target_pairs={{0,1},{1,0},{2,3},{3,2},{4,5},{5,4},{6,7},{7,6},{8,9},{9,8},{10,11... | collective-permute-start | bytes 7864328 | tf_op jit(solution)/shard_map/ppermute | solution.py:76
  546.8 53.4 %all-to-all-start.4 = ((bf16[4,128,2560]{2,1,0:T(8,128)(2,1)}), bf16[4,128,2560]{2,1,0:T(8,128)(2,1)}, u32[]{:S(2)}, u32[]{:S(2)}) async-start(bf16[4,128,2560]{2,1,0:T(8,128)(2,1)} %bitcast.124), calls=%async_computation.4 | async-start | bytes 5242880 | tf_op jit(solution)/shard_map/all_to_all | solution.py:1044
  606.0 21.5 %all-to-all-start.5 = ((bf16[64,32,128]{2,1,0:T(8,128)(2,1)}), bf16[64,32,128]{2,1,0:T(8,128)(2,1)S(1)}, u32[]{:S(2)}, u32[]{:S(2)}) async-start(bf16[64,32,128]{2,1,0:T(8,128)(2,1)} %bitcast.133), calls=%async_computation.5 | async-start | bytes 1048576 | tf_op jit(solution)/shard_map/all_to_all | solution.py:1106
  622.7 46.8 %collective-permute-start.65 = (bf16[5,1280,128]{2,1,0:T(8,128)(2,1)}, bf16[5,1280,128]{2,1,0:T(8,128)(2,1)}, u32[]{:S(2)}, u32[]{:S(2)}) collective-permute-start(bf16[5,1280,128]{2,1,0:T(8,128)(2,1)} %get-tuple-element.161.refs_1_), channel_id=1, source_target_pairs={{0,1},{1,0},{2,3},{3,2},{4,5},{5,4},{6,7},{7,6},{8,9},{9,8},{10,11... | collective-permute-start | bytes 4915208 | tf_op jit(solution)/shard_map/ppermute | solution.py:76
  625.4 44.2 %collective-permute-start.66 = (bf16[5,128,1280]{2,1,0:T(8,128)(2,1)}, bf16[5,128,1280]{2,1,0:T(8,128)(2,1)}, u32[]{:S(2)}, u32[]{:S(2)}) collective-permute-start(bf16[5,128,1280]{2,1,0:T(8,128)(2,1)} %get-tuple-element.162.refs_3_), channel_id=1, source_target_pairs={{0,1},{1,0},{2,3},{3,2},{4,5},{5,4},{6,7},{7,6},{8,9},{9,8},{10,11... | collective-permute-start | bytes 4915208 | tf_op jit(solution)/shard_map/ppermute | solution.py:76
  641.1 20.5 %all-to-all-start.7 = ((bf16[64,32,128]{2,1,0:T(8,128)(2,1)}), bf16[64,32,128]{2,1,0:T(8,128)(2,1)S(1)}, u32[]{:S(2)}, u32[]{:S(2)}) async-start(bf16[64,32,128]{2,1,0:T(8,128)(2,1)} %broadcast_in_dim.62), calls=%async_computation.7 | async-start | bytes 1048576 | tf_op jit(solution)/shard_map/all_to_all | solution.py:1124
  (131 other events, 1019.1 us)
Sparse Core Ops, SparseCore 0:
  52.2 128.8 all-gather.8
  183.2 105.3 all-gather.10
  489.1 68.0 all-gather.14
  558.7 60.0 all-gather.12
